TPU v7x, 32 devices: a whole 2x2x4 slice. The times are simulated.
32 devices in a mesh: lat: 4 (over z), lon: 8 (over y, x, core).
Axes of the slice: x: 2, y: 2, z: 4, core: 2. Of those that a mesh axis runs over, the one named last changes fastest.
Arguments:
- atm_flux: bfloat16 [8, 256, 1024], P(None, 'lat', 'lon'), may hold values from -6 to 6
- sea_mask: int32 [256, 1024], P('lat', 'lon'), may hold values 0 or 1
- src_block: int32 [8192], P(('lat', 'lon')), may hold values from 0 to 63
- dest_dev: int32 [8192, 1], P(('lat', 'lon')), may hold values from 0 to 31; in each aligned block of 256 rows (0 to 255, 256 to 511, ...) at most 16 rows name the same one
- dest_block: int32 [8192], P(('lat', 'lon')), may hold values from 0 to 31
- intersection_weights: bfloat16 [8192, 128, 128], P(('lat', 'lon')), may hold values from -0.5 to 0.5
- coupling: float32 [4, 8], replicated, may hold values from -2 to 2
- inverses: float32 [4, 128, 8, 80, 80], P(None, 'lat', 'lon'), may hold values from -2 to 2
- ocean_state: float32 [4, 80, 128, 1024], P(None, None, 'lat', 'lon'), may hold values from -6 to 6
- depth_levels: int32 [128, 1024], P('lat', 'lon'), may hold values from 0 to 80
Outputs:
- ocean_out: float32 [4, 80, 128, 1024], P(None, None, 'lat', 'lon')
Inputs may be any that keep to these rules, and one draw needn't show every extreme that they name: `dest_dev`: among the 256 pairs of one device no destination device is named more than 16 times, and in every draw some device names one destination exactly 16 times.
All inputs are finite; a program needn't handle non-finite values. No bound on the sum of `sea_mask` on one device may be relied on, other than what follows from the above.
Results may differ from a plain program's by a relative error of at most 0.0003.
Values sent between devices are 32-bit elements; how exact they have to be, the bound alone decides.
No kernel may reach another device: no remote copies, remote signals or barrier semaphores. Data moves between devices by JAX's collectives and lax.ppermute only.
A program may use at most 128 MiB of HBM per device.

v0:
```python
import jax
import jax.numpy as jnp
from jax import lax
from jax.sharding import PartitionSpec as P

diffusion_rate = 0.2


def padded_2(cells, sides, width):
    for axis, dim in sides:
        count = lax.axis_size(axis)
        head = lax.slice_in_dim(cells, 0, width, axis=dim)
        tail = lax.slice_in_dim(cells, cells.shape[dim] - width, cells.shape[dim], axis=dim)
        cells = jnp.concatenate(
            [
                lax.ppermute(tail, axis, [(i, (i + 1) % count) for i in range(count)]),
                cells,
                lax.ppermute(head, axis, [((i + 1) % count, i) for i in range(count)]),
            ],
            axis=dim,
        )
    return cells


def on_device(
    atm_flux,
    sea_mask,
    src_block,
    dest_dev,
    dest_block,
    intersection_weights,
    coupling,
    inverses,
    ocean_state,
    depth_levels,
):
    lat_count = lax.axis_size("lat")
    blocks_dev = ocean_state.shape[2]
    depth_pad = padded_2(depth_levels, (("lat", 0), ("lon", 1)), 1)
    masked = atm_flux * sea_mask.astype(jnp.bfloat16)
    picked = jnp.take(masked, src_block, axis=1)
    contrib = jnp.einsum(
        "fka,kao->kfo", picked, intersection_weights, preferred_element_type=jnp.float32
    )
    tile_shape = contrib.shape[1:]
    destination = dest_dev[:, 0]
    target = destination * blocks_dev + dest_block
    inside = (target >= 0) & (target < blocks_dev * lax.axis_size(("lat", "lon")))
    placed = jnp.where(inside, target, blocks_dev * lax.axis_size(("lat", "lon")))
    received = lax.psum_scatter(
        jnp.zeros((blocks_dev * lax.axis_size(("lat", "lon")),) + tile_shape, jnp.float32)
        .at[placed]
        .add(contrib, mode="drop"),
        ("lat", "lon"),
        scatter_dimension=0,
        tiled=True,
    )
    forcing = jnp.einsum("qf,rfo->qro", coupling, received, precision=lax.Precision.HIGHEST)
    level_ids = jnp.arange(ocean_state.shape[1], dtype=jnp.int32)[:, None, None]
    active = level_ids < depth_levels[None]
    surface = ocean_state[:, 0] + forcing
    rhs = jnp.concatenate([surface[:, None], ocean_state[:, 1:]], axis=1)
    rhs = jnp.where(active[None], rhs, jnp.float32(0.0))
    solved = jnp.einsum("qrlm,qmrx->qlrx", inverses[:, :, 0], rhs, precision=lax.Precision.HIGHEST)
    mixed = jnp.where(active[None], solved, ocean_state)
    padded = padded_2(mixed, (("lat", 2), ("lon", 3)), 1)
    lat_here = lax.axis_index("lat")
    row_ids = jnp.arange(blocks_dev + 2, dtype=jnp.int32)
    band_edge = (row_ids == 0) & (lat_here == 0) | (row_ids == blocks_dev + 1) & (
        lat_here == lat_count - 1
    )
    depth_pad = jnp.where(band_edge[:, None], 0, depth_pad)
    active_pad = level_ids < depth_pad[None]
    neighbours = [
        (padded[:, :, 1:-1, 2:], active_pad[:, 1:-1, 2:]),
        (padded[:, :, 1:-1, :-2], active_pad[:, 1:-1, :-2]),
        (padded[:, :, 2:, 1:-1], active_pad[:, 2:, 1:-1]),
        (padded[:, :, :-2, 1:-1], active_pad[:, :-2, 1:-1]),
    ]
    total = jnp.zeros_like(mixed)
    for values, flags in neighbours:
        total = total + jnp.where(flags[None], values - mixed, jnp.float32(0.0))
    return mixed + diffusion_rate * jnp.where(active[None], total, jnp.float32(0.0))


def solution(mesh):
    placed = (
        P(None, "lat", "lon"),
        P("lat", "lon"),
        P(("lat", "lon")),
        P(("lat", "lon"), None),
        P(("lat", "lon")),
        P(("lat", "lon"), None, None),
        P(),
        P(None, "lat", "lon", None, None),
        P(None, None, "lat", "lon"),
        P("lat", "lon"),
    )
    return jax.shard_map(
        on_device,
        mesh=mesh,
        in_specs=placed,
        out_specs=P(None, None, "lat", "lon"),
        check_vma=False,
    )
```

profile of v0, /device:TPU:0, one launch (start us, length us, event | category | flops | bytes accessed | tf_op | source)
XLA Modules:
  0.0 260.1 jit_solution(10069298703118464648)
XLA Ops:
  6.5 0.7 compare_select_fusion
  7.2 0.7 compare_and_fusion
  7.9 0.7 broadcast_multiply_fusion
  8.6 0.8 convert_element_type.3
  9.4 0.7 compare_select_fusion.1
  10.1 1.0 copy_multiply_fusion
  11.0 0.8 gather_fusion
  11.9 4.7 %fusion.24 = f32[256,8,128]{2,1,0:T(8,128)S(1)} fusion(bf16[256,128,128]{2,1,0:T(8,128)(2,1)} %param.15, bf16[256,8,128]{2,1,0:T(8,128)(2,1)S(1)} %gather_fusion, pred[256]{0:T(512)(128)(4,1)S(1)} %compare_and_fusion), kind=kOutput, calls=%fused_computation.38 | convolution fusion | flops 67371008 | bytes 9961728 | tf_op jit(solution)/shard_map/fka,kao->kfo/dot_general | solution.py:42
  16.6 2.2 broadcast_in_dim.94
  18.8 25.1 %scatter_fusion = f32[1024,8,128]{2,1,0:T(8,128)} fusion(f32[1024,8,128]{2,1,0:T(8,128)} %broadcast_in_dim.94, s32[256]{0:T(256)S(1)} %compare_select_fusion.1, f32[256,8,128]{2,1,0:T(8,128)S(1)} %fusion.24), kind=kCustom, calls=%fused_computation.1 | custom fusion | flops 262144 | bytes 3146752 | tf_op jit(solution)/shard_map/scatter-add | solution.py:53
  44.0 5.1 %collective-permute-start.1 = (s32[1,128]{1,0:T(1,128)S(1)}, s32[1,128]{1,0:T(1,128)S(1)}, u32[]{:S(2)}, u32[]{:S(2)}) collective-permute-start(s32[1,128]{1,0:T(1,128)S(1)} %get-tuple-element.16), channel_id=1, source_target_pairs={{8,0},{16,8},{24,16},{0,24},{9,1},{17,9},{25,17},{1,25},{10,2},{18... | collective-permute-start | bytes 1544 | tf_op jit(solution)/shard_map/ppermute | solution.py:18
  49.1 0.2 iota_compare_fusion.1
  49.3 1.1 collective-permute-done.1
  50.4 4.0 %collective-permute-done = s32[1,128]{1,0:T(1,128)S(1)} collective-permute-done((s32[1,128]{1,0:T(1,128)S(1)}, s32[1,128]{1,0:T(1,128)S(1)}, u32[]{:S(2)}, u32[]{:S(2)}) %collective-permute-start) | collective-permute-done | bytes 544 | tf_op jit(solution)/shard_map/ppermute | solution.py:16
  54.5 0.5 collective-permute-start.3
  55.0 5.4 %copy.38 = f32[4,79,32,128]{3,1,2,0:T(8,128)} copy(f32[4,79,32,128]{3,2,1,0:T(8,128)S(1)} %slice-done) | data formatting | bytes 10354688
  60.5 127.2 %reduce-scatter.2.cloned.1.call-done = f32[32,8,128]{2,1,0:T(8,128)} async-done(((f32[1024,8,128]{2,1,0:T(8,128)}), f32[32,8,128]{2,1,0:T(8,128)}) %reduce-scatter.2.cloned.1.call-update) | async-done | bytes 131088 | tf_op jit(solution)/shard_map/reduce_scatter | solution.py:50
  187.8 1.2 fusion.23
  189.0 13.7 %bitcast_select_fusion = f32[4,80,32,128]{3,1,2,0:T(8,128)S(1)} fusion(pred[80,32,128]{2,0,1:T(8,128)(4,1)S(1)} %iota_compare_fusion.1, f32[4,32,1,80,80]{4,3,2,1,0:T(8,128)} %param.17, f32[4,79,32,128]{3,1,2,0:T(8,128)} %copy.38, f32[4,1,32,128]{3,1,2,0:T(1,128)S(1)} %copy.25, f32[4,80,32,128]{3,2,1,0:T(8,128)} %param.18), kind=kOutput, calls=%fused_computation.29 | convolution fusion | flops 1262223360 | bytes 19333120 | tf_op jit(solution)/shard_map/qrlm,qmrx->qlrx/dot_general | solution.py:64
  202.8 3.8 %collective-permute-start.5 = (f32[4,80,1,128]{3,1,2,0:T(8,128)S(1)}, f32[4,80,1,128]{3,1,2,0:T(8,128)S(1)}, u32[]{:S(2)}, u32[]{:S(2)}) collective-permute-start(f32[4,80,1,128]{3,1,2,0:T(8,128)S(1)} %get-tuple-element.7), channel_id=1, source_target_pairs={{8,0},{16,8},{24,16},{0,24},{9,1},{17,9},{25,17},{1,25},{10,2},{18... | collective-permute-start | bytes 491528 | tf_op jit(solution)/shard_map/ppermute | solution.py:18
  206.7 0.4 iota_compare_fusion
  207.0 3.0 %collective-permute-done.4 = f32[4,80,1,128]{3,1,2,0:T(8,128)S(1)} collective-permute-done((f32[4,80,1,128]{3,1,2,0:T(8,128)S(1)}, f32[4,80,1,128]{3,1,2,0:T(8,128)S(1)}, u32[]{:S(2)}, u32[]{:S(2)}) %collective-permute-start.4) | collective-permute-done | bytes 163872 | tf_op jit(solution)/shard_map/ppermute | solution.py:16
  210.2 0.4 pad_maximum_fusion
  210.6 6.0 %fusion.33 = (f32[4,80,34,1]{3,1,2,0:T(8,128)}, f32[4,80,34,1]{3,1,2,0:T(8,128)}) fusion(f32[4,80,34,128]{3,1,2,0:T(8,128)S(1)} %pad_maximum_fusion), kind=kLoop, calls=%fused_computation.58 | loop fusion | bytes 174080 | tf_op jit(solution)/shard_map/slice | solution.py:12
  216.7 3.5 %copy.29 = f32[4,80,34,1]{1,0,3,2:T(4,128)S(1)} copy(f32[4,80,34,1]{3,1,2,0:T(8,128)} %get-tuple-element.6) | data formatting | bytes 87040 | tf_op jit(solution)/shard_map/slice | solution.py:13
  220.2 3.5 %copy.27 = f32[4,80,34,1]{1,0,3,2:T(4,128)S(1)} copy(f32[4,80,34,1]{3,1,2,0:T(8,128)} %get-tuple-element.5) | data formatting | bytes 87040 | tf_op jit(solution)/shard_map/slice | solution.py:12
  223.8 2.7 %collective-permute-start.6 = (f32[4,80,34,1]{1,0,3,2:T(4,128)S(1)}, f32[4,80,34,1]{1,0,3,2:T(4,128)S(1)}, u32[]{:S(2)}, u32[]{:S(2)}) collective-permute-start(f32[4,80,34,1]{1,0,3,2:T(4,128)S(1)} %copy.27), channel_id=1, source_target_pairs={{1,0},{2,1},{3,2},{4,3},{5,4},{6,5},{7,6},{0,7},{9,8},{10,9},{11,1... | collective-permute-start | bytes 130568 | tf_op jit(solution)/shard_map/ppermute | solution.py:18
  226.4 1.1 fusion.35
  227.6 3.3 %copy.30 = f32[4,80,34,1]{3,1,2,0:T(8,128)} copy(f32[4,80,34,1]{1,0,3,2:T(4,128)S(1)} %collective-permute-done.7) | data formatting | bytes 87040 | tf_op jit(solution)/shard_map/ppermute | solution.py:16
  230.8 3.3 %copy.28 = f32[4,80,34,1]{3,1,2,0:T(8,128)} copy(f32[4,80,34,1]{1,0,3,2:T(4,128)S(1)} %collective-permute-done.6) | data formatting | bytes 87040 | tf_op jit(solution)/shard_map/ppermute | solution.py:18
  234.2 15.1 %fusion.5 = f32[4,80,32,128]{3,1,2,0:T(8,128)S(1)} fusion(f32[4,80,32,128]{3,1,2,0:T(8,128)} %copy-done.2, f32[4,80,1,128]{3,1,2,0:T(8,128)S(1)} %collective-permute-done.4, f32[4,80,1,128]{3,1,2,0:T(8,128)S(1)} %collective-permute-done.5, f32[4,80,34,1]{3,1,2,0:T(8,128)} %copy.30, f32[4,80,34,1]{3,1,2,0:T(8,128)} %copy.28, ...), kind=kLoop, calls=%fused_computation.9 | loop fusion | flops 28835840 | bytes 12538880 | tf_op jit(solution)/shard_map/add | solution.py:83
  249.3 4.0 %copy.31 = f32[4,80,32,128]{3,2,1,0:T(8,128)} copy(f32[4,80,32,128]{3,1,2,0:T(8,128)S(1)} %fusion.5) | data formatting | bytes 10485760 | tf_op jit(solution)/shard_map/add | solution.py:83
  (31 shorter events, 0.6 us)
Async XLA Ops:
  6.5 181.2 %copy-start = (f32[4,8]{1,0:T(4,128)S(1)}, f32[4,8]{1,0:T(4,128)}, u32[]{:S(2)}) copy-start(f32[4,8]{1,0:T(4,128)} %param.16) | copy-start | bytes 388
  6.5 181.2 %reduce-scatter.2.cloned.1.call-start = ((), (), s32[]{:S(2)}) async-start(), calls=%async_computation.1 | async-start | bytes 4325376 | tf_op jit(solution)/shard_map/reduce_scatter | solution.py:50
  16.6 27.4 %copy-start.3 = (s32[32,128]{1,0:T(8,128)S(1)}, s32[32,128]{1,0:T(8,128)}, u32[]{:S(2)}) copy-start(s32[32,128]{1,0:T(8,128)} %param.19) | copy-start | bytes 49156
  44.0 6.4 %collective-permute-start.1 = (s32[1,128]{1,0:T(1,128)S(1)}, s32[1,128]{1,0:T(1,128)S(1)}, u32[]{:S(2)}, u32[]{:S(2)}) collective-permute-start(s32[1,128]{1,0:T(1,128)S(1)} %get-tuple-element.16), channel_id=1, source_target_pairs={{8,0},{16,8},{24,16},{0,24},{9,1},{17,9},{25,17},{1,25},{10,2},{18... | collective-permute-start | bytes 1544 | tf_op jit(solution)/shard_map/ppermute | solution.py:18
  49.1 5.3 %collective-permute-start = (s32[1,128]{1,0:T(1,128)S(1)}, s32[1,128]{1,0:T(1,128)S(1)}, u32[]{:S(2)}, u32[]{:S(2)}) collective-permute-start(s32[1,128]{1,0:T(1,128)S(1)} %get-tuple-element.15), channel_id=1, source_target_pairs={{0,8},{8,16},{16,24},{24,0},{1,9},{9,17},{17,25},{25,1},{2,10},{10... | collective-permute-start | bytes 1544 | tf_op jit(solution)/shard_map/ppermute | solution.py:16
  49.3 5.8 %slice-start = ((f32[4,80,32,128]{3,2,1,0:T(8,128)}), f32[4,79,32,128]{3,2,1,0:T(8,128)S(1)}, s32[]{:S(2)}) async-start(f32[4,80,32,128]{3,2,1,0:T(8,128)} %param.18), calls=%async_computation.2 | async-start | bytes 10354688 | tf_op jit(solution)/shard_map/slice | solution.py:62
  54.5 5.9 %collective-permute-start.3 = (s32[34,1]{1,0:T(8,128)S(1)}, s32[34,1]{1,0:T(8,128)S(1)}, u32[]{:S(2)}, u32[]{:S(2)}) collective-permute-start(s32[34,1]{1,0:T(8,128)S(1)} %get-tuple-element.14), channel_id=1, source_target_pairs={{1,0},{2,1},{3,2},{4,3},{5,4},{6,5},{7,6},{0,7},{9,8},{10,9},{11,1... | collective-permute-start | bytes 416 | tf_op jit(solution)/shard_map/ppermute | solution.py:18
  55.0 132.7 %slice-start.1 = ((f32[4,80,32,128]{3,2,1,0:T(8,128)}), f32[4,1,32,128]{3,2,1,0:T(8,128)S(1)}, s32[]{:S(2)}) async-start(f32[4,80,32,128]{3,2,1,0:T(8,128)} %param.18), calls=%async_computation.3 | async-start | bytes 131072 | tf_op jit(solution)/shard_map/slice | solution.py:61
  55.0 5.4 %collective-permute-start.2 = (s32[34,1]{1,0:T(8,128)S(1)}, s32[34,1]{1,0:T(8,128)S(1)}, u32[]{:S(2)}, u32[]{:S(2)}) collective-permute-start(s32[34,1]{1,0:T(8,128)S(1)} %get-tuple-element.13), channel_id=1, source_target_pairs={{0,1},{1,2},{2,3},{3,4},{4,5},{5,6},{6,7},{7,0},{8,9},{9,10},{10,1... | collective-permute-start | bytes 416 | tf_op jit(solution)/shard_map/ppermute | solution.py:16
  202.7 7.4 %copy-start.2 = (f32[4,80,32,128]{3,1,2,0:T(8,128)}, f32[4,80,32,128]{3,1,2,0:T(8,128)S(1)}, u32[]{:S(2)}) copy-start(f32[4,80,32,128]{3,1,2,0:T(8,128)S(1)} %bitcast_select_fusion) | copy-start | bytes 15728644
  202.8 7.3 %collective-permute-start.4 = (f32[4,80,1,128]{3,1,2,0:T(8,128)S(1)}, f32[4,80,1,128]{3,1,2,0:T(8,128)S(1)}, u32[]{:S(2)}, u32[]{:S(2)}) collective-permute-start(f32[4,80,1,128]{3,1,2,0:T(8,128)S(1)} %get-tuple-element.8), channel_id=1, source_target_pairs={{0,8},{8,16},{16,24},{24,0},{1,9},{9,17},{17,25},{25,1},{2,10},{10... | collective-permute-start | bytes 491528 | tf_op jit(solution)/shard_map/ppermute | solution.py:16
  202.8 7.3 %collective-permute-start.5 = (f32[4,80,1,128]{3,1,2,0:T(8,128)S(1)}, f32[4,80,1,128]{3,1,2,0:T(8,128)S(1)}, u32[]{:S(2)}, u32[]{:S(2)}) collective-permute-start(f32[4,80,1,128]{3,1,2,0:T(8,128)S(1)} %get-tuple-element.7), channel_id=1, source_target_pairs={{8,0},{16,8},{24,16},{0,24},{9,1},{17,9},{25,17},{1,25},{10,2},{18... | collective-permute-start | bytes 491528 | tf_op jit(solution)/shard_map/ppermute | solution.py:18
  220.2 7.4 %collective-permute-start.7 = (f32[4,80,34,1]{1,0,3,2:T(4,128)S(1)}, f32[4,80,34,1]{1,0,3,2:T(4,128)S(1)}, u32[]{:S(2)}, u32[]{:S(2)}) collective-permute-start(f32[4,80,34,1]{1,0,3,2:T(4,128)S(1)} %copy.29), channel_id=1, source_target_pairs={{0,1},{1,2},{2,3},{3,4},{4,5},{5,6},{6,7},{7,0},{8,9},{9,10},{10,1... | collective-permute-start | bytes 130568 | tf_op jit(solution)/shard_map/ppermute | solution.py:16
  223.8 7.1 %collective-permute-start.6 = (f32[4,80,34,1]{1,0,3,2:T(4,128)S(1)}, f32[4,80,34,1]{1,0,3,2:T(4,128)S(1)}, u32[]{:S(2)}, u32[]{:S(2)}) collective-permute-start(f32[4,80,34,1]{1,0,3,2:T(4,128)S(1)} %copy.27), channel_id=1, source_target_pairs={{1,0},{2,1},{3,2},{4,3},{5,4},{6,5},{7,6},{0,7},{9,8},{10,9},{11,1... | collective-permute-start | bytes 130568 | tf_op jit(solution)/shard_map/ppermute | solution.py:18
  234.2 19.1 %copy-start.1 = (f32[4,8]{1,0:T(4,128)S(1)}, f32[4,8]{1,0:T(4,128)}, u32[]{:S(2)}) copy-start(f32[4,8]{1,0:T(4,128)} %param.16) | copy-start | bytes 388
Sparse Core Ops, SparseCore 0:
  44.1 143.5 reduce-scatter.1
where the time goes:
time: 261 us; the launch traced here: 260 us
  waiting for transfers between devices  135 us (52%)
  other arithmetic  45.8 us (18%)
  local copies, waits for them, and re-layouts  33.4 us (13%)
  matrix products  19.6 us (8%)
  between operations  13.6 us (5%)
  starting transfers between devices  12.2 us (5%)
    reduce_scatter x1, waiting for transfers between devices, on_device(): lax.psum_scatter(jnp.zeros((blocks_dev * lax.axis_size(('lat', 'lon')),)...  127 us
    scatter-add x1, other arithmetic, on_device(): received = lax.psum_scatter(jnp.zeros((blocks_dev * lax.axis_size(('lat',...  25.1 us
    add x1, other arithmetic, on_device(): mixed + diffusion_rate * jnp.where(active[None], total, jnp.float32(0.0))  15.1 us
    dot_general x1, matrix products, on_device(): jnp.einsum('qrlm,qmrx->qlrx', inverses[:, :, 0], rhs, precision=lax.Preci...  13.7 us
    ppermute x4, starting transfers between devices, padded_2(): lax.ppermute(head, axis, [((i + 1) % count, i) for i in range(count)])  12.1 us
    slice x3, local copies, waits for them, and re-layouts, padded_2(): head = lax.slice_in_dim(cells, 0, width, axis=dim)  9.59 us
    ppermute x4, waiting for transfers between devices, padded_2(): lax.ppermute(tail, axis, [(i, (i + 1) % count) for i in range(count)])  7.08 us
    unnamed x9, local copies, waits for them, and re-layouts  5.38 us
  transfers between devices with their start and end apart: 9, of which 5 were waited for; matrix products, arithmetic and copies ran while one was open for 5% of the time, Pallas kernels for 0%

commit v1 on v0

v1 whole, which is shorter than its diff:
```python
import functools

import jax
import jax.numpy as jnp
from jax import lax
from jax.experimental import pallas as pl
from jax.experimental.pallas import tpu as pltpu
from jax.sharding import PartitionSpec as P

diffusion_rate = 0.2
LANES = 128
SUB = 8
f32 = jnp.float32
bf16 = jnp.bfloat16


def split(x):
    high = x.astype(bf16)
    return high, (x - high.astype(f32)).astype(bf16)


def iota(shape, dim):
    return lax.broadcasted_iota(jnp.int32, shape, dim)


def regrid_kernel(cap, batch, unroll, src, dev, blk, coupling, atm, mask, weights, out, rows, count):
    step = pl.program_id(0)
    fluxes, atm_rows, _ = atm.shape
    fields = coupling.shape[0]
    devices = out.shape[0]

    @pl.when(step == 0)
    def _():
        def clear(d, carry):
            count[d] = 0
            out[d, 0 : fields * cap] = jnp.zeros((fields * cap, LANES), f32)
            out[d, fields * cap :] = jnp.full((SUB, LANES), -1.0, f32)
            return carry

        lax.fori_loop(0, devices, clear, 0)
        for tile in range(atm_rows // 16):
            here = slice(tile * 16, tile * 16 + 16)
            sea = mask[here, :].astype(f32)
            flux = [atm[f, here, :].astype(f32) * sea for f in range(fluxes)]
            for q in range(fields):
                total = coupling[q, 0] * flux[0]
                for f in range(1, fluxes):
                    total = total + coupling[q, f] * flux[f]
                high = total.astype(bf16).astype(f32)
                rows[pl.ds(tile * 16 * SUB + q, 16, stride=SUB), :] = high
                rows[pl.ds(tile * 16 * SUB + fields + q, 16, stride=SUB), :] = total - high

    lane = iota((1, LANES), 1) % cap

    def some(k, carry):
        for u in range(unroll):
            n = k * unroll + u
            p = step * batch + n
            d = dev[p]
            slot = jnp.minimum(count[d], cap - 1)
            count[d] = slot + 1
            x = rows[pl.ds(pl.multiple_of(src[p] * SUB, SUB), SUB), :].astype(bf16)
            both = jnp.dot(x, weights[n], preferred_element_type=f32)
            total = both[0:fields] + both[fields : 2 * fields]
            for q in range(fields):
                out[d, pl.ds(q * cap + slot, 1), :] = total[q : q + 1]
            ids = out[d, pl.ds(fields * cap, 1), :]
            out[d, pl.ds(fields * cap, 1), :] = jnp.where(lane == slot, blk[p].astype(f32), ids)
        return carry

    lax.fori_loop(0, batch // unroll, some, 0)


def regrid(cap, devices, src, dev, blk, coupling, atm, mask, weights):
    pairs, depth, width = weights.shape
    fields = coupling.shape[0]
    batch = 32
    whole = pl.BlockSpec(memory_space=pltpu.VMEM)
    smem = pl.BlockSpec(memory_space=pltpu.SMEM)
    tall = fields * cap + SUB
    return pl.pallas_call(
        functools.partial(regrid_kernel, cap, batch, 8),
        grid=(pairs // batch,),
        in_specs=[smem, smem, smem, smem, whole, whole, pl.BlockSpec((batch, depth, width), lambda s: (s, 0, 0))],
        out_specs=pl.BlockSpec((devices, tall, LANES), lambda s: (0, 0, 0)),
        out_shape=jax.ShapeDtypeStruct((devices, tall, LANES), f32),
        scratch_shapes=[
            pltpu.VMEM((atm.shape[1] * SUB, LANES), f32),
            pltpu.SMEM((devices,), jnp.int32),
        ],
        compiler_params=pltpu.CompilerParams(vmem_limit_bytes=24 << 20),
        cost_estimate=pl.CostEstimate(flops=2 * 8 * pairs * depth * width, bytes_accessed=10 << 20, transcendentals=0),
        name="regrid",
    )(src, dev, blk, coupling, atm, mask, weights)


def mix_kernel(depth_ref, state, inv, mixed, north, south, side):
    chunk = pl.program_id(1)
    chunks = pl.num_programs(1)
    levels = state.shape[1]
    oy = depth_ref.shape[0]
    flat = state.reshape(levels * SUB, LANES)
    level = iota((levels, LANES), 0)
    lane = iota((levels, LANES), 1)

    def message(ref, value, depth_row, matrix):
        ref[0, 0:levels] = value
        square = jnp.concatenate([matrix, jnp.zeros((levels, LANES - levels), f32)], axis=1)
        square = jnp.concatenate([square, jnp.zeros((LANES - levels, LANES), f32)], axis=0)
        first = square.T[0:1]
        ref[0, levels : levels + SUB] = jnp.concatenate(
            [depth_row.astype(f32), first, jnp.zeros((SUB - 2, LANES), f32)], axis=0
        )

    @pl.when(chunk == 0)
    def _():
        side[0, 0:levels] = jnp.zeros((levels, LANES), f32)
        turned = jnp.concatenate([depth_ref[...].astype(f32), jnp.zeros((LANES - oy, LANES), f32)], axis=0).T
        edge = turned[0:1] + pltpu.roll(turned[LANES - SUB :], oy, 1)[SUB - 1 : SUB]
        side[0, levels : levels + SUB] = jnp.broadcast_to(edge, (SUB, LANES))

    depth = depth_ref[pl.ds(pl.multiple_of(chunk * SUB, SUB), SUB), :]
    edges = side[0, 0:levels]
    for i in range(SUB):
        active = level < depth[i : i + 1]
        x = flat[pl.ds(i, levels, stride=SUB), :]
        a = inv[0, i, 0]
        a_high, a_low = split(a)
        r_high, r_low = split(jnp.where(active, x, 0.0))
        product = jnp.dot(
            jnp.concatenate([a_high, a_low], axis=0),
            jnp.concatenate([r_high, r_low], axis=1),
            preferred_element_type=f32,
        )
        solved = product[:levels, :LANES] + (product[levels:, :LANES] + product[:levels, LANES:])
        m = jnp.where(active, solved, x)
        mixed[0, i] = m
        row = chunk * SUB + i
        edges = jnp.where(lane == row, m[:, 0:1], edges)
        edges = jnp.where(lane == oy + row, m[:, LANES - 1 : LANES], edges)
        edges = jnp.where(lane == 2 * oy + row, a[:, 0:1], edges)
        if i == 0:

            @pl.when(chunk == 0)
            def _():
                message(north, m, depth[0:1], a)

        if i == SUB - 1:

            @pl.when(chunk == chunks - 1)
            def _():
                message(south, m, depth[SUB - 1 : SUB], a)

    side[0, 0:levels] = edges


def mix(depth, state, inverses):
    fields, levels, oy, ox = state.shape
    edge = pl.BlockSpec((1, levels + SUB, ox), lambda q, c: (q, 0, 0))
    edge_shape = jax.ShapeDtypeStruct((fields, levels + SUB, ox), f32)
    return pl.pallas_call(
        mix_kernel,
        grid=(fields, oy // SUB),
        in_specs=[
            pl.BlockSpec(memory_space=pltpu.VMEM),
            pl.BlockSpec((1, levels, SUB, ox), lambda q, c: (q, 0, c, 0)),
            pl.BlockSpec((1, SUB, 1, levels, levels), lambda q, c: (q, c, 0, 0, 0)),
        ],
        out_specs=[pl.BlockSpec((1, SUB, levels, ox), lambda q, c: (q, c, 0, 0)), edge, edge, edge],
        out_shape=[jax.ShapeDtypeStruct((fields, oy, levels, ox), f32), edge_shape, edge_shape, edge_shape],
        compiler_params=pltpu.CompilerParams(vmem_limit_bytes=24 << 20),
        cost_estimate=pl.CostEstimate(flops=2 * 4 * fields * oy * levels * levels * ox, bytes_accessed=16 << 20, transcendentals=0),
        name="mix",
    )(depth, state, inverses)


def gather_kernel(cap, fields, oy, recv, forcing, edges):
    devices = recv.shape[0]
    group = LANES // cap
    lane = iota((1, LANES), 1) // cap
    row = iota((oy, LANES), 0).astype(f32)
    totals = [jnp.zeros((oy, LANES), f32) for _ in range(fields)]
    for tile in range(devices // group):
        ids = jnp.full((1, LANES), -1.0, f32)
        for s in range(group):
            ids = jnp.where(lane == s, recv[tile * group + s, fields * cap : fields * cap + 1, :], ids)
        hot = (row == ids).astype(f32).astype(bf16)
        for q in range(fields):
            x = jnp.concatenate(
                [recv[tile * group + s, q * cap : (q + 1) * cap, :] for s in range(group)], axis=0
            )
            high, low = split(x)
            totals[q] = totals[q] + (
                jnp.dot(hot, high, preferred_element_type=f32) + jnp.dot(hot, low, preferred_element_type=f32)
            )
    everything = jnp.concatenate(totals, axis=0)
    forcing[...] = everything
    turned = everything.T
    edges[...] = jnp.concatenate(
        [t[0:1] for t in totals]
        + [t[oy - 1 : oy] for t in totals]
        + [turned[0:1], turned[LANES - 1 : LANES], jnp.zeros((2 * SUB - 2 * fields - 2, LANES), f32)],
        axis=0,
    )


def gather(cap, fields, oy, recv):
    whole = pl.BlockSpec(memory_space=pltpu.VMEM)
    return pl.pallas_call(
        functools.partial(gather_kernel, cap, fields, oy),
        in_specs=[whole],
        out_specs=[whole, whole],
        out_shape=[jax.ShapeDtypeStruct((fields * oy, LANES), f32), jax.ShapeDtypeStruct((2 * SUB, LANES), f32)],
        compiler_params=pltpu.CompilerParams(vmem_limit_bytes=24 << 20),
        name="gather",
    )(recv)


def finish_kernel(
    depth_ref, forcing, own, mixed, above, below, north, south, east, west, g_north, g_south, g_east, g_west,
    out, z_above, z_below, z_east, z_west, column, bounds,
):
    chunk = pl.program_id(0)
    chunks = pl.num_programs(0)
    fields, _, levels, _ = mixed.shape
    oy = depth_ref.shape[0]
    level = iota((levels, LANES), 0)
    lanes = iota((SUB, LANES), 1)
    start = chunk * SUB
    flat = out.reshape(fields * levels * SUB, LANES)

    def outer_row(ref, g_ref, first):
        return ref[0, levels : levels + 1, :].astype(jnp.int32)

    def from_neighbour(target, ref, g_ref, first):
        names = jnp.concatenate(
            [ref[q, levels + 1 : levels + 2, :] for q in range(fields)]
            + [jnp.zeros((LANES - fields, LANES), f32)],
            axis=0,
        ).T
        active = level < outer_row(ref, g_ref, first)
        for q in range(fields):
            value = ref[q, 0:levels] + names[0:levels, q : q + 1] * g_ref[first + q : first + q + 1, :]
            target[q] = jnp.where(active, value, 0.0)

    def from_here(target, ref, row):
        active = level < depth_ref[pl.ds(row, 1), :]
        for q in range(fields):
            a = pltpu.roll(own[q, 0:levels], 2 * LANES - (2 * oy + row), 1)
            value = ref[q, 0] + a[:, 0:1] * forcing[pl.ds(q * oy + row, 1), :]
            target[q] = jnp.where(active, value, 0.0)

    @pl.when(chunk == 0)
    def _():
        from_neighbour(z_above, north, g_north, fields)
        for target, ref, g_ref, line, place in (
            (z_east, east, g_east, 2 * fields, 0),
            (z_west, west, g_west, 2 * fields + 1, oy),
        ):
            shift = (LANES - place) % LANES
            depth = ref[0, levels : levels + SUB, :]
            depth = pltpu.roll(depth, shift, 1) if shift else depth
            active = level < depth[0:1].astype(jnp.int32)
            line_all = jnp.broadcast_to(g_ref[line : line + 1, :], (SUB, LANES))
            for q in range(fields):
                value = ref[q, 0:levels]
                value = pltpu.roll(value, shift, 1) if shift else value
                a = pltpu.roll(ref[q, 0:levels], LANES - 2 * oy, 1)
                g = pltpu.roll(line_all, (LANES - q * oy) % LANES, 1) if q else line_all
                target[q] = jnp.where(active, value + a * g[0:1], 0.0)

    @pl.when(chunk > 0)
    def _():
        from_here(z_above, above, start - 1)
        for q in range(fields):
            z_east[q] = pltpu.roll(z_east[q], LANES - SUB, 1)
            z_west[q] = pltpu.roll(z_west[q], LANES - SUB, 1)

    @pl.when(chunk == chunks - 1)
    def _():
        from_neighbour(z_below, south, g_south, 0)

    @pl.when(chunk < chunks - 1)
    def _():
        from_here(z_below, below, start + SUB)

    for q in range(fields):
        column[q] = pltpu.roll(own[q, 0:levels], 2 * LANES - (2 * oy + start), 1)

    depth = depth_ref[pl.ds(pl.multiple_of(start, SUB), SUB), :]
    up = jnp.where(chunk == 0, outer_row(north, g_north, fields), depth_ref[pl.ds(jnp.maximum(start - 1, 0), 1), :])
    down = jnp.where(
        chunk == chunks - 1,
        outer_row(south, g_south, 0),
        depth_ref[pl.ds(jnp.minimum(start + SUB, oy - 1), 1), :],
    )
    def upright(ref, place):
        line = jnp.broadcast_to(ref[0, levels : levels + 1, :], (SUB, LANES))
        here = jnp.where(lanes == iota((SUB, LANES), 0) + place + start, line, 0.0)
        return jnp.sum(here, axis=1, keepdims=True).astype(jnp.int32)

    bounds[0] = jnp.where(lanes == LANES - 1, upright(east, 0), pltpu.roll(depth, LANES - 1, 1))
    bounds[1] = jnp.where(lanes == 0, upright(west, oy), pltpu.roll(depth, 1, 1))

    tile_level = iota((SUB, LANES), 0)

    def tile(t, carry):
        first = pl.multiple_of(t * SUB, SUB)
        here = pl.ds(first, SUB)
        lev = tile_level + first
        row_depth = [up] + [depth[i : i + 1] for i in range(SUB)] + [down]
        act = [lev < d for d in row_depth]
        one = [jnp.where(a, 1.0, 0.0) for a in act]
        scale, keep = [], []
        for i in range(SUB):
            sides = jnp.where(lev < bounds[0, i : i + 1], 1.0, 0.0) + jnp.where(lev < bounds[1, i : i + 1], 1.0, 0.0)
            scale.append(diffusion_rate * one[i + 1])
            keep.append(1.0 - scale[i] * ((one[i] + one[i + 2]) + sides))
        for q in range(fields):
            a = column[q, here, :]
            ze, zw = z_east[q, here, :], z_west[q, here, :]
            z, m = [z_above[q, here, :]], []
            for i in range(SUB):
                m0 = mixed[q, i, here, :]
                forced = m0 + a[:, i : i + 1] * forcing[pl.ds(q * oy + start + i, 1), :]
                z.append(jnp.where(act[i + 1], forced, 0.0))
                m.append(jnp.where(act[i + 1], forced, m0))
            z.append(z_below[q, here, :])
            for i in range(SUB):
                to_east = pltpu.roll(jnp.where(lanes == 0, ze[:, i : i + 1], z[i + 1]), LANES - 1, 1)
                to_west = pltpu.roll(jnp.where(lanes == LANES - 1, zw[:, i : i + 1], z[i + 1]), 1, 1)
                result = m[i] * keep[i] + scale[i] * ((z[i] + z[i + 2]) + (to_east + to_west))
                flat[pl.ds(q * levels * SUB + first * SUB + i, SUB, stride=SUB), :] = result
        return carry

    lax.fori_loop(0, levels // SUB, tile, 0)


def finish(depth, forcing, own, mixed, halos, g_halos):
    fields, oy, levels, ox = mixed.shape
    whole = pl.BlockSpec(memory_space=pltpu.VMEM)
    edge = pltpu.VMEM((fields, levels, ox), f32)
    return pl.pallas_call(
        finish_kernel,
        grid=(oy // SUB,),
        in_specs=[
            whole,
            whole,
            whole,
            pl.BlockSpec((fields, SUB, levels, ox), lambda c: (0, c, 0, 0)),
            pl.BlockSpec((fields, 1, levels, ox), lambda c: (0, jnp.maximum(c * SUB - 1, 0), 0, 0)),
            pl.BlockSpec((fields, 1, levels, ox), lambda c: (0, jnp.minimum(c * SUB + SUB, oy - 1), 0, 0)),
        ]
        + [whole] * 8,
        out_specs=pl.BlockSpec((fields, levels, SUB, ox), lambda c: (0, 0, c, 0)),
        out_shape=jax.ShapeDtypeStruct((fields, levels, oy, ox), f32),
        scratch_shapes=[edge, edge, edge, edge, edge, pltpu.VMEM((2, SUB, ox), jnp.int32)],
        compiler_params=pltpu.CompilerParams(vmem_limit_bytes=32 << 20),
        cost_estimate=pl.CostEstimate(flops=20 * fields * oy * levels * ox, bytes_accessed=12 << 20, transcendentals=0),
        name="finish",
    )(depth, forcing, own, mixed, mixed, mixed, *halos, *g_halos)


def shift(x, axis, step, wrap):
    count = lax.axis_size(axis)
    pairs = [(i, (i + step) % count) for i in range(count) if wrap or 0 <= i + step < count]
    return lax.ppermute(x, axis, pairs)


def on_device(
    atm_flux, sea_mask, src_block, dest_dev, dest_block, intersection_weights, coupling, inverses, ocean_state,
    depth_levels,
):
    devices = lax.axis_size("lat") * lax.axis_size("lon")
    fields, levels, oy, ox = ocean_state.shape
    cap = max(SUB, 2 * src_block.shape[0] // devices)
    slots = regrid(
        cap, devices, src_block, dest_dev[:, 0], dest_block, coupling, atm_flux, sea_mask, intersection_weights
    )
    received = lax.all_to_all(slots, ("lat", "lon"), 0, 0, tiled=True)
    mixed, north, south, side = mix(depth_levels, ocean_state, inverses)
    halos = (
        shift(south, "lat", 1, False),
        shift(north, "lat", -1, False),
        shift(side, "lon", -1, True),
        shift(side, "lon", 1, True),
    )
    forcing, edges = gather(cap, fields, oy, received)
    g_halos = (
        shift(edges, "lat", 1, False),
        shift(edges, "lat", -1, False),
        shift(edges, "lon", -1, True),
        shift(edges, "lon", 1, True),
    )
    return finish(depth_levels, forcing, side, mixed, halos, g_halos)


def solution(mesh):
    placed = (
        P(None, "lat", "lon"),
        P("lat", "lon"),
        P(("lat", "lon")),
        P(("lat", "lon"), None),
        P(("lat", "lon")),
        P(("lat", "lon"), None, None),
        P(),
        P(None, "lat", "lon", None, None),
        P(None, None, "lat", "lon"),
        P("lat", "lon"),
    )
    return jax.shard_map(
        on_device,
        mesh=mesh,
        in_specs=placed,
        out_specs=P(None, None, "lat", "lon"),
        check_vma=False,
    )
```

time: 261 us -> 93.2 us (0.36)
  waiting for transfers between devices: 135 us -> 2.98 us
  Pallas kernels: 0 us -> 48.5 us
  other arithmetic: 45.8 us -> 0 us
  matrix products: 19.6 us -> 0 us
  local copies, waits for them, and re-layouts: 33.4 us -> 17.6 us
  between operations: 13.6 us -> 0.14 us
  starting transfers between devices: 12.2 us -> 23.5 us
    reduce_scatter x1 -> x0, waiting for transfers between devices: 127 us -> none  [on_device(): lax.psum_scatter(jnp.zeros((blocks_dev * lax.axis_size(('lat', 'lon')),)...]
    pallas_call x0 -> x4, Pallas kernels: none -> 48.5 us  [the longest x1 26.7 us: finish(): pl.pallas_call(finish_kernel, grid=(oy // SUB,), in_specs=[whole, whole,...]
    scatter-add x1 -> x0, other arithmetic: 25.1 us -> none  [on_device(): received = lax.psum_scatter(jnp.zeros((blocks_dev * lax.axis_size(('lat',...]
    dot_general x3 -> x0, matrix products: 19.6 us -> none  [the longest x1 13.7 us: on_device(): jnp.einsum('qrlm,qmrx->qlrx', inverses[:, :, 0], rhs, precision=lax.Preci...]
    add x1 -> x0, other arithmetic: 15.1 us -> none  [on_device(): mixed + diffusion_rate * jnp.where(active[None], total, jnp.float32(0.0))]
    slice x11 -> x0, local copies, waits for them, and re-layouts: 14.3 us -> none  [the longest x3 9.59 us: padded_2(): head = lax.slice_in_dim(cells, 0, width, axis=dim)]
    unnamed x9 -> x24, local copies, waits for them, and re-layouts: 5.38 us -> 17.6 us
    all_to_all x0 -> x1, starting transfers between devices: none -> 7.29 us  [on_device(): received = lax.all_to_all(slots, ('lat', 'lon'), 0, 0, tiled=True)]
  transfers between devices with their start and end apart: 9 -> 9, of which waited for: 5 -> 3; matrix products, arithmetic and copies ran while one was open for 5% -> 0% of each run, Pallas kernels for 0% -> 15%
where the time goes in v1:
time: 93.2 us; the launch traced here: 92.7 us
  Pallas kernels  48.5 us (52%)
  starting transfers between devices  23.5 us (25%)
  local copies, waits for them, and re-layouts  17.6 us (19%)
  waiting for transfers between devices  2.98 us (3%)
    pallas_call x1, Pallas kernels, finish(): pl.pallas_call(finish_kernel, grid=(oy // SUB,), in_specs=[whole, whole,...  26.7 us
    unnamed x24, local copies, waits for them, and re-layouts  17.6 us
    ppermute x8, starting transfers between devices, shift(): return lax.ppermute(x, axis, pairs)  16.2 us
    pallas_call x1, Pallas kernels, mix(): pl.pallas_call(mix_kernel, grid=(fields, oy // SUB), in_specs=[pl.BlockSp...  13.1 us
    pallas_call x1, Pallas kernels, regrid(): pl.pallas_call(functools.partial(regrid_kernel, cap, batch, 8), grid=(pai...  8.27 us
    all_to_all x1, starting transfers between devices, on_device(): received = lax.all_to_all(slots, ('lat', 'lon'), 0, 0, tiled=True)  7.29 us
    ppermute x8, waiting for transfers between devices, shift(): return lax.ppermute(x, axis, pairs)  1.97 us
  transfers between devices with their start and end apart: 9, of which 3 were waited for; matrix products, arithmetic and copies ran while one was open for 0% of the time, Pallas kernels for 15%

profile of v1, /device:TPU:0, one launch (start us, length us, event | category | flops | bytes accessed | tf_op | source)
XLA Modules:
  0.0 92.7 jit_solution(4677255565388724651)
XLA Ops:
  0.0 3.4 %copy-done.2 = bf16[256,128,128]{2,1,0:T(8,128)(2,1)S(1)} copy-done((bf16[256,128,128]{2,1,0:T(8,128)(2,1)S(1)}, bf16[256,128,128]{2,1,0:T(8,128)(2,1)}, u32[]{:S(2)}) %copy-start.2) | copy-done | bytes 8388632
  3.4 0.9 copy-done.5
  4.3 0.8 copy-done.7
  5.0 0.7 copy-done.8
  5.7 0.7 copy-done.9
  6.4 0.7 copy-done.10
  7.1 0.7 copy-done.11
  7.8 8.3 %regrid.1 = f32[32,72,128]{2,1,0:T(8,128)} custom-call(s32[256]{0:T(256)S(1)} %copy-done.9, s32[256]{0:T(256)S(1)} %bitcast.1, s32[256]{0:T(256)S(1)} %copy-done.11, f32[4,8]{1,0:T(4,128)S(1)} %copy-done.8, bf16[8,64,128]{2,1,0:T(8,128)(2,1)S(1)} %copy-done.5, s32[64,128]{1,0:T(8,128)S(1)} %copy-done.7, bf16[256,128,128]{2,1,0:T(8,128)(2,1)S(1)} %copy-done.2), custom_call_target="tpu_custom_call" | custom-call | flops 67108864 | bytes 10485760 | tf_op jit(solution)/shard_map/regrid/pallas_call | solution.py:81
  16.0 7.3 %all-to-all-start = ((f32[32,72,128]{2,1,0:T(8,128)}), f32[32,72,128]{2,1,0:T(8,128)S(1)}, u32[]{:S(2)}, u32[]{:S(2)}) async-start(f32[32,72,128]{2,1,0:T(8,128)} %regrid.1), calls=%async_computation | async-start | bytes 2359296 | tf_op jit(solution)/shard_map/all_to_all | solution.py:380
  23.3 0.0 copy-start.3
  23.4 2.5 %copy-done.3 = f32[4,80,32,128]{3,2,1,0:T(8,128)S(1)} copy-done((f32[4,80,32,128]{3,2,1,0:T(8,128)S(1)}, f32[4,80,32,128]{3,2,1,0:T(8,128)}, u32[]{:S(2)}) %copy-start.3) | copy-done | bytes 5242904
  25.8 2.5 %copy-done.4 = f32[4,32,1,80,80]{4,3,2,1,0:T(8,128)S(1)} copy-done((f32[4,32,1,80,80]{4,3,2,1,0:T(8,128)S(1)}, f32[4,32,1,80,80]{4,3,2,1,0:T(8,128)}, u32[]{:S(2)}) %copy-start.4) | copy-done | bytes 3276824
  28.3 13.1 %mix.1 = (f32[4,32,80,128]{3,2,1,0:T(8,128)S(1)}, f32[4,88,128]{2,1,0:T(8,128)S(1)}, f32[4,88,128]{2,1,0:T(8,128)S(1)}, f32[4,88,128]{2,1,0:T(8,128)S(1)}) custom-call(s32[32,128]{1,0:T(8,128)S(1)} %copy-done.6, f32[4,80,32,128]{3,2,1,0:T(8,128)S(1)} %copy-done.3, f32[4,32,1,80,80]{4,3,2,1,0:T(8,128)S(1)} %copy-done.4), custom_call_target="tpu_custom_call" | custom-call | flops 838860800 | bytes 16777216 | tf_op jit(solution)/shard_map/mix/pallas_call | solution.py:161
  41.4 2.4 %copy-done = f32[4,32,80,128]{3,2,1,0:T(8,128)} copy-done((f32[4,32,80,128]{3,2,1,0:T(8,128)}, f32[4,32,80,128]{3,2,1,0:T(8,128)S(1)}, u32[]{:S(2)}) %copy-start) | copy-done | bytes 5242904
  43.8 3.7 %collective-permute-start = (f32[4,88,128]{2,1,0:T(8,128)S(1)}, f32[4,88,128]{2,1,0:T(8,128)S(1)}, u32[]{:S(2)}, u32[]{:S(2)}) collective-permute-start(f32[4,88,128]{2,1,0:T(8,128)S(1)} %get-tuple-element.14), channel_id=1, source_target_pairs={{0,8},{8,16},{16,24},{1,9},{9,17},{17,25},{2,10},{10,18},{18,26},{... | collective-permute-start | bytes 540680 | tf_op jit(solution)/shard_map/ppermute | solution.py:367
  47.5 1.3 %collective-permute-start.1 = (f32[4,88,128]{2,1,0:T(8,128)S(1)}, f32[4,88,128]{2,1,0:T(8,128)S(1)}, u32[]{:S(2)}, u32[]{:S(2)}) collective-permute-start(f32[4,88,128]{2,1,0:T(8,128)S(1)} %get-tuple-element.15), channel_id=1, source_target_pairs={{8,0},{16,8},{24,16},{9,1},{17,9},{25,17},{10,2},{18,10},{26,18},{... | collective-permute-start | bytes 540680 | tf_op jit(solution)/shard_map/ppermute | solution.py:367
  48.8 0.1 collective-permute-start.3
  48.8 2.6 %collective-permute-start.2 = (f32[4,88,128]{2,1,0:T(8,128)S(1)}, f32[4,88,128]{2,1,0:T(8,128)S(1)}, u32[]{:S(2)}, u32[]{:S(2)}) collective-permute-start(f32[4,88,128]{2,1,0:T(8,128)S(1)} %get-tuple-element.12.own), channel_id=1, source_target_pairs={{0,7},{1,0},{2,1},{3,2},{4,3},{5,4},{6,5},{7,6},{8,15},{9,8},{10,9... | collective-permute-start | bytes 540680 | tf_op jit(solution)/shard_map/ppermute | solution.py:367
  51.5 1.0 %all-to-all-done.recv = f32[32,72,128]{2,1,0:T(8,128)S(1)} async-done(((f32[32,72,128]{2,1,0:T(8,128)}), f32[32,72,128]{2,1,0:T(8,128)S(1)}, u32[]{:S(2)}, u32[]{:S(2)}) %all-to-all-start) | async-done | bytes 1179680 | tf_op jit(solution)/shard_map/all_to_all | solution.py:380
  52.5 0.4 gather.1
  52.9 0.1 collective-permute-start.7
  53.0 0.0 collective-permute-done.north
  53.0 2.6 %collective-permute-start.6 = (f32[16,128]{1,0:T(8,128)S(1)}, f32[16,128]{1,0:T(8,128)S(1)}, u32[]{:S(2)}, u32[]{:S(2)}) collective-permute-start(f32[16,128]{1,0:T(8,128)S(1)} %get-tuple-element.16), channel_id=1, source_target_pairs={{0,7},{1,0},{2,1},{3,2},{4,3},{5,4},{6,5},{7,6},{8,15},{9,8},{10,9... | collective-permute-start | bytes 24584 | tf_op jit(solution)/shard_map/ppermute | solution.py:367
  55.6 0.6 collective-permute-done.1.south
  56.3 1.3 %collective-permute-start.5 = (f32[16,128]{1,0:T(8,128)S(1)}, f32[16,128]{1,0:T(8,128)S(1)}, u32[]{:S(2)}, u32[]{:S(2)}) collective-permute-start(f32[16,128]{1,0:T(8,128)S(1)} %get-tuple-element.16), channel_id=1, source_target_pairs={{8,0},{16,8},{24,16},{9,1},{17,9},{25,17},{10,2},{18,10},{26,18},{... | collective-permute-start | bytes 24584 | tf_op jit(solution)/shard_map/ppermute | solution.py:367
  57.6 0.0 collective-permute-done.3.west
  57.6 4.5 %collective-permute-start.4 = (f32[16,128]{1,0:T(8,128)S(1)}, f32[16,128]{1,0:T(8,128)S(1)}, u32[]{:S(2)}, u32[]{:S(2)}) collective-permute-start(f32[16,128]{1,0:T(8,128)S(1)} %get-tuple-element.16), channel_id=1, source_target_pairs={{0,8},{8,16},{16,24},{1,9},{9,17},{17,25},{2,10},{10,18},{18,26},{... | collective-permute-start | bytes 24584 | tf_op jit(solution)/shard_map/ppermute | solution.py:367
  62.1 0.0 collective-permute-done.2.east
  62.2 0.0 collective-permute-done.6.g_east
  62.2 1.3 %collective-permute-done.4.g_north = f32[16,128]{1,0:T(8,128)S(1)} collective-permute-done((f32[16,128]{1,0:T(8,128)S(1)}, f32[16,128]{1,0:T(8,128)S(1)}, u32[]{:S(2)}, u32[]{:S(2)}) %collective-permute-start.4) | collective-permute-done | bytes 8224 | tf_op jit(solution)/shard_map/ppermute | solution.py:367
  63.5 2.5 %copy-done.1 = f32[4,32,80,128]{3,2,1,0:T(8,128)S(1)} copy-done((f32[4,32,80,128]{3,2,1,0:T(8,128)S(1)}, f32[4,32,80,128]{3,2,1,0:T(8,128)}, u32[]{:S(2)}) %copy-start.1) | copy-done | bytes 5242904
  66.0 26.7 %finish.1 = f32[4,80,32,128]{3,2,1,0:T(8,128)} custom-call(s32[32,128]{1,0:T(8,128)S(1)} %copy-done.6, f32[128,128]{1,0:T(8,128)S(1)} %get-tuple-element.11.forcing, f32[4,88,128]{2,1,0:T(8,128)S(1)} %get-tuple-element.12.own, f32[4,32,80,128]{3,2,1,0:T(8,128)S(1)} %copy-done.1, f32[4,32,80,128]{3,2,1,0:T(8,128)S(1)} %copy-done.1, ...), custom_call_target="tpu_custom_call" | custom-call | flops 26214400 | bytes 12582912 | tf_op jit(solution)/shard_map/finish/pallas_call | solution.py:343
  (14 shorter events, 0.0 us)
Async XLA Ops:
  0.0 3.4 %copy-start.2 = (bf16[256,128,128]{2,1,0:T(8,128)(2,1)S(1)}, bf16[256,128,128]{2,1,0:T(8,128)(2,1)}, u32[]{:S(2)}) copy-start(bf16[256,128,128]{2,1,0:T(8,128)(2,1)} %weights.1) | copy-start | bytes 25165828
  3.4 0.9 copy-start.5
  4.3 0.8 copy-start.7
  5.0 0.7 copy-start.8
  5.7 0.7 copy-start.9
  6.4 0.7 copy-start.10
  7.1 0.7 copy-start.11
  7.8 15.6 %copy-start.6 = (s32[32,128]{1,0:T(8,128)S(1)}, s32[32,128]{1,0:T(8,128)}, u32[]{:S(2)}) copy-start(s32[32,128]{1,0:T(8,128)} %depth_ref.3) | copy-start | bytes 49156
  16.0 36.4 %all-to-all-start = ((f32[32,72,128]{2,1,0:T(8,128)}), f32[32,72,128]{2,1,0:T(8,128)S(1)}, u32[]{:S(2)}, u32[]{:S(2)}) async-start(f32[32,72,128]{2,1,0:T(8,128)} %regrid.1), calls=%async_computation | async-start | bytes 2359296 | tf_op jit(solution)/shard_map/all_to_all | solution.py:380
  23.3 2.5 %copy-start.3 = (f32[4,80,32,128]{3,2,1,0:T(8,128)S(1)}, f32[4,80,32,128]{3,2,1,0:T(8,128)}, u32[]{:S(2)}) copy-start(f32[4,80,32,128]{3,2,1,0:T(8,128)} %state.1) | copy-start | bytes 15728644
  25.8 2.5 %copy-start.4 = (f32[4,32,1,80,80]{4,3,2,1,0:T(8,128)S(1)}, f32[4,32,1,80,80]{4,3,2,1,0:T(8,128)}, u32[]{:S(2)}) copy-start(f32[4,32,1,80,80]{4,3,2,1,0:T(8,128)} %inv.1) | copy-start | bytes 9830404
  41.4 2.4 %copy-start = (f32[4,32,80,128]{3,2,1,0:T(8,128)}, f32[4,32,80,128]{3,2,1,0:T(8,128)S(1)}, u32[]{:S(2)}) copy-start(f32[4,32,80,128]{3,2,1,0:T(8,128)S(1)} %get-tuple-element.13.mixed.above.below) | copy-start | bytes 15728644
  43.8 9.2 %collective-permute-start = (f32[4,88,128]{2,1,0:T(8,128)S(1)}, f32[4,88,128]{2,1,0:T(8,128)S(1)}, u32[]{:S(2)}, u32[]{:S(2)}) collective-permute-start(f32[4,88,128]{2,1,0:T(8,128)S(1)} %get-tuple-element.14), channel_id=1, source_target_pairs={{0,8},{8,16},{16,24},{1,9},{9,17},{17,25},{2,10},{10,18},{18,26},{... | collective-permute-start | bytes 540680 | tf_op jit(solution)/shard_map/ppermute | solution.py:367
  47.5 8.8 %collective-permute-start.1 = (f32[4,88,128]{2,1,0:T(8,128)S(1)}, f32[4,88,128]{2,1,0:T(8,128)S(1)}, u32[]{:S(2)}, u32[]{:S(2)}) collective-permute-start(f32[4,88,128]{2,1,0:T(8,128)S(1)} %get-tuple-element.15), channel_id=1, source_target_pairs={{8,0},{16,8},{24,16},{9,1},{17,9},{25,17},{10,2},{18,10},{26,18},{... | collective-permute-start | bytes 540680 | tf_op jit(solution)/shard_map/ppermute | solution.py:367
  48.8 8.8 %collective-permute-start.3 = (f32[4,88,128]{2,1,0:T(8,128)S(1)}, f32[4,88,128]{2,1,0:T(8,128)S(1)}, u32[]{:S(2)}, u32[]{:S(2)}) collective-permute-start(f32[4,88,128]{2,1,0:T(8,128)S(1)} %get-tuple-element.12.own), channel_id=1, source_target_pairs={{0,1},{1,2},{2,3},{3,4},{4,5},{5,6},{6,7},{7,0},{8,9},{9,10},{10,1... | collective-permute-start | bytes 540680 | tf_op jit(solution)/shard_map/ppermute | solution.py:367
  48.8 13.3 %collective-permute-start.2 = (f32[4,88,128]{2,1,0:T(8,128)S(1)}, f32[4,88,128]{2,1,0:T(8,128)S(1)}, u32[]{:S(2)}, u32[]{:S(2)}) collective-permute-start(f32[4,88,128]{2,1,0:T(8,128)S(1)} %get-tuple-element.12.own), channel_id=1, source_target_pairs={{0,7},{1,0},{2,1},{3,2},{4,3},{5,4},{6,5},{7,6},{8,15},{9,8},{10,9... | collective-permute-start | bytes 540680 | tf_op jit(solution)/shard_map/ppermute | solution.py:367
  52.9 9.2 %collective-permute-start.7 = (f32[16,128]{1,0:T(8,128)S(1)}, f32[16,128]{1,0:T(8,128)S(1)}, u32[]{:S(2)}, u32[]{:S(2)}) collective-permute-start(f32[16,128]{1,0:T(8,128)S(1)} %get-tuple-element.16), channel_id=1, source_target_pairs={{0,1},{1,2},{2,3},{3,4},{4,5},{5,6},{6,7},{7,0},{8,9},{9,10},{10,1... | collective-permute-start | bytes 24584 | tf_op jit(solution)/shard_map/ppermute | solution.py:367
  53.0 9.1 %collective-permute-start.6 = (f32[16,128]{1,0:T(8,128)S(1)}, f32[16,128]{1,0:T(8,128)S(1)}, u32[]{:S(2)}, u32[]{:S(2)}) collective-permute-start(f32[16,128]{1,0:T(8,128)S(1)} %get-tuple-element.16), channel_id=1, source_target_pairs={{0,7},{1,0},{2,1},{3,2},{4,3},{5,4},{6,5},{7,6},{8,15},{9,8},{10,9... | collective-permute-start | bytes 24584 | tf_op jit(solution)/shard_map/ppermute | solution.py:367
  56.3 5.9 %collective-permute-start.5 = (f32[16,128]{1,0:T(8,128)S(1)}, f32[16,128]{1,0:T(8,128)S(1)}, u32[]{:S(2)}, u32[]{:S(2)}) collective-permute-start(f32[16,128]{1,0:T(8,128)S(1)} %get-tuple-element.16), channel_id=1, source_target_pairs={{8,0},{16,8},{24,16},{9,1},{17,9},{25,17},{10,2},{18,10},{26,18},{... | collective-permute-start | bytes 24584 | tf_op jit(solution)/shard_map/ppermute | solution.py:367
  57.6 5.9 %collective-permute-start.4 = (f32[16,128]{1,0:T(8,128)S(1)}, f32[16,128]{1,0:T(8,128)S(1)}, u32[]{:S(2)}, u32[]{:S(2)}) collective-permute-start(f32[16,128]{1,0:T(8,128)S(1)} %get-tuple-element.16), channel_id=1, source_target_pairs={{0,8},{8,16},{16,24},{1,9},{9,17},{17,25},{2,10},{10,18},{18,26},{... | collective-permute-start | bytes 24584 | tf_op jit(solution)/shard_map/ppermute | solution.py:367
  63.5 2.5 %copy-start.1 = (f32[4,32,80,128]{3,2,1,0:T(8,128)S(1)}, f32[4,32,80,128]{3,2,1,0:T(8,128)}, u32[]{:S(2)}) copy-start(f32[4,32,80,128]{3,2,1,0:T(8,128)} %copy-done) | copy-start | bytes 15728644

commit v2 on v0

v2 whole, which is shorter than its diff:
```python
import functools

import jax
import jax.numpy as jnp
from jax import lax
from jax.experimental import pallas as pl
from jax.experimental.pallas import tpu as pltpu
from jax.sharding import PartitionSpec as P

diffusion_rate = 0.2
LANES = 128
HALF = 64
SUB = 8
f32 = jnp.float32
bf16 = jnp.bfloat16
HBM = pl.BlockSpec(memory_space=pltpu.HBM)
VMEM = pl.BlockSpec(memory_space=pltpu.VMEM)


def split(x):
    high = x.astype(bf16)
    return high, (x - high.astype(f32)).astype(bf16)


def in_hbm(*arrays):
    return [pltpu.with_memory_space_constraint(x, pltpu.HBM) for x in arrays]


def iota(shape, dim):
    return lax.broadcasted_iota(jnp.int32, shape, dim)


def matmul(a, b):
    return jnp.dot(a, b, preferred_element_type=f32)


def padded_rows(x, rows):
    return x if x.shape[0] == rows else jnp.concatenate([x, jnp.zeros((rows - x.shape[0], LANES), x.dtype)], axis=0)


def regrid_kernel(
    cap, lon, oy, batch, src_h, dev_h, blk_h, coupling_h, atm_h, mask_h, weights_h,
    out, rows, ids, count, src, dev, blk, coupling, atm, mask, weights, small_sem, big_sem,
):
    fluxes, atm_rows, _ = atm.shape
    fields = coupling.shape[0]
    devices = out.shape[0]
    per = fields * cap
    parts = weights.shape[0] // batch

    def big(k):
        here = pl.ds(pl.multiple_of(k * batch, batch), batch)
        return pltpu.make_async_copy(weights_h.at[here], weights.at[here], big_sem.at[k])

    small = [
        pltpu.make_async_copy(a, b, small_sem.at[k])
        for k, (a, b) in enumerate(
            (
                (coupling_h, coupling), (atm_h, atm), (mask_h, mask),
                (src_h, src), (dev_h, dev), (blk_h, blk),
            )
        )
    ]
    for copy in small:
        copy.start()
    for k in range(parts):
        big(k).start()

    def clear(d, carry):
        count[d] = 0
        out[d] = jnp.zeros(out.shape[1:], f32)
        return carry

    lax.fori_loop(0, devices, clear, 0)
    ids[...] = jnp.full(ids.shape, -1, jnp.int32)
    for copy in small:
        copy.wait()
    for tile in range(atm_rows // 16):
        here = slice(tile * 16, tile * 16 + 16)
        sea = mask[here, :].astype(f32)
        flux = [atm[f, here, :].astype(f32) * sea for f in range(fluxes)]
        for q in range(fields):
            total = coupling[q, 0] * flux[0]
            for f in range(1, fluxes):
                total = total + coupling[q, f] * flux[f]
            high = total.astype(bf16).astype(f32)
            rows[pl.ds(tile * 16 * SUB + q, 16, stride=SUB), :] = high
            rows[pl.ds(tile * 16 * SUB + fields + q, 16, stride=SUB), :] = total - high

    lane = iota((1, LANES), 1)
    lane_slot = (lane % per) // fields
    lane_row = (lane % fields) * oy

    def part(k, carry):
        big(k).wait()
        for u in range(batch):
            p = k * batch + u
            d = dev[p]
            slot = jnp.minimum(count[d], cap - 1)
            count[d] = slot + 1
            x = rows[pl.ds(pl.multiple_of(src[p] * SUB, SUB), SUB), :].astype(bf16)
            both = matmul(x, weights[p])
            out[d, pl.ds(slot * fields, fields), :] = both[0:fields] + both[fields : 2 * fields]
            line = ids[pl.ds(d, 1), :]
            ids[pl.ds(d, 1), :] = jnp.where(lane_slot == slot, lane_row + blk[p], line)
        return carry

    lax.fori_loop(0, parts, part, 0)

    wide = iota((SUB, LANES), 1)
    tall = iota((SUB, LANES), 0)
    first_half = wide < HALF
    wanted = jnp.where(
        (tall < fields) & first_half,
        tall * oy + oy - 1,
        jnp.where((tall >= fields) & ~first_half, (tall - fields) * oy, -5),
    )

    def halo(d):
        east = jnp.where(d % lon == lon - 1, d - (lon - 1), d + 1)
        west = jnp.where(d % lon == 0, d + (lon - 1), d - 1)
        own = ids[pl.ds(d, 1), :].astype(f32)
        sides = jnp.where(lane < HALF, ids[pl.ds(east, 1), :], ids[pl.ds(west, 1), :]).astype(f32)
        turned = jnp.concatenate(
            [padded_rows(out[east, 0:per], HALF), padded_rows(out[west, 0:per], HALF)], axis=0
        ).T
        columns = jnp.where(lane < HALF, turned[0:1], turned[LANES - 1 : LANES])
        out[d, per : per + SUB] = jnp.concatenate([own, sides, columns, jnp.zeros((SUB - 3, LANES), f32)], axis=0)
        north = jnp.maximum(d - lon, 0)
        south = jnp.minimum(d + lon, devices - 1)
        named = jnp.where(
            first_half,
            jnp.where(d >= lon, ids[pl.ds(north, 1), :], -9),
            jnp.where(d < devices - lon, ids[pl.ds(south, 1), :], -9),
        )
        chosen = jnp.where(named == wanted, 1.0, 0.0).astype(bf16)
        high, low = split(
            jnp.concatenate([padded_rows(out[north, 0:per], HALF), padded_rows(out[south, 0:per], HALF)], axis=0)
        )
        both = matmul(chosen, jnp.concatenate([high, low], axis=1))
        out[d, per + SUB : per + 2 * SUB] = both[:, :LANES] + both[:, LANES:]

    def halos(k, carry):
        for u in range(4):
            halo(k * 4 + u)
        return carry

    lax.fori_loop(0, devices // 4, halos, 0)


def regrid(cap, devices, lon, oy, src, dev, blk, coupling, atm, mask, weights):
    pairs, depth, width = weights.shape
    fields = coupling.shape[0]
    batch = 32
    tall = fields * cap + 2 * SUB
    return pl.pallas_call(
        functools.partial(regrid_kernel, cap, lon, oy, batch),
        in_specs=[HBM] * 7,
        out_specs=VMEM,
        out_shape=jax.ShapeDtypeStruct((devices, tall, LANES), f32),
        scratch_shapes=[
            pltpu.VMEM((atm.shape[1] * SUB, LANES), f32),
            pltpu.VMEM((devices, LANES), jnp.int32),
            pltpu.SMEM((devices,), jnp.int32),
            pltpu.SMEM(src.shape, jnp.int32),
            pltpu.SMEM(dev.shape, jnp.int32),
            pltpu.SMEM(blk.shape, jnp.int32),
            pltpu.SMEM(coupling.shape, f32),
            pltpu.VMEM(atm.shape, bf16),
            pltpu.VMEM(mask.shape, jnp.int32),
            pltpu.VMEM(weights.shape, bf16),
            pltpu.SemaphoreType.DMA((6,)),
            pltpu.SemaphoreType.DMA((pairs // batch,)),
        ],
        compiler_params=pltpu.CompilerParams(vmem_limit_bytes=20 << 20),
        cost_estimate=pl.CostEstimate(flops=2 * 8 * pairs * depth * width, bytes_accessed=10 << 20, transcendentals=0),
        name="regrid",
    )(*in_hbm(src, dev, blk, coupling, atm, mask, weights))


def mix_kernel(depth_h, state_h, inv_h, mixed, north, south, side, depth_ref, state, inv, sems):
    fields, levels, oy, _ = state.shape
    copies = [pltpu.make_async_copy(depth_h, depth_ref, sems.at[2 * fields])]
    copies[0].start()
    for q in range(fields):
        for k, (a, b) in enumerate(((state_h, state), (inv_h, inv))):
            pltpu.make_async_copy(a.at[q], b.at[q], sems.at[2 * q + k]).start()
    copies[0].wait()
    level = iota((levels, LANES), 0)
    lane = iota((levels, LANES), 1)
    pick_row = iota((LANES, LANES), 0)
    pick_lane = iota((LANES, LANES), 1)
    turned = padded_rows(depth_ref[...].astype(f32), LANES).T
    edge_depth = turned[0:1] + pltpu.roll(turned[LANES - SUB :], oy, 1)[SUB - 1 : SUB]

    def message(ref, q, row):
        ref[q, 0:levels] = mixed[q, row]
        square = jnp.concatenate([inv[q, row, 0], jnp.zeros((levels, LANES - levels), f32)], axis=1)
        first = padded_rows(square, LANES).T[0:1]
        ref[q, levels : levels + SUB] = jnp.concatenate(
            [depth_ref[row : row + 1, :].astype(f32), first, jnp.zeros((SUB - 2, LANES), f32)], axis=0
        )

    def field(q, carry):
        for k, (a, b) in enumerate(((state_h, state), (inv_h, inv))):
            pltpu.make_async_copy(a.at[q], b.at[q], sems.at[2 * q + k]).wait()
        flat = state.at[q].reshape(levels * oy, LANES)

        def chunk(c, edges):
            for i in range(SUB):
                row = c * SUB + i
                active = level < depth_ref[pl.ds(row, 1), :]
                x = flat[pl.ds(row, levels, stride=oy), :]
                a = inv[q, row, 0]
                a_high, a_low = split(a)
                r_high, r_low = split(jnp.where(active, x, 0.0))
                product = matmul(
                    jnp.concatenate([a_high, a_low], axis=0), jnp.concatenate([r_high, r_low], axis=1)
                )
                solved = product[:levels, :LANES] + (product[levels:, :LANES] + product[:levels, LANES:])
                m = jnp.where(active, solved, x)
                mixed[q, row] = m
                m_high, m_low = split(m)
                pick = (
                    ((pick_row == 0) & (pick_lane == row)) | ((pick_row == LANES - 1) & (pick_lane == oy + row))
                ).astype(f32).astype(bf16)
                edges = edges + matmul(
                    jnp.concatenate([m_high, m_low], axis=1), jnp.concatenate([pick, pick], axis=0)
                )
                edges = jnp.where(lane == 2 * oy + row, a[:, 0:1], edges)
            return edges

        side[q, 0:levels] = lax.fori_loop(0, oy // SUB, chunk, jnp.zeros((levels, LANES), f32))
        side[q, levels : levels + SUB] = jnp.broadcast_to(edge_depth, (SUB, LANES))
        message(north, q, 0)
        message(south, q, oy - 1)
        return carry

    lax.fori_loop(0, fields, field, 0)


def mix(depth, state, inverses):
    fields, levels, oy, ox = state.shape
    edge_shape = jax.ShapeDtypeStruct((fields, levels + SUB, ox), f32)
    return pl.pallas_call(
        mix_kernel,
        in_specs=[HBM] * 3,
        out_specs=[VMEM] * 4,
        out_shape=[jax.ShapeDtypeStruct((fields, oy, levels, ox), f32), edge_shape, edge_shape, edge_shape],
        scratch_shapes=[
            pltpu.VMEM(depth.shape, jnp.int32),
            pltpu.VMEM(state.shape, f32),
            pltpu.VMEM(inverses.shape, f32),
            pltpu.SemaphoreType.DMA((2 * fields + 1,)),
        ],
        compiler_params=pltpu.CompilerParams(vmem_limit_bytes=28 << 20),
        cost_estimate=pl.CostEstimate(flops=2 * 4 * fields * oy * levels * levels * ox, bytes_accessed=16 << 20, transcendentals=0),
        name="mix",
    )(*in_hbm(depth, state, inverses))


def finish_kernel(
    cap, recv, depth_ref, own, mixed, north, south, east, west,
    out_h, forcing, z, m, keep, column, halo, z_north, z_south, stage, sems,
):
    fields, oy, levels, _ = mixed.shape
    devices = recv.shape[0]
    per = fields * cap
    group = LANES // per
    level = iota((levels, LANES), 0)
    lanes = iota((levels, LANES), 1)
    square_row = iota((LANES, LANES), 0)
    square_lane = iota((LANES, LANES), 1)
    line = iota((1, LANES), 1)

    total = jnp.zeros((LANES, 2 * LANES), f32)
    for tile in range(devices // group):
        ids = recv[tile * group, per : per + 1, :]
        for s in range(1, group):
            ids = jnp.where(line // per == s, recv[tile * group + s, per : per + 1, :], ids)
        hot = jnp.where(square_row.astype(f32) == ids, 1.0, 0.0).astype(bf16)
        high, low = split(jnp.concatenate([recv[tile * group + s, 0:per, :] for s in range(group)], axis=0))
        total = total + matmul(hot, jnp.concatenate([high, low], axis=1))
    forcing[...] = total[:, :LANES] + total[:, LANES:]
    rows = recv[0, per + SUB : per + 2 * SUB, :]
    for d in range(1, devices):
        rows = rows + recv[d, per + SUB : per + 2 * SUB, :]
    spread = jnp.zeros((oy, LANES), f32)
    row = iota((oy, LANES), 0).astype(f32)
    lane_base = ((line % fields) * oy).astype(f32)
    for d in range(devices):
        spread = spread + jnp.where(
            recv[d, per + 1 : per + 2, :] - lane_base == row, recv[d, per + 2 : per + 3, :], 0.0
        )
    high, low = split(padded_rows(spread, LANES).T)
    small_row, small_lane = iota((SUB, LANES), 0), iota((SUB, LANES), 1)
    pick = jnp.where(
        (small_lane % fields == small_row % fields)
        & (small_lane % HALF < per)
        & ((small_lane < HALF) == (small_row < fields)),
        1.0,
        0.0,
    ).astype(bf16)
    columns = matmul(pick, high) + matmul(pick, low)

    depth = depth_ref[...]
    wide = iota((oy, LANES), 1)

    def upright(ref, place):
        value = jnp.where(wide == iota((oy, LANES), 0) + place, ref[0, levels : levels + 1, :], 0.0)
        return jnp.sum(value, axis=1, keepdims=True).astype(jnp.int32)

    to_east = jnp.where(wide == LANES - 1, upright(east, 0), pltpu.roll(depth, LANES - 1, 1))
    to_west = jnp.where(wide == 0, upright(west, oy), pltpu.roll(depth, 1, 1))
    to_north = jnp.concatenate([north[0, levels : levels + 1, :].astype(jnp.int32), depth[: oy - 1]], axis=0)
    to_south = jnp.concatenate([depth[1:], south[0, levels : levels + 1, :].astype(jnp.int32)], axis=0)
    for i in range(oy):
        sides = jnp.where(level < to_east[i : i + 1], diffusion_rate, 0.0)
        for other in (to_west, to_north, to_south):
            sides = sides + jnp.where(level < other[i : i + 1], diffusion_rate, 0.0)
        keep[i] = jnp.where(level < depth[i : i + 1], 1.0 - sides, 1.0)

    def outer(target, ref, first):
        names = padded_rows(
            jnp.concatenate([ref[q, levels + 1 : levels + 2, :] for q in range(fields)], axis=0), LANES
        ).T
        active = level < ref[0, levels : levels + 1, :].astype(jnp.int32)
        for q in range(fields):
            value = ref[q, 0:levels] + names[0:levels, q : q + 1] * rows[first + q : first + q + 1]
            target[q] = jnp.where(active, value, 0.0)

    outer(z_north, north, 0)
    outer(z_south, south, fields)
    east_depth = east[0, levels : levels + 1, :].astype(jnp.int32)
    west_depth = west[0, levels : levels + 1, :].astype(jnp.int32)
    west_columns = pltpu.roll(columns, oy, 1)
    for q in range(fields):
        z_east = east[q, 0:levels] + pltpu.roll(east[q, 0:levels], LANES - 2 * oy, 1) * columns[q : q + 1]
        z_east = jnp.where(level < east_depth, z_east, 0.0)
        z_west = west[q, 0:levels] + pltpu.roll(west[q, 0:levels], LANES - oy, 1) * west_columns[fields + q : fields + q + 1]
        z_west = jnp.where(level < west_depth, z_west, 0.0)
        both = jnp.where(lanes < oy, z_east, z_west)
        high = both.astype(bf16).astype(f32)
        halo[q] = jnp.where(lanes < HALF, high, pltpu.roll(both - high, HALF, 1)).astype(bf16)
        a = own[q, 0:levels]
        first = pltpu.roll(a, LANES - 2 * oy, 1)
        low = pltpu.roll(a, LANES - oy, 1)
        low = low - low.astype(bf16).astype(f32)
        column[q] = jnp.where(
            lanes < oy, first, jnp.where(lanes < 2 * oy, low, jnp.where(lanes < 3 * oy, a, 0.0))
        ).astype(bf16)

    to_both = jnp.where(
        (square_row == square_lane + 1) | (square_row == square_lane - 1), 1.0, 0.0
    ).astype(bf16)
    own_row = iota((oy, LANES), 0)

    def field(q, carry):
        z[0] = z_north[q]
        z[oy + 1] = z_south[q]
        g_high, g_low = split(forcing[pl.ds(pl.multiple_of(q * oy, oy), oy), :])
        g_high, g_low = g_high.astype(f32), g_low.astype(f32)

        def solve(c, carry):
            for i in range(SUB):
                r = c * SUB + i
                here = own_row == r
                high = jnp.where(here, g_high, 0.0)
                low = jnp.where(here, g_low, 0.0)
                spread = padded_rows(jnp.concatenate([high, high, low], axis=0), LANES).astype(bf16)
                m0 = mixed[q, r]
                forced = m0 + matmul(column[q], spread)
                active = level < depth_ref[pl.ds(r, 1), :]
                z[r + 1] = jnp.where(active, forced, 0.0)
                m[r] = jnp.where(active, forced, m0)
            return carry

        lax.fori_loop(0, oy // SUB, solve, 0)
        flat = stage.at[q].reshape(levels * oy, LANES)

        def diffuse(c, carry):
            for i in range(SUB):
                r = c * SUB + i
                high, low = split(z[r + 1])
                edge = jnp.where(
                    ((square_row % HALF == r) & (square_lane == LANES - 1))
                    | ((square_row % HALF == oy + r) & (square_lane == 0)),
                    1.0,
                    0.0,
                ).astype(bf16)
                sides = matmul(
                    jnp.concatenate([high, low, halo[q]], axis=1),
                    jnp.concatenate([to_both, to_both, edge], axis=0),
                )
                scale = jnp.where(level < depth_ref[pl.ds(r, 1), :], diffusion_rate, 0.0)
                flat[pl.ds(r, levels, stride=oy), :] = m[r] * keep[r] + scale * ((z[r] + z[r + 2]) + sides)
            return carry

        lax.fori_loop(0, oy // SUB, diffuse, 0)
        pltpu.make_async_copy(stage.at[q], out_h.at[q], sems.at[q]).start()
        return carry

    lax.fori_loop(0, fields, field, 0)
    for q in range(fields):
        pltpu.make_async_copy(stage.at[q], out_h.at[q], sems.at[q]).wait()


def finish(cap, received, depth, own, mixed, halos):
    fields, oy, levels, ox = mixed.shape
    edge = pltpu.VMEM((fields, levels, ox), f32)
    return pl.pallas_call(
        functools.partial(finish_kernel, cap),
        in_specs=[VMEM] * 8,
        out_specs=HBM,
        out_shape=jax.ShapeDtypeStruct((fields, levels, oy, ox), f32),
        scratch_shapes=[
            pltpu.VMEM((fields * oy, ox), f32),
            pltpu.VMEM((oy + 2, levels, ox), f32),
            pltpu.VMEM((oy, levels, ox), f32),
            pltpu.VMEM((oy, levels, ox), f32),
            pltpu.VMEM((fields, levels, ox), bf16),
            pltpu.VMEM((fields, levels, ox), bf16),
            edge,
            edge,
            pltpu.VMEM((fields, levels, oy, ox), f32),
            pltpu.SemaphoreType.DMA((fields,)),
        ],
        compiler_params=pltpu.CompilerParams(vmem_limit_bytes=24 << 20),
        cost_estimate=pl.CostEstimate(flops=20 * fields * oy * levels * ox, bytes_accessed=12 << 20, transcendentals=0),
        name="finish",
    )(received, depth, own, mixed, *halos)


def shift(x, axis, step, wrap):
    count = lax.axis_size(axis)
    pairs = [(i, (i + step) % count) for i in range(count) if wrap or 0 <= i + step < count]
    return lax.ppermute(x, axis, pairs)


def on_device(
    atm_flux, sea_mask, src_block, dest_dev, dest_block, intersection_weights, coupling, inverses, ocean_state,
    depth_levels,
):
    lon = lax.axis_size("lon")
    devices = lax.axis_size("lat") * lon
    oy = ocean_state.shape[2]
    cap = max(SUB, 2 * src_block.shape[0] // devices)
    slots = regrid(
        cap, devices, lon, oy, src_block, dest_dev[:, 0], dest_block, coupling, atm_flux, sea_mask,
        intersection_weights,
    )
    received = lax.all_to_all(slots, ("lat", "lon"), 0, 0, tiled=True)
    mixed, north, south, side = mix(depth_levels, ocean_state, inverses)
    halos = (
        shift(south, "lat", 1, False),
        shift(north, "lat", -1, False),
        shift(side, "lon", -1, True),
        shift(side, "lon", 1, True),
    )
    return finish(cap, received, depth_levels, side, mixed, halos)


def solution(mesh):
    placed = (
        P(None, "lat", "lon"),
        P("lat", "lon"),
        P(("lat", "lon")),
        P(("lat", "lon"), None),
        P(("lat", "lon")),
        P(("lat", "lon"), None, None),
        P(),
        P(None, "lat", "lon", None, None),
        P(None, None, "lat", "lon"),
        P("lat", "lon"),
    )
    return jax.shard_map(
        on_device,
        mesh=mesh,
        in_specs=placed,
        out_specs=P(None, None, "lat", "lon"),
        check_vma=False,
    )
```

time: 261 us -> 81.9 us (0.31)
  waiting for transfers between devices: 135 us -> 4.23 us
  Pallas kernels: 0 us -> 57.1 us
  other arithmetic: 45.8 us -> 0 us
  local copies, waits for them, and re-layouts: 33.4 us -> 4.84 us
  matrix products: 19.6 us -> 0 us
  between operations: 13.6 us -> 0.09 us
  starting transfers between devices: 12.2 us -> 15 us
    reduce_scatter x1 -> x0, waiting for transfers between devices: 127 us -> none  [on_device(): lax.psum_scatter(jnp.zeros((blocks_dev * lax.axis_size(('lat', 'lon')),)...]
    pallas_call x0 -> x3, Pallas kernels: none -> 57.1 us  [the longest x1 26.1 us: mix(): pl.pallas_call(mix_kernel, in_specs=[HBM] * 3, out_specs=[VMEM] * 4, out_...]
    scatter-add x1 -> x0, other arithmetic: 25.1 us -> none  [on_device(): received = lax.psum_scatter(jnp.zeros((blocks_dev * lax.axis_size(('lat',...]
    dot_general x3 -> x0, matrix products: 19.6 us -> none  [the longest x1 13.7 us: on_device(): jnp.einsum('qrlm,qmrx->qlrx', inverses[:, :, 0], rhs, precision=lax.Preci...]
    add x1 -> x0, other arithmetic: 15.1 us -> none  [on_device(): mixed + diffusion_rate * jnp.where(active[None], total, jnp.float32(0.0))]
    slice x11 -> x0, local copies, waits for them, and re-layouts: 14.3 us -> none  [the longest x3 9.59 us: padded_2(): head = lax.slice_in_dim(cells, 0, width, axis=dim)]
    all_to_all x0 -> x1, starting transfers between devices: none -> 7.31 us  [on_device(): received = lax.all_to_all(slots, ('lat', 'lon'), 0, 0, tiled=True)]
    ppermute x2 -> x0, local copies, waits for them, and re-layouts: 6.6 us -> none  [the longest x1 3.34 us: padded_2(): lax.ppermute(head, axis, [((i + 1) % count, i) for i in range(count)])]
  transfers between devices with their start and end apart: 9 -> 5, of which waited for: 5 -> 2; matrix products, arithmetic and copies ran while one was open for 5% -> 0% of each run, Pallas kernels for 0% -> 32%
where the time goes in v2:
time: 81.9 us; the launch traced here: 81.2 us
  Pallas kernels  57.1 us (70%)
  starting transfers between devices  15 us (18%)
  local copies, waits for them, and re-layouts  4.84 us (6%)
  waiting for transfers between devices  4.23 us (5%)
    pallas_call x1, Pallas kernels, mix(): pl.pallas_call(mix_kernel, in_specs=[HBM] * 3, out_specs=[VMEM] * 4, out_...  26.1 us
    pallas_call x1, Pallas kernels, finish(): pl.pallas_call(functools.partial(finish_kernel, cap), in_specs=[VMEM] * 8...  16.7 us
    pallas_call x1, Pallas kernels, regrid(): pl.pallas_call(functools.partial(regrid_kernel, cap, lon, oy, batch), in_...  14.3 us
    ppermute x4, starting transfers between devices, shift(): return lax.ppermute(x, axis, pairs)  7.66 us
    all_to_all x1, starting transfers between devices, on_device(): received = lax.all_to_all(slots, ('lat', 'lon'), 0, 0, tiled=True)  7.31 us
    unnamed x6, local copies, waits for them, and re-layouts  4.84 us
    ppermute x4, waiting for transfers between devices, shift(): return lax.ppermute(x, axis, pairs)  4.22 us
  transfers between devices with their start and end apart: 5, of which 2 were waited for; matrix products, arithmetic and copies ran while one was open for 0% of the time, Pallas kernels for 32%

profile of v2, /device:TPU:0, one launch (start us, length us, event | category | flops | bytes accessed | tf_op | source)
XLA Modules:
  0.0 81.2 jit_solution(2797830470426322900)
XLA Ops:
  0.0 14.3 %regrid.1 = f32[32,80,128]{2,1,0:T(8,128)} custom-call(s32[256]{0:T(256)} %src_h.1, s32[256]{0:T(256)} %bitcast.1, s32[256]{0:T(256)} %blk_h.1, f32[4,8]{1,0:T(4,128)} %coupling_h.1, bf16[8,64,128]{2,1,0:T(8,128)(2,1)} %atm_h.1, s32[64,128]{1,0:T(8,128)} %mask_h.1, bf16[256,128,128]{2,1,0:T(8,128)(2,1)} %weights_h.1), custom_call_target="tpu_custom_call" | custom-call | flops 67108864 | bytes 10485760 | tf_op jit(solution)/shard_map/regrid/pallas_call | solution.py:156
  14.3 7.3 %all-to-all-start = ((f32[32,80,128]{2,1,0:T(8,128)}), f32[32,80,128]{2,1,0:T(8,128)S(1)}, u32[]{:S(2)}, u32[]{:S(2)}) async-start(f32[32,80,128]{2,1,0:T(8,128)} %regrid.1), calls=%async_computation | async-start | bytes 2621440 | tf_op jit(solution)/shard_map/all_to_all | solution.py:452
  21.6 0.0 copy-start.2
  21.6 26.1 %mix.1 = (f32[4,32,80,128]{3,2,1,0:T(8,128)S(1)}, f32[4,88,128]{2,1,0:T(8,128)S(1)}, f32[4,88,128]{2,1,0:T(8,128)S(1)}, f32[4,88,128]{2,1,0:T(8,128)S(1)}) custom-call(s32[32,128]{1,0:T(8,128)} %depth_ref.1, f32[4,80,32,128]{3,2,1,0:T(8,128)} %state_h.1, f32[4,32,1,80,80]{4,3,2,1,0:T(8,128)} %inv_h.1), custom_call_target="tpu_custom_call" | custom-call | flops 838860800 | bytes 16777216 | tf_op jit(solution)/shard_map/mix/pallas_call | solution.py:245
  47.7 0.0 copy-start
  47.8 2.3 %copy-done = f32[4,32,80,128]{3,2,1,0:T(8,128)} copy-done((f32[4,32,80,128]{3,2,1,0:T(8,128)}, f32[4,32,80,128]{3,2,1,0:T(8,128)S(1)}, u32[]{:S(2)}) %copy-start) | copy-done | bytes 5242904
  50.1 3.7 %collective-permute-start = (f32[4,88,128]{2,1,0:T(8,128)S(1)}, f32[4,88,128]{2,1,0:T(8,128)S(1)}, u32[]{:S(2)}, u32[]{:S(2)}) collective-permute-start(f32[4,88,128]{2,1,0:T(8,128)S(1)} %get-tuple-element.11), channel_id=1, source_target_pairs={{0,8},{8,16},{16,24},{1,9},{9,17},{17,25},{2,10},{10,18},{18,26},{... | collective-permute-start | bytes 540680 | tf_op jit(solution)/shard_map/ppermute | solution.py:437
  53.8 1.3 %collective-permute-start.1 = (f32[4,88,128]{2,1,0:T(8,128)S(1)}, f32[4,88,128]{2,1,0:T(8,128)S(1)}, u32[]{:S(2)}, u32[]{:S(2)}) collective-permute-start(f32[4,88,128]{2,1,0:T(8,128)S(1)} %get-tuple-element.12), channel_id=1, source_target_pairs={{8,0},{16,8},{24,16},{9,1},{17,9},{25,17},{10,2},{18,10},{26,18},{... | collective-permute-start | bytes 540680 | tf_op jit(solution)/shard_map/ppermute | solution.py:437
  55.1 0.1 collective-permute-start.3
  55.2 2.6 %collective-permute-start.2 = (f32[4,88,128]{2,1,0:T(8,128)S(1)}, f32[4,88,128]{2,1,0:T(8,128)S(1)}, u32[]{:S(2)}, u32[]{:S(2)}) collective-permute-start(f32[4,88,128]{2,1,0:T(8,128)S(1)} %get-tuple-element.9.own), channel_id=1, source_target_pairs={{0,7},{1,0},{2,1},{3,2},{4,3},{5,4},{6,5},{7,6},{8,15},{9,8},{10,9... | collective-permute-start | bytes 540680 | tf_op jit(solution)/shard_map/ppermute | solution.py:437
  57.8 0.1 collective-permute-done.north
  57.9 4.1 %collective-permute-done.1.south = f32[4,88,128]{2,1,0:T(8,128)S(1)} collective-permute-done((f32[4,88,128]{2,1,0:T(8,128)S(1)}, f32[4,88,128]{2,1,0:T(8,128)S(1)}, u32[]{:S(2)}, u32[]{:S(2)}) %collective-permute-start.1) | collective-permute-done | bytes 180256 | tf_op jit(solution)/shard_map/ppermute | solution.py:437
  62.0 0.0 collective-permute-done.3.west
  62.0 0.0 collective-permute-done.2.east
  62.0 0.0 all-to-all-done.recv
  62.0 0.0 copy-done.2
  62.0 0.0 copy-start.1
  62.0 2.5 %copy-done.1 = f32[4,32,80,128]{3,2,1,0:T(8,128)S(1)} copy-done((f32[4,32,80,128]{3,2,1,0:T(8,128)S(1)}, f32[4,32,80,128]{3,2,1,0:T(8,128)}, u32[]{:S(2)}) %copy-start.1) | copy-done | bytes 5242904
  64.5 16.7 %finish.1 = f32[4,80,32,128]{3,2,1,0:T(8,128)} custom-call(f32[32,80,128]{2,1,0:T(8,128)S(1)} %all-to-all-done.recv, s32[32,128]{1,0:T(8,128)S(1)} %copy-done.2, f32[4,88,128]{2,1,0:T(8,128)S(1)} %get-tuple-element.9.own, f32[4,32,80,128]{3,2,1,0:T(8,128)S(1)} %copy-done.1, f32[4,88,128]{2,1,0:T(8,128)S(1)} %collective-permute-done.north, ...), custom_call_target="tpu_custom_call" | custom-call | flops 26214400 | bytes 12582912 | tf_op jit(solution)/shard_map/finish/pallas_call | solution.py:411
Async XLA Ops:
  14.3 47.7 %all-to-all-start = ((f32[32,80,128]{2,1,0:T(8,128)}), f32[32,80,128]{2,1,0:T(8,128)S(1)}, u32[]{:S(2)}, u32[]{:S(2)}) async-start(f32[32,80,128]{2,1,0:T(8,128)} %regrid.1), calls=%async_computation | async-start | bytes 2621440 | tf_op jit(solution)/shard_map/all_to_all | solution.py:452
  21.6 40.4 %copy-start.2 = (s32[32,128]{1,0:T(8,128)S(1)}, s32[32,128]{1,0:T(8,128)}, u32[]{:S(2)}) copy-start(s32[32,128]{1,0:T(8,128)} %depth_ref.1) | copy-start | bytes 49156
  47.7 2.4 %copy-start = (f32[4,32,80,128]{3,2,1,0:T(8,128)}, f32[4,32,80,128]{3,2,1,0:T(8,128)S(1)}, u32[]{:S(2)}) copy-start(f32[4,32,80,128]{3,2,1,0:T(8,128)S(1)} %get-tuple-element.10.mixed) | copy-start | bytes 15728644
  50.1 7.8 %collective-permute-start = (f32[4,88,128]{2,1,0:T(8,128)S(1)}, f32[4,88,128]{2,1,0:T(8,128)S(1)}, u32[]{:S(2)}, u32[]{:S(2)}) collective-permute-start(f32[4,88,128]{2,1,0:T(8,128)S(1)} %get-tuple-element.11), channel_id=1, source_target_pairs={{0,8},{8,16},{16,24},{1,9},{9,17},{17,25},{2,10},{10,18},{18,26},{... | collective-permute-start | bytes 540680 | tf_op jit(solution)/shard_map/ppermute | solution.py:437
  53.8 8.2 %collective-permute-start.1 = (f32[4,88,128]{2,1,0:T(8,128)S(1)}, f32[4,88,128]{2,1,0:T(8,128)S(1)}, u32[]{:S(2)}, u32[]{:S(2)}) collective-permute-start(f32[4,88,128]{2,1,0:T(8,128)S(1)} %get-tuple-element.12), channel_id=1, source_target_pairs={{8,0},{16,8},{24,16},{9,1},{17,9},{25,17},{10,2},{18,10},{26,18},{... | collective-permute-start | bytes 540680 | tf_op jit(solution)/shard_map/ppermute | solution.py:437
  55.1 6.9 %collective-permute-start.3 = (f32[4,88,128]{2,1,0:T(8,128)S(1)}, f32[4,88,128]{2,1,0:T(8,128)S(1)}, u32[]{:S(2)}, u32[]{:S(2)}) collective-permute-start(f32[4,88,128]{2,1,0:T(8,128)S(1)} %get-tuple-element.9.own), channel_id=1, source_target_pairs={{0,1},{1,2},{2,3},{3,4},{4,5},{5,6},{6,7},{7,0},{8,9},{9,10},{10,1... | collective-permute-start | bytes 540680 | tf_op jit(solution)/shard_map/ppermute | solution.py:437
  55.2 6.9 %collective-permute-start.2 = (f32[4,88,128]{2,1,0:T(8,128)S(1)}, f32[4,88,128]{2,1,0:T(8,128)S(1)}, u32[]{:S(2)}, u32[]{:S(2)}) collective-permute-start(f32[4,88,128]{2,1,0:T(8,128)S(1)} %get-tuple-element.9.own), channel_id=1, source_target_pairs={{0,7},{1,0},{2,1},{3,2},{4,3},{5,4},{6,5},{7,6},{8,15},{9,8},{10,9... | collective-permute-start | bytes 540680 | tf_op jit(solution)/shard_map/ppermute | solution.py:437
  62.0 2.5 %copy-start.1 = (f32[4,32,80,128]{3,2,1,0:T(8,128)S(1)}, f32[4,32,80,128]{3,2,1,0:T(8,128)}, u32[]{:S(2)}) copy-start(f32[4,32,80,128]{3,2,1,0:T(8,128)} %copy-done) | copy-start | bytes 15728644

commit v3 on v2

v3 whole, which is shorter than its diff:
```python
import functools

import jax
import jax.numpy as jnp
from jax import lax
from jax.experimental import pallas as pl
from jax.experimental.pallas import tpu as pltpu
from jax.sharding import PartitionSpec as P

diffusion_rate = 0.2
LANES = 128
HALF = 64
SUB = 8
f32 = jnp.float32
bf16 = jnp.bfloat16
HBM = pl.BlockSpec(memory_space=pltpu.HBM)
VMEM = pl.BlockSpec(memory_space=pltpu.VMEM)


def split(x):
    high = x.astype(bf16)
    return high, (x - high.astype(f32)).astype(bf16)


def in_hbm(*arrays):
    return [pltpu.with_memory_space_constraint(x, pltpu.HBM) for x in arrays]


def iota(shape, dim):
    return lax.broadcasted_iota(jnp.int32, shape, dim)


def matmul(a, b):
    return jnp.dot(a, b, preferred_element_type=f32)


def padded_rows(x, rows):
    return x if x.shape[0] == rows else jnp.concatenate([x, jnp.zeros((rows - x.shape[0], LANES), x.dtype)], axis=0)


def regrid_kernel(
    cap, lon, oy, batch, src_h, dev_h, blk_h, coupling_h, atm_h, mask_h, weights_h,
    out, rows, ids, count, src, dev, blk, coupling, atm, mask, weights, small_sem, big_sem,
):
    fluxes, atm_rows, _ = atm.shape
    fields = coupling.shape[0]
    devices = out.shape[0]
    per = fields * cap
    parts = weights.shape[0] // batch

    def big(k):
        here = pl.ds(pl.multiple_of(k * batch, batch), batch)
        return pltpu.make_async_copy(weights_h.at[here], weights.at[here], big_sem.at[k])

    small = [
        pltpu.make_async_copy(a, b, small_sem.at[k])
        for k, (a, b) in enumerate(
            (
                (coupling_h, coupling), (atm_h, atm), (mask_h, mask),
                (src_h, src), (dev_h, dev), (blk_h, blk),
            )
        )
    ]
    for copy in small:
        copy.start()
    for k in range(parts):
        big(k).start()

    def clear(d, carry):
        count[d] = 0
        out[d] = jnp.zeros(out.shape[1:], f32)
        return carry

    lax.fori_loop(0, devices, clear, 0)
    ids[...] = jnp.full(ids.shape, -1, jnp.int32)
    for copy in small:
        copy.wait()
    for tile in range(atm_rows // 16):
        here = slice(tile * 16, tile * 16 + 16)
        sea = mask[here, :].astype(f32)
        flux = [atm[f, here, :].astype(f32) * sea for f in range(fluxes)]
        for q in range(fields):
            total = coupling[q, 0] * flux[0]
            for f in range(1, fluxes):
                total = total + coupling[q, f] * flux[f]
            high = total.astype(bf16).astype(f32)
            rows[pl.ds(tile * 16 * SUB + q, 16, stride=SUB), :] = high
            rows[pl.ds(tile * 16 * SUB + fields + q, 16, stride=SUB), :] = total - high

    lane = iota((1, LANES), 1)
    lane_slot = (lane % per) // fields
    lane_row = (lane % fields) * oy

    def part(k, carry):
        big(k).wait()
        for u in range(batch):
            p = k * batch + u
            d = dev[p]
            slot = jnp.minimum(count[d], cap - 1)
            count[d] = slot + 1
            x = rows[pl.ds(pl.multiple_of(src[p] * SUB, SUB), SUB), :].astype(bf16)
            both = matmul(x, weights[p])
            out[d, pl.ds(slot * fields, fields), :] = both[0:fields] + both[fields : 2 * fields]
            line = ids[pl.ds(d, 1), :]
            ids[pl.ds(d, 1), :] = jnp.where(lane_slot == slot, lane_row + blk[p], line)
        return carry

    lax.fori_loop(0, parts, part, 0)

    tall = iota((SUB, LANES), 0)
    wide = iota((SUB, LANES), 1)
    wanted = jnp.where(tall < fields, tall * oy + oy - 1, (tall - fields) * oy)
    wanted = jnp.where(wide % HALF < per, wanted, -5)

    def neighbours(d):
        east = jnp.where(d % lon == lon - 1, d - (lon - 1), d + 1)
        west = jnp.where(d % lon == 0, d + (lon - 1), d - 1)
        return east, west

    def halo(k):
        d = 2 * k
        stack = jnp.concatenate([padded_rows(out[d + u, 0:per], HALF) for u in range(2)], axis=0)
        turned = stack.T
        first, last = turned[0:1], turned[LANES - 1 : LANES]
        first_swapped = pltpu.roll(turned[0:SUB], HALF, 1)[0:1]
        last_swapped = pltpu.roll(turned[LANES - SUB : LANES], HALF, 1)[SUB - 1 : SUB]
        high, low = split(stack)
        for u in range(2):
            east, west = neighbours(d + u)
            out[d + u, per : per + 1] = ids[pl.ds(d + u, 1), :].astype(f32)
            sides = jnp.where(lane < HALF, ids[pl.ds(east, 1), :], ids[pl.ds(west, 1), :])
            out[d + u, per + 1 : per + 2] = sides.astype(f32)
            column = first if u == 0 else first_swapped
            out[west, per + 2 : per + 3] = jnp.where(lane < HALF, column, out[west, per + 2 : per + 3])
            column = last_swapped if u == 0 else last
            out[east, per + 2 : per + 3] = jnp.where(lane < HALF, out[east, per + 2 : per + 3], column)
            chosen = jnp.where(ids[pl.ds(d + u, 1), :] == wanted, 1.0, 0.0).astype(bf16)
            here = slice(u * HALF, u * HALF + HALF)
            sums = matmul(chosen, jnp.concatenate([high[here], low[here]], axis=0))

            @pl.when(d + u < devices - lon)
            def _():
                out[d + u + lon, per + SUB : per + SUB + fields] = sums[0:fields]

            @pl.when(d + u >= lon)
            def _():
                out[d + u - lon, per + SUB + fields : per + SUB + 2 * fields] = sums[fields : 2 * fields]

    def halos(k, carry):
        for u in range(2):
            halo(k * 2 + u)
        return carry

    lax.fori_loop(0, devices // 4, halos, 0)


def regrid(cap, devices, lon, oy, src, dev, blk, coupling, atm, mask, weights):
    pairs, depth, width = weights.shape
    fields = coupling.shape[0]
    batch = 32
    tall = fields * cap + 2 * SUB
    return pl.pallas_call(
        functools.partial(regrid_kernel, cap, lon, oy, batch),
        in_specs=[HBM] * 7,
        out_specs=VMEM,
        out_shape=jax.ShapeDtypeStruct((devices, tall, LANES), f32),
        scratch_shapes=[
            pltpu.VMEM((atm.shape[1] * SUB, LANES), f32),
            pltpu.VMEM((devices, LANES), jnp.int32),
            pltpu.SMEM((devices,), jnp.int32),
            pltpu.SMEM(src.shape, jnp.int32),
            pltpu.SMEM(dev.shape, jnp.int32),
            pltpu.SMEM(blk.shape, jnp.int32),
            pltpu.SMEM(coupling.shape, f32),
            pltpu.VMEM(atm.shape, bf16),
            pltpu.VMEM(mask.shape, jnp.int32),
            pltpu.VMEM(weights.shape, bf16),
            pltpu.SemaphoreType.DMA((6,)),
            pltpu.SemaphoreType.DMA((pairs // batch,)),
        ],
        compiler_params=pltpu.CompilerParams(vmem_limit_bytes=20 << 20),
        cost_estimate=pl.CostEstimate(flops=2 * 8 * pairs * depth * width, bytes_accessed=10 << 20, transcendentals=0),
        name="regrid",
    )(*in_hbm(src, dev, blk, coupling, atm, mask, weights))


def mix_kernel(
    depth_h, state_h, inv_h, mixed_h, first_h, north, south, side, depth_ref, mixed, inv, first, in_sems, out_sems
):
    fields, oy, levels, _ = mixed.shape
    depth_copy = pltpu.make_async_copy(depth_h, depth_ref, in_sems.at[2 * fields])
    depth_copy.start()
    for q in range(fields):
        for i in range(oy):
            pltpu.make_async_copy(state_h.at[q, :, i, :], mixed.at[q, i], in_sems.at[2 * q]).start()
        pltpu.make_async_copy(inv_h.at[q], inv.at[q], in_sems.at[2 * q + 1]).start()
    depth_copy.wait()
    level = iota((levels, LANES), 0)
    lane = iota((levels, LANES), 1)
    line = iota((1, LANES), 1)
    edge_depth = jnp.zeros((SUB, LANES), f32)
    for i in range(oy):
        turned = pltpu.roll(jnp.broadcast_to(depth_ref[i : i + 1, :].astype(f32), (SUB, LANES)), 2 * i + 1, 1)
        edge_depth = jnp.where(line // 2 == i, turned, edge_depth)

    def message(ref, q, row):
        ref[q, 0:levels] = mixed[q, row]
        names = padded_rows(first[q, row], LANES).T[0:1]
        ref[q, levels : levels + SUB] = jnp.concatenate(
            [depth_ref[row : row + 1, :].astype(f32), names, jnp.zeros((SUB - 2, LANES), f32)], axis=0
        )

    def field(q, carry):
        pltpu.make_async_copy(mixed_h.at[q], mixed.at[q], in_sems.at[2 * q]).wait()
        pltpu.make_async_copy(inv_h.at[q], inv.at[q], in_sems.at[2 * q + 1]).wait()

        def chunk(c, edges):
            here = jnp.zeros((levels, LANES), f32)
            for i in range(SUB):
                row = c * SUB + i
                active = level < depth_ref[pl.ds(row, 1), :]
                x = mixed[q, row]
                a = inv[q, row, 0]
                a_high, a_low = split(a)
                r_high, r_low = split(jnp.where(active, x, 0.0))
                product = matmul(
                    jnp.concatenate([a_high, a_low], axis=0), jnp.concatenate([r_high, r_low], axis=1)
                )
                solved = product[:levels, :LANES] + (product[levels:, :LANES] + product[:levels, LANES:])
                m = jnp.where(active, solved, x)
                mixed[q, row] = m
                column = jnp.broadcast_to(a[:, 0:1], (levels, LANES))
                first[q, row] = column
                here = jnp.where(lane // 2 == i, pltpu.roll(m, 2 * i + 1, 1), here)
                here = jnp.where(lane // 2 == HALF // 2 + i, column, here)
            return edges + pltpu.roll(here, 2 * SUB * c, 1)

        side[q, 0:levels] = lax.fori_loop(0, oy // SUB, chunk, jnp.zeros((levels, LANES), f32))
        side[q, levels : levels + SUB] = edge_depth
        message(north, q, 0)
        message(south, q, oy - 1)
        pltpu.make_async_copy(mixed.at[q], mixed_h.at[q], out_sems.at[2 * q]).start()
        pltpu.make_async_copy(first.at[q], first_h.at[q], out_sems.at[2 * q + 1]).start()
        return carry

    lax.fori_loop(0, fields, field, 0)
    for q in range(fields):
        pltpu.make_async_copy(mixed.at[q], mixed_h.at[q], out_sems.at[2 * q]).wait()
        pltpu.make_async_copy(first.at[q], first_h.at[q], out_sems.at[2 * q + 1]).wait()


def mix(depth, state, inverses):
    fields, levels, oy, ox = state.shape
    edge_shape = jax.ShapeDtypeStruct((fields, levels + SUB, ox), f32)
    full = (fields, oy, levels, ox)
    return pl.pallas_call(
        mix_kernel,
        in_specs=[HBM] * 3,
        out_specs=[HBM] * 2 + [VMEM] * 3,
        out_shape=[pltpu.HBM(full, f32), pltpu.HBM(full, f32), edge_shape, edge_shape, edge_shape],
        scratch_shapes=[
            pltpu.VMEM(depth.shape, jnp.int32),
            pltpu.VMEM(full, f32),
            pltpu.VMEM(inverses.shape, f32),
            pltpu.VMEM(full, f32),
            pltpu.SemaphoreType.DMA((2 * fields + 1,)),
            pltpu.SemaphoreType.DMA((2 * fields,)),
        ],
        compiler_params=pltpu.CompilerParams(vmem_limit_bytes=32 << 20),
        cost_estimate=pl.CostEstimate(flops=2 * 4 * fields * oy * levels * levels * ox, bytes_accessed=16 << 20, transcendentals=0),
        name="mix",
    )(*in_hbm(depth, state, inverses))


def finish_kernel(
    cap, recv, depth_ref, mixed_h, first_h, north, south, east, west,
    out_h, forcing, z, keep, halo, z_north, z_south, mixed, first, stage, in_sems, out_sems,
):
    fields, oy, levels, _ = mixed.shape
    devices = recv.shape[0]
    per = fields * cap
    group = LANES // per
    level = iota((levels, LANES), 0)
    lanes = iota((levels, LANES), 1)
    square_row = iota((LANES, LANES), 0)
    square_lane = iota((LANES, LANES), 1)
    line = iota((1, LANES), 1)
    even = line % 2 == 0
    for q in range(fields):
        pltpu.make_async_copy(mixed_h.at[q], mixed.at[q], in_sems.at[2 * q]).start()
        pltpu.make_async_copy(first_h.at[q], first.at[q], in_sems.at[2 * q + 1]).start()

    total = jnp.zeros((LANES, 2 * LANES), f32)
    for tile in range(devices // group):
        ids = recv[tile * group, per : per + 1, :]
        for s in range(1, group):
            ids = jnp.where(line // per == s, recv[tile * group + s, per : per + 1, :], ids)
        hot = jnp.where(square_row.astype(f32) == ids, 1.0, 0.0).astype(bf16)
        high, low = split(jnp.concatenate([recv[tile * group + s, 0:per, :] for s in range(group)], axis=0))
        total = total + matmul(hot, jnp.concatenate([high, low], axis=1))
    forcing[...] = total[:, :LANES] + total[:, LANES:]
    rows = recv[0, per + SUB : per + 2 * SUB, :]
    for d in range(1, devices):
        rows = rows + recv[d, per + SUB : per + 2 * SUB, :]
    spread = jnp.zeros((2 * oy, LANES), f32)
    row = iota((2 * oy, LANES), 0).astype(f32)
    lane_base = ((line % fields) * oy).astype(f32)
    lane_side = (line // HALF).astype(f32)
    for d in range(devices):
        place = 2.0 * (recv[d, per + 1 : per + 2, :] - lane_base) + lane_side
        spread = spread + jnp.where(place == row, recv[d, per + 2 : per + 3, :], 0.0)
    high, low = split(padded_rows(spread, LANES).T)
    small_row, small_lane = iota((SUB, LANES), 0), iota((SUB, LANES), 1)
    pick = jnp.where((small_lane % fields == small_row) & (small_lane % HALF < per), 1.0, 0.0).astype(bf16)
    columns = matmul(pick, high) + matmul(pick, low)

    depth = depth_ref[...]
    wide = iota((oy, LANES), 1)

    def upright(ref, place):
        value = jnp.where(wide == 2 * iota((oy, LANES), 0) + place, ref[0, levels : levels + 1, :], 0.0)
        return jnp.sum(value, axis=1, keepdims=True).astype(jnp.int32)

    to_east = jnp.where(wide == LANES - 1, upright(east, 1), pltpu.roll(depth, LANES - 1, 1))
    to_west = jnp.where(wide == 0, upright(west, 0), pltpu.roll(depth, 1, 1))
    to_north = jnp.concatenate([north[0, levels : levels + 1, :].astype(jnp.int32), depth[: oy - 1]], axis=0)
    to_south = jnp.concatenate([depth[1:], south[0, levels : levels + 1, :].astype(jnp.int32)], axis=0)
    for i in range(oy):
        sides = jnp.where(level < to_east[i : i + 1], diffusion_rate, 0.0)
        for other in (to_west, to_north, to_south):
            sides = sides + jnp.where(level < other[i : i + 1], diffusion_rate, 0.0)
        keep[i] = jnp.where(level < depth[i : i + 1], 1.0 - sides, 1.0)

    def outer(target, ref, start):
        names = padded_rows(
            jnp.concatenate([ref[q, levels + 1 : levels + 2, :] for q in range(fields)], axis=0), LANES
        ).T
        active = level < ref[0, levels : levels + 1, :].astype(jnp.int32)
        for q in range(fields):
            value = ref[q, 0:levels] + names[0:levels, q : q + 1] * rows[start + q : start + q + 1]
            target[q] = jnp.where(active, value, 0.0)

    outer(z_north, north, 0)
    outer(z_south, south, fields)
    for q in range(fields):
        cells = jnp.where(even, pltpu.roll(east[q], LANES - 1, 1), pltpu.roll(west[q], 1, 1))
        names = pltpu.roll(jnp.where(even, east[q], west[q]), HALF, 1)
        active = level < cells[levels : levels + 1].astype(jnp.int32)
        value = cells[0:levels] + names[0:levels] * columns[q : q + 1]
        halo[q] = jnp.where(active & (line < 2 * oy), value, 0.0)

    both = jnp.where((square_row == square_lane + 1) | (square_row == square_lane - 1), 1.0, 0.0).astype(bf16)
    both = jnp.concatenate([both, both], axis=0)
    ends = (lanes == 0) | (lanes == LANES - 1)

    def field(q, carry):
        pltpu.make_async_copy(mixed_h.at[q], mixed.at[q], in_sems.at[2 * q]).wait()
        pltpu.make_async_copy(first_h.at[q], first.at[q], in_sems.at[2 * q + 1]).wait()
        z[0] = z_north[q]
        z[oy + 1] = z_south[q]

        def solve(c, carry):
            for i in range(SUB):
                r = c * SUB + i
                m0 = mixed[q, r]
                forced = m0 + first[q, r] * forcing[pl.ds(q * oy + r, 1), :]
                active = level < depth_ref[pl.ds(r, 1), :]
                z[r + 1] = jnp.where(active, forced, 0.0)
                mixed[q, r] = jnp.where(active, forced, m0)
            return carry

        lax.fori_loop(0, oy // SUB, solve, 0)

        def diffuse(c, carry):
            start = c * SUB
            high, low = split(z[pl.ds(start + 1, SUB)].reshape(SUB * levels, LANES))
            sides = matmul(jnp.concatenate([high, low], axis=1), both)
            edge = pltpu.roll(halo[q], (LANES - 2 * SUB * c) % LANES, 1)
            for i in range(SUB):
                r = start + i
                outside = jnp.where(ends, pltpu.roll(edge, LANES - 1 - 2 * i, 1), 0.0)
                around = (z[r] + z[r + 2]) + (sides[i * levels : (i + 1) * levels] + outside)
                scale = jnp.where(level < depth_ref[pl.ds(r, 1), :], diffusion_rate, 0.0)
                stage[q, r] = mixed[q, r] * keep[r] + scale * around
                pltpu.make_async_copy(stage.at[q, r], out_h.at[q, :, r, :], out_sems.at[q]).start()
            return carry

        lax.fori_loop(0, oy // SUB, diffuse, 0)
        return carry

    lax.fori_loop(0, fields, field, 0)
    for q in range(fields):
        pltpu.make_async_copy(stage.at[q], mixed_h.at[q], out_sems.at[q]).wait()


def finish(cap, received, depth, mixed, first, halos):
    fields, oy, levels, ox = mixed.shape
    edge = pltpu.VMEM((fields, levels, ox), f32)
    full = pltpu.VMEM((fields, oy, levels, ox), f32)
    return pl.pallas_call(
        functools.partial(finish_kernel, cap),
        in_specs=[VMEM] * 2 + [HBM] * 2 + [VMEM] * 4,
        out_specs=HBM,
        out_shape=pltpu.HBM((fields, levels, oy, ox), f32),
        scratch_shapes=[
            pltpu.VMEM((fields * oy, ox), f32),
            pltpu.VMEM((oy + 2, levels, ox), f32),
            pltpu.VMEM((oy, levels, ox), f32),
            edge,
            edge,
            edge,
            full,
            full,
            full,
            pltpu.SemaphoreType.DMA((2 * fields,)),
            pltpu.SemaphoreType.DMA((fields,)),
        ],
        compiler_params=pltpu.CompilerParams(vmem_limit_bytes=32 << 20),
        cost_estimate=pl.CostEstimate(flops=20 * fields * oy * levels * ox, bytes_accessed=12 << 20, transcendentals=0),
        name="finish",
    )(received, depth, *in_hbm(mixed, first), *halos)


def shift(x, axis, step, wrap):
    count = lax.axis_size(axis)
    pairs = [(i, (i + step) % count) for i in range(count) if wrap or 0 <= i + step < count]
    return lax.ppermute(x, axis, pairs)


def on_device(
    atm_flux, sea_mask, src_block, dest_dev, dest_block, intersection_weights, coupling, inverses, ocean_state,
    depth_levels,
):
    lon = lax.axis_size("lon")
    devices = lax.axis_size("lat") * lon
    oy = ocean_state.shape[2]
    cap = max(SUB, 2 * src_block.shape[0] // devices)
    slots = regrid(
        cap, devices, lon, oy, src_block, dest_dev[:, 0], dest_block, coupling, atm_flux, sea_mask,
        intersection_weights,
    )
    received = lax.all_to_all(slots, ("lat", "lon"), 0, 0, tiled=True)
    mixed, first, north, south, side = mix(depth_levels, ocean_state, inverses)
    halos = (
        shift(south, "lat", 1, False),
        shift(north, "lat", -1, False),
        shift(side, "lon", -1, True),
        shift(side, "lon", 1, True),
    )
    return finish(cap, received, depth_levels, mixed, first, halos)


def solution(mesh):
    placed = (
        P(None, "lat", "lon"),
        P("lat", "lon"),
        P(("lat", "lon")),
        P(("lat", "lon"), None),
        P(("lat", "lon")),
        P(("lat", "lon"), None, None),
        P(),
        P(None, "lat", "lon", None, None),
        P(None, None, "lat", "lon"),
        P("lat", "lon"),
    )
    return jax.shard_map(
        on_device,
        mesh=mesh,
        in_specs=placed,
        out_specs=P(None, None, "lat", "lon"),
        check_vma=False,
    )
```

time: 81.9 us -> 62.3 us (0.76)
  Pallas kernels: 57.1 us -> 32.6 us
  waiting for transfers between devices: 4.23 us -> 13.5 us
  local copies, waits for them, and re-layouts: 4.84 us -> 0.01 us
    pallas_call x2, Pallas kernels: 42.8 us -> 21.2 us  [the longest x1 11.4 us: mix(): pl.pallas_call(mix_kernel, in_specs=[HBM] * 3, out_specs=[HBM] * 2 + [VME...]
    all_to_all x1, waiting for transfers between devices: 0.01 us -> 6.39 us  [on_device(): received = lax.all_to_all(slots, ('lat', 'lon'), 0, 0, tiled=True)]
    unnamed x6 -> x2, local copies, waits for them, and re-layouts: 4.84 us -> 0.01 us
    pallas_call x1, Pallas kernels: 14.3 us -> 11.4 us  [regrid(): pl.pallas_call(functools.partial(regrid_kernel, cap, lon, oy, batch), in_...]
    ppermute x4, waiting for transfers between devices: 4.22 us -> 7.1 us  [shift(): return lax.ppermute(x, axis, pairs)]
  transfers between devices with their start and end apart: 5 -> 5, of which waited for: 2 -> 3; matrix products, arithmetic and copies ran while one was open for 0% -> 0% of each run, Pallas kernels for 32% -> 19%
where the time goes in v3:
time: 62.3 us; the launch traced here: 61.1 us
  Pallas kernels  32.6 us (52%)
  starting transfers between devices  15 us (24%)
  waiting for transfers between devices  13.5 us (22%)
    pallas_call x1, Pallas kernels, mix(): pl.pallas_call(mix_kernel, in_specs=[HBM] * 3, out_specs=[HBM] * 2 + [VME...  11.4 us
    pallas_call x1, Pallas kernels, regrid(): pl.pallas_call(functools.partial(regrid_kernel, cap, lon, oy, batch), in_...  11.4 us
    pallas_call x1, Pallas kernels, finish(): pl.pallas_call(functools.partial(finish_kernel, cap), in_specs=[VMEM] * 2...  9.81 us
    ppermute x4, starting transfers between devices, shift(): return lax.ppermute(x, axis, pairs)  7.67 us
    all_to_all x1, starting transfers between devices, on_device(): received = lax.all_to_all(slots, ('lat', 'lon'), 0, 0, tiled=True)  7.31 us
    ppermute x4, waiting for transfers between devices, shift(): return lax.ppermute(x, axis, pairs)  7.1 us
    all_to_all x1, waiting for transfers between devices, on_device(): received = lax.all_to_all(slots, ('lat', 'lon'), 0, 0, tiled=True)  6.39 us
  transfers between devices with their start and end apart: 5, of which 3 were waited for; matrix products, arithmetic and copies ran while one was open for 0% of the time, Pallas kernels for 19%

profile of v3, /device:TPU:0, one launch (start us, length us, event | category | flops | bytes accessed | tf_op | source)
XLA Modules:
  0.0 61.1 jit_solution(2805381152927843866)
XLA Ops:
  0.0 11.4 %regrid.1 = f32[32,80,128]{2,1,0:T(8,128)} custom-call(s32[256]{0:T(256)} %src_h.1, s32[256]{0:T(256)} %bitcast.1, s32[256]{0:T(256)} %blk_h.1, f32[4,8]{1,0:T(4,128)} %coupling_h.1, bf16[8,64,128]{2,1,0:T(8,128)(2,1)} %atm_h.1, s32[64,128]{1,0:T(8,128)} %mask_h.1, bf16[256,128,128]{2,1,0:T(8,128)(2,1)} %weights_h.1), custom_call_target="tpu_custom_call" | custom-call | flops 67108864 | bytes 10485760 | tf_op jit(solution)/shard_map/regrid/pallas_call | solution.py:162
  11.4 7.3 %all-to-all-start = ((f32[32,80,128]{2,1,0:T(8,128)}), f32[32,80,128]{2,1,0:T(8,128)S(1)}, u32[]{:S(2)}, u32[]{:S(2)}) async-start(f32[32,80,128]{2,1,0:T(8,128)} %regrid.1), calls=%async_computation | async-start | bytes 2621440 | tf_op jit(solution)/shard_map/all_to_all | solution.py:442
  18.7 0.0 copy-start
  18.7 11.4 %mix.1 = (f32[4,32,80,128]{3,2,1,0:T(8,128)}, f32[4,32,80,128]{3,2,1,0:T(8,128)}, f32[4,88,128]{2,1,0:T(8,128)S(1)}, f32[4,88,128]{2,1,0:T(8,128)S(1)}, f32[4,88,128]{2,1,0:T(8,128)S(1)}) custom-call(s32[32,128]{1,0:T(8,128)} %depth_ref.1, f32[4,80,32,128]{3,2,1,0:T(8,128)} %state_h.1, f32[4,32,1,80,80]{4,3,2,1,0:T(8,128)} %inv_h.1), custom_call_target="tpu_custom_call" | custom-call | flops 838860800 | bytes 16777216 | tf_op jit(solution)/shard_map/mix/pallas_call | solution.py:256
  30.1 3.7 %collective-permute-start = (f32[4,88,128]{2,1,0:T(8,128)S(1)}, f32[4,88,128]{2,1,0:T(8,128)S(1)}, u32[]{:S(2)}, u32[]{:S(2)}) collective-permute-start(f32[4,88,128]{2,1,0:T(8,128)S(1)} %get-tuple-element.12), channel_id=1, source_target_pairs={{0,8},{8,16},{16,24},{1,9},{9,17},{17,25},{2,10},{10,18},{18,26},{... | collective-permute-start | bytes 540680 | tf_op jit(solution)/shard_map/ppermute | solution.py:427
  33.8 1.3 %collective-permute-start.1 = (f32[4,88,128]{2,1,0:T(8,128)S(1)}, f32[4,88,128]{2,1,0:T(8,128)S(1)}, u32[]{:S(2)}, u32[]{:S(2)}) collective-permute-start(f32[4,88,128]{2,1,0:T(8,128)S(1)} %get-tuple-element.13), channel_id=1, source_target_pairs={{8,0},{16,8},{24,16},{9,1},{17,9},{25,17},{10,2},{18,10},{26,18},{... | collective-permute-start | bytes 540680 | tf_op jit(solution)/shard_map/ppermute | solution.py:427
  35.1 0.1 collective-permute-start.3
  35.2 2.6 %collective-permute-start.2 = (f32[4,88,128]{2,1,0:T(8,128)S(1)}, f32[4,88,128]{2,1,0:T(8,128)S(1)}, u32[]{:S(2)}, u32[]{:S(2)}) collective-permute-start(f32[4,88,128]{2,1,0:T(8,128)S(1)} %get-tuple-element.14), channel_id=1, source_target_pairs={{0,7},{1,0},{2,1},{3,2},{4,3},{5,4},{6,5},{7,6},{8,15},{9,8},{10,9... | collective-permute-start | bytes 540680 | tf_op jit(solution)/shard_map/ppermute | solution.py:427
  37.8 6.7 %collective-permute-done.north = f32[4,88,128]{2,1,0:T(8,128)S(1)} collective-permute-done((f32[4,88,128]{2,1,0:T(8,128)S(1)}, f32[4,88,128]{2,1,0:T(8,128)S(1)}, u32[]{:S(2)}, u32[]{:S(2)}) %collective-permute-start) | collective-permute-done | bytes 180256 | tf_op jit(solution)/shard_map/ppermute | solution.py:427
  44.5 0.4 collective-permute-done.1.south
  44.9 0.0 collective-permute-done.3.west
  44.9 0.0 collective-permute-done.2.east
  44.9 6.4 %all-to-all-done.recv = f32[32,80,128]{2,1,0:T(8,128)S(1)} async-done(((f32[32,80,128]{2,1,0:T(8,128)}), f32[32,80,128]{2,1,0:T(8,128)S(1)}, u32[]{:S(2)}, u32[]{:S(2)}) %all-to-all-start) | async-done | bytes 1310752 | tf_op jit(solution)/shard_map/all_to_all | solution.py:442
  51.3 0.0 copy-done
  51.3 9.8 %finish.1 = f32[4,80,32,128]{3,2,1,0:T(8,128)} custom-call(f32[32,80,128]{2,1,0:T(8,128)S(1)} %all-to-all-done.recv, s32[32,128]{1,0:T(8,128)S(1)} %copy-done, f32[4,32,80,128]{3,2,1,0:T(8,128)} %get-tuple-element.10.mixed_h, f32[4,32,80,128]{3,2,1,0:T(8,128)} %get-tuple-element.11.first_h, f32[4,88,128]{2,1,0:T(8,128)S(1)} %collective-permute-done.north, ...), custom_call_target="tpu_custom_call" | custom-call | flops 26214400 | bytes 12582912 | tf_op jit(solution)/shard_map/finish/pallas_call | solution.py:400
Async XLA Ops:
  11.4 39.9 %all-to-all-start = ((f32[32,80,128]{2,1,0:T(8,128)}), f32[32,80,128]{2,1,0:T(8,128)S(1)}, u32[]{:S(2)}, u32[]{:S(2)}) async-start(f32[32,80,128]{2,1,0:T(8,128)} %regrid.1), calls=%async_computation | async-start | bytes 2621440 | tf_op jit(solution)/shard_map/all_to_all | solution.py:442
  18.7 32.6 %copy-start = (s32[32,128]{1,0:T(8,128)S(1)}, s32[32,128]{1,0:T(8,128)}, u32[]{:S(2)}) copy-start(s32[32,128]{1,0:T(8,128)} %depth_ref.1) | copy-start | bytes 49156
  30.1 14.4 %collective-permute-start = (f32[4,88,128]{2,1,0:T(8,128)S(1)}, f32[4,88,128]{2,1,0:T(8,128)S(1)}, u32[]{:S(2)}, u32[]{:S(2)}) collective-permute-start(f32[4,88,128]{2,1,0:T(8,128)S(1)} %get-tuple-element.12), channel_id=1, source_target_pairs={{0,8},{8,16},{16,24},{1,9},{9,17},{17,25},{2,10},{10,18},{18,26},{... | collective-permute-start | bytes 540680 | tf_op jit(solution)/shard_map/ppermute | solution.py:427
  33.8 11.1 %collective-permute-start.1 = (f32[4,88,128]{2,1,0:T(8,128)S(1)}, f32[4,88,128]{2,1,0:T(8,128)S(1)}, u32[]{:S(2)}, u32[]{:S(2)}) collective-permute-start(f32[4,88,128]{2,1,0:T(8,128)S(1)} %get-tuple-element.13), channel_id=1, source_target_pairs={{8,0},{16,8},{24,16},{9,1},{17,9},{25,17},{10,2},{18,10},{26,18},{... | collective-permute-start | bytes 540680 | tf_op jit(solution)/shard_map/ppermute | solution.py:427
  35.1 9.8 %collective-permute-start.3 = (f32[4,88,128]{2,1,0:T(8,128)S(1)}, f32[4,88,128]{2,1,0:T(8,128)S(1)}, u32[]{:S(2)}, u32[]{:S(2)}) collective-permute-start(f32[4,88,128]{2,1,0:T(8,128)S(1)} %get-tuple-element.14), channel_id=1, source_target_pairs={{0,1},{1,2},{2,3},{3,4},{4,5},{5,6},{6,7},{7,0},{8,9},{9,10},{10,1... | collective-permute-start | bytes 540680 | tf_op jit(solution)/shard_map/ppermute | solution.py:427
  35.2 9.7 %collective-permute-start.2 = (f32[4,88,128]{2,1,0:T(8,128)S(1)}, f32[4,88,128]{2,1,0:T(8,128)S(1)}, u32[]{:S(2)}, u32[]{:S(2)}) collective-permute-start(f32[4,88,128]{2,1,0:T(8,128)S(1)} %get-tuple-element.14), channel_id=1, source_target_pairs={{0,7},{1,0},{2,1},{3,2},{4,3},{5,4},{6,5},{7,6},{8,15},{9,8},{10,9... | collective-permute-start | bytes 540680 | tf_op jit(solution)/shard_map/ppermute | solution.py:427

commit v4 on v3

--- a/solution.py
+++ b/solution.py
@@ -39,7 +39,7 @@
 
 
 def regrid_kernel(
-    cap, lon, oy, batch, src_h, dev_h, blk_h, coupling_h, atm_h, mask_h, weights_h,
+    cap, lat, lon, oy, batch, src_h, dev_h, blk_h, coupling_h, atm_h, mask_h, weights_h,
     out, rows, ids, count, src, dev, blk, coupling, atm, mask, weights, small_sem, big_sem,
 ):
     fluxes, atm_rows, _ = atm.shape
@@ -91,76 +91,66 @@
     lane_slot = (lane % per) // fields
     lane_row = (lane % fields) * oy
 
+    def place(d):
+        return lax.rem(d, lon) * lat + lax.div(d, lon)
+
     def part(k, carry):
         big(k).wait()
-        for u in range(batch):
+        for u in range(0, batch, 2):
             p = k * batch + u
-            d = dev[p]
-            slot = jnp.minimum(count[d], cap - 1)
-            count[d] = slot + 1
-            x = rows[pl.ds(pl.multiple_of(src[p] * SUB, SUB), SUB), :].astype(bf16)
-            both = matmul(x, weights[p])
-            out[d, pl.ds(slot * fields, fields), :] = both[0:fields] + both[fields : 2 * fields]
-            line = ids[pl.ds(d, 1), :]
-            ids[pl.ds(d, 1), :] = jnp.where(lane_slot == slot, lane_row + blk[p], line)
+            x = jnp.concatenate(
+                [rows[pl.ds(pl.multiple_of(src[p + v] * SUB, SUB), SUB), :] for v in range(2)], axis=0
+            ).astype(bf16)
+            both = matmul(x, jnp.concatenate([weights[p], weights[p + 1]], axis=1))
+            for v in range(2):
+                d = dev[p + v]
+                slot = jnp.minimum(count[d], cap - 1)
+                count[d] = slot + 1
+                half = both[v * SUB : v * SUB + SUB, v * LANES : (v + 1) * LANES]
+                out[place(d), pl.ds(slot * fields, fields), :] = half[0:fields] + half[fields : 2 * fields]
+                line = ids[pl.ds(d, 1), :]
+                ids[pl.ds(d, 1), :] = jnp.where(lane_slot == slot, lane_row + blk[p + v], line)
         return carry
 
     lax.fori_loop(0, parts, part, 0)
-
-    tall = iota((SUB, LANES), 0)
-    wide = iota((SUB, LANES), 1)
-    wanted = jnp.where(tall < fields, tall * oy + oy - 1, (tall - fields) * oy)
-    wanted = jnp.where(wide % HALF < per, wanted, -5)
-
-    def neighbours(d):
-        east = jnp.where(d % lon == lon - 1, d - (lon - 1), d + 1)
-        west = jnp.where(d % lon == 0, d + (lon - 1), d - 1)
-        return east, west
 
     def halo(k):
         d = 2 * k
-        stack = jnp.concatenate([padded_rows(out[d + u, 0:per], HALF) for u in range(2)], axis=0)
-        turned = stack.T
+        turned = jnp.concatenate(
+            [padded_rows(out[place(d + u), 0:per], HALF) for u in range(2)], axis=0
+        ).T
         first, last = turned[0:1], turned[LANES - 1 : LANES]
         first_swapped = pltpu.roll(turned[0:SUB], HALF, 1)[0:1]
         last_swapped = pltpu.roll(turned[LANES - SUB : LANES], HALF, 1)[SUB - 1 : SUB]
-        high, low = split(stack)
         for u in range(2):
-            east, west = neighbours(d + u)
-            out[d + u, per : per + 1] = ids[pl.ds(d + u, 1), :].astype(f32)
+            b = lax.rem(d + u, lon)
+            east = jnp.where(b == lon - 1, d + u - (lon - 1), d + u + 1)
+            west = jnp.where(b == 0, d + u + (lon - 1), d + u - 1)
+            here, to_east, to_west = place(d + u), place(east), place(west)
+            out[here, per : per + 1] = ids[pl.ds(d + u, 1), :].astype(f32)
             sides = jnp.where(lane < HALF, ids[pl.ds(east, 1), :], ids[pl.ds(west, 1), :])
-            out[d + u, per + 1 : per + 2] = sides.astype(f32)
+            out[here, per + 1 : per + 2] = sides.astype(f32)
             column = first if u == 0 else first_swapped
-            out[west, per + 2 : per + 3] = jnp.where(lane < HALF, column, out[west, per + 2 : per + 3])
+            out[to_west, per + 2 : per + 3] = jnp.where(lane < HALF, column, out[to_west, per + 2 : per + 3])
             column = last_swapped if u == 0 else last
-            out[east, per + 2 : per + 3] = jnp.where(lane < HALF, out[east, per + 2 : per + 3], column)
-            chosen = jnp.where(ids[pl.ds(d + u, 1), :] == wanted, 1.0, 0.0).astype(bf16)
-            here = slice(u * HALF, u * HALF + HALF)
-            sums = matmul(chosen, jnp.concatenate([high[here], low[here]], axis=0))
-
-            @pl.when(d + u < devices - lon)
-            def _():
-                out[d + u + lon, per + SUB : per + SUB + fields] = sums[0:fields]
-
-            @pl.when(d + u >= lon)
-            def _():
-                out[d + u - lon, per + SUB + fields : per + SUB + 2 * fields] = sums[fields : 2 * fields]
+            out[to_east, per + 2 : per + 3] = jnp.where(lane < HALF, out[to_east, per + 2 : per + 3], column)
 
     def halos(k, carry):
-        for u in range(2):
-            halo(k * 2 + u)
+        for u in range(4):
+            halo(k * 4 + u)
         return carry
 
-    lax.fori_loop(0, devices // 4, halos, 0)
-
-
-def regrid(cap, devices, lon, oy, src, dev, blk, coupling, atm, mask, weights):
+    lax.fori_loop(0, devices // 8, halos, 0)
+
+
+def regrid(cap, lat, lon, oy, src, dev, blk, coupling, atm, mask, weights):
     pairs, depth, width = weights.shape
     fields = coupling.shape[0]
     batch = 32
-    tall = fields * cap + 2 * SUB
+    devices = lat * lon
+    tall = fields * cap + SUB
     return pl.pallas_call(
-        functools.partial(regrid_kernel, cap, lon, oy, batch),
+        functools.partial(regrid_kernel, cap, lat, lon, oy, batch),
         in_specs=[HBM] * 7,
         out_specs=VMEM,
         out_shape=jax.ShapeDtypeStruct((devices, tall, LANES), f32),
@@ -272,14 +262,65 @@
     )(*in_hbm(depth, state, inverses))
 
 
+def collect_kernel(cap, fields, oy, recv, out):
+    lat = out.shape[0]
+    lon = recv.shape[0] // lat
+    per = fields * cap
+    group = LANES // per
+    forced = fields * oy
+    square_row = iota((LANES, LANES), 0).astype(f32)
+    line = iota((1, LANES), 1)
+    row = iota((2 * oy, LANES), 0).astype(f32)
+    lane_base = ((line % fields) * oy).astype(f32)
+    lane_side = (line // HALF).astype(f32)
+    small_row, small_lane = iota((SUB, LANES), 0), iota((SUB, LANES), 1)
+    pick = jnp.where((small_lane % fields == small_row) & (small_lane % HALF < per), 1.0, 0.0).astype(bf16)
+    nothing = jnp.zeros((fields, LANES), f32)
+    for a in range(lat):
+        total = jnp.zeros((LANES, 2 * LANES), f32)
+        for tile in range(lon // group):
+            places = [(tile * group + s) * lat + a for s in range(group)]
+            ids = recv[places[0], per : per + 1, :]
+            for s in range(1, group):
+                ids = jnp.where(line // per == s, recv[places[s], per : per + 1, :], ids)
+            hot = jnp.where(square_row == ids, 1.0, 0.0).astype(bf16)
+            high, low = split(jnp.concatenate([recv[p, 0:per, :] for p in places], axis=0))
+            total = total + matmul(hot, jnp.concatenate([high, low], axis=1))
+        total = total[:, :LANES] + total[:, LANES:]
+        out[a, 0:forced] = total
+        if a == 0:
+            out[a, forced : forced + fields] = nothing
+        if a == lat - 1:
+            out[a, forced + fields : forced + 2 * fields] = nothing
+        for q in range(fields):
+            if a + 1 < lat:
+                out[a + 1, forced + q : forced + q + 1] = total[q * oy + oy - 1 : q * oy + oy]
+            if a > 0:
+                out[a - 1, forced + fields + q : forced + fields + q + 1] = total[q * oy : q * oy + 1]
+        spread = jnp.zeros((2 * oy, LANES), f32)
+        for b in range(lon):
+            place = 2.0 * (recv[b * lat + a, per + 1 : per + 2, :] - lane_base) + lane_side
+            spread = spread + jnp.where(place == row, recv[b * lat + a, per + 2 : per + 3, :], 0.0)
+        high, low = split(padded_rows(spread, LANES).T)
+        out[a, forced + SUB : forced + 2 * SUB] = matmul(pick, high) + matmul(pick, low)
+
+
+def collect(cap, fields, oy, lat, received):
+    return pl.pallas_call(
+        functools.partial(collect_kernel, cap, fields, oy),
+        in_specs=[VMEM],
+        out_specs=VMEM,
+        out_shape=jax.ShapeDtypeStruct((lat, fields * oy + 2 * SUB, LANES), f32),
+        compiler_params=pltpu.CompilerParams(vmem_limit_bytes=16 << 20),
+        name="collect",
+    )(received)
+
+
 def finish_kernel(
-    cap, recv, depth_ref, mixed_h, first_h, north, south, east, west,
+    recv, depth_ref, mixed_h, first_h, north, south, east, west,
     out_h, forcing, z, keep, halo, z_north, z_south, mixed, first, stage, in_sems, out_sems,
 ):
     fields, oy, levels, _ = mixed.shape
-    devices = recv.shape[0]
-    per = fields * cap
-    group = LANES // per
     level = iota((levels, LANES), 0)
     lanes = iota((levels, LANES), 1)
     square_row = iota((LANES, LANES), 0)
@@ -290,29 +331,13 @@
         pltpu.make_async_copy(mixed_h.at[q], mixed.at[q], in_sems.at[2 * q]).start()
         pltpu.make_async_copy(first_h.at[q], first.at[q], in_sems.at[2 * q + 1]).start()
 
-    total = jnp.zeros((LANES, 2 * LANES), f32)
-    for tile in range(devices // group):
-        ids = recv[tile * group, per : per + 1, :]
-        for s in range(1, group):
-            ids = jnp.where(line // per == s, recv[tile * group + s, per : per + 1, :], ids)
-        hot = jnp.where(square_row.astype(f32) == ids, 1.0, 0.0).astype(bf16)
-        high, low = split(jnp.concatenate([recv[tile * group + s, 0:per, :] for s in range(group)], axis=0))
-        total = total + matmul(hot, jnp.concatenate([high, low], axis=1))
-    forcing[...] = total[:, :LANES] + total[:, LANES:]
-    rows = recv[0, per + SUB : per + 2 * SUB, :]
-    for d in range(1, devices):
-        rows = rows + recv[d, per + SUB : per + 2 * SUB, :]
-    spread = jnp.zeros((2 * oy, LANES), f32)
-    row = iota((2 * oy, LANES), 0).astype(f32)
-    lane_base = ((line % fields) * oy).astype(f32)
-    lane_side = (line // HALF).astype(f32)
-    for d in range(devices):
-        place = 2.0 * (recv[d, per + 1 : per + 2, :] - lane_base) + lane_side
-        spread = spread + jnp.where(place == row, recv[d, per + 2 : per + 3, :], 0.0)
-    high, low = split(padded_rows(spread, LANES).T)
-    small_row, small_lane = iota((SUB, LANES), 0), iota((SUB, LANES), 1)
-    pick = jnp.where((small_lane % fields == small_row) & (small_lane % HALF < per), 1.0, 0.0).astype(bf16)
-    columns = matmul(pick, high) + matmul(pick, low)
+    total = recv[0]
+    for a in range(1, recv.shape[0]):
+        total = total + recv[a]
+    forced_rows = fields * oy
+    forcing[...] = total[0:forced_rows]
+    rows = total[forced_rows : forced_rows + SUB]
+    columns = total[forced_rows + SUB :]
 
     depth = depth_ref[...]
     wide = iota((oy, LANES), 1)
@@ -393,12 +418,12 @@
         pltpu.make_async_copy(stage.at[q], mixed_h.at[q], out_sems.at[q]).wait()
 
 
-def finish(cap, received, depth, mixed, first, halos):
+def finish(received, depth, mixed, first, halos):
     fields, oy, levels, ox = mixed.shape
     edge = pltpu.VMEM((fields, levels, ox), f32)
     full = pltpu.VMEM((fields, oy, levels, ox), f32)
     return pl.pallas_call(
-        functools.partial(finish_kernel, cap),
+        finish_kernel,
         in_specs=[VMEM] * 2 + [HBM] * 2 + [VMEM] * 4,
         out_specs=HBM,
         out_shape=pltpu.HBM((fields, levels, oy, ox), f32),
@@ -431,15 +456,14 @@
     atm_flux, sea_mask, src_block, dest_dev, dest_block, intersection_weights, coupling, inverses, ocean_state,
     depth_levels,
 ):
-    lon = lax.axis_size("lon")
-    devices = lax.axis_size("lat") * lon
-    oy = ocean_state.shape[2]
-    cap = max(SUB, 2 * src_block.shape[0] // devices)
+    lat, lon = lax.axis_size("lat"), lax.axis_size("lon")
+    fields, _, oy, _ = ocean_state.shape
+    cap = max(SUB, 2 * src_block.shape[0] // (lat * lon))
     slots = regrid(
-        cap, devices, lon, oy, src_block, dest_dev[:, 0], dest_block, coupling, atm_flux, sea_mask,
+        cap, lat, lon, oy, src_block, dest_dev[:, 0], dest_block, coupling, atm_flux, sea_mask,
         intersection_weights,
     )
-    received = lax.all_to_all(slots, ("lat", "lon"), 0, 0, tiled=True)
+    in_plane = lax.all_to_all(slots, "lon", 0, 0, tiled=True)
     mixed, first, north, south, side = mix(depth_levels, ocean_state, inverses)
     halos = (
         shift(south, "lat", 1, False),
@@ -447,7 +471,8 @@
         shift(side, "lon", -1, True),
         shift(side, "lon", 1, True),
     )
-    return finish(cap, received, depth_levels, mixed, first, halos)
+    received = lax.all_to_all(collect(cap, fields, oy, lat, in_plane), "lat", 0, 0, tiled=True)
+    return finish(received, depth_levels, mixed, first, halos)
 
 
 def solution(mesh):

time: 62.3 us -> 70.1 us (1.13); the launches traced: 61.1 us -> 69.8 us
  blocking collectives: 0 us -> 21.7 us
  waiting for transfers between devices: 13.5 us -> 5.07 us
  Pallas kernels: 32.6 us -> 30.2 us
  starting transfers between devices: 15 us -> 12.8 us
    all_to_all x0 -> x1, blocking collectives: none -> 21.7 us  [on_device(): in_plane = lax.all_to_all(slots, 'lon', 0, 0, tiled=True)]
    all_to_all x1, waiting for transfers between devices: 6.39 us -> 0.01 us  [on_device(): lax.all_to_all(collect(cap, fields, oy, lat, in_plane), 'lat', 0, 0, tile...]
    all_to_all x1, starting transfers between devices: 7.31 us -> 4.87 us  [on_device(): lax.all_to_all(collect(cap, fields, oy, lat, in_plane), 'lat', 0, 0, tile...]
    pallas_call x2 -> x3, Pallas kernels: 21.2 us -> 18.8 us  [the longest x1 9.49 us: finish(): pl.pallas_call(finish_kernel, in_specs=[VMEM] * 2 + [HBM] * 2 + [VMEM] *...]
    ppermute x4, waiting for transfers between devices: 7.1 us -> 5.07 us  [shift(): return lax.ppermute(x, axis, pairs)]
  transfers between devices with their start and end apart: 5 -> 5, of which waited for: 3 -> 2; matrix products, arithmetic and copies ran while one was open for 0% -> 0% of each run, Pallas kernels for 19% -> 16%
where the time goes in v4:
time: 70.1 us; the launch traced here: 69.8 us
  Pallas kernels  30.2 us (43%)
  blocking collectives  21.7 us (31%)
  starting transfers between devices  12.8 us (18%)
  waiting for transfers between devices  5.07 us (7%)
    all_to_all x1, blocking collectives, on_device(): in_plane = lax.all_to_all(slots, 'lon', 0, 0, tiled=True)  21.7 us
    pallas_call x1, Pallas kernels, mix(): pl.pallas_call(mix_kernel, in_specs=[HBM] * 3, out_specs=[HBM] * 2 + [VME...  11.4 us
    pallas_call x1, Pallas kernels, finish(): pl.pallas_call(finish_kernel, in_specs=[VMEM] * 2 + [HBM] * 2 + [VMEM] *...  9.49 us
    pallas_call x1, Pallas kernels, regrid(): pl.pallas_call(functools.partial(regrid_kernel, cap, lat, lon, oy, batch)...  7.99 us
    ppermute x4, starting transfers between devices, shift(): return lax.ppermute(x, axis, pairs)  7.92 us
    ppermute x4, waiting for transfers between devices, shift(): return lax.ppermute(x, axis, pairs)  5.07 us
    all_to_all x1, starting transfers between devices, on_device(): lax.all_to_all(collect(cap, fields, oy, lat, in_plane), 'lat', 0, 0, tile...  4.87 us
  transfers between devices with their start and end apart: 5, of which 2 were waited for; matrix products, arithmetic and copies ran while one was open for 0% of the time, Pallas kernels for 16%

profile of v4, /device:TPU:0, one launch (start us, length us, event | category | flops | bytes accessed | tf_op | source)
XLA Modules:
  0.0 69.8 jit_solution(12218673451415570765)
XLA Ops:
  0.0 8.0 %regrid.1 = f32[32,72,128]{2,1,0:T(8,128)S(1)} custom-call(s32[256]{0:T(256)} %src_h.1, s32[256]{0:T(256)} %bitcast.1, s32[256]{0:T(256)} %blk_h.1, f32[4,8]{1,0:T(4,128)} %coupling_h.1, bf16[8,64,128]{2,1,0:T(8,128)(2,1)} %atm_h.1, s32[64,128]{1,0:T(8,128)} %mask_h.1, bf16[256,128,128]{2,1,0:T(8,128)(2,1)} %weights_h.1), custom_call_target="tpu_custom_call" | custom-call | flops 67108864 | bytes 10485760 | tf_op jit(solution)/shard_map/regrid/pallas_call | solution.py:152
  8.0 21.7 %all_to_all.10.recv = f32[32,72,128]{2,1,0:T(8,128)S(1)} all-to-all(f32[32,72,128]{2,1,0:T(8,128)S(1)} %regrid.1), channel_id=1, replica_groups=mesh['lat'=4,'lon'=8] {'lon'}, dimensions={0} | all-to-all | bytes 2359296 | tf_op jit(solution)/shard_map/all_to_all | solution.py:466
  29.7 1.3 %collect.1 = f32[4,144,128]{2,1,0:T(8,128)} custom-call(f32[32,72,128]{2,1,0:T(8,128)S(1)} %all_to_all.10.recv), custom_call_target="tpu_custom_call" | custom-call | tf_op jit(solution)/shard_map/collect/pallas_call | solution.py:309
  31.0 4.9 %all-to-all-start.1 = ((f32[4,144,128]{2,1,0:T(8,128)}), f32[4,144,128]{2,1,0:T(8,128)S(1)}, u32[]{:S(2)}, u32[]{:S(2)}) async-start(f32[4,144,128]{2,1,0:T(8,128)} %collect.1), calls=%async_computation.1 | async-start | bytes 589824 | tf_op jit(solution)/shard_map/all_to_all | solution.py:474
  35.9 0.0 copy-start
  35.9 11.4 %mix.1 = (f32[4,32,80,128]{3,2,1,0:T(8,128)}, f32[4,32,80,128]{3,2,1,0:T(8,128)}, f32[4,88,128]{2,1,0:T(8,128)S(1)}, f32[4,88,128]{2,1,0:T(8,128)S(1)}, f32[4,88,128]{2,1,0:T(8,128)S(1)}) custom-call(s32[32,128]{1,0:T(8,128)} %depth_ref.1, f32[4,80,32,128]{3,2,1,0:T(8,128)} %state_h.1, f32[4,32,1,80,80]{4,3,2,1,0:T(8,128)} %inv_h.1), custom_call_target="tpu_custom_call" | custom-call | flops 838860800 | bytes 16777216 | tf_op jit(solution)/shard_map/mix/pallas_call | solution.py:246
  47.3 3.9 %collective-permute-start = (f32[4,88,128]{2,1,0:T(8,128)S(1)}, f32[4,88,128]{2,1,0:T(8,128)S(1)}, u32[]{:S(2)}, u32[]{:S(2)}) collective-permute-start(f32[4,88,128]{2,1,0:T(8,128)S(1)} %get-tuple-element.12), channel_id=1, source_target_pairs={{0,8},{8,16},{16,24},{1,9},{9,17},{17,25},{2,10},{10,18},{18,26},{... | collective-permute-start | bytes 540680 | tf_op jit(solution)/shard_map/ppermute | solution.py:452
  51.3 1.3 %collective-permute-start.1 = (f32[4,88,128]{2,1,0:T(8,128)S(1)}, f32[4,88,128]{2,1,0:T(8,128)S(1)}, u32[]{:S(2)}, u32[]{:S(2)}) collective-permute-start(f32[4,88,128]{2,1,0:T(8,128)S(1)} %get-tuple-element.13), channel_id=1, source_target_pairs={{8,0},{16,8},{24,16},{9,1},{17,9},{25,17},{10,2},{18,10},{26,18},{... | collective-permute-start | bytes 540680 | tf_op jit(solution)/shard_map/ppermute | solution.py:452
  52.6 0.1 collective-permute-start.3
  52.6 2.6 %collective-permute-start.2 = (f32[4,88,128]{2,1,0:T(8,128)S(1)}, f32[4,88,128]{2,1,0:T(8,128)S(1)}, u32[]{:S(2)}, u32[]{:S(2)}) collective-permute-start(f32[4,88,128]{2,1,0:T(8,128)S(1)} %get-tuple-element.14), channel_id=1, source_target_pairs={{0,7},{1,0},{2,1},{3,2},{4,3},{5,4},{6,5},{7,6},{8,15},{9,8},{10,9... | collective-permute-start | bytes 540680 | tf_op jit(solution)/shard_map/ppermute | solution.py:452
  55.3 0.0 collective-permute-done.north
  55.3 3.4 %collective-permute-done.1.south = f32[4,88,128]{2,1,0:T(8,128)S(1)} collective-permute-done((f32[4,88,128]{2,1,0:T(8,128)S(1)}, f32[4,88,128]{2,1,0:T(8,128)S(1)}, u32[]{:S(2)}, u32[]{:S(2)}) %collective-permute-start.1) | collective-permute-done | bytes 180256 | tf_op jit(solution)/shard_map/ppermute | solution.py:452
  58.7 1.7 %collective-permute-done.3.west = f32[4,88,128]{2,1,0:T(8,128)S(1)} collective-permute-done((f32[4,88,128]{2,1,0:T(8,128)S(1)}, f32[4,88,128]{2,1,0:T(8,128)S(1)}, u32[]{:S(2)}, u32[]{:S(2)}) %collective-permute-start.3) | collective-permute-done | bytes 180256 | tf_op jit(solution)/shard_map/ppermute | solution.py:452
  60.3 0.0 collective-permute-done.2.east
  60.3 0.0 all-to-all-done.1.recv
  60.3 0.0 copy-done
  60.3 9.5 %finish.1 = f32[4,80,32,128]{3,2,1,0:T(8,128)} custom-call(f32[4,144,128]{2,1,0:T(8,128)S(1)} %all-to-all-done.1.recv, s32[32,128]{1,0:T(8,128)S(1)} %copy-done, f32[4,32,80,128]{3,2,1,0:T(8,128)} %get-tuple-element.10.mixed_h, f32[4,32,80,128]{3,2,1,0:T(8,128)} %get-tuple-element.11.first_h, f32[4,88,128]{2,1,0:T(8,128)S(1)} %collective-permute-done.north, ...), custom_call_target="tpu_custom_call" | custom-call | flops 26214400 | bytes 12582912 | tf_op jit(solution)/shard_map/finish/pallas_call | solution.py:425
Async XLA Ops:
  31.0 29.3 %all-to-all-start.1 = ((f32[4,144,128]{2,1,0:T(8,128)}), f32[4,144,128]{2,1,0:T(8,128)S(1)}, u32[]{:S(2)}, u32[]{:S(2)}) async-start(f32[4,144,128]{2,1,0:T(8,128)} %collect.1), calls=%async_computation.1 | async-start | bytes 589824 | tf_op jit(solution)/shard_map/all_to_all | solution.py:474
  35.9 24.4 %copy-start = (s32[32,128]{1,0:T(8,128)S(1)}, s32[32,128]{1,0:T(8,128)}, u32[]{:S(2)}) copy-start(s32[32,128]{1,0:T(8,128)} %depth_ref.1) | copy-start | bytes 49156
  47.3 7.9 %collective-permute-start = (f32[4,88,128]{2,1,0:T(8,128)S(1)}, f32[4,88,128]{2,1,0:T(8,128)S(1)}, u32[]{:S(2)}, u32[]{:S(2)}) collective-permute-start(f32[4,88,128]{2,1,0:T(8,128)S(1)} %get-tuple-element.12), channel_id=1, source_target_pairs={{0,8},{8,16},{16,24},{1,9},{9,17},{17,25},{2,10},{10,18},{18,26},{... | collective-permute-start | bytes 540680 | tf_op jit(solution)/shard_map/ppermute | solution.py:452
  51.3 7.4 %collective-permute-start.1 = (f32[4,88,128]{2,1,0:T(8,128)S(1)}, f32[4,88,128]{2,1,0:T(8,128)S(1)}, u32[]{:S(2)}, u32[]{:S(2)}) collective-permute-start(f32[4,88,128]{2,1,0:T(8,128)S(1)} %get-tuple-element.13), channel_id=1, source_target_pairs={{8,0},{16,8},{24,16},{9,1},{17,9},{25,17},{10,2},{18,10},{26,18},{... | collective-permute-start | bytes 540680 | tf_op jit(solution)/shard_map/ppermute | solution.py:452
  52.6 7.8 %collective-permute-start.3 = (f32[4,88,128]{2,1,0:T(8,128)S(1)}, f32[4,88,128]{2,1,0:T(8,128)S(1)}, u32[]{:S(2)}, u32[]{:S(2)}) collective-permute-start(f32[4,88,128]{2,1,0:T(8,128)S(1)} %get-tuple-element.14), channel_id=1, source_target_pairs={{0,1},{1,2},{2,3},{3,4},{4,5},{5,6},{6,7},{7,0},{8,9},{9,10},{10,1... | collective-permute-start | bytes 540680 | tf_op jit(solution)/shard_map/ppermute | solution.py:452
  52.6 7.7 %collective-permute-start.2 = (f32[4,88,128]{2,1,0:T(8,128)S(1)}, f32[4,88,128]{2,1,0:T(8,128)S(1)}, u32[]{:S(2)}, u32[]{:S(2)}) collective-permute-start(f32[4,88,128]{2,1,0:T(8,128)S(1)} %get-tuple-element.14), channel_id=1, source_target_pairs={{0,7},{1,0},{2,1},{3,2},{4,3},{5,4},{6,5},{7,6},{8,15},{9,8},{10,9... | collective-permute-start | bytes 540680 | tf_op jit(solution)/shard_map/ppermute | solution.py:452

commit v5 on v4

--- a/solution.py
+++ b/solution.py
@@ -175,14 +175,15 @@
 
 
 def mix_kernel(
-    depth_h, state_h, inv_h, mixed_h, first_h, north, south, side, depth_ref, mixed, inv, first, in_sems, out_sems
+    depth_h, state_h, inv_h, mixed_h, first_h, north, south, side,
+    depth_ref, state, mixed, inv, first, in_sems, out_sems,
 ):
     fields, oy, levels, _ = mixed.shape
     depth_copy = pltpu.make_async_copy(depth_h, depth_ref, in_sems.at[2 * fields])
     depth_copy.start()
     for q in range(fields):
         for i in range(oy):
-            pltpu.make_async_copy(state_h.at[q, :, i, :], mixed.at[q, i], in_sems.at[2 * q]).start()
+            pltpu.make_async_copy(state_h.at[q, :, i, :], state.at[q, i], in_sems.at[2 * q]).start()
         pltpu.make_async_copy(inv_h.at[q], inv.at[q], in_sems.at[2 * q + 1]).start()
     depth_copy.wait()
     level = iota((levels, LANES), 0)
@@ -201,7 +202,7 @@
         )
 
     def field(q, carry):
-        pltpu.make_async_copy(mixed_h.at[q], mixed.at[q], in_sems.at[2 * q]).wait()
+        pltpu.make_async_copy(mixed_h.at[q], state.at[q], in_sems.at[2 * q]).wait()
         pltpu.make_async_copy(inv_h.at[q], inv.at[q], in_sems.at[2 * q + 1]).wait()
 
         def chunk(c, edges):
@@ -209,7 +210,7 @@
             for i in range(SUB):
                 row = c * SUB + i
                 active = level < depth_ref[pl.ds(row, 1), :]
-                x = mixed[q, row]
+                x = state[q, row]
                 a = inv[q, row, 0]
                 a_high, a_low = split(a)
                 r_high, r_low = split(jnp.where(active, x, 0.0))
@@ -251,6 +252,7 @@
         scratch_shapes=[
             pltpu.VMEM(depth.shape, jnp.int32),
             pltpu.VMEM(full, f32),
+            pltpu.VMEM(full, f32),
             pltpu.VMEM(inverses.shape, f32),
             pltpu.VMEM(full, f32),
             pltpu.SemaphoreType.DMA((2 * fields + 1,)),
@@ -262,7 +264,7 @@
     )(*in_hbm(depth, state, inverses))
 
 
-def collect_kernel(cap, fields, oy, recv, out):
+def collect_kernel(cap, fields, oy, recv, after, out):
     lat = out.shape[0]
     lon = recv.shape[0] // lat
     per = fields * cap
@@ -305,15 +307,15 @@
         out[a, forced + SUB : forced + 2 * SUB] = matmul(pick, high) + matmul(pick, low)
 
 
-def collect(cap, fields, oy, lat, received):
+def collect(cap, fields, oy, lat, received, after):
     return pl.pallas_call(
         functools.partial(collect_kernel, cap, fields, oy),
-        in_specs=[VMEM],
+        in_specs=[VMEM, pl.BlockSpec(memory_space=pl.ANY)],
         out_specs=VMEM,
         out_shape=jax.ShapeDtypeStruct((lat, fields * oy + 2 * SUB, LANES), f32),
         compiler_params=pltpu.CompilerParams(vmem_limit_bytes=16 << 20),
         name="collect",
-    )(received)
+    )(received, after)
 
 
 def finish_kernel(
@@ -354,7 +356,7 @@
         sides = jnp.where(level < to_east[i : i + 1], diffusion_rate, 0.0)
         for other in (to_west, to_north, to_south):
             sides = sides + jnp.where(level < other[i : i + 1], diffusion_rate, 0.0)
-        keep[i] = jnp.where(level < depth[i : i + 1], 1.0 - sides, 1.0)
+        keep[i] = 1.0 - sides
 
     def outer(target, ref, start):
         names = padded_rows(
@@ -387,11 +389,8 @@
         def solve(c, carry):
             for i in range(SUB):
                 r = c * SUB + i
-                m0 = mixed[q, r]
-                forced = m0 + first[q, r] * forcing[pl.ds(q * oy + r, 1), :]
-                active = level < depth_ref[pl.ds(r, 1), :]
-                z[r + 1] = jnp.where(active, forced, 0.0)
-                mixed[q, r] = jnp.where(active, forced, m0)
+                forced = mixed[q, r] + first[q, r] * forcing[pl.ds(q * oy + r, 1), :]
+                z[r + 1] = jnp.where(level < depth_ref[pl.ds(r, 1), :], forced, 0.0)
             return carry
 
         lax.fori_loop(0, oy // SUB, solve, 0)
@@ -405,8 +404,10 @@
                 r = start + i
                 outside = jnp.where(ends, pltpu.roll(edge, LANES - 1 - 2 * i, 1), 0.0)
                 around = (z[r] + z[r + 2]) + (sides[i * levels : (i + 1) * levels] + outside)
-                scale = jnp.where(level < depth_ref[pl.ds(r, 1), :], diffusion_rate, 0.0)
-                stage[q, r] = mixed[q, r] * keep[r] + scale * around
+                active = level < depth_ref[pl.ds(r, 1), :]
+                stage[q, r] = jnp.where(active, z[r + 1] * keep[r] + diffusion_rate * around, mixed[q, r])
+            for i in range(SUB):
+                r = start + i
                 pltpu.make_async_copy(stage.at[q, r], out_h.at[q, :, r, :], out_sems.at[q]).start()
             return carry
 
@@ -471,7 +472,7 @@
         shift(side, "lon", -1, True),
         shift(side, "lon", 1, True),
     )
-    received = lax.all_to_all(collect(cap, fields, oy, lat, in_plane), "lat", 0, 0, tiled=True)
+    received = lax.all_to_all(collect(cap, fields, oy, lat, in_plane, side), "lat", 0, 0, tiled=True)
     return finish(received, depth_levels, mixed, first, halos)
 
 

time: 70.1 us -> 60 us (0.86)
  blocking collectives: 21.7 us -> 0 us
  waiting for transfers between devices: 5.07 us -> 10.5 us
  starting transfers between devices: 12.8 us -> 18 us
  Pallas kernels: 30.2 us -> 31.2 us
    all_to_all x1 -> x0, blocking collectives: 21.7 us -> none  [on_device(): in_plane = lax.all_to_all(slots, 'lon', 0, 0, tiled=True)]
    all_to_all x1 -> x2, waiting for transfers between devices: 0.01 us -> 5.36 us  [the longest x1 5.36 us: on_device(): in_plane = lax.all_to_all(slots, 'lon', 0, 0, tiled=True)]
    all_to_all x1 -> x2, starting transfers between devices: 4.87 us -> 10.1 us  [the longest x1 5.18 us: on_device(): in_plane = lax.all_to_all(slots, 'lon', 0, 0, tiled=True)]
    pallas_call x1, Pallas kernels: 7.99 us -> 8.99 us  [regrid(): pl.pallas_call(functools.partial(regrid_kernel, cap, lat, lon, oy, batch)...]
  transfers between devices with their start and end apart: 5 -> 6, of which waited for: 2 -> 3; matrix products, arithmetic and copies ran while one was open for 0% -> 0% of each run, Pallas kernels for 16% -> 19%
where the time goes in v5:
time: 60 us; the launch traced here: 59.7 us
  Pallas kernels  31.2 us (52%)
  starting transfers between devices  18 us (30%)
  waiting for transfers between devices  10.5 us (18%)
    pallas_call x1, Pallas kernels, mix(): pl.pallas_call(mix_kernel, in_specs=[HBM] * 3, out_specs=[HBM] * 2 + [VME...  11.4 us
    pallas_call x1, Pallas kernels, finish(): pl.pallas_call(finish_kernel, in_specs=[VMEM] * 2 + [HBM] * 2 + [VMEM] *...  9.45 us
    pallas_call x1, Pallas kernels, regrid(): pl.pallas_call(functools.partial(regrid_kernel, cap, lat, lon, oy, batch)...  8.99 us
    ppermute x4, starting transfers between devices, shift(): return lax.ppermute(x, axis, pairs)  7.91 us
    all_to_all x1, waiting for transfers between devices, on_device(): in_plane = lax.all_to_all(slots, 'lon', 0, 0, tiled=True)  5.36 us
    all_to_all x1, starting transfers between devices, on_device(): in_plane = lax.all_to_all(slots, 'lon', 0, 0, tiled=True)  5.18 us
    ppermute x4, waiting for transfers between devices, shift(): return lax.ppermute(x, axis, pairs)  5.1 us
    all_to_all x1, starting transfers between devices, on_device(): lax.all_to_all(collect(cap, fields, oy, lat, in_plane, side), 'lat', 0, 0...  4.87 us
  transfers between devices with their start and end apart: 6, of which 3 were waited for; matrix products, arithmetic and copies ran while one was open for 0% of the time, Pallas kernels for 19%

profile of v5, /device:TPU:0, one launch (start us, length us, event | category | flops | bytes accessed | tf_op | source)
XLA Modules:
  0.0 59.7 jit_solution(607741723821782667)
XLA Ops:
  0.0 9.0 %regrid.1 = f32[32,72,128]{2,1,0:T(8,128)} custom-call(s32[256]{0:T(256)} %src_h.1, s32[256]{0:T(256)} %bitcast.1, s32[256]{0:T(256)} %blk_h.1, f32[4,8]{1,0:T(4,128)} %coupling_h.1, bf16[8,64,128]{2,1,0:T(8,128)(2,1)} %atm_h.1, s32[64,128]{1,0:T(8,128)} %mask_h.1, bf16[256,128,128]{2,1,0:T(8,128)(2,1)} %weights_h.1), custom_call_target="tpu_custom_call" | custom-call | flops 67108864 | bytes 10485760 | tf_op jit(solution)/shard_map/regrid/pallas_call | solution.py:152
  9.0 5.2 %all-to-all-start = ((f32[32,72,128]{2,1,0:T(8,128)}), f32[32,72,128]{2,1,0:T(8,128)S(1)}, u32[]{:S(2)}, u32[]{:S(2)}) async-start(f32[32,72,128]{2,1,0:T(8,128)} %regrid.1), calls=%async_computation | async-start | bytes 2359296 | tf_op jit(solution)/shard_map/all_to_all | solution.py:467
  14.2 0.0 copy-start
  14.2 11.4 %mix.1 = (f32[4,32,80,128]{3,2,1,0:T(8,128)}, f32[4,32,80,128]{3,2,1,0:T(8,128)}, f32[4,88,128]{2,1,0:T(8,128)S(1)}, f32[4,88,128]{2,1,0:T(8,128)S(1)}, f32[4,88,128]{2,1,0:T(8,128)S(1)}) custom-call(s32[32,128]{1,0:T(8,128)} %depth_ref.1, f32[4,80,32,128]{3,2,1,0:T(8,128)} %state_h.1, f32[4,32,1,80,80]{4,3,2,1,0:T(8,128)} %inv_h.1), custom_call_target="tpu_custom_call" | custom-call | flops 838860800 | bytes 16777216 | tf_op jit(solution)/shard_map/mix/pallas_call | solution.py:247
  25.6 5.4 %all-to-all-done.recv = f32[32,72,128]{2,1,0:T(8,128)S(1)} async-done(((f32[32,72,128]{2,1,0:T(8,128)}), f32[32,72,128]{2,1,0:T(8,128)S(1)}, u32[]{:S(2)}, u32[]{:S(2)}) %all-to-all-start) | async-done | bytes 1179680 | tf_op jit(solution)/shard_map/all_to_all | solution.py:467
  31.0 1.3 %collect.1 = f32[4,144,128]{2,1,0:T(8,128)} custom-call(f32[32,72,128]{2,1,0:T(8,128)S(1)} %all-to-all-done.recv, f32[4,88,128]{2,1,0:T(8,128)S(1)} %get-tuple-element.10.after), custom_call_target="tpu_custom_call" | custom-call | tf_op jit(solution)/shard_map/collect/pallas_call | solution.py:311
  32.3 4.9 %all-to-all-start.1 = ((f32[4,144,128]{2,1,0:T(8,128)}), f32[4,144,128]{2,1,0:T(8,128)S(1)}, u32[]{:S(2)}, u32[]{:S(2)}) async-start(f32[4,144,128]{2,1,0:T(8,128)} %collect.1), calls=%async_computation.1 | async-start | bytes 589824 | tf_op jit(solution)/shard_map/all_to_all | solution.py:475
  37.2 3.9 %collective-permute-start = (f32[4,88,128]{2,1,0:T(8,128)S(1)}, f32[4,88,128]{2,1,0:T(8,128)S(1)}, u32[]{:S(2)}, u32[]{:S(2)}) collective-permute-start(f32[4,88,128]{2,1,0:T(8,128)S(1)} %get-tuple-element.13), channel_id=1, source_target_pairs={{0,8},{8,16},{16,24},{1,9},{9,17},{17,25},{2,10},{10,18},{18,26},{... | collective-permute-start | bytes 540680 | tf_op jit(solution)/shard_map/ppermute | solution.py:453
  41.1 1.3 %collective-permute-start.1 = (f32[4,88,128]{2,1,0:T(8,128)S(1)}, f32[4,88,128]{2,1,0:T(8,128)S(1)}, u32[]{:S(2)}, u32[]{:S(2)}) collective-permute-start(f32[4,88,128]{2,1,0:T(8,128)S(1)} %get-tuple-element.14), channel_id=1, source_target_pairs={{8,0},{16,8},{24,16},{9,1},{17,9},{25,17},{10,2},{18,10},{26,18},{... | collective-permute-start | bytes 540680 | tf_op jit(solution)/shard_map/ppermute | solution.py:453
  42.4 0.1 collective-permute-start.3
  42.5 2.6 %collective-permute-start.2 = (f32[4,88,128]{2,1,0:T(8,128)S(1)}, f32[4,88,128]{2,1,0:T(8,128)S(1)}, u32[]{:S(2)}, u32[]{:S(2)}) collective-permute-start(f32[4,88,128]{2,1,0:T(8,128)S(1)} %get-tuple-element.10.after), channel_id=1, source_target_pairs={{0,7},{1,0},{2,1},{3,2},{4,3},{5,4},{6,5},{7,6},{8,15},{9,8},{10,9... | collective-permute-start | bytes 540680 | tf_op jit(solution)/shard_map/ppermute | solution.py:453
  45.1 0.0 collective-permute-done.north
  45.1 3.4 %collective-permute-done.1.south = f32[4,88,128]{2,1,0:T(8,128)S(1)} collective-permute-done((f32[4,88,128]{2,1,0:T(8,128)S(1)}, f32[4,88,128]{2,1,0:T(8,128)S(1)}, u32[]{:S(2)}, u32[]{:S(2)}) %collective-permute-start.1) | collective-permute-done | bytes 180256 | tf_op jit(solution)/shard_map/ppermute | solution.py:453
  48.5 1.7 %collective-permute-done.3.west = f32[4,88,128]{2,1,0:T(8,128)S(1)} collective-permute-done((f32[4,88,128]{2,1,0:T(8,128)S(1)}, f32[4,88,128]{2,1,0:T(8,128)S(1)}, u32[]{:S(2)}, u32[]{:S(2)}) %collective-permute-start.3) | collective-permute-done | bytes 180256 | tf_op jit(solution)/shard_map/ppermute | solution.py:453
  50.2 0.0 collective-permute-done.2.east
  50.2 0.0 all-to-all-done.1.recv
  50.2 0.0 copy-done
  50.2 9.4 %finish.1 = f32[4,80,32,128]{3,2,1,0:T(8,128)} custom-call(f32[4,144,128]{2,1,0:T(8,128)S(1)} %all-to-all-done.1.recv, s32[32,128]{1,0:T(8,128)S(1)} %copy-done, f32[4,32,80,128]{3,2,1,0:T(8,128)} %get-tuple-element.11.mixed_h, f32[4,32,80,128]{3,2,1,0:T(8,128)} %get-tuple-element.12.first_h, f32[4,88,128]{2,1,0:T(8,128)S(1)} %collective-permute-done.north, ...), custom_call_target="tpu_custom_call" | custom-call | flops 26214400 | bytes 12582912 | tf_op jit(solution)/shard_map/finish/pallas_call | solution.py:426
Async XLA Ops:
  9.0 22.0 %all-to-all-start = ((f32[32,72,128]{2,1,0:T(8,128)}), f32[32,72,128]{2,1,0:T(8,128)S(1)}, u32[]{:S(2)}, u32[]{:S(2)}) async-start(f32[32,72,128]{2,1,0:T(8,128)} %regrid.1), calls=%async_computation | async-start | bytes 2359296 | tf_op jit(solution)/shard_map/all_to_all | solution.py:467
  14.2 36.0 %copy-start = (s32[32,128]{1,0:T(8,128)S(1)}, s32[32,128]{1,0:T(8,128)}, u32[]{:S(2)}) copy-start(s32[32,128]{1,0:T(8,128)} %depth_ref.1) | copy-start | bytes 49156
  32.3 17.9 %all-to-all-start.1 = ((f32[4,144,128]{2,1,0:T(8,128)}), f32[4,144,128]{2,1,0:T(8,128)S(1)}, u32[]{:S(2)}, u32[]{:S(2)}) async-start(f32[4,144,128]{2,1,0:T(8,128)} %collect.1), calls=%async_computation.1 | async-start | bytes 589824 | tf_op jit(solution)/shard_map/all_to_all | solution.py:475
  37.2 7.9 %collective-permute-start = (f32[4,88,128]{2,1,0:T(8,128)S(1)}, f32[4,88,128]{2,1,0:T(8,128)S(1)}, u32[]{:S(2)}, u32[]{:S(2)}) collective-permute-start(f32[4,88,128]{2,1,0:T(8,128)S(1)} %get-tuple-element.13), channel_id=1, source_target_pairs={{0,8},{8,16},{16,24},{1,9},{9,17},{17,25},{2,10},{10,18},{18,26},{... | collective-permute-start | bytes 540680 | tf_op jit(solution)/shard_map/ppermute | solution.py:453
  41.1 7.4 %collective-permute-start.1 = (f32[4,88,128]{2,1,0:T(8,128)S(1)}, f32[4,88,128]{2,1,0:T(8,128)S(1)}, u32[]{:S(2)}, u32[]{:S(2)}) collective-permute-start(f32[4,88,128]{2,1,0:T(8,128)S(1)} %get-tuple-element.14), channel_id=1, source_target_pairs={{8,0},{16,8},{24,16},{9,1},{17,9},{25,17},{10,2},{18,10},{26,18},{... | collective-permute-start | bytes 540680 | tf_op jit(solution)/shard_map/ppermute | solution.py:453
  42.4 7.8 %collective-permute-start.3 = (f32[4,88,128]{2,1,0:T(8,128)S(1)}, f32[4,88,128]{2,1,0:T(8,128)S(1)}, u32[]{:S(2)}, u32[]{:S(2)}) collective-permute-start(f32[4,88,128]{2,1,0:T(8,128)S(1)} %get-tuple-element.10.after), channel_id=1, source_target_pairs={{0,1},{1,2},{2,3},{3,4},{4,5},{5,6},{6,7},{7,0},{8,9},{9,10},{10,1... | collective-permute-start | bytes 540680 | tf_op jit(solution)/shard_map/ppermute | solution.py:453
  42.5 7.7 %collective-permute-start.2 = (f32[4,88,128]{2,1,0:T(8,128)S(1)}, f32[4,88,128]{2,1,0:T(8,128)S(1)}, u32[]{:S(2)}, u32[]{:S(2)}) collective-permute-start(f32[4,88,128]{2,1,0:T(8,128)S(1)} %get-tuple-element.10.after), channel_id=1, source_target_pairs={{0,7},{1,0},{2,1},{3,2},{4,3},{5,4},{6,5},{7,6},{8,15},{9,8},{10,9... | collective-permute-start | bytes 540680 | tf_op jit(solution)/shard_map/ppermute | solution.py:453

commit v6 on v5

--- a/solution.py
+++ b/solution.py
@@ -40,7 +40,7 @@
 
 def regrid_kernel(
     cap, lat, lon, oy, batch, src_h, dev_h, blk_h, coupling_h, atm_h, mask_h, weights_h,
-    out, rows, ids, count, src, dev, blk, coupling, atm, mask, weights, small_sem, big_sem,
+    out_h, out, rows, ids, count, src, dev, blk, coupling, atm, mask, weights, small_sem, big_sem, out_sem,
 ):
     fluxes, atm_rows, _ = atm.shape
     fields = coupling.shape[0]
@@ -113,6 +113,11 @@
         return carry
 
     lax.fori_loop(0, parts, part, 0)
+
+    def send(k, start, stop):
+        return pltpu.make_async_copy(out.at[:, start:stop, :], out_h.at[:, start:stop, :], out_sem.at[k])
+
+    send(0, 0, per).start()
 
     def halo(k):
         d = 2 * k
@@ -141,6 +146,9 @@
         return carry
 
     lax.fori_loop(0, devices // 8, halos, 0)
+    send(1, per, per + SUB).start()
+    send(0, 0, per).wait()
+    send(1, per, per + SUB).wait()
 
 
 def regrid(cap, lat, lon, oy, src, dev, blk, coupling, atm, mask, weights):
@@ -152,9 +160,10 @@
     return pl.pallas_call(
         functools.partial(regrid_kernel, cap, lat, lon, oy, batch),
         in_specs=[HBM] * 7,
-        out_specs=VMEM,
-        out_shape=jax.ShapeDtypeStruct((devices, tall, LANES), f32),
+        out_specs=HBM,
+        out_shape=pltpu.HBM((devices, tall, LANES), f32),
         scratch_shapes=[
+            pltpu.VMEM((devices, tall, LANES), f32),
             pltpu.VMEM((atm.shape[1] * SUB, LANES), f32),
             pltpu.VMEM((devices, LANES), jnp.int32),
             pltpu.SMEM((devices,), jnp.int32),
@@ -167,6 +176,7 @@
             pltpu.VMEM(weights.shape, bf16),
             pltpu.SemaphoreType.DMA((6,)),
             pltpu.SemaphoreType.DMA((pairs // batch,)),
+            pltpu.SemaphoreType.DMA((2,)),
         ],
         compiler_params=pltpu.CompilerParams(vmem_limit_bytes=20 << 20),
         cost_estimate=pl.CostEstimate(flops=2 * 8 * pairs * depth * width, bytes_accessed=10 << 20, transcendentals=0),
@@ -175,8 +185,7 @@
 
 
 def mix_kernel(
-    depth_h, state_h, inv_h, mixed_h, first_h, north, south, side,
-    depth_ref, state, mixed, inv, first, in_sems, out_sems,
+    depth_h, state_h, inv_h, mixed_h, north, south, side, depth_ref, state, mixed, inv, in_sems, out_sems
 ):
     fields, oy, levels, _ = mixed.shape
     depth_copy = pltpu.make_async_copy(depth_h, depth_ref, in_sems.at[2 * fields])
@@ -196,7 +205,8 @@
 
     def message(ref, q, row):
         ref[q, 0:levels] = mixed[q, row]
-        names = padded_rows(first[q, row], LANES).T[0:1]
+        square = jnp.concatenate([inv[q, row, 0], jnp.zeros((levels, LANES - levels), f32)], axis=1)
+        names = padded_rows(square, LANES).T[0:1]
         ref[q, levels : levels + SUB] = jnp.concatenate(
             [depth_ref[row : row + 1, :].astype(f32), names, jnp.zeros((SUB - 2, LANES), f32)], axis=0
         )
@@ -220,24 +230,20 @@
                 solved = product[:levels, :LANES] + (product[levels:, :LANES] + product[:levels, LANES:])
                 m = jnp.where(active, solved, x)
                 mixed[q, row] = m
-                column = jnp.broadcast_to(a[:, 0:1], (levels, LANES))
-                first[q, row] = column
                 here = jnp.where(lane // 2 == i, pltpu.roll(m, 2 * i + 1, 1), here)
-                here = jnp.where(lane // 2 == HALF // 2 + i, column, here)
+                here = jnp.where(lane // 2 == HALF // 2 + i, a[:, 0:1], here)
             return edges + pltpu.roll(here, 2 * SUB * c, 1)
 
         side[q, 0:levels] = lax.fori_loop(0, oy // SUB, chunk, jnp.zeros((levels, LANES), f32))
         side[q, levels : levels + SUB] = edge_depth
         message(north, q, 0)
         message(south, q, oy - 1)
-        pltpu.make_async_copy(mixed.at[q], mixed_h.at[q], out_sems.at[2 * q]).start()
-        pltpu.make_async_copy(first.at[q], first_h.at[q], out_sems.at[2 * q + 1]).start()
+        pltpu.make_async_copy(mixed.at[q], mixed_h.at[q], out_sems.at[q]).start()
         return carry
 
     lax.fori_loop(0, fields, field, 0)
     for q in range(fields):
-        pltpu.make_async_copy(mixed.at[q], mixed_h.at[q], out_sems.at[2 * q]).wait()
-        pltpu.make_async_copy(first.at[q], first_h.at[q], out_sems.at[2 * q + 1]).wait()
+        pltpu.make_async_copy(mixed.at[q], mixed_h.at[q], out_sems.at[q]).wait()
 
 
 def mix(depth, state, inverses):
@@ -247,16 +253,15 @@
     return pl.pallas_call(
         mix_kernel,
         in_specs=[HBM] * 3,
-        out_specs=[HBM] * 2 + [VMEM] * 3,
-        out_shape=[pltpu.HBM(full, f32), pltpu.HBM(full, f32), edge_shape, edge_shape, edge_shape],
+        out_specs=[HBM] + [VMEM] * 3,
+        out_shape=[pltpu.HBM(full, f32), edge_shape, edge_shape, edge_shape],
         scratch_shapes=[
             pltpu.VMEM(depth.shape, jnp.int32),
             pltpu.VMEM(full, f32),
             pltpu.VMEM(full, f32),
             pltpu.VMEM(inverses.shape, f32),
-            pltpu.VMEM(full, f32),
             pltpu.SemaphoreType.DMA((2 * fields + 1,)),
-            pltpu.SemaphoreType.DMA((2 * fields,)),
+            pltpu.SemaphoreType.DMA((fields,)),
         ],
         compiler_params=pltpu.CompilerParams(vmem_limit_bytes=32 << 20),
         cost_estimate=pl.CostEstimate(flops=2 * 4 * fields * oy * levels * levels * ox, bytes_accessed=16 << 20, transcendentals=0),
@@ -264,7 +269,7 @@
     )(*in_hbm(depth, state, inverses))
 
 
-def collect_kernel(cap, fields, oy, recv, after, out):
+def collect_kernel(cap, fields, oy, recv, after_north, after_south, out):
     lat = out.shape[0]
     lon = recv.shape[0] // lat
     per = fields * cap
@@ -310,17 +315,18 @@
 def collect(cap, fields, oy, lat, received, after):
     return pl.pallas_call(
         functools.partial(collect_kernel, cap, fields, oy),
-        in_specs=[VMEM, pl.BlockSpec(memory_space=pl.ANY)],
+        in_specs=[VMEM] + [pl.BlockSpec(memory_space=pl.ANY)] * 2,
         out_specs=VMEM,
         out_shape=jax.ShapeDtypeStruct((lat, fields * oy + 2 * SUB, LANES), f32),
         compiler_params=pltpu.CompilerParams(vmem_limit_bytes=16 << 20),
         name="collect",
-    )(received, after)
+    )(received, *after)
 
 
 def finish_kernel(
-    recv, depth_ref, mixed_h, first_h, north, south, east, west,
-    out_h, forcing, z, keep, halo, z_north, z_south, mixed, first, stage, in_sems, out_sems,
+    recv, depth_ref, mixed_h, own_h, north_h, south_h, east_h, west_h,
+    out_h, own, north, south, east, west, forcing, z, keep, halo, z_north, z_south, mixed, stage,
+    edge_sems, in_sems, out_sems,
 ):
     fields, oy, levels, _ = mixed.shape
     level = iota((levels, LANES), 0)
@@ -329,9 +335,22 @@
     square_lane = iota((LANES, LANES), 1)
     line = iota((1, LANES), 1)
     even = line % 2 == 0
+    edges = [
+        pltpu.make_async_copy(a, b, edge_sems.at[k])
+        for k, (a, b) in enumerate(
+            ((own_h, own), (north_h, north), (south_h, south), (east_h, east), (west_h, west))
+        )
+    ]
+    for copy in edges:
+        copy.start()
+
+    def load(q, c):
+        here = (q, pl.ds(pl.multiple_of(c * SUB, SUB), SUB))
+        return pltpu.make_async_copy(mixed_h.at[here], mixed.at[here], in_sems.at[q, c])
+
     for q in range(fields):
-        pltpu.make_async_copy(mixed_h.at[q], mixed.at[q], in_sems.at[2 * q]).start()
-        pltpu.make_async_copy(first_h.at[q], first.at[q], in_sems.at[2 * q + 1]).start()
+        for c in range(oy // SUB):
+            load(q, c).start()
 
     total = recv[0]
     for a in range(1, recv.shape[0]):
@@ -341,6 +360,8 @@
     rows = total[forced_rows : forced_rows + SUB]
     columns = total[forced_rows + SUB :]
 
+    for copy in edges:
+        copy.wait()
     depth = depth_ref[...]
     wide = iota((oy, LANES), 1)
 
@@ -381,15 +402,15 @@
     ends = (lanes == 0) | (lanes == LANES - 1)
 
     def field(q, carry):
-        pltpu.make_async_copy(mixed_h.at[q], mixed.at[q], in_sems.at[2 * q]).wait()
-        pltpu.make_async_copy(first_h.at[q], first.at[q], in_sems.at[2 * q + 1]).wait()
         z[0] = z_north[q]
         z[oy + 1] = z_south[q]
 
         def solve(c, carry):
+            load(q, c).wait()
+            names = pltpu.roll(own[q, 0:levels], (LANES - 2 * SUB * c) % LANES, 1)
             for i in range(SUB):
                 r = c * SUB + i
-                forced = mixed[q, r] + first[q, r] * forcing[pl.ds(q * oy + r, 1), :]
+                forced = mixed[q, r] + names[:, HALF + 2 * i : HALF + 2 * i + 1] * forcing[pl.ds(q * oy + r, 1), :]
                 z[r + 1] = jnp.where(level < depth_ref[pl.ds(r, 1), :], forced, 0.0)
             return carry
 
@@ -419,16 +440,18 @@
         pltpu.make_async_copy(stage.at[q], mixed_h.at[q], out_sems.at[q]).wait()
 
 
-def finish(received, depth, mixed, first, halos):
+def finish(received, depth, own, mixed, halos):
     fields, oy, levels, ox = mixed.shape
     edge = pltpu.VMEM((fields, levels, ox), f32)
+    message = pltpu.VMEM((fields, levels + SUB, ox), f32)
     full = pltpu.VMEM((fields, oy, levels, ox), f32)
     return pl.pallas_call(
         finish_kernel,
-        in_specs=[VMEM] * 2 + [HBM] * 2 + [VMEM] * 4,
+        in_specs=[VMEM] * 2 + [HBM] * 6,
         out_specs=HBM,
         out_shape=pltpu.HBM((fields, levels, oy, ox), f32),
-        scratch_shapes=[
+        scratch_shapes=[message] * 5
+        + [
             pltpu.VMEM((fields * oy, ox), f32),
             pltpu.VMEM((oy + 2, levels, ox), f32),
             pltpu.VMEM((oy, levels, ox), f32),
@@ -437,14 +460,14 @@
             edge,
             full,
             full,
-            full,
-            pltpu.SemaphoreType.DMA((2 * fields,)),
+            pltpu.SemaphoreType.DMA((5,)),
+            pltpu.SemaphoreType.DMA((fields, oy // SUB)),
             pltpu.SemaphoreType.DMA((fields,)),
         ],
         compiler_params=pltpu.CompilerParams(vmem_limit_bytes=32 << 20),
         cost_estimate=pl.CostEstimate(flops=20 * fields * oy * levels * ox, bytes_accessed=12 << 20, transcendentals=0),
         name="finish",
-    )(received, depth, *in_hbm(mixed, first), *halos)
+    )(received, depth, *in_hbm(mixed, own, *halos))
 
 
 def shift(x, axis, step, wrap):
@@ -465,15 +488,15 @@
         intersection_weights,
     )
     in_plane = lax.all_to_all(slots, "lon", 0, 0, tiled=True)
-    mixed, first, north, south, side = mix(depth_levels, ocean_state, inverses)
+    mixed, north, south, side = mix(depth_levels, ocean_state, inverses)
     halos = (
         shift(south, "lat", 1, False),
         shift(north, "lat", -1, False),
         shift(side, "lon", -1, True),
         shift(side, "lon", 1, True),
     )
-    received = lax.all_to_all(collect(cap, fields, oy, lat, in_plane, side), "lat", 0, 0, tiled=True)
-    return finish(received, depth_levels, mixed, first, halos)
+    received = lax.all_to_all(collect(cap, fields, oy, lat, in_plane, halos[0:2]), "lat", 0, 0, tiled=True)
+    return finish(received, depth_levels, side, mixed, halos)
 
 
 def solution(mesh):

time: 60 us -> 65 us (1.083)
  waiting for transfers between devices: 10.5 us -> 13.8 us
  Pallas kernels: 31.2 us -> 34.4 us
  starting transfers between devices: 18 us -> 16.5 us
    ppermute x4, waiting for transfers between devices: 5.1 us -> 10.7 us  [shift(): return lax.ppermute(x, axis, pairs)]
    all_to_all x1, waiting for transfers between devices: 5.36 us -> 0.01 us  [on_device(): in_plane = lax.all_to_all(slots, 'lon', 0, 0, tiled=True)]
    pallas_call x2, Pallas kernels: 20.9 us -> 24.4 us  [the longest x1 13.5 us: finish(): pl.pallas_call(finish_kernel, in_specs=[VMEM] * 2 + [HBM] * 6, out_specs=...]
    all_to_all x1, waiting for transfers between devices: 0.01 us -> 3.1 us  [on_device(): lax.all_to_all(collect(cap, fields, oy, lat, in_plane, halos[0:2]), 'lat'...]
    all_to_all x1, starting transfers between devices: 4.87 us -> 3.84 us  [on_device(): lax.all_to_all(collect(cap, fields, oy, lat, in_plane, halos[0:2]), 'lat'...]
  transfers between devices with their start and end apart: 6 -> 6, of which waited for: 3 -> 5; matrix products, arithmetic and copies ran while one was open for 0% -> 0% of each run, Pallas kernels for 19% -> 17%
where the time goes in v6:
time: 65 us; the launch traced here: 64.7 us
  Pallas kernels  34.4 us (53%)
  starting transfers between devices  16.5 us (25%)
  waiting for transfers between devices  13.8 us (21%)
    pallas_call x1, Pallas kernels, finish(): pl.pallas_call(finish_kernel, in_specs=[VMEM] * 2 + [HBM] * 6, out_specs=...  13.5 us
    pallas_call x1, Pallas kernels, mix(): pl.pallas_call(mix_kernel, in_specs=[HBM] * 3, out_specs=[HBM] + [VMEM] *...  10.9 us
    ppermute x4, waiting for transfers between devices, shift(): return lax.ppermute(x, axis, pairs)  10.7 us
    pallas_call x1, Pallas kernels, regrid(): pl.pallas_call(functools.partial(regrid_kernel, cap, lat, lon, oy, batch)...  8.69 us
    ppermute x4, starting transfers between devices, shift(): return lax.ppermute(x, axis, pairs)  7.42 us
    all_to_all x1, starting transfers between devices, on_device(): in_plane = lax.all_to_all(slots, 'lon', 0, 0, tiled=True)  5.18 us
    all_to_all x1, starting transfers between devices, on_device(): lax.all_to_all(collect(cap, fields, oy, lat, in_plane, halos[0:2]), 'lat'...  3.84 us
    all_to_all x1, waiting for transfers between devices, on_device(): lax.all_to_all(collect(cap, fields, oy, lat, in_plane, halos[0:2]), 'lat'...  3.1 us
  transfers between devices with their start and end apart: 6, of which 5 were waited for; matrix products, arithmetic and copies ran while one was open for 0% of the time, Pallas kernels for 17%

profile of v6, /device:TPU:0, one launch (start us, length us, event | category | flops | bytes accessed | tf_op | source)
XLA Modules:
  0.0 64.7 jit_solution(4898929089847116816)
XLA Ops:
  0.0 8.7 %regrid.1 = f32[32,72,128]{2,1,0:T(8,128)} custom-call(s32[256]{0:T(256)} %src_h.1, s32[256]{0:T(256)} %bitcast.1, s32[256]{0:T(256)} %blk_h.1, f32[4,8]{1,0:T(4,128)} %coupling_h.1, bf16[8,64,128]{2,1,0:T(8,128)(2,1)} %atm_h.1, s32[64,128]{1,0:T(8,128)} %mask_h.1, bf16[256,128,128]{2,1,0:T(8,128)(2,1)} %weights_h.1), custom_call_target="tpu_custom_call" | custom-call | flops 67108864 | bytes 10485760 | tf_op jit(solution)/shard_map/regrid/pallas_call | solution.py:160
  8.7 5.2 %all-to-all-start = ((f32[32,72,128]{2,1,0:T(8,128)}), f32[32,72,128]{2,1,0:T(8,128)S(1)}, u32[]{:S(2)}, u32[]{:S(2)}) async-start(f32[32,72,128]{2,1,0:T(8,128)} %regrid.1), calls=%async_computation | async-start | bytes 2359296 | tf_op jit(solution)/shard_map/all_to_all | solution.py:490
  13.9 0.0 copy-start.3
  13.9 10.9 %mix.1 = (f32[4,32,80,128]{3,2,1,0:T(8,128)}, f32[4,88,128]{2,1,0:T(8,128)S(1)}, f32[4,88,128]{2,1,0:T(8,128)S(1)}, f32[4,88,128]{2,1,0:T(8,128)S(1)}) custom-call(s32[32,128]{1,0:T(8,128)} %depth_ref.1, f32[4,80,32,128]{3,2,1,0:T(8,128)} %state_h.1, f32[4,32,1,80,80]{4,3,2,1,0:T(8,128)} %inv_h.1), custom_call_target="tpu_custom_call" | custom-call | flops 838860800 | bytes 16777216 | tf_op jit(solution)/shard_map/mix/pallas_call | solution.py:253
  24.8 0.0 copy-start.2
  24.8 3.5 %collective-permute-start = (f32[4,88,128]{2,1,0:T(8,128)S(1)}, f32[4,88,128]{2,1,0:T(8,128)S(1)}, u32[]{:S(2)}, u32[]{:S(2)}) collective-permute-start(f32[4,88,128]{2,1,0:T(8,128)S(1)} %get-tuple-element.9), channel_id=1, source_target_pairs={{0,8},{8,16},{16,24},{1,9},{9,17},{17,25},{2,10},{10,18},{18,26},{... | collective-permute-start | bytes 540680 | tf_op jit(solution)/shard_map/ppermute | solution.py:476
  28.3 1.3 %collective-permute-start.1 = (f32[4,88,128]{2,1,0:T(8,128)S(1)}, f32[4,88,128]{2,1,0:T(8,128)S(1)}, u32[]{:S(2)}, u32[]{:S(2)}) collective-permute-start(f32[4,88,128]{2,1,0:T(8,128)S(1)} %get-tuple-element.10), channel_id=1, source_target_pairs={{8,0},{16,8},{24,16},{9,1},{17,9},{25,17},{10,2},{18,10},{26,18},{... | collective-permute-start | bytes 540680 | tf_op jit(solution)/shard_map/ppermute | solution.py:476
  29.6 3.1 %collective-permute-done.after_north.north_h = f32[4,88,128]{2,1,0:T(8,128)S(1)} collective-permute-done((f32[4,88,128]{2,1,0:T(8,128)S(1)}, f32[4,88,128]{2,1,0:T(8,128)S(1)}, u32[]{:S(2)}, u32[]{:S(2)}) %collective-permute-start) | collective-permute-done | bytes 180256 | tf_op jit(solution)/shard_map/ppermute | solution.py:476
  32.8 0.0 copy-start
  32.8 4.1 %collective-permute-done.1.after_south.south_h = f32[4,88,128]{2,1,0:T(8,128)S(1)} collective-permute-done((f32[4,88,128]{2,1,0:T(8,128)S(1)}, f32[4,88,128]{2,1,0:T(8,128)S(1)}, u32[]{:S(2)}, u32[]{:S(2)}) %collective-permute-start.1) | collective-permute-done | bytes 180256 | tf_op jit(solution)/shard_map/ppermute | solution.py:476
  36.9 0.0 copy-start.1
  36.9 0.0 all-to-all-done.recv
  36.9 1.3 %collect.1 = f32[4,144,128]{2,1,0:T(8,128)} custom-call(f32[32,72,128]{2,1,0:T(8,128)S(1)} %all-to-all-done.recv, f32[4,88,128]{2,1,0:T(8,128)S(1)} %collective-permute-done.after_north.north_h, f32[4,88,128]{2,1,0:T(8,128)S(1)} %collective-permute-done.1.after_south.south_h), custom_call_target="tpu_custom_call" | custom-call | tf_op jit(solution)/shard_map/collect/pallas_call | solution.py:316
  38.2 3.8 %all-to-all-start.1 = ((f32[4,144,128]{2,1,0:T(8,128)}), f32[4,144,128]{2,1,0:T(8,128)S(1)}, u32[]{:S(2)}, u32[]{:S(2)}) async-start(f32[4,144,128]{2,1,0:T(8,128)} %collect.1), calls=%async_computation.1 | async-start | bytes 589824 | tf_op jit(solution)/shard_map/all_to_all | solution.py:498
  42.0 0.0 collective-permute-start.3
  42.0 2.6 %collective-permute-start.2 = (f32[4,88,128]{2,1,0:T(8,128)S(1)}, f32[4,88,128]{2,1,0:T(8,128)S(1)}, u32[]{:S(2)}, u32[]{:S(2)}) collective-permute-start(f32[4,88,128]{2,1,0:T(8,128)S(1)} %get-tuple-element.12.own_h), channel_id=1, source_target_pairs={{0,7},{1,0},{2,1},{3,2},{4,3},{5,4},{6,5},{7,6},{8,15},{9,8},{10,9... | collective-permute-start | bytes 540680 | tf_op jit(solution)/shard_map/ppermute | solution.py:476
  44.7 3.2 %collective-permute-done.3.west_h = f32[4,88,128]{2,1,0:T(8,128)S(1)} collective-permute-done((f32[4,88,128]{2,1,0:T(8,128)S(1)}, f32[4,88,128]{2,1,0:T(8,128)S(1)}, u32[]{:S(2)}, u32[]{:S(2)}) %collective-permute-start.3) | collective-permute-done | bytes 180256 | tf_op jit(solution)/shard_map/ppermute | solution.py:476
  47.9 0.0 copy-start.4
  47.9 0.2 collective-permute-done.2.east_h
  48.1 0.0 copy-start.5
  48.1 3.1 %all-to-all-done.1.recv = f32[4,144,128]{2,1,0:T(8,128)S(1)} async-done(((f32[4,144,128]{2,1,0:T(8,128)}), f32[4,144,128]{2,1,0:T(8,128)S(1)}, u32[]{:S(2)}, u32[]{:S(2)}) %all-to-all-start.1) | async-done | bytes 294944 | tf_op jit(solution)/shard_map/all_to_all | solution.py:498
  51.2 0.0 copy-done.2
  51.2 0.0 copy-done
  51.2 0.0 copy-done.1
  51.2 0.0 copy-done.4
  51.2 0.0 copy-done.5
  51.2 0.0 copy-done.3
  51.2 13.5 %finish.1 = f32[4,80,32,128]{3,2,1,0:T(8,128)} custom-call(f32[4,144,128]{2,1,0:T(8,128)S(1)} %all-to-all-done.1.recv, s32[32,128]{1,0:T(8,128)S(1)} %copy-done.3, f32[4,32,80,128]{3,2,1,0:T(8,128)} %get-tuple-element.11.mixed_h, f32[4,88,128]{2,1,0:T(8,128)} %copy-done.2, f32[4,88,128]{2,1,0:T(8,128)} %copy-done, f32[4,88,128]{2,1,0:T(8,128)} %copy-done.1, ...), custom_call_target="tpu_custom_call" | custom-call | flops 26214400 | bytes 12582912 | tf_op jit(solution)/shard_map/finish/pallas_call | solution.py:448
Async XLA Ops:
  8.7 28.2 %all-to-all-start = ((f32[32,72,128]{2,1,0:T(8,128)}), f32[32,72,128]{2,1,0:T(8,128)S(1)}, u32[]{:S(2)}, u32[]{:S(2)}) async-start(f32[32,72,128]{2,1,0:T(8,128)} %regrid.1), calls=%async_computation | async-start | bytes 2359296 | tf_op jit(solution)/shard_map/all_to_all | solution.py:490
  13.9 37.3 %copy-start.3 = (s32[32,128]{1,0:T(8,128)S(1)}, s32[32,128]{1,0:T(8,128)}, u32[]{:S(2)}) copy-start(s32[32,128]{1,0:T(8,128)} %depth_ref.1) | copy-start | bytes 49156
  24.8 26.4 %copy-start.2 = (f32[4,88,128]{2,1,0:T(8,128)}, f32[4,88,128]{2,1,0:T(8,128)S(1)}, u32[]{:S(2)}) copy-start(f32[4,88,128]{2,1,0:T(8,128)S(1)} %get-tuple-element.12.own_h) | copy-start | bytes 540676
  24.8 7.9 %collective-permute-start = (f32[4,88,128]{2,1,0:T(8,128)S(1)}, f32[4,88,128]{2,1,0:T(8,128)S(1)}, u32[]{:S(2)}, u32[]{:S(2)}) collective-permute-start(f32[4,88,128]{2,1,0:T(8,128)S(1)} %get-tuple-element.9), channel_id=1, source_target_pairs={{0,8},{8,16},{16,24},{1,9},{9,17},{17,25},{2,10},{10,18},{18,26},{... | collective-permute-start | bytes 540680 | tf_op jit(solution)/shard_map/ppermute | solution.py:476
  28.3 8.6 %collective-permute-start.1 = (f32[4,88,128]{2,1,0:T(8,128)S(1)}, f32[4,88,128]{2,1,0:T(8,128)S(1)}, u32[]{:S(2)}, u32[]{:S(2)}) collective-permute-start(f32[4,88,128]{2,1,0:T(8,128)S(1)} %get-tuple-element.10), channel_id=1, source_target_pairs={{8,0},{16,8},{24,16},{9,1},{17,9},{25,17},{10,2},{18,10},{26,18},{... | collective-permute-start | bytes 540680 | tf_op jit(solution)/shard_map/ppermute | solution.py:476
  32.8 18.4 %copy-start = (f32[4,88,128]{2,1,0:T(8,128)}, f32[4,88,128]{2,1,0:T(8,128)S(1)}, u32[]{:S(2)}) copy-start(f32[4,88,128]{2,1,0:T(8,128)S(1)} %collective-permute-done.after_north.north_h) | copy-start | bytes 540676
  36.9 14.3 %copy-start.1 = (f32[4,88,128]{2,1,0:T(8,128)}, f32[4,88,128]{2,1,0:T(8,128)S(1)}, u32[]{:S(2)}) copy-start(f32[4,88,128]{2,1,0:T(8,128)S(1)} %collective-permute-done.1.after_south.south_h) | copy-start | bytes 540676
  38.2 13.0 %all-to-all-start.1 = ((f32[4,144,128]{2,1,0:T(8,128)}), f32[4,144,128]{2,1,0:T(8,128)S(1)}, u32[]{:S(2)}, u32[]{:S(2)}) async-start(f32[4,144,128]{2,1,0:T(8,128)} %collect.1), calls=%async_computation.1 | async-start | bytes 589824 | tf_op jit(solution)/shard_map/all_to_all | solution.py:498
  42.0 5.8 %collective-permute-start.3 = (f32[4,88,128]{2,1,0:T(8,128)S(1)}, f32[4,88,128]{2,1,0:T(8,128)S(1)}, u32[]{:S(2)}, u32[]{:S(2)}) collective-permute-start(f32[4,88,128]{2,1,0:T(8,128)S(1)} %get-tuple-element.12.own_h), channel_id=1, source_target_pairs={{0,1},{1,2},{2,3},{3,4},{4,5},{5,6},{6,7},{7,0},{8,9},{9,10},{10,1... | collective-permute-start | bytes 540680 | tf_op jit(solution)/shard_map/ppermute | solution.py:476
  42.0 6.0 %collective-permute-start.2 = (f32[4,88,128]{2,1,0:T(8,128)S(1)}, f32[4,88,128]{2,1,0:T(8,128)S(1)}, u32[]{:S(2)}, u32[]{:S(2)}) collective-permute-start(f32[4,88,128]{2,1,0:T(8,128)S(1)} %get-tuple-element.12.own_h), channel_id=1, source_target_pairs={{0,7},{1,0},{2,1},{3,2},{4,3},{5,4},{6,5},{7,6},{8,15},{9,8},{10,9... | collective-permute-start | bytes 540680 | tf_op jit(solution)/shard_map/ppermute | solution.py:476
  47.9 3.3 %copy-start.4 = (f32[4,88,128]{2,1,0:T(8,128)}, f32[4,88,128]{2,1,0:T(8,128)S(1)}, u32[]{:S(2)}) copy-start(f32[4,88,128]{2,1,0:T(8,128)S(1)} %collective-permute-done.3.west_h) | copy-start | bytes 540676
  48.1 3.1 %copy-start.5 = (f32[4,88,128]{2,1,0:T(8,128)}, f32[4,88,128]{2,1,0:T(8,128)S(1)}, u32[]{:S(2)}) copy-start(f32[4,88,128]{2,1,0:T(8,128)S(1)} %collective-permute-done.2.east_h) | copy-start | bytes 540676

commit v7 on v5

--- a/solution.py
+++ b/solution.py
@@ -40,7 +40,7 @@
 
 def regrid_kernel(
     cap, lat, lon, oy, batch, src_h, dev_h, blk_h, coupling_h, atm_h, mask_h, weights_h,
-    out, rows, ids, count, src, dev, blk, coupling, atm, mask, weights, small_sem, big_sem,
+    out_h, out, rows, ids, count, src, dev, blk, coupling, atm, mask, weights, small_sem, big_sem, out_sem,
 ):
     fluxes, atm_rows, _ = atm.shape
     fields = coupling.shape[0]
@@ -113,6 +113,11 @@
         return carry
 
     lax.fori_loop(0, parts, part, 0)
+
+    def send(k, start, stop):
+        return pltpu.make_async_copy(out.at[:, start:stop, :], out_h.at[:, start:stop, :], out_sem.at[k])
+
+    send(0, 0, per).start()
 
     def halo(k):
         d = 2 * k
@@ -141,6 +146,9 @@
         return carry
 
     lax.fori_loop(0, devices // 8, halos, 0)
+    send(1, per, per + SUB).start()
+    send(0, 0, per).wait()
+    send(1, per, per + SUB).wait()
 
 
 def regrid(cap, lat, lon, oy, src, dev, blk, coupling, atm, mask, weights):
@@ -152,9 +160,10 @@
     return pl.pallas_call(
         functools.partial(regrid_kernel, cap, lat, lon, oy, batch),
         in_specs=[HBM] * 7,
-        out_specs=VMEM,
-        out_shape=jax.ShapeDtypeStruct((devices, tall, LANES), f32),
+        out_specs=HBM,
+        out_shape=pltpu.HBM((devices, tall, LANES), f32),
         scratch_shapes=[
+            pltpu.VMEM((devices, tall, LANES), f32),
             pltpu.VMEM((atm.shape[1] * SUB, LANES), f32),
             pltpu.VMEM((devices, LANES), jnp.int32),
             pltpu.SMEM((devices,), jnp.int32),
@@ -167,6 +176,7 @@
             pltpu.VMEM(weights.shape, bf16),
             pltpu.SemaphoreType.DMA((6,)),
             pltpu.SemaphoreType.DMA((pairs // batch,)),
+            pltpu.SemaphoreType.DMA((2,)),
         ],
         compiler_params=pltpu.CompilerParams(vmem_limit_bytes=20 << 20),
         cost_estimate=pl.CostEstimate(flops=2 * 8 * pairs * depth * width, bytes_accessed=10 << 20, transcendentals=0),
@@ -174,8 +184,65 @@
     )(*in_hbm(src, dev, blk, coupling, atm, mask, weights))
 
 
+def solve_row(a, x, active):
+    levels = x.shape[0]
+    a_high, a_low = split(a)
+    r_high, r_low = split(jnp.where(active, x, 0.0))
+    product = matmul(jnp.concatenate([a_high, a_low], axis=0), jnp.concatenate([r_high, r_low], axis=1))
+    solved = product[:levels, :LANES] + (product[levels:, :LANES] + product[:levels, LANES:])
+    return jnp.where(active, solved, x)
+
+
+def outer_rows_kernel(depth_h, state_h, inv_h, north, south, depth_ref, state, inv, sems):
+    _, fields, levels, _ = state.shape
+    oy = depth_ref.shape[0]
+    ends = (0, oy - 1)
+    copies = [pltpu.make_async_copy(depth_h, depth_ref, sems.at[2 * fields, 0])]
+    for q in range(fields):
+        for k, row in enumerate(ends):
+            copies.append(pltpu.make_async_copy(state_h.at[q, :, row, :], state.at[k, q], sems.at[2 * q, k]))
+            copies.append(pltpu.make_async_copy(inv_h.at[q, row, 0], inv.at[k, q], sems.at[2 * q + 1, k]))
+    for copy in copies:
+        copy.start()
+    level = iota((levels, LANES), 0)
+    for copy in copies:
+        copy.wait()
+    for k, (row, ref) in enumerate(zip(ends, (north, south))):
+        depth = depth_ref[row : row + 1, :]
+        names = jnp.zeros((levels, LANES), f32)
+        for q in range(fields):
+            a = inv[k, q]
+            ref[q, 0:levels] = solve_row(a, state[k, q], level < depth)
+            names = jnp.where(iota((levels, LANES), 1) == q, a[:, 0:1], names)
+        names = padded_rows(names, LANES).T
+        for q in range(fields):
+            ref[q, levels : levels + SUB] = jnp.concatenate(
+                [depth.astype(f32), names[q : q + 1], jnp.zeros((SUB - 2, LANES), f32)], axis=0
+            )
+
+
+def outer_rows(depth, state, inverses):
+    fields, levels, _, ox = state.shape
+    edge_shape = jax.ShapeDtypeStruct((fields, levels + SUB, ox), f32)
+    return pl.pallas_call(
+        outer_rows_kernel,
+        in_specs=[HBM] * 3,
+        out_specs=[VMEM] * 2,
+        out_shape=[edge_shape, edge_shape],
+        scratch_shapes=[
+            pltpu.VMEM(depth.shape, jnp.int32),
+            pltpu.VMEM((2, fields, levels, ox), f32),
+            pltpu.VMEM((2, fields, levels, levels), f32),
+            pltpu.SemaphoreType.DMA((2 * fields + 1, 2)),
+        ],
+        compiler_params=pltpu.CompilerParams(vmem_limit_bytes=8 << 20),
+        cost_estimate=pl.CostEstimate(flops=16 * fields * levels * levels * ox, bytes_accessed=1 << 20, transcendentals=0),
+        name="outer_rows",
+    )(*in_hbm(depth, state, inverses))
+
+
 def mix_kernel(
-    depth_h, state_h, inv_h, mixed_h, first_h, north, south, side,
+    depth_h, state_h, inv_h, after, mixed_h, first_h, side,
     depth_ref, state, mixed, inv, first, in_sems, out_sems,
 ):
     fields, oy, levels, _ = mixed.shape
@@ -194,42 +261,26 @@
         turned = pltpu.roll(jnp.broadcast_to(depth_ref[i : i + 1, :].astype(f32), (SUB, LANES)), 2 * i + 1, 1)
         edge_depth = jnp.where(line // 2 == i, turned, edge_depth)
 
-    def message(ref, q, row):
-        ref[q, 0:levels] = mixed[q, row]
-        names = padded_rows(first[q, row], LANES).T[0:1]
-        ref[q, levels : levels + SUB] = jnp.concatenate(
-            [depth_ref[row : row + 1, :].astype(f32), names, jnp.zeros((SUB - 2, LANES), f32)], axis=0
-        )
-
     def field(q, carry):
         pltpu.make_async_copy(mixed_h.at[q], state.at[q], in_sems.at[2 * q]).wait()
         pltpu.make_async_copy(inv_h.at[q], inv.at[q], in_sems.at[2 * q + 1]).wait()
 
         def chunk(c, edges):
-            here = jnp.zeros((levels, LANES), f32)
+            cells = jnp.zeros((levels, LANES), bf16)
+            names = jnp.zeros((levels, LANES), f32)
             for i in range(SUB):
                 row = c * SUB + i
-                active = level < depth_ref[pl.ds(row, 1), :]
-                x = state[q, row]
                 a = inv[q, row, 0]
-                a_high, a_low = split(a)
-                r_high, r_low = split(jnp.where(active, x, 0.0))
-                product = matmul(
-                    jnp.concatenate([a_high, a_low], axis=0), jnp.concatenate([r_high, r_low], axis=1)
-                )
-                solved = product[:levels, :LANES] + (product[levels:, :LANES] + product[:levels, LANES:])
-                m = jnp.where(active, solved, x)
+                m = solve_row(a, state[q, row], level < depth_ref[pl.ds(row, 1), :])
                 mixed[q, row] = m
                 column = jnp.broadcast_to(a[:, 0:1], (levels, LANES))
                 first[q, row] = column
-                here = jnp.where(lane // 2 == i, pltpu.roll(m, 2 * i + 1, 1), here)
-                here = jnp.where(lane // 2 == HALF // 2 + i, column, here)
-            return edges + pltpu.roll(here, 2 * SUB * c, 1)
+                cells = jnp.where(lane // 2 == i, pltpu.roll(m.astype(bf16), 2 * i + 1, 1), cells)
+                names = jnp.where(lane // 2 == HALF // 2 + i, column, names)
+            return edges + pltpu.roll(cells.astype(f32) + names, 2 * SUB * c, 1)
 
         side[q, 0:levels] = lax.fori_loop(0, oy // SUB, chunk, jnp.zeros((levels, LANES), f32))
         side[q, levels : levels + SUB] = edge_depth
-        message(north, q, 0)
-        message(south, q, oy - 1)
         pltpu.make_async_copy(mixed.at[q], mixed_h.at[q], out_sems.at[2 * q]).start()
         pltpu.make_async_copy(first.at[q], first_h.at[q], out_sems.at[2 * q + 1]).start()
         return carry
@@ -240,15 +291,15 @@
         pltpu.make_async_copy(first.at[q], first_h.at[q], out_sems.at[2 * q + 1]).wait()
 
 
-def mix(depth, state, inverses):
+def mix(depth, state, inverses, after):
     fields, levels, oy, ox = state.shape
     edge_shape = jax.ShapeDtypeStruct((fields, levels + SUB, ox), f32)
     full = (fields, oy, levels, ox)
     return pl.pallas_call(
         mix_kernel,
-        in_specs=[HBM] * 3,
-        out_specs=[HBM] * 2 + [VMEM] * 3,
-        out_shape=[pltpu.HBM(full, f32), pltpu.HBM(full, f32), edge_shape, edge_shape, edge_shape],
+        in_specs=[HBM] * 3 + [pl.BlockSpec(memory_space=pl.ANY)],
+        out_specs=[HBM] * 2 + [VMEM],
+        out_shape=[pltpu.HBM(full, f32), pltpu.HBM(full, f32), edge_shape],
         scratch_shapes=[
             pltpu.VMEM(depth.shape, jnp.int32),
             pltpu.VMEM(full, f32),
@@ -261,10 +312,10 @@
         compiler_params=pltpu.CompilerParams(vmem_limit_bytes=32 << 20),
         cost_estimate=pl.CostEstimate(flops=2 * 4 * fields * oy * levels * levels * ox, bytes_accessed=16 << 20, transcendentals=0),
         name="mix",
-    )(*in_hbm(depth, state, inverses))
-
-
-def collect_kernel(cap, fields, oy, recv, after, out):
+    )(*in_hbm(depth, state, inverses), after)
+
+
+def collect_kernel(cap, fields, oy, recv, after_mix, after_north, after_south, out):
     lat = out.shape[0]
     lon = recv.shape[0] // lat
     per = fields * cap
@@ -310,17 +361,17 @@
 def collect(cap, fields, oy, lat, received, after):
     return pl.pallas_call(
         functools.partial(collect_kernel, cap, fields, oy),
-        in_specs=[VMEM, pl.BlockSpec(memory_space=pl.ANY)],
+        in_specs=[VMEM] + [pl.BlockSpec(memory_space=pl.ANY)] * 3,
         out_specs=VMEM,
         out_shape=jax.ShapeDtypeStruct((lat, fields * oy + 2 * SUB, LANES), f32),
         compiler_params=pltpu.CompilerParams(vmem_limit_bytes=16 << 20),
         name="collect",
-    )(received, after)
+    )(received, *after)
 
 
 def finish_kernel(
-    recv, depth_ref, mixed_h, first_h, north, south, east, west,
-    out_h, forcing, z, keep, halo, z_north, z_south, mixed, first, stage, in_sems, out_sems,
+    recv, depth_ref, mixed_h, first_h, north_h, south_h, east, west,
+    out_h, north, south, forcing, z, keep, halo, z_north, z_south, mixed, first, stage, edge_sems, in_sems, out_sems,
 ):
     fields, oy, levels, _ = mixed.shape
     level = iota((levels, LANES), 0)
@@ -329,9 +380,24 @@
     square_lane = iota((LANES, LANES), 1)
     line = iota((1, LANES), 1)
     even = line % 2 == 0
+    edges = [
+        pltpu.make_async_copy(a, b, edge_sems.at[k])
+        for k, (a, b) in enumerate(((north_h, north), (south_h, south)))
+    ]
+    for copy in edges:
+        copy.start()
+
+    def loads(q, c):
+        here = (q, pl.ds(pl.multiple_of(c * SUB, SUB), SUB))
+        return [
+            pltpu.make_async_copy(a.at[here], b.at[here], in_sems.at[k, q, c])
+            for k, (a, b) in enumerate(((mixed_h, mixed), (first_h, first)))
+        ]
+
     for q in range(fields):
-        pltpu.make_async_copy(mixed_h.at[q], mixed.at[q], in_sems.at[2 * q]).start()
-        pltpu.make_async_copy(first_h.at[q], first.at[q], in_sems.at[2 * q + 1]).start()
+        for c in range(oy // SUB):
+            for copy in loads(q, c):
+                copy.start()
 
     total = recv[0]
     for a in range(1, recv.shape[0]):
@@ -341,6 +407,8 @@
     rows = total[forced_rows : forced_rows + SUB]
     columns = total[forced_rows + SUB :]
 
+    for copy in edges:
+        copy.wait()
     depth = depth_ref[...]
     wide = iota((oy, LANES), 1)
 
@@ -374,19 +442,19 @@
         names = pltpu.roll(jnp.where(even, east[q], west[q]), HALF, 1)
         active = level < cells[levels : levels + 1].astype(jnp.int32)
         value = cells[0:levels] + names[0:levels] * columns[q : q + 1]
-        halo[q] = jnp.where(active & (line < 2 * oy), value, 0.0)
+        halo[q] = jnp.where(active & (line < 2 * oy), value, 0.0).astype(bf16)
 
     both = jnp.where((square_row == square_lane + 1) | (square_row == square_lane - 1), 1.0, 0.0).astype(bf16)
     both = jnp.concatenate([both, both], axis=0)
     ends = (lanes == 0) | (lanes == LANES - 1)
 
     def field(q, carry):
-        pltpu.make_async_copy(mixed_h.at[q], mixed.at[q], in_sems.at[2 * q]).wait()
-        pltpu.make_async_copy(first_h.at[q], first.at[q], in_sems.at[2 * q + 1]).wait()
         z[0] = z_north[q]
         z[oy + 1] = z_south[q]
 
         def solve(c, carry):
+            for copy in loads(q, c):
+                copy.wait()
             for i in range(SUB):
                 r = c * SUB + i
                 forced = mixed[q, r] + first[q, r] * forcing[pl.ds(q * oy + r, 1), :]
@@ -399,10 +467,10 @@
             start = c * SUB
             high, low = split(z[pl.ds(start + 1, SUB)].reshape(SUB * levels, LANES))
             sides = matmul(jnp.concatenate([high, low], axis=1), both)
-            edge = pltpu.roll(halo[q], (LANES - 2 * SUB * c) % LANES, 1)
+            edge = pltpu.roll(halo[q].astype(f32), (LANES - 2 * SUB * c) % LANES, 1).astype(bf16)
             for i in range(SUB):
                 r = start + i
-                outside = jnp.where(ends, pltpu.roll(edge, LANES - 1 - 2 * i, 1), 0.0)
+                outside = jnp.where(ends, pltpu.roll(edge, LANES - 1 - 2 * i, 1).astype(f32), 0.0)
                 around = (z[r] + z[r + 2]) + (sides[i * levels : (i + 1) * levels] + outside)
                 active = level < depth_ref[pl.ds(r, 1), :]
                 stage[q, r] = jnp.where(active, z[r + 1] * keep[r] + diffusion_rate * around, mixed[q, r])
@@ -422,29 +490,33 @@
 def finish(received, depth, mixed, first, halos):
     fields, oy, levels, ox = mixed.shape
     edge = pltpu.VMEM((fields, levels, ox), f32)
+    message = pltpu.VMEM((fields, levels + SUB, ox), f32)
     full = pltpu.VMEM((fields, oy, levels, ox), f32)
     return pl.pallas_call(
         finish_kernel,
-        in_specs=[VMEM] * 2 + [HBM] * 2 + [VMEM] * 4,
+        in_specs=[VMEM] * 2 + [HBM] * 4 + [VMEM] * 2,
         out_specs=HBM,
         out_shape=pltpu.HBM((fields, levels, oy, ox), f32),
         scratch_shapes=[
+            message,
+            message,
             pltpu.VMEM((fields * oy, ox), f32),
             pltpu.VMEM((oy + 2, levels, ox), f32),
             pltpu.VMEM((oy, levels, ox), f32),
-            edge,
+            pltpu.VMEM((fields, levels, ox), bf16),
             edge,
             edge,
             full,
             full,
             full,
-            pltpu.SemaphoreType.DMA((2 * fields,)),
+            pltpu.SemaphoreType.DMA((2,)),
+            pltpu.SemaphoreType.DMA((2, fields, oy // SUB)),
             pltpu.SemaphoreType.DMA((fields,)),
         ],
         compiler_params=pltpu.CompilerParams(vmem_limit_bytes=32 << 20),
         cost_estimate=pl.CostEstimate(flops=20 * fields * oy * levels * ox, bytes_accessed=12 << 20, transcendentals=0),
         name="finish",
-    )(received, depth, *in_hbm(mixed, first), *halos)
+    )(received, depth, *in_hbm(mixed, first, *halos[0:2]), *halos[2:])
 
 
 def shift(x, axis, step, wrap):
@@ -465,14 +537,15 @@
         intersection_weights,
     )
     in_plane = lax.all_to_all(slots, "lon", 0, 0, tiled=True)
-    mixed, first, north, south, side = mix(depth_levels, ocean_state, inverses)
+    north, south = outer_rows(depth_levels, ocean_state, inverses)
+    mixed, first, side = mix(depth_levels, ocean_state, inverses, north)
     halos = (
         shift(south, "lat", 1, False),
         shift(north, "lat", -1, False),
         shift(side, "lon", -1, True),
         shift(side, "lon", 1, True),
     )
-    received = lax.all_to_all(collect(cap, fields, oy, lat, in_plane, side), "lat", 0, 0, tiled=True)
+    received = lax.all_to_all(collect(cap, fields, oy, lat, in_plane, (side, *halos[0:2])), "lat", 0, 0, tiled=True)
     return finish(received, depth_levels, mixed, first, halos)
 
 

time: 60 us -> 60.6 us (1.010)
  waiting for transfers between devices: 10.5 us -> 7.08 us
  Pallas kernels: 31.2 us -> 34.4 us
    all_to_all x1, waiting for transfers between devices: 5.36 us -> 0.01 us  [on_device(): in_plane = lax.all_to_all(slots, 'lon', 0, 0, tiled=True)]
    pallas_call x2 -> x3, Pallas kernels: 20.9 us -> 24.4 us  [the longest x1 11.6 us: finish(): pl.pallas_call(finish_kernel, in_specs=[VMEM] * 2 + [HBM] * 4 + [VMEM] *...]
    all_to_all x1, waiting for transfers between devices: 0.01 us -> 3.33 us  [on_device(): lax.all_to_all(collect(cap, fields, oy, lat, in_plane, (side, *halos[0:2]...]
    ppermute x4, waiting for transfers between devices: 5.1 us -> 3.75 us  [shift(): return lax.ppermute(x, axis, pairs)]
    all_to_all x1, starting transfers between devices: 4.87 us -> 5.94 us  [on_device(): lax.all_to_all(collect(cap, fields, oy, lat, in_plane, (side, *halos[0:2]...]
  transfers between devices with their start and end apart: 6 -> 6, of which waited for: 3 -> 3; matrix products, arithmetic and copies ran while one was open for 0% -> 0% of each run, Pallas kernels for 19% -> 21%
where the time goes in v7:
time: 60.6 us; the launch traced here: 60.1 us
  Pallas kernels  34.4 us (57%)
  starting transfers between devices  18.6 us (31%)
  waiting for transfers between devices  7.08 us (12%)
    pallas_call x1, Pallas kernels, finish(): pl.pallas_call(finish_kernel, in_specs=[VMEM] * 2 + [HBM] * 4 + [VMEM] *...  11.6 us
    pallas_call x1, Pallas kernels, mix(): pl.pallas_call(mix_kernel, in_specs=[HBM] * 3 + [pl.BlockSpec(memory_spac...  11.2 us
    pallas_call x1, Pallas kernels, regrid(): pl.pallas_call(functools.partial(regrid_kernel, cap, lat, lon, oy, batch)...  8.64 us
    ppermute x4, starting transfers between devices, shift(): return lax.ppermute(x, axis, pairs)  7.42 us
    all_to_all x1, starting transfers between devices, on_device(): lax.all_to_all(collect(cap, fields, oy, lat, in_plane, (side, *halos[0:2]...  5.94 us
    all_to_all x1, starting transfers between devices, on_device(): in_plane = lax.all_to_all(slots, 'lon', 0, 0, tiled=True)  5.19 us
    ppermute x4, waiting for transfers between devices, shift(): return lax.ppermute(x, axis, pairs)  3.75 us
    all_to_all x1, waiting for transfers between devices, on_device(): lax.all_to_all(collect(cap, fields, oy, lat, in_plane, (side, *halos[0:2]...  3.33 us
  transfers between devices with their start and end apart: 6, of which 3 were waited for; matrix products, arithmetic and copies ran while one was open for 0% of the time, Pallas kernels for 21%

profile of v7, /device:TPU:0, one launch (start us, length us, event | category | flops | bytes accessed | tf_op | source)
XLA Modules:
  0.0 60.1 jit_solution(8797484035252697855)
XLA Ops:
  0.0 8.6 %regrid.1 = f32[32,72,128]{2,1,0:T(8,128)} custom-call(s32[256]{0:T(256)} %src_h.1, s32[256]{0:T(256)} %bitcast.1, s32[256]{0:T(256)} %blk_h.1, f32[4,8]{1,0:T(4,128)} %coupling_h.1, bf16[8,64,128]{2,1,0:T(8,128)(2,1)} %atm_h.1, s32[64,128]{1,0:T(8,128)} %mask_h.1, bf16[256,128,128]{2,1,0:T(8,128)(2,1)} %weights_h.1), custom_call_target="tpu_custom_call" | custom-call | flops 67108864 | bytes 10485760 | tf_op jit(solution)/shard_map/regrid/pallas_call | solution.py:160
  8.7 5.2 %all-to-all-start = ((f32[32,72,128]{2,1,0:T(8,128)}), f32[32,72,128]{2,1,0:T(8,128)S(1)}, u32[]{:S(2)}, u32[]{:S(2)}) async-start(f32[32,72,128]{2,1,0:T(8,128)} %regrid.1), calls=%async_computation | async-start | bytes 2359296 | tf_op jit(solution)/shard_map/all_to_all | solution.py:539
  13.8 1.6 %outer_rows.1 = (f32[4,88,128]{2,1,0:T(8,128)S(1)}, f32[4,88,128]{2,1,0:T(8,128)S(1)}) custom-call(s32[32,128]{1,0:T(8,128)} %depth_ref.1, f32[4,80,32,128]{3,2,1,0:T(8,128)} %state_h.3, f32[4,32,1,80,80]{4,3,2,1,0:T(8,128)} %inv_h.3), custom_call_target="tpu_custom_call" | custom-call | flops 52428800 | bytes 1048576 | tf_op jit(solution)/shard_map/outer_rows/pallas_call | solution.py:227
  15.5 3.5 %collective-permute-start = (f32[4,88,128]{2,1,0:T(8,128)S(1)}, f32[4,88,128]{2,1,0:T(8,128)S(1)}, u32[]{:S(2)}, u32[]{:S(2)}) collective-permute-start(f32[4,88,128]{2,1,0:T(8,128)S(1)} %get-tuple-element.12), channel_id=1, source_target_pairs={{0,8},{8,16},{16,24},{1,9},{9,17},{17,25},{2,10},{10,18},{18,26},{... | collective-permute-start | bytes 540680 | tf_op jit(solution)/shard_map/ppermute | solution.py:525
  19.0 0.0 copy-start.2
  19.0 1.3 %collective-permute-start.1 = (f32[4,88,128]{2,1,0:T(8,128)S(1)}, f32[4,88,128]{2,1,0:T(8,128)S(1)}, u32[]{:S(2)}, u32[]{:S(2)}) collective-permute-start(f32[4,88,128]{2,1,0:T(8,128)S(1)} %get-tuple-element.10.after), channel_id=1, source_target_pairs={{8,0},{16,8},{24,16},{9,1},{17,9},{25,17},{10,2},{18,10},{26,18},{... | collective-permute-start | bytes 540680 | tf_op jit(solution)/shard_map/ppermute | solution.py:525
  20.3 11.2 %mix.1 = (f32[4,32,80,128]{3,2,1,0:T(8,128)}, f32[4,32,80,128]{3,2,1,0:T(8,128)}, f32[4,88,128]{2,1,0:T(8,128)S(1)}) custom-call(s32[32,128]{1,0:T(8,128)} %depth_ref.1, f32[4,80,32,128]{3,2,1,0:T(8,128)} %state_h.3, f32[4,32,1,80,80]{4,3,2,1,0:T(8,128)} %inv_h.3, f32[4,88,128]{2,1,0:T(8,128)S(1)} %get-tuple-element.10.after), custom_call_target="tpu_custom_call" | custom-call | flops 838860800 | bytes 16777216 | tf_op jit(solution)/shard_map/mix/pallas_call | solution.py:298
  31.5 0.0 collective-permute-done.after_north.north_h
  31.5 0.0 copy-start
  31.5 0.0 collective-permute-done.1.after_south.south_h
  31.5 0.0 copy-start.1
  31.5 0.0 all-to-all-done.recv
  31.6 1.3 %collect.1 = f32[4,144,128]{2,1,0:T(8,128)} custom-call(f32[32,72,128]{2,1,0:T(8,128)S(1)} %all-to-all-done.recv, f32[4,88,128]{2,1,0:T(8,128)S(1)} %get-tuple-element.11.after_mix, f32[4,88,128]{2,1,0:T(8,128)S(1)} %collective-permute-done.after_north.north_h, f32[4,88,128]{2,1,0:T(8,128)S(1)} %collective-permute-done.1.after_south.south_h), custom_call_target="tpu_custom_call" | custom-call | tf_op jit(solution)/shard_map/collect/pallas_call | solution.py:362
  32.9 5.9 %all-to-all-start.1 = ((f32[4,144,128]{2,1,0:T(8,128)}), f32[4,144,128]{2,1,0:T(8,128)S(1)}, u32[]{:S(2)}, u32[]{:S(2)}) async-start(f32[4,144,128]{2,1,0:T(8,128)} %collect.1), calls=%async_computation.1 | async-start | bytes 589824 | tf_op jit(solution)/shard_map/all_to_all | solution.py:548
  38.8 0.0 collective-permute-start.3
  38.8 2.6 %collective-permute-start.2 = (f32[4,88,128]{2,1,0:T(8,128)S(1)}, f32[4,88,128]{2,1,0:T(8,128)S(1)}, u32[]{:S(2)}, u32[]{:S(2)}) collective-permute-start(f32[4,88,128]{2,1,0:T(8,128)S(1)} %get-tuple-element.11.after_mix), channel_id=1, source_target_pairs={{0,7},{1,0},{2,1},{3,2},{4,3},{5,4},{6,5},{7,6},{8,15},{9,8},{10,9... | collective-permute-start | bytes 540680 | tf_op jit(solution)/shard_map/ppermute | solution.py:525
  41.5 3.2 %collective-permute-done.3.west = f32[4,88,128]{2,1,0:T(8,128)S(1)} collective-permute-done((f32[4,88,128]{2,1,0:T(8,128)S(1)}, f32[4,88,128]{2,1,0:T(8,128)S(1)}, u32[]{:S(2)}, u32[]{:S(2)}) %collective-permute-start.3) | collective-permute-done | bytes 180256 | tf_op jit(solution)/shard_map/ppermute | solution.py:525
  44.6 0.6 collective-permute-done.2.east
  45.2 3.3 %all-to-all-done.1.recv = f32[4,144,128]{2,1,0:T(8,128)S(1)} async-done(((f32[4,144,128]{2,1,0:T(8,128)}), f32[4,144,128]{2,1,0:T(8,128)S(1)}, u32[]{:S(2)}, u32[]{:S(2)}) %all-to-all-start.1) | async-done | bytes 294944 | tf_op jit(solution)/shard_map/all_to_all | solution.py:548
  48.5 0.0 copy-done
  48.5 0.0 copy-done.1
  48.5 0.0 copy-done.2
  48.5 11.6 %finish.1 = f32[4,80,32,128]{3,2,1,0:T(8,128)} custom-call(f32[4,144,128]{2,1,0:T(8,128)S(1)} %all-to-all-done.1.recv, s32[32,128]{1,0:T(8,128)S(1)} %copy-done.2, f32[4,32,80,128]{3,2,1,0:T(8,128)} %get-tuple-element.13.mixed_h, f32[4,32,80,128]{3,2,1,0:T(8,128)} %get-tuple-element.14.first_h, f32[4,88,128]{2,1,0:T(8,128)} %copy-done, ...), custom_call_target="tpu_custom_call" | custom-call | flops 26214400 | bytes 12582912 | tf_op jit(solution)/shard_map/finish/pallas_call | solution.py:495
Async XLA Ops:
  8.7 22.9 %all-to-all-start = ((f32[32,72,128]{2,1,0:T(8,128)}), f32[32,72,128]{2,1,0:T(8,128)S(1)}, u32[]{:S(2)}, u32[]{:S(2)}) async-start(f32[32,72,128]{2,1,0:T(8,128)} %regrid.1), calls=%async_computation | async-start | bytes 2359296 | tf_op jit(solution)/shard_map/all_to_all | solution.py:539
  15.5 16.0 %collective-permute-start = (f32[4,88,128]{2,1,0:T(8,128)S(1)}, f32[4,88,128]{2,1,0:T(8,128)S(1)}, u32[]{:S(2)}, u32[]{:S(2)}) collective-permute-start(f32[4,88,128]{2,1,0:T(8,128)S(1)} %get-tuple-element.12), channel_id=1, source_target_pairs={{0,8},{8,16},{16,24},{1,9},{9,17},{17,25},{2,10},{10,18},{18,26},{... | collective-permute-start | bytes 540680 | tf_op jit(solution)/shard_map/ppermute | solution.py:525
  19.0 29.6 %copy-start.2 = (s32[32,128]{1,0:T(8,128)S(1)}, s32[32,128]{1,0:T(8,128)}, u32[]{:S(2)}) copy-start(s32[32,128]{1,0:T(8,128)} %depth_ref.1) | copy-start | bytes 49156
  19.0 12.6 %collective-permute-start.1 = (f32[4,88,128]{2,1,0:T(8,128)S(1)}, f32[4,88,128]{2,1,0:T(8,128)S(1)}, u32[]{:S(2)}, u32[]{:S(2)}) collective-permute-start(f32[4,88,128]{2,1,0:T(8,128)S(1)} %get-tuple-element.10.after), channel_id=1, source_target_pairs={{8,0},{16,8},{24,16},{9,1},{17,9},{25,17},{10,2},{18,10},{26,18},{... | collective-permute-start | bytes 540680 | tf_op jit(solution)/shard_map/ppermute | solution.py:525
  31.5 17.0 %copy-start = (f32[4,88,128]{2,1,0:T(8,128)}, f32[4,88,128]{2,1,0:T(8,128)S(1)}, u32[]{:S(2)}) copy-start(f32[4,88,128]{2,1,0:T(8,128)S(1)} %collective-permute-done.after_north.north_h) | copy-start | bytes 540676
  31.5 17.0 %copy-start.1 = (f32[4,88,128]{2,1,0:T(8,128)}, f32[4,88,128]{2,1,0:T(8,128)S(1)}, u32[]{:S(2)}) copy-start(f32[4,88,128]{2,1,0:T(8,128)S(1)} %collective-permute-done.1.after_south.south_h) | copy-start | bytes 540676
  32.9 15.7 %all-to-all-start.1 = ((f32[4,144,128]{2,1,0:T(8,128)}), f32[4,144,128]{2,1,0:T(8,128)S(1)}, u32[]{:S(2)}, u32[]{:S(2)}) async-start(f32[4,144,128]{2,1,0:T(8,128)} %collect.1), calls=%async_computation.1 | async-start | bytes 589824 | tf_op jit(solution)/shard_map/all_to_all | solution.py:548
  38.8 5.8 %collective-permute-start.3 = (f32[4,88,128]{2,1,0:T(8,128)S(1)}, f32[4,88,128]{2,1,0:T(8,128)S(1)}, u32[]{:S(2)}, u32[]{:S(2)}) collective-permute-start(f32[4,88,128]{2,1,0:T(8,128)S(1)} %get-tuple-element.11.after_mix), channel_id=1, source_target_pairs={{0,1},{1,2},{2,3},{3,4},{4,5},{5,6},{6,7},{7,0},{8,9},{9,10},{10,1... | collective-permute-start | bytes 540680 | tf_op jit(solution)/shard_map/ppermute | solution.py:525
  38.8 6.4 %collective-permute-start.2 = (f32[4,88,128]{2,1,0:T(8,128)S(1)}, f32[4,88,128]{2,1,0:T(8,128)S(1)}, u32[]{:S(2)}, u32[]{:S(2)}) collective-permute-start(f32[4,88,128]{2,1,0:T(8,128)S(1)} %get-tuple-element.11.after_mix), channel_id=1, source_target_pairs={{0,7},{1,0},{2,1},{3,2},{4,3},{5,4},{6,5},{7,6},{8,15},{9,8},{10,9... | collective-permute-start | bytes 540680 | tf_op jit(solution)/shard_map/ppermute | solution.py:525

commit v8 on v7

--- a/solution.py
+++ b/solution.py
@@ -47,6 +47,7 @@
     devices = out.shape[0]
     per = fields * cap
     parts = weights.shape[0] // batch
+    ahead = min(3, parts)
 
     def big(k):
         here = pl.ds(pl.multiple_of(k * batch, batch), batch)
@@ -63,7 +64,7 @@
     ]
     for copy in small:
         copy.start()
-    for k in range(parts):
+    for k in range(ahead):
         big(k).start()
 
     def clear(d, carry):
@@ -96,6 +97,11 @@
 
     def part(k, carry):
         big(k).wait()
+
+        @pl.when(k + ahead < parts)
+        def _():
+            big(k + ahead).start()
+
         for u in range(0, batch, 2):
             p = k * batch + u
             x = jnp.concatenate(
@@ -246,12 +252,18 @@
     depth_ref, state, mixed, inv, first, in_sems, out_sems,
 ):
     fields, oy, levels, _ = mixed.shape
-    depth_copy = pltpu.make_async_copy(depth_h, depth_ref, in_sems.at[2 * fields])
+    depth_copy = pltpu.make_async_copy(depth_h, depth_ref, in_sems.at[2 * fields, 0])
     depth_copy.start()
-    for q in range(fields):
-        for i in range(oy):
-            pltpu.make_async_copy(state_h.at[q, :, i, :], state.at[q, i], in_sems.at[2 * q]).start()
-        pltpu.make_async_copy(inv_h.at[q], inv.at[q], in_sems.at[2 * q + 1]).start()
+
+    def load(q, c):
+        for i in range(SUB):
+            row = c * SUB + i
+            pltpu.make_async_copy(state_h.at[q, :, row, :], state.at[q, row], in_sems.at[2 * q, c]).start()
+        here = (q, pl.ds(c * SUB, SUB))
+        pltpu.make_async_copy(inv_h.at[here], inv.at[here], in_sems.at[2 * q + 1, c]).start()
+
+    for c in range(oy // SUB):
+        load(0, c)
     depth_copy.wait()
     level = iota((levels, LANES), 0)
     lane = iota((levels, LANES), 1)
@@ -262,11 +274,16 @@
         edge_depth = jnp.where(line // 2 == i, turned, edge_depth)
 
     def field(q, carry):
-        pltpu.make_async_copy(mixed_h.at[q], state.at[q], in_sems.at[2 * q]).wait()
-        pltpu.make_async_copy(inv_h.at[q], inv.at[q], in_sems.at[2 * q + 1]).wait()
-
         def chunk(c, edges):
-            cells = jnp.zeros((levels, LANES), bf16)
+            here = (q, pl.ds(pl.multiple_of(c * SUB, SUB), SUB))
+            pltpu.make_async_copy(mixed_h.at[here], state.at[here], in_sems.at[2 * q, c]).wait()
+            pltpu.make_async_copy(inv_h.at[here], inv.at[here], in_sems.at[2 * q + 1, c]).wait()
+
+            @pl.when(q + 1 < fields)
+            def _():
+                load(q + 1, c)
+
+            cells = jnp.zeros((levels, LANES), f32)
             names = jnp.zeros((levels, LANES), f32)
             for i in range(SUB):
                 row = c * SUB + i
@@ -275,14 +292,14 @@
                 mixed[q, row] = m
                 column = jnp.broadcast_to(a[:, 0:1], (levels, LANES))
                 first[q, row] = column
-                cells = jnp.where(lane // 2 == i, pltpu.roll(m.astype(bf16), 2 * i + 1, 1), cells)
+                cells = jnp.where(lane // 2 == i, pltpu.roll(m, 2 * i + 1, 1), cells)
                 names = jnp.where(lane // 2 == HALF // 2 + i, column, names)
-            return edges + pltpu.roll(cells.astype(f32) + names, 2 * SUB * c, 1)
+            pltpu.make_async_copy(mixed.at[here], mixed_h.at[here], out_sems.at[2 * q]).start()
+            pltpu.make_async_copy(first.at[here], first_h.at[here], out_sems.at[2 * q + 1]).start()
+            return edges + pltpu.roll(cells + names, 2 * SUB * c, 1)
 
         side[q, 0:levels] = lax.fori_loop(0, oy // SUB, chunk, jnp.zeros((levels, LANES), f32))
         side[q, levels : levels + SUB] = edge_depth
-        pltpu.make_async_copy(mixed.at[q], mixed_h.at[q], out_sems.at[2 * q]).start()
-        pltpu.make_async_copy(first.at[q], first_h.at[q], out_sems.at[2 * q + 1]).start()
         return carry
 
     lax.fori_loop(0, fields, field, 0)
@@ -306,7 +323,7 @@
             pltpu.VMEM(full, f32),
             pltpu.VMEM(inverses.shape, f32),
             pltpu.VMEM(full, f32),
-            pltpu.SemaphoreType.DMA((2 * fields + 1,)),
+            pltpu.SemaphoreType.DMA((2 * fields + 1, oy // SUB)),
             pltpu.SemaphoreType.DMA((2 * fields,)),
         ],
         compiler_params=pltpu.CompilerParams(vmem_limit_bytes=32 << 20),
@@ -394,10 +411,9 @@
             for k, (a, b) in enumerate(((mixed_h, mixed), (first_h, first)))
         ]
 
-    for q in range(fields):
-        for c in range(oy // SUB):
-            for copy in loads(q, c):
-                copy.start()
+    for c in range(oy // SUB):
+        for copy in loads(0, c):
+            copy.start()
 
     total = recv[0]
     for a in range(1, recv.shape[0]):
@@ -442,7 +458,7 @@
         names = pltpu.roll(jnp.where(even, east[q], west[q]), HALF, 1)
         active = level < cells[levels : levels + 1].astype(jnp.int32)
         value = cells[0:levels] + names[0:levels] * columns[q : q + 1]
-        halo[q] = jnp.where(active & (line < 2 * oy), value, 0.0).astype(bf16)
+        halo[q] = jnp.where(active & (line < 2 * oy), value, 0.0)
 
     both = jnp.where((square_row == square_lane + 1) | (square_row == square_lane - 1), 1.0, 0.0).astype(bf16)
     both = jnp.concatenate([both, both], axis=0)
@@ -455,6 +471,12 @@
         def solve(c, carry):
             for copy in loads(q, c):
                 copy.wait()
+
+            @pl.when(q + 1 < fields)
+            def _():
+                for copy in loads(q + 1, c):
+                    copy.start()
+
             for i in range(SUB):
                 r = c * SUB + i
                 forced = mixed[q, r] + first[q, r] * forcing[pl.ds(q * oy + r, 1), :]
@@ -467,10 +489,10 @@
             start = c * SUB
             high, low = split(z[pl.ds(start + 1, SUB)].reshape(SUB * levels, LANES))
             sides = matmul(jnp.concatenate([high, low], axis=1), both)
-            edge = pltpu.roll(halo[q].astype(f32), (LANES - 2 * SUB * c) % LANES, 1).astype(bf16)
+            edge = pltpu.roll(halo[q], (LANES - 2 * SUB * c) % LANES, 1)
             for i in range(SUB):
                 r = start + i
-                outside = jnp.where(ends, pltpu.roll(edge, LANES - 1 - 2 * i, 1).astype(f32), 0.0)
+                outside = jnp.where(ends, pltpu.roll(edge, LANES - 1 - 2 * i, 1), 0.0)
                 around = (z[r] + z[r + 2]) + (sides[i * levels : (i + 1) * levels] + outside)
                 active = level < depth_ref[pl.ds(r, 1), :]
                 stage[q, r] = jnp.where(active, z[r + 1] * keep[r] + diffusion_rate * around, mixed[q, r])
@@ -503,7 +525,7 @@
             pltpu.VMEM((fields * oy, ox), f32),
             pltpu.VMEM((oy + 2, levels, ox), f32),
             pltpu.VMEM((oy, levels, ox), f32),
-            pltpu.VMEM((fields, levels, ox), bf16),
+            edge,
             edge,
             edge,
             full,

time: 60.6 us -> 58.2 us (0.960)
  Pallas kernels: 34.4 us -> 31.9 us
    pallas_call x1, Pallas kernels: 11.6 us -> 10.3 us  [finish(): pl.pallas_call(finish_kernel, in_specs=[VMEM] * 2 + [HBM] * 4 + [VMEM] *...]
    pallas_call x1, Pallas kernels: 11.2 us -> 10.3 us  [mix(): pl.pallas_call(mix_kernel, in_specs=[HBM] * 3 + [pl.BlockSpec(memory_spac...]
  transfers between devices with their start and end apart: 6 -> 6, of which waited for: 3 -> 4; matrix products, arithmetic and copies ran while one was open for 0% -> 0% of each run, Pallas kernels for 21% -> 21%
where the time goes in v8:
time: 58.2 us; the launch traced here: 57.6 us
  Pallas kernels  31.9 us (55%)
  starting transfers between devices  18.5 us (32%)
  waiting for transfers between devices  7.17 us (12%)
    pallas_call x1, Pallas kernels, finish(): pl.pallas_call(finish_kernel, in_specs=[VMEM] * 2 + [HBM] * 4 + [VMEM] *...  10.3 us
    pallas_call x1, Pallas kernels, mix(): pl.pallas_call(mix_kernel, in_specs=[HBM] * 3 + [pl.BlockSpec(memory_spac...  10.3 us
    pallas_call x1, Pallas kernels, regrid(): pl.pallas_call(functools.partial(regrid_kernel, cap, lat, lon, oy, batch)...  8.39 us
    ppermute x4, starting transfers between devices, shift(): return lax.ppermute(x, axis, pairs)  7.42 us
    all_to_all x1, starting transfers between devices, on_device(): lax.all_to_all(collect(cap, fields, oy, lat, in_plane, (side, *halos[0:2]...  5.86 us
    all_to_all x1, starting transfers between devices, on_device(): in_plane = lax.all_to_all(slots, 'lon', 0, 0, tiled=True)  5.18 us
    ppermute x4, waiting for transfers between devices, shift(): return lax.ppermute(x, axis, pairs)  3.75 us
    all_to_all x1, waiting for transfers between devices, on_device(): lax.all_to_all(collect(cap, fields, oy, lat, in_plane, (side, *halos[0:2]...  3.34 us
  transfers between devices with their start and end apart: 6, of which 4 were waited for; matrix products, arithmetic and copies ran while one was open for 0% of the time, Pallas kernels for 21%

profile of v8, /device:TPU:0, one launch (start us, length us, event | category | flops | bytes accessed | tf_op | source)
XLA Modules:
  0.0 57.6 jit_solution(6703011717251622214)
XLA Ops:
  0.0 8.4 %regrid.1 = f32[32,72,128]{2,1,0:T(8,128)} custom-call(s32[256]{0:T(256)} %src_h.1, s32[256]{0:T(256)} %bitcast.1, s32[256]{0:T(256)} %blk_h.1, f32[4,8]{1,0:T(4,128)} %coupling_h.1, bf16[8,64,128]{2,1,0:T(8,128)(2,1)} %atm_h.1, s32[64,128]{1,0:T(8,128)} %mask_h.1, bf16[256,128,128]{2,1,0:T(8,128)(2,1)} %weights_h.1), custom_call_target="tpu_custom_call" | custom-call | flops 67108864 | bytes 10485760 | tf_op jit(solution)/shard_map/regrid/pallas_call | solution.py:166
  8.4 5.2 %all-to-all-start = ((f32[32,72,128]{2,1,0:T(8,128)}), f32[32,72,128]{2,1,0:T(8,128)S(1)}, u32[]{:S(2)}, u32[]{:S(2)}) async-start(f32[32,72,128]{2,1,0:T(8,128)} %regrid.1), calls=%async_computation | async-start | bytes 2359296 | tf_op jit(solution)/shard_map/all_to_all | solution.py:561
  13.6 1.6 %outer_rows.1 = (f32[4,88,128]{2,1,0:T(8,128)S(1)}, f32[4,88,128]{2,1,0:T(8,128)S(1)}) custom-call(s32[32,128]{1,0:T(8,128)} %depth_ref.1, f32[4,80,32,128]{3,2,1,0:T(8,128)} %state_h.3, f32[4,32,1,80,80]{4,3,2,1,0:T(8,128)} %inv_h.3), custom_call_target="tpu_custom_call" | custom-call | flops 52428800 | bytes 1048576 | tf_op jit(solution)/shard_map/outer_rows/pallas_call | solution.py:233
  15.2 3.5 %collective-permute-start = (f32[4,88,128]{2,1,0:T(8,128)S(1)}, f32[4,88,128]{2,1,0:T(8,128)S(1)}, u32[]{:S(2)}, u32[]{:S(2)}) collective-permute-start(f32[4,88,128]{2,1,0:T(8,128)S(1)} %get-tuple-element.12), channel_id=1, source_target_pairs={{0,8},{8,16},{16,24},{1,9},{9,17},{17,25},{2,10},{10,18},{18,26},{... | collective-permute-start | bytes 540680 | tf_op jit(solution)/shard_map/ppermute | solution.py:547
  18.7 0.0 copy-start.2
  18.7 1.3 %collective-permute-start.1 = (f32[4,88,128]{2,1,0:T(8,128)S(1)}, f32[4,88,128]{2,1,0:T(8,128)S(1)}, u32[]{:S(2)}, u32[]{:S(2)}) collective-permute-start(f32[4,88,128]{2,1,0:T(8,128)S(1)} %get-tuple-element.10.after), channel_id=1, source_target_pairs={{8,0},{16,8},{24,16},{9,1},{17,9},{25,17},{10,2},{18,10},{26,18},{... | collective-permute-start | bytes 540680 | tf_op jit(solution)/shard_map/ppermute | solution.py:547
  20.0 10.3 %mix.1 = (f32[4,32,80,128]{3,2,1,0:T(8,128)}, f32[4,32,80,128]{3,2,1,0:T(8,128)}, f32[4,88,128]{2,1,0:T(8,128)S(1)}) custom-call(s32[32,128]{1,0:T(8,128)} %depth_ref.1, f32[4,80,32,128]{3,2,1,0:T(8,128)} %state_h.3, f32[4,32,1,80,80]{4,3,2,1,0:T(8,128)} %inv_h.3, f32[4,88,128]{2,1,0:T(8,128)S(1)} %get-tuple-element.10.after), custom_call_target="tpu_custom_call" | custom-call | flops 838860800 | bytes 16777216 | tf_op jit(solution)/shard_map/mix/pallas_call | solution.py:315
  30.3 0.0 collective-permute-done.after_north.north_h
  30.3 0.0 copy-start
  30.3 0.0 collective-permute-done.1.after_south.south_h
  30.3 0.0 copy-start.1
  30.3 0.1 all-to-all-done.recv
  30.4 1.3 %collect.1 = f32[4,144,128]{2,1,0:T(8,128)} custom-call(f32[32,72,128]{2,1,0:T(8,128)S(1)} %all-to-all-done.recv, f32[4,88,128]{2,1,0:T(8,128)S(1)} %get-tuple-element.11.after_mix, f32[4,88,128]{2,1,0:T(8,128)S(1)} %collective-permute-done.after_north.north_h, f32[4,88,128]{2,1,0:T(8,128)S(1)} %collective-permute-done.1.after_south.south_h), custom_call_target="tpu_custom_call" | custom-call | tf_op jit(solution)/shard_map/collect/pallas_call | solution.py:379
  31.7 5.9 %all-to-all-start.1 = ((f32[4,144,128]{2,1,0:T(8,128)}), f32[4,144,128]{2,1,0:T(8,128)S(1)}, u32[]{:S(2)}, u32[]{:S(2)}) async-start(f32[4,144,128]{2,1,0:T(8,128)} %collect.1), calls=%async_computation.1 | async-start | bytes 589824 | tf_op jit(solution)/shard_map/all_to_all | solution.py:570
  37.6 0.0 collective-permute-start.3
  37.6 2.6 %collective-permute-start.2 = (f32[4,88,128]{2,1,0:T(8,128)S(1)}, f32[4,88,128]{2,1,0:T(8,128)S(1)}, u32[]{:S(2)}, u32[]{:S(2)}) collective-permute-start(f32[4,88,128]{2,1,0:T(8,128)S(1)} %get-tuple-element.11.after_mix), channel_id=1, source_target_pairs={{0,7},{1,0},{2,1},{3,2},{4,3},{5,4},{6,5},{7,6},{8,15},{9,8},{10,9... | collective-permute-start | bytes 540680 | tf_op jit(solution)/shard_map/ppermute | solution.py:547
  40.2 3.2 %collective-permute-done.3.west = f32[4,88,128]{2,1,0:T(8,128)S(1)} collective-permute-done((f32[4,88,128]{2,1,0:T(8,128)S(1)}, f32[4,88,128]{2,1,0:T(8,128)S(1)}, u32[]{:S(2)}, u32[]{:S(2)}) %collective-permute-start.3) | collective-permute-done | bytes 180256 | tf_op jit(solution)/shard_map/ppermute | solution.py:547
  43.4 0.6 collective-permute-done.2.east
  44.0 3.3 %all-to-all-done.1.recv = f32[4,144,128]{2,1,0:T(8,128)S(1)} async-done(((f32[4,144,128]{2,1,0:T(8,128)}), f32[4,144,128]{2,1,0:T(8,128)S(1)}, u32[]{:S(2)}, u32[]{:S(2)}) %all-to-all-start.1) | async-done | bytes 294944 | tf_op jit(solution)/shard_map/all_to_all | solution.py:570
  47.3 0.0 copy-done
  47.3 0.0 copy-done.1
  47.3 0.0 copy-done.2
  47.3 10.3 %finish.1 = f32[4,80,32,128]{3,2,1,0:T(8,128)} custom-call(f32[4,144,128]{2,1,0:T(8,128)S(1)} %all-to-all-done.1.recv, s32[32,128]{1,0:T(8,128)S(1)} %copy-done.2, f32[4,32,80,128]{3,2,1,0:T(8,128)} %get-tuple-element.13.mixed_h, f32[4,32,80,128]{3,2,1,0:T(8,128)} %get-tuple-element.14.first_h, f32[4,88,128]{2,1,0:T(8,128)} %copy-done, ...), custom_call_target="tpu_custom_call" | custom-call | flops 26214400 | bytes 12582912 | tf_op jit(solution)/shard_map/finish/pallas_call | solution.py:517
Async XLA Ops:
  8.4 22.0 %all-to-all-start = ((f32[32,72,128]{2,1,0:T(8,128)}), f32[32,72,128]{2,1,0:T(8,128)S(1)}, u32[]{:S(2)}, u32[]{:S(2)}) async-start(f32[32,72,128]{2,1,0:T(8,128)} %regrid.1), calls=%async_computation | async-start | bytes 2359296 | tf_op jit(solution)/shard_map/all_to_all | solution.py:561
  15.2 15.1 %collective-permute-start = (f32[4,88,128]{2,1,0:T(8,128)S(1)}, f32[4,88,128]{2,1,0:T(8,128)S(1)}, u32[]{:S(2)}, u32[]{:S(2)}) collective-permute-start(f32[4,88,128]{2,1,0:T(8,128)S(1)} %get-tuple-element.12), channel_id=1, source_target_pairs={{0,8},{8,16},{16,24},{1,9},{9,17},{17,25},{2,10},{10,18},{18,26},{... | collective-permute-start | bytes 540680 | tf_op jit(solution)/shard_map/ppermute | solution.py:547
  18.7 28.6 %copy-start.2 = (s32[32,128]{1,0:T(8,128)S(1)}, s32[32,128]{1,0:T(8,128)}, u32[]{:S(2)}) copy-start(s32[32,128]{1,0:T(8,128)} %depth_ref.1) | copy-start | bytes 49156
  18.7 11.6 %collective-permute-start.1 = (f32[4,88,128]{2,1,0:T(8,128)S(1)}, f32[4,88,128]{2,1,0:T(8,128)S(1)}, u32[]{:S(2)}, u32[]{:S(2)}) collective-permute-start(f32[4,88,128]{2,1,0:T(8,128)S(1)} %get-tuple-element.10.after), channel_id=1, source_target_pairs={{8,0},{16,8},{24,16},{9,1},{17,9},{25,17},{10,2},{18,10},{26,18},{... | collective-permute-start | bytes 540680 | tf_op jit(solution)/shard_map/ppermute | solution.py:547
  30.3 17.0 %copy-start = (f32[4,88,128]{2,1,0:T(8,128)}, f32[4,88,128]{2,1,0:T(8,128)S(1)}, u32[]{:S(2)}) copy-start(f32[4,88,128]{2,1,0:T(8,128)S(1)} %collective-permute-done.after_north.north_h) | copy-start | bytes 540676
  30.3 17.0 %copy-start.1 = (f32[4,88,128]{2,1,0:T(8,128)}, f32[4,88,128]{2,1,0:T(8,128)S(1)}, u32[]{:S(2)}) copy-start(f32[4,88,128]{2,1,0:T(8,128)S(1)} %collective-permute-done.1.after_south.south_h) | copy-start | bytes 540676
  31.7 15.6 %all-to-all-start.1 = ((f32[4,144,128]{2,1,0:T(8,128)}), f32[4,144,128]{2,1,0:T(8,128)S(1)}, u32[]{:S(2)}, u32[]{:S(2)}) async-start(f32[4,144,128]{2,1,0:T(8,128)} %collect.1), calls=%async_computation.1 | async-start | bytes 589824 | tf_op jit(solution)/shard_map/all_to_all | solution.py:570
  37.6 5.8 %collective-permute-start.3 = (f32[4,88,128]{2,1,0:T(8,128)S(1)}, f32[4,88,128]{2,1,0:T(8,128)S(1)}, u32[]{:S(2)}, u32[]{:S(2)}) collective-permute-start(f32[4,88,128]{2,1,0:T(8,128)S(1)} %get-tuple-element.11.after_mix), channel_id=1, source_target_pairs={{0,1},{1,2},{2,3},{3,4},{4,5},{5,6},{6,7},{7,0},{8,9},{9,10},{10,1... | collective-permute-start | bytes 540680 | tf_op jit(solution)/shard_map/ppermute | solution.py:547
  37.6 6.4 %collective-permute-start.2 = (f32[4,88,128]{2,1,0:T(8,128)S(1)}, f32[4,88,128]{2,1,0:T(8,128)S(1)}, u32[]{:S(2)}, u32[]{:S(2)}) collective-permute-start(f32[4,88,128]{2,1,0:T(8,128)S(1)} %get-tuple-element.11.after_mix), channel_id=1, source_target_pairs={{0,7},{1,0},{2,1},{3,2},{4,3},{5,4},{6,5},{7,6},{8,15},{9,8},{10,9... | collective-permute-start | bytes 540680 | tf_op jit(solution)/shard_map/ppermute | solution.py:547

commit v9 on v8

--- a/solution.py
+++ b/solution.py
@@ -92,7 +92,11 @@
     lane_slot = (lane % per) // fields
     lane_row = (lane % fields) * oy
 
+    bits = lon.bit_length() - 1
+
     def place(d):
+        if lon == 1 << bits:
+            return (d & (lon - 1)) * lat + lax.shift_right_logical(d, bits)
         return lax.rem(d, lon) * lat + lax.div(d, lon)
 
     def part(k, carry):
@@ -405,7 +409,7 @@
         copy.start()
 
     def loads(q, c):
-        here = (q, pl.ds(pl.multiple_of(c * SUB, SUB), SUB))
+        here = (q, pl.ds(c * SUB, SUB))
         return [
             pltpu.make_async_copy(a.at[here], b.at[here], in_sems.at[k, q, c])
             for k, (a, b) in enumerate(((mixed_h, mixed), (first_h, first)))
@@ -465,43 +469,41 @@
     ends = (lanes == 0) | (lanes == LANES - 1)
 
     def field(q, carry):
+        @pl.when(q + 1 < fields)
+        def _():
+            for c in range(oy // SUB):
+                for copy in loads(q + 1, c):
+                    copy.start()
+
         z[0] = z_north[q]
         z[oy + 1] = z_south[q]
-
-        def solve(c, carry):
+        edge = halo[q]
+
+        def solve(c):
             for copy in loads(q, c):
                 copy.wait()
-
-            @pl.when(q + 1 < fields)
-            def _():
-                for copy in loads(q + 1, c):
-                    copy.start()
-
-            for i in range(SUB):
-                r = c * SUB + i
+            for r in range(c * SUB, (c + 1) * SUB):
                 forced = mixed[q, r] + first[q, r] * forcing[pl.ds(q * oy + r, 1), :]
-                z[r + 1] = jnp.where(level < depth_ref[pl.ds(r, 1), :], forced, 0.0)
-            return carry
-
-        lax.fori_loop(0, oy // SUB, solve, 0)
-
-        def diffuse(c, carry):
+                z[r + 1] = jnp.where(level < depth_ref[r : r + 1, :], forced, 0.0)
+
+        def diffuse(c):
             start = c * SUB
-            high, low = split(z[pl.ds(start + 1, SUB)].reshape(SUB * levels, LANES))
+            high, low = split(z[start + 1 : start + 1 + SUB].reshape(SUB * levels, LANES))
             sides = matmul(jnp.concatenate([high, low], axis=1), both)
-            edge = pltpu.roll(halo[q], (LANES - 2 * SUB * c) % LANES, 1)
             for i in range(SUB):
                 r = start + i
-                outside = jnp.where(ends, pltpu.roll(edge, LANES - 1 - 2 * i, 1), 0.0)
+                outside = jnp.where(ends, pltpu.roll(edge, LANES - 1 - 2 * r, 1), 0.0)
                 around = (z[r] + z[r + 2]) + (sides[i * levels : (i + 1) * levels] + outside)
-                active = level < depth_ref[pl.ds(r, 1), :]
+                active = level < depth_ref[r : r + 1, :]
                 stage[q, r] = jnp.where(active, z[r + 1] * keep[r] + diffusion_rate * around, mixed[q, r])
-            for i in range(SUB):
-                r = start + i
+            for r in range(start, start + SUB):
                 pltpu.make_async_copy(stage.at[q, r], out_h.at[q, :, r, :], out_sems.at[q]).start()
-            return carry
-
-        lax.fori_loop(0, oy // SUB, diffuse, 0)
+
+        solve(0)
+        for c in range(1, oy // SUB):
+            solve(c)
+            diffuse(c - 1)
+        diffuse(oy // SUB - 1)
         return carry
 
     lax.fori_loop(0, fields, field, 0)

time: 58.2 us -> 56.9 us (0.978)
  Pallas kernels: 31.9 us -> 30.6 us
    pallas_call x1, Pallas kernels: 10.3 us -> 9.22 us  [finish(): pl.pallas_call(finish_kernel, in_specs=[VMEM] * 2 + [HBM] * 4 + [VMEM] *...]
where the time goes in v9:
time: 56.9 us; the launch traced here: 56.4 us
  Pallas kernels  30.6 us (54%)
  starting transfers between devices  18.5 us (33%)
  waiting for transfers between devices  7.17 us (13%)
    pallas_call x1, Pallas kernels, mix(): pl.pallas_call(mix_kernel, in_specs=[HBM] * 3 + [pl.BlockSpec(memory_spac...  10.3 us
    pallas_call x1, Pallas kernels, finish(): pl.pallas_call(finish_kernel, in_specs=[VMEM] * 2 + [HBM] * 4 + [VMEM] *...  9.22 us
    pallas_call x1, Pallas kernels, regrid(): pl.pallas_call(functools.partial(regrid_kernel, cap, lat, lon, oy, batch)...  8.24 us
    ppermute x4, starting transfers between devices, shift(): return lax.ppermute(x, axis, pairs)  7.43 us
    all_to_all x1, starting transfers between devices, on_device(): lax.all_to_all(collect(cap, fields, oy, lat, in_plane, (side, *halos[0:2]...  5.87 us
    all_to_all x1, starting transfers between devices, on_device(): in_plane = lax.all_to_all(slots, 'lon', 0, 0, tiled=True)  5.18 us
    ppermute x4, waiting for transfers between devices, shift(): return lax.ppermute(x, axis, pairs)  3.75 us
    all_to_all x1, waiting for transfers between devices, on_device(): lax.all_to_all(collect(cap, fields, oy, lat, in_plane, (side, *halos[0:2]...  3.34 us
  transfers between devices with their start and end apart: 6, of which 4 were waited for; matrix products, arithmetic and copies ran while one was open for 0% of the time, Pallas kernels for 21%

profile of v9, /device:TPU:0, one launch (start us, length us, event | category | flops | bytes accessed | tf_op | source)
XLA Modules:
  0.0 56.4 jit_solution(8007006929289451565)
XLA Ops:
  0.0 8.2 %regrid.1 = f32[32,72,128]{2,1,0:T(8,128)} custom-call(s32[256]{0:T(256)} %src_h.1, s32[256]{0:T(256)} %bitcast.1, s32[256]{0:T(256)} %blk_h.1, f32[4,8]{1,0:T(4,128)} %coupling_h.1, bf16[8,64,128]{2,1,0:T(8,128)(2,1)} %atm_h.1, s32[64,128]{1,0:T(8,128)} %mask_h.1, bf16[256,128,128]{2,1,0:T(8,128)(2,1)} %weights_h.1), custom_call_target="tpu_custom_call" | custom-call | flops 67108864 | bytes 10485760 | tf_op jit(solution)/shard_map/regrid/pallas_call | solution.py:170
  8.3 5.2 %all-to-all-start = ((f32[32,72,128]{2,1,0:T(8,128)}), f32[32,72,128]{2,1,0:T(8,128)S(1)}, u32[]{:S(2)}, u32[]{:S(2)}) async-start(f32[32,72,128]{2,1,0:T(8,128)} %regrid.1), calls=%async_computation | async-start | bytes 2359296 | tf_op jit(solution)/shard_map/all_to_all | solution.py:563
  13.4 1.6 %outer_rows.1 = (f32[4,88,128]{2,1,0:T(8,128)S(1)}, f32[4,88,128]{2,1,0:T(8,128)S(1)}) custom-call(s32[32,128]{1,0:T(8,128)} %depth_ref.1, f32[4,80,32,128]{3,2,1,0:T(8,128)} %state_h.3, f32[4,32,1,80,80]{4,3,2,1,0:T(8,128)} %inv_h.3), custom_call_target="tpu_custom_call" | custom-call | flops 52428800 | bytes 1048576 | tf_op jit(solution)/shard_map/outer_rows/pallas_call | solution.py:237
  15.0 3.5 %collective-permute-start = (f32[4,88,128]{2,1,0:T(8,128)S(1)}, f32[4,88,128]{2,1,0:T(8,128)S(1)}, u32[]{:S(2)}, u32[]{:S(2)}) collective-permute-start(f32[4,88,128]{2,1,0:T(8,128)S(1)} %get-tuple-element.12), channel_id=1, source_target_pairs={{0,8},{8,16},{16,24},{1,9},{9,17},{17,25},{2,10},{10,18},{18,26},{... | collective-permute-start | bytes 540680 | tf_op jit(solution)/shard_map/ppermute | solution.py:549
  18.5 0.0 copy-start.2
  18.6 1.3 %collective-permute-start.1 = (f32[4,88,128]{2,1,0:T(8,128)S(1)}, f32[4,88,128]{2,1,0:T(8,128)S(1)}, u32[]{:S(2)}, u32[]{:S(2)}) collective-permute-start(f32[4,88,128]{2,1,0:T(8,128)S(1)} %get-tuple-element.10.after), channel_id=1, source_target_pairs={{8,0},{16,8},{24,16},{9,1},{17,9},{25,17},{10,2},{18,10},{26,18},{... | collective-permute-start | bytes 540680 | tf_op jit(solution)/shard_map/ppermute | solution.py:549
  19.9 10.3 %mix.1 = (f32[4,32,80,128]{3,2,1,0:T(8,128)}, f32[4,32,80,128]{3,2,1,0:T(8,128)}, f32[4,88,128]{2,1,0:T(8,128)S(1)}) custom-call(s32[32,128]{1,0:T(8,128)} %depth_ref.1, f32[4,80,32,128]{3,2,1,0:T(8,128)} %state_h.3, f32[4,32,1,80,80]{4,3,2,1,0:T(8,128)} %inv_h.3, f32[4,88,128]{2,1,0:T(8,128)S(1)} %get-tuple-element.10.after), custom_call_target="tpu_custom_call" | custom-call | flops 838860800 | bytes 16777216 | tf_op jit(solution)/shard_map/mix/pallas_call | solution.py:319
  30.1 0.0 collective-permute-done.after_north.north_h
  30.1 0.0 copy-start
  30.1 0.0 collective-permute-done.1.after_south.south_h
  30.2 0.0 copy-start.1
  30.2 0.1 all-to-all-done.recv
  30.2 1.3 %collect.1 = f32[4,144,128]{2,1,0:T(8,128)} custom-call(f32[32,72,128]{2,1,0:T(8,128)S(1)} %all-to-all-done.recv, f32[4,88,128]{2,1,0:T(8,128)S(1)} %get-tuple-element.11.after_mix, f32[4,88,128]{2,1,0:T(8,128)S(1)} %collective-permute-done.after_north.north_h, f32[4,88,128]{2,1,0:T(8,128)S(1)} %collective-permute-done.1.after_south.south_h), custom_call_target="tpu_custom_call" | custom-call | tf_op jit(solution)/shard_map/collect/pallas_call | solution.py:383
  31.6 5.9 %all-to-all-start.1 = ((f32[4,144,128]{2,1,0:T(8,128)}), f32[4,144,128]{2,1,0:T(8,128)S(1)}, u32[]{:S(2)}, u32[]{:S(2)}) async-start(f32[4,144,128]{2,1,0:T(8,128)} %collect.1), calls=%async_computation.1 | async-start | bytes 589824 | tf_op jit(solution)/shard_map/all_to_all | solution.py:572
  37.4 0.0 collective-permute-start.3
  37.4 2.6 %collective-permute-start.2 = (f32[4,88,128]{2,1,0:T(8,128)S(1)}, f32[4,88,128]{2,1,0:T(8,128)S(1)}, u32[]{:S(2)}, u32[]{:S(2)}) collective-permute-start(f32[4,88,128]{2,1,0:T(8,128)S(1)} %get-tuple-element.11.after_mix), channel_id=1, source_target_pairs={{0,7},{1,0},{2,1},{3,2},{4,3},{5,4},{6,5},{7,6},{8,15},{9,8},{10,9... | collective-permute-start | bytes 540680 | tf_op jit(solution)/shard_map/ppermute | solution.py:549
  40.1 3.2 %collective-permute-done.3.west = f32[4,88,128]{2,1,0:T(8,128)S(1)} collective-permute-done((f32[4,88,128]{2,1,0:T(8,128)S(1)}, f32[4,88,128]{2,1,0:T(8,128)S(1)}, u32[]{:S(2)}, u32[]{:S(2)}) %collective-permute-start.3) | collective-permute-done | bytes 180256 | tf_op jit(solution)/shard_map/ppermute | solution.py:549
  43.2 0.6 %collective-permute-done.2.east = f32[4,88,128]{2,1,0:T(8,128)S(1)} collective-permute-done((f32[4,88,128]{2,1,0:T(8,128)S(1)}, f32[4,88,128]{2,1,0:T(8,128)S(1)}, u32[]{:S(2)}, u32[]{:S(2)}) %collective-permute-start.2) | collective-permute-done | bytes 180256 | tf_op jit(solution)/shard_map/ppermute | solution.py:549
  43.8 3.3 %all-to-all-done.1.recv = f32[4,144,128]{2,1,0:T(8,128)S(1)} async-done(((f32[4,144,128]{2,1,0:T(8,128)}), f32[4,144,128]{2,1,0:T(8,128)S(1)}, u32[]{:S(2)}, u32[]{:S(2)}) %all-to-all-start.1) | async-done | bytes 294944 | tf_op jit(solution)/shard_map/all_to_all | solution.py:572
  47.2 0.0 copy-done
  47.2 0.0 copy-done.1
  47.2 0.0 copy-done.2
  47.2 9.2 %finish.1 = f32[4,80,32,128]{3,2,1,0:T(8,128)} custom-call(f32[4,144,128]{2,1,0:T(8,128)S(1)} %all-to-all-done.1.recv, s32[32,128]{1,0:T(8,128)S(1)} %copy-done.2, f32[4,32,80,128]{3,2,1,0:T(8,128)} %get-tuple-element.13.mixed_h, f32[4,32,80,128]{3,2,1,0:T(8,128)} %get-tuple-element.14.first_h, f32[4,88,128]{2,1,0:T(8,128)} %copy-done, ...), custom_call_target="tpu_custom_call" | custom-call | flops 26214400 | bytes 12582912 | tf_op jit(solution)/shard_map/finish/pallas_call | solution.py:519
Async XLA Ops:
  8.3 22.0 %all-to-all-start = ((f32[32,72,128]{2,1,0:T(8,128)}), f32[32,72,128]{2,1,0:T(8,128)S(1)}, u32[]{:S(2)}, u32[]{:S(2)}) async-start(f32[32,72,128]{2,1,0:T(8,128)} %regrid.1), calls=%async_computation | async-start | bytes 2359296 | tf_op jit(solution)/shard_map/all_to_all | solution.py:563
  15.0 15.1 %collective-permute-start = (f32[4,88,128]{2,1,0:T(8,128)S(1)}, f32[4,88,128]{2,1,0:T(8,128)S(1)}, u32[]{:S(2)}, u32[]{:S(2)}) collective-permute-start(f32[4,88,128]{2,1,0:T(8,128)S(1)} %get-tuple-element.12), channel_id=1, source_target_pairs={{0,8},{8,16},{16,24},{1,9},{9,17},{17,25},{2,10},{10,18},{18,26},{... | collective-permute-start | bytes 540680 | tf_op jit(solution)/shard_map/ppermute | solution.py:549
  18.5 28.6 %copy-start.2 = (s32[32,128]{1,0:T(8,128)S(1)}, s32[32,128]{1,0:T(8,128)}, u32[]{:S(2)}) copy-start(s32[32,128]{1,0:T(8,128)} %depth_ref.1) | copy-start | bytes 49156
  18.6 11.6 %collective-permute-start.1 = (f32[4,88,128]{2,1,0:T(8,128)S(1)}, f32[4,88,128]{2,1,0:T(8,128)S(1)}, u32[]{:S(2)}, u32[]{:S(2)}) collective-permute-start(f32[4,88,128]{2,1,0:T(8,128)S(1)} %get-tuple-element.10.after), channel_id=1, source_target_pairs={{8,0},{16,8},{24,16},{9,1},{17,9},{25,17},{10,2},{18,10},{26,18},{... | collective-permute-start | bytes 540680 | tf_op jit(solution)/shard_map/ppermute | solution.py:549
  30.1 17.0 %copy-start = (f32[4,88,128]{2,1,0:T(8,128)}, f32[4,88,128]{2,1,0:T(8,128)S(1)}, u32[]{:S(2)}) copy-start(f32[4,88,128]{2,1,0:T(8,128)S(1)} %collective-permute-done.after_north.north_h) | copy-start | bytes 540676
  30.2 17.0 %copy-start.1 = (f32[4,88,128]{2,1,0:T(8,128)}, f32[4,88,128]{2,1,0:T(8,128)S(1)}, u32[]{:S(2)}) copy-start(f32[4,88,128]{2,1,0:T(8,128)S(1)} %collective-permute-done.1.after_south.south_h) | copy-start | bytes 540676
  31.6 15.6 %all-to-all-start.1 = ((f32[4,144,128]{2,1,0:T(8,128)}), f32[4,144,128]{2,1,0:T(8,128)S(1)}, u32[]{:S(2)}, u32[]{:S(2)}) async-start(f32[4,144,128]{2,1,0:T(8,128)} %collect.1), calls=%async_computation.1 | async-start | bytes 589824 | tf_op jit(solution)/shard_map/all_to_all | solution.py:572
  37.4 5.8 %collective-permute-start.3 = (f32[4,88,128]{2,1,0:T(8,128)S(1)}, f32[4,88,128]{2,1,0:T(8,128)S(1)}, u32[]{:S(2)}, u32[]{:S(2)}) collective-permute-start(f32[4,88,128]{2,1,0:T(8,128)S(1)} %get-tuple-element.11.after_mix), channel_id=1, source_target_pairs={{0,1},{1,2},{2,3},{3,4},{4,5},{5,6},{6,7},{7,0},{8,9},{9,10},{10,1... | collective-permute-start | bytes 540680 | tf_op jit(solution)/shard_map/ppermute | solution.py:549
  37.4 6.4 %collective-permute-start.2 = (f32[4,88,128]{2,1,0:T(8,128)S(1)}, f32[4,88,128]{2,1,0:T(8,128)S(1)}, u32[]{:S(2)}, u32[]{:S(2)}) collective-permute-start(f32[4,88,128]{2,1,0:T(8,128)S(1)} %get-tuple-element.11.after_mix), channel_id=1, source_target_pairs={{0,7},{1,0},{2,1},{3,2},{4,3},{5,4},{6,5},{7,6},{8,15},{9,8},{10,9... | collective-permute-start | bytes 540680 | tf_op jit(solution)/shard_map/ppermute | solution.py:549

commit v10 on v9

--- a/solution.py
+++ b/solution.py
@@ -38,9 +38,39 @@
     return x if x.shape[0] == rows else jnp.concatenate([x, jnp.zeros((rows - x.shape[0], LANES), x.dtype)], axis=0)
 
 
+def solve_row(a, x, active):
+    levels = x.shape[0]
+    a_high, a_low = split(a)
+    r_high, r_low = split(jnp.where(active, x, 0.0))
+    product = matmul(jnp.concatenate([a_high, a_low], axis=0), jnp.concatenate([r_high, r_low], axis=1))
+    solved = product[:levels, :LANES] + (product[levels:, :LANES] + product[:levels, LANES:])
+    return jnp.where(active, solved, x)
+
+
+def outer_messages(refs, depth_ref, state, inv):
+    _, fields, levels, _ = state.shape
+    oy = depth_ref.shape[0]
+    level = iota((levels, LANES), 0)
+    for k, (row, ref) in enumerate(zip((0, oy - 1), refs)):
+        depth = depth_ref[row : row + 1, :]
+        names = jnp.zeros((levels, LANES), f32)
+        for q in range(fields):
+            a = inv[k, q]
+            ref[q, 0:levels] = solve_row(a, state[k, q], level < depth)
+            names = jnp.where(iota((levels, LANES), 1) == q, a[:, 0:1], names)
+        names = padded_rows(names, LANES).T
+        for q in range(fields):
+            ref[q, levels : levels + SUB] = jnp.concatenate(
+                [depth.astype(f32), names[q : q + 1], jnp.zeros((SUB - 2, LANES), f32)], axis=0
+            )
+
+
 def regrid_kernel(
-    cap, lat, lon, oy, batch, src_h, dev_h, blk_h, coupling_h, atm_h, mask_h, weights_h,
-    out_h, out, rows, ids, count, src, dev, blk, coupling, atm, mask, weights, small_sem, big_sem, out_sem,
+    cap, lat, lon, oy, batch,
+    src_h, dev_h, blk_h, coupling_h, atm_h, mask_h, weights_h, depth_h, state_h, inv_h,
+    out_h, north, south,
+    out, rows, ids, count, src, dev, blk, coupling, atm, mask, weights, depth_ref, state, inv,
+    small_sem, outer_sem, big_sem, out_sem,
 ):
     fluxes, atm_rows, _ = atm.shape
     fields = coupling.shape[0]
@@ -62,7 +92,12 @@
             )
         )
     ]
-    for copy in small:
+    outer = [pltpu.make_async_copy(depth_h, depth_ref, outer_sem.at[2 * fields, 0])]
+    for q in range(fields):
+        for k, row in enumerate((0, oy - 1)):
+            outer.append(pltpu.make_async_copy(state_h.at[q, :, row, :], state.at[k, q], outer_sem.at[2 * q, k]))
+            outer.append(pltpu.make_async_copy(inv_h.at[q, row, 0], inv.at[k, q], outer_sem.at[2 * q + 1, k]))
+    for copy in small + outer:
         copy.start()
     for k in range(ahead):
         big(k).start()
@@ -87,6 +122,10 @@
             high = total.astype(bf16).astype(f32)
             rows[pl.ds(tile * 16 * SUB + q, 16, stride=SUB), :] = high
             rows[pl.ds(tile * 16 * SUB + fields + q, 16, stride=SUB), :] = total - high
+
+    for copy in outer:
+        copy.wait()
+    outer_messages((north, south), depth_ref, state, inv)
 
     lane = iota((1, LANES), 1)
     lane_slot = (lane % per) // fields
@@ -161,17 +200,18 @@
     send(1, per, per + SUB).wait()
 
 
-def regrid(cap, lat, lon, oy, src, dev, blk, coupling, atm, mask, weights):
-    pairs, depth, width = weights.shape
-    fields = coupling.shape[0]
+def regrid(cap, lat, lon, src, dev, blk, coupling, atm, mask, weights, depth, ocean, inverses):
+    pairs, cells, width = weights.shape
+    fields, levels, oy, ox = ocean.shape
+    message = jax.ShapeDtypeStruct((fields, levels + SUB, ox), f32)
     batch = 32
     devices = lat * lon
     tall = fields * cap + SUB
     return pl.pallas_call(
         functools.partial(regrid_kernel, cap, lat, lon, oy, batch),
-        in_specs=[HBM] * 7,
-        out_specs=HBM,
-        out_shape=pltpu.HBM((devices, tall, LANES), f32),
+        in_specs=[HBM] * 10,
+        out_specs=[HBM, VMEM, VMEM],
+        out_shape=[pltpu.HBM((devices, tall, LANES), f32), message, message],
         scratch_shapes=[
             pltpu.VMEM((devices, tall, LANES), f32),
             pltpu.VMEM((atm.shape[1] * SUB, LANES), f32),
@@ -184,76 +224,23 @@
             pltpu.VMEM(atm.shape, bf16),
             pltpu.VMEM(mask.shape, jnp.int32),
             pltpu.VMEM(weights.shape, bf16),
+            pltpu.VMEM(depth.shape, jnp.int32),
+            pltpu.VMEM((2, fields, levels, ox), f32),
+            pltpu.VMEM((2, fields, levels, levels), f32),
             pltpu.SemaphoreType.DMA((6,)),
+            pltpu.SemaphoreType.DMA((2 * fields + 1, 2)),
             pltpu.SemaphoreType.DMA((pairs // batch,)),
             pltpu.SemaphoreType.DMA((2,)),
         ],
         compiler_params=pltpu.CompilerParams(vmem_limit_bytes=20 << 20),
-        cost_estimate=pl.CostEstimate(flops=2 * 8 * pairs * depth * width, bytes_accessed=10 << 20, transcendentals=0),
+        cost_estimate=pl.CostEstimate(flops=2 * 8 * pairs * cells * width, bytes_accessed=10 << 20, transcendentals=0),
         name="regrid",
-    )(*in_hbm(src, dev, blk, coupling, atm, mask, weights))
-
-
-def solve_row(a, x, active):
-    levels = x.shape[0]
-    a_high, a_low = split(a)
-    r_high, r_low = split(jnp.where(active, x, 0.0))
-    product = matmul(jnp.concatenate([a_high, a_low], axis=0), jnp.concatenate([r_high, r_low], axis=1))
-    solved = product[:levels, :LANES] + (product[levels:, :LANES] + product[:levels, LANES:])
-    return jnp.where(active, solved, x)
-
-
-def outer_rows_kernel(depth_h, state_h, inv_h, north, south, depth_ref, state, inv, sems):
-    _, fields, levels, _ = state.shape
-    oy = depth_ref.shape[0]
-    ends = (0, oy - 1)
-    copies = [pltpu.make_async_copy(depth_h, depth_ref, sems.at[2 * fields, 0])]
-    for q in range(fields):
-        for k, row in enumerate(ends):
-            copies.append(pltpu.make_async_copy(state_h.at[q, :, row, :], state.at[k, q], sems.at[2 * q, k]))
-            copies.append(pltpu.make_async_copy(inv_h.at[q, row, 0], inv.at[k, q], sems.at[2 * q + 1, k]))
-    for copy in copies:
-        copy.start()
-    level = iota((levels, LANES), 0)
-    for copy in copies:
-        copy.wait()
-    for k, (row, ref) in enumerate(zip(ends, (north, south))):
-        depth = depth_ref[row : row + 1, :]
-        names = jnp.zeros((levels, LANES), f32)
-        for q in range(fields):
-            a = inv[k, q]
-            ref[q, 0:levels] = solve_row(a, state[k, q], level < depth)
-            names = jnp.where(iota((levels, LANES), 1) == q, a[:, 0:1], names)
-        names = padded_rows(names, LANES).T
-        for q in range(fields):
-            ref[q, levels : levels + SUB] = jnp.concatenate(
-                [depth.astype(f32), names[q : q + 1], jnp.zeros((SUB - 2, LANES), f32)], axis=0
-            )
-
-
-def outer_rows(depth, state, inverses):
-    fields, levels, _, ox = state.shape
-    edge_shape = jax.ShapeDtypeStruct((fields, levels + SUB, ox), f32)
-    return pl.pallas_call(
-        outer_rows_kernel,
-        in_specs=[HBM] * 3,
-        out_specs=[VMEM] * 2,
-        out_shape=[edge_shape, edge_shape],
-        scratch_shapes=[
-            pltpu.VMEM(depth.shape, jnp.int32),
-            pltpu.VMEM((2, fields, levels, ox), f32),
-            pltpu.VMEM((2, fields, levels, levels), f32),
-            pltpu.SemaphoreType.DMA((2 * fields + 1, 2)),
-        ],
-        compiler_params=pltpu.CompilerParams(vmem_limit_bytes=8 << 20),
-        cost_estimate=pl.CostEstimate(flops=16 * fields * levels * levels * ox, bytes_accessed=1 << 20, transcendentals=0),
-        name="outer_rows",
-    )(*in_hbm(depth, state, inverses))
+    )(*in_hbm(src, dev, blk, coupling, atm, mask, weights, depth, ocean, inverses))
 
 
 def mix_kernel(
-    depth_h, state_h, inv_h, after, mixed_h, first_h, side,
-    depth_ref, state, mixed, inv, first, in_sems, out_sems,
+    depth_h, state_h, inv_h, mixed_h, first_h, to_east, to_west,
+    depth_ref, state, mixed, inv, first, side, in_sems, out_sems,
 ):
     fields, oy, levels, _ = mixed.shape
     depth_copy = pltpu.make_async_copy(depth_h, depth_ref, in_sems.at[2 * fields, 0])
@@ -278,62 +265,63 @@
         edge_depth = jnp.where(line // 2 == i, turned, edge_depth)
 
     def field(q, carry):
-        def chunk(c, edges):
-            here = (q, pl.ds(pl.multiple_of(c * SUB, SUB), SUB))
+        @pl.when(q + 1 < fields)
+        def _():
+            for c in range(oy // SUB):
+                load(q + 1, c)
+
+        cells = jnp.zeros((levels, LANES), f32)
+        for c in range(oy // SUB):
+            here = (q, pl.ds(c * SUB, SUB))
             pltpu.make_async_copy(mixed_h.at[here], state.at[here], in_sems.at[2 * q, c]).wait()
             pltpu.make_async_copy(inv_h.at[here], inv.at[here], in_sems.at[2 * q + 1, c]).wait()
-
-            @pl.when(q + 1 < fields)
-            def _():
-                load(q + 1, c)
-
-            cells = jnp.zeros((levels, LANES), f32)
-            names = jnp.zeros((levels, LANES), f32)
-            for i in range(SUB):
-                row = c * SUB + i
+            for row in range(c * SUB, (c + 1) * SUB):
                 a = inv[q, row, 0]
-                m = solve_row(a, state[q, row], level < depth_ref[pl.ds(row, 1), :])
+                m = solve_row(a, state[q, row], level < depth_ref[row : row + 1, :])
                 mixed[q, row] = m
                 column = jnp.broadcast_to(a[:, 0:1], (levels, LANES))
                 first[q, row] = column
-                cells = jnp.where(lane // 2 == i, pltpu.roll(m, 2 * i + 1, 1), cells)
-                names = jnp.where(lane // 2 == HALF // 2 + i, column, names)
+                cells = jnp.where(lane // 2 == row, pltpu.roll(m, 2 * row + 1, 1), cells)
+                cells = jnp.where(lane // 2 == HALF // 2 + row, column, cells)
             pltpu.make_async_copy(mixed.at[here], mixed_h.at[here], out_sems.at[2 * q]).start()
             pltpu.make_async_copy(first.at[here], first_h.at[here], out_sems.at[2 * q + 1]).start()
-            return edges + pltpu.roll(cells + names, 2 * SUB * c, 1)
-
-        side[q, 0:levels] = lax.fori_loop(0, oy // SUB, chunk, jnp.zeros((levels, LANES), f32))
+        side[q, 0:levels] = cells
         side[q, levels : levels + SUB] = edge_depth
         return carry
 
     lax.fori_loop(0, fields, field, 0)
+    even = line % 2 == 0
+    for k in range(fields // 2):
+        to_east[k] = jnp.where(even, side[2 * k], pltpu.roll(side[2 * k + 1], 1, 1))
+        to_west[k] = jnp.where(even, pltpu.roll(side[2 * k], LANES - 1, 1), side[2 * k + 1])
     for q in range(fields):
         pltpu.make_async_copy(mixed.at[q], mixed_h.at[q], out_sems.at[2 * q]).wait()
         pltpu.make_async_copy(first.at[q], first_h.at[q], out_sems.at[2 * q + 1]).wait()
 
 
-def mix(depth, state, inverses, after):
+def mix(depth, state, inverses):
     fields, levels, oy, ox = state.shape
-    edge_shape = jax.ShapeDtypeStruct((fields, levels + SUB, ox), f32)
+    edge_shape = jax.ShapeDtypeStruct((fields // 2, levels + SUB, ox), f32)
     full = (fields, oy, levels, ox)
     return pl.pallas_call(
         mix_kernel,
-        in_specs=[HBM] * 3 + [pl.BlockSpec(memory_space=pl.ANY)],
-        out_specs=[HBM] * 2 + [VMEM],
-        out_shape=[pltpu.HBM(full, f32), pltpu.HBM(full, f32), edge_shape],
+        in_specs=[HBM] * 3,
+        out_specs=[HBM] * 2 + [VMEM] * 2,
+        out_shape=[pltpu.HBM(full, f32), pltpu.HBM(full, f32), edge_shape, edge_shape],
         scratch_shapes=[
             pltpu.VMEM(depth.shape, jnp.int32),
             pltpu.VMEM(full, f32),
             pltpu.VMEM(full, f32),
             pltpu.VMEM(inverses.shape, f32),
             pltpu.VMEM(full, f32),
+            pltpu.VMEM((fields, levels + SUB, ox), f32),
             pltpu.SemaphoreType.DMA((2 * fields + 1, oy // SUB)),
             pltpu.SemaphoreType.DMA((2 * fields,)),
         ],
         compiler_params=pltpu.CompilerParams(vmem_limit_bytes=32 << 20),
         cost_estimate=pl.CostEstimate(flops=2 * 4 * fields * oy * levels * levels * ox, bytes_accessed=16 << 20, transcendentals=0),
         name="mix",
-    )(*in_hbm(depth, state, inverses), after)
+    )(*in_hbm(depth, state, inverses))
 
 
 def collect_kernel(cap, fields, oy, recv, after_mix, after_north, after_south, out):
@@ -432,12 +420,12 @@
     depth = depth_ref[...]
     wide = iota((oy, LANES), 1)
 
-    def upright(ref, place):
-        value = jnp.where(wide == 2 * iota((oy, LANES), 0) + place, ref[0, levels : levels + 1, :], 0.0)
+    def upright(ref):
+        value = jnp.where(wide == 2 * iota((oy, LANES), 0), ref[0, levels : levels + 1, :], 0.0)
         return jnp.sum(value, axis=1, keepdims=True).astype(jnp.int32)
 
-    to_east = jnp.where(wide == LANES - 1, upright(east, 1), pltpu.roll(depth, LANES - 1, 1))
-    to_west = jnp.where(wide == 0, upright(west, 0), pltpu.roll(depth, 1, 1))
+    to_east = jnp.where(wide == LANES - 1, upright(east), pltpu.roll(depth, LANES - 1, 1))
+    to_west = jnp.where(wide == 0, upright(west), pltpu.roll(depth, 1, 1))
     to_north = jnp.concatenate([north[0, levels : levels + 1, :].astype(jnp.int32), depth[: oy - 1]], axis=0)
     to_south = jnp.concatenate([depth[1:], south[0, levels : levels + 1, :].astype(jnp.int32)], axis=0)
     for i in range(oy):
@@ -458,8 +446,11 @@
     outer(z_north, north, 0)
     outer(z_south, south, fields)
     for q in range(fields):
-        cells = jnp.where(even, pltpu.roll(east[q], LANES - 1, 1), pltpu.roll(west[q], 1, 1))
-        names = pltpu.roll(jnp.where(even, east[q], west[q]), HALF, 1)
+        if q % 2:
+            cells = jnp.where(even, pltpu.roll(east[q // 2], LANES - 1, 1), west[q // 2])
+        else:
+            cells = jnp.where(even, east[q // 2], pltpu.roll(west[q // 2], 1, 1))
+        names = pltpu.roll(cells, HALF, 1)
         active = level < cells[levels : levels + 1].astype(jnp.int32)
         value = cells[0:levels] + names[0:levels] * columns[q : q + 1]
         halo[q] = jnp.where(active & (line < 2 * oy), value, 0.0)
@@ -556,20 +547,19 @@
     lat, lon = lax.axis_size("lat"), lax.axis_size("lon")
     fields, _, oy, _ = ocean_state.shape
     cap = max(SUB, 2 * src_block.shape[0] // (lat * lon))
-    slots = regrid(
-        cap, lat, lon, oy, src_block, dest_dev[:, 0], dest_block, coupling, atm_flux, sea_mask,
-        intersection_weights,
+    slots, north, south = regrid(
+        cap, lat, lon, src_block, dest_dev[:, 0], dest_block, coupling, atm_flux, sea_mask,
+        intersection_weights, depth_levels, ocean_state, inverses,
     )
     in_plane = lax.all_to_all(slots, "lon", 0, 0, tiled=True)
-    north, south = outer_rows(depth_levels, ocean_state, inverses)
-    mixed, first, side = mix(depth_levels, ocean_state, inverses, north)
+    mixed, first, to_east, to_west = mix(depth_levels, ocean_state, inverses)
     halos = (
         shift(south, "lat", 1, False),
         shift(north, "lat", -1, False),
-        shift(side, "lon", -1, True),
-        shift(side, "lon", 1, True),
+        shift(to_west, "lon", -1, True),
+        shift(to_east, "lon", 1, True),
     )
-    received = lax.all_to_all(collect(cap, fields, oy, lat, in_plane, (side, *halos[0:2])), "lat", 0, 0, tiled=True)
+    received = lax.all_to_all(collect(cap, fields, oy, lat, in_plane, (to_east, *halos[0:2])), "lat", 0, 0, tiled=True)
     return finish(received, depth_levels, mixed, first, halos)
 
 

time: 56.9 us -> 55.4 us (0.974)
  waiting for transfers between devices: 7.17 us -> 10.4 us
  starting transfers between devices: 18.5 us -> 15.3 us
  Pallas kernels: 30.6 us -> 29.1 us
    all_to_all x1, waiting for transfers between devices: 0.08 us -> 2.56 us  [on_device(): in_plane = lax.all_to_all(slots, 'lon', 0, 0, tiled=True)]
    pallas_call x2 -> x1, Pallas kernels: 11.9 us -> 9.41 us  [mix(): pl.pallas_call(mix_kernel, in_specs=[HBM] * 3, out_specs=[HBM] * 2 + [VME...]
    ppermute x4, starting transfers between devices: 7.43 us -> 5.28 us  [shift(): return lax.ppermute(x, axis, pairs)]
    all_to_all x1, starting transfers between devices: 5.87 us -> 4.87 us  [on_device(): lax.all_to_all(collect(cap, fields, oy, lat, in_plane, (to_east, *halos[0...]
    ppermute x4, waiting for transfers between devices: 3.75 us -> 4.71 us  [shift(): return lax.ppermute(x, axis, pairs)]
    pallas_call x1, Pallas kernels: 8.24 us -> 9.13 us  [regrid(): pl.pallas_call(functools.partial(regrid_kernel, cap, lat, lon, oy, batch)...]
  transfers between devices with their start and end apart: 6 -> 6, of which waited for: 4 -> 4; matrix products, arithmetic and copies ran while one was open for 0% -> 0% of each run, Pallas kernels for 21% -> 17%
where the time goes in v10:
time: 55.4 us; the launch traced here: 54.9 us
  Pallas kernels  29.1 us (53%)
  starting transfers between devices  15.3 us (28%)
  waiting for transfers between devices  10.4 us (19%)
    pallas_call x1, Pallas kernels, mix(): pl.pallas_call(mix_kernel, in_specs=[HBM] * 3, out_specs=[HBM] * 2 + [VME...  9.41 us
    pallas_call x1, Pallas kernels, finish(): pl.pallas_call(finish_kernel, in_specs=[VMEM] * 2 + [HBM] * 4 + [VMEM] *...  9.22 us
    pallas_call x1, Pallas kernels, regrid(): pl.pallas_call(functools.partial(regrid_kernel, cap, lat, lon, oy, batch)...  9.13 us
    ppermute x4, starting transfers between devices, shift(): return lax.ppermute(x, axis, pairs)  5.28 us
    all_to_all x1, starting transfers between devices, on_device(): in_plane = lax.all_to_all(slots, 'lon', 0, 0, tiled=True)  5.19 us
    all_to_all x1, starting transfers between devices, on_device(): lax.all_to_all(collect(cap, fields, oy, lat, in_plane, (to_east, *halos[0...  4.87 us
    ppermute x4, waiting for transfers between devices, shift(): return lax.ppermute(x, axis, pairs)  4.71 us
    all_to_all x1, waiting for transfers between devices, on_device(): lax.all_to_all(collect(cap, fields, oy, lat, in_plane, (to_east, *halos[0...  3.1 us
  transfers between devices with their start and end apart: 6, of which 4 were waited for; matrix products, arithmetic and copies ran while one was open for 0% of the time, Pallas kernels for 17%

profile of v10, /device:TPU:0, one launch (start us, length us, event | category | flops | bytes accessed | tf_op | source)
XLA Modules:
  0.0 54.9 jit_solution(5512302214015730028)
XLA Ops:
  0.0 9.1 %regrid.1 = (f32[32,72,128]{2,1,0:T(8,128)}, f32[4,88,128]{2,1,0:T(8,128)S(1)}, f32[4,88,128]{2,1,0:T(8,128)S(1)}) custom-call(s32[256]{0:T(256)} %src_h.1, s32[256]{0:T(256)} %bitcast.1, s32[256]{0:T(256)} %blk_h.1, f32[4,8]{1,0:T(4,128)} %coupling_h.1, bf16[8,64,128]{2,1,0:T(8,128)(2,1)} %atm_h.1, s32[64,128]{1,0:T(8,128)} %mask_h.1, ...), custom_call_target="tpu_custom_call" | custom-call | flops 67108864 | bytes 10485760 | tf_op jit(solution)/shard_map/regrid/pallas_call | solution.py:210
  9.1 5.2 %all-to-all-start = ((f32[32,72,128]{2,1,0:T(8,128)}), f32[32,72,128]{2,1,0:T(8,128)S(1)}, u32[]{:S(2)}, u32[]{:S(2)}) async-start(f32[32,72,128]{2,1,0:T(8,128)} %get-tuple-element.12), calls=%async_computation | async-start | bytes 2359296 | tf_op jit(solution)/shard_map/all_to_all | solution.py:554
  14.3 3.5 %collective-permute-start = (f32[4,88,128]{2,1,0:T(8,128)S(1)}, f32[4,88,128]{2,1,0:T(8,128)S(1)}, u32[]{:S(2)}, u32[]{:S(2)}) collective-permute-start(f32[4,88,128]{2,1,0:T(8,128)S(1)} %get-tuple-element.14), channel_id=1, source_target_pairs={{0,8},{8,16},{16,24},{1,9},{9,17},{17,25},{2,10},{10,18},{18,26},{... | collective-permute-start | bytes 540680 | tf_op jit(solution)/shard_map/ppermute | solution.py:540
  17.8 0.0 copy-start.2
  17.8 1.3 %collective-permute-start.1 = (f32[4,88,128]{2,1,0:T(8,128)S(1)}, f32[4,88,128]{2,1,0:T(8,128)S(1)}, u32[]{:S(2)}, u32[]{:S(2)}) collective-permute-start(f32[4,88,128]{2,1,0:T(8,128)S(1)} %get-tuple-element.15), channel_id=1, source_target_pairs={{8,0},{16,8},{24,16},{9,1},{17,9},{25,17},{10,2},{18,10},{26,18},{... | collective-permute-start | bytes 540680 | tf_op jit(solution)/shard_map/ppermute | solution.py:540
  19.1 9.4 %mix.1 = (f32[4,32,80,128]{3,2,1,0:T(8,128)}, f32[4,32,80,128]{3,2,1,0:T(8,128)}, f32[2,88,128]{2,1,0:T(8,128)S(1)}, f32[2,88,128]{2,1,0:T(8,128)S(1)}) custom-call(s32[32,128]{1,0:T(8,128)} %depth_ref.1, f32[4,80,32,128]{3,2,1,0:T(8,128)} %state_h.3, f32[4,32,1,80,80]{4,3,2,1,0:T(8,128)} %inv_h.3), custom_call_target="tpu_custom_call" | custom-call | flops 838860800 | bytes 16777216 | tf_op jit(solution)/shard_map/mix/pallas_call | solution.py:306
  28.5 0.0 collective-permute-done.after_north.north_h
  28.5 0.0 copy-start
  28.6 0.0 collective-permute-done.1.after_south.south_h
  28.6 0.0 copy-start.1
  28.6 2.6 %all-to-all-done.recv = f32[32,72,128]{2,1,0:T(8,128)S(1)} async-done(((f32[32,72,128]{2,1,0:T(8,128)}), f32[32,72,128]{2,1,0:T(8,128)S(1)}, u32[]{:S(2)}, u32[]{:S(2)}) %all-to-all-start) | async-done | bytes 1179680 | tf_op jit(solution)/shard_map/all_to_all | solution.py:554
  31.1 1.3 %collect.1 = f32[4,144,128]{2,1,0:T(8,128)} custom-call(f32[32,72,128]{2,1,0:T(8,128)S(1)} %all-to-all-done.recv, f32[2,88,128]{2,1,0:T(8,128)S(1)} %get-tuple-element.13.after_mix, f32[4,88,128]{2,1,0:T(8,128)S(1)} %collective-permute-done.after_north.north_h, f32[4,88,128]{2,1,0:T(8,128)S(1)} %collective-permute-done.1.after_south.south_h), custom_call_target="tpu_custom_call" | custom-call | tf_op jit(solution)/shard_map/collect/pallas_call | solution.py:371
  32.4 4.9 %all-to-all-start.1 = ((f32[4,144,128]{2,1,0:T(8,128)}), f32[4,144,128]{2,1,0:T(8,128)S(1)}, u32[]{:S(2)}, u32[]{:S(2)}) async-start(f32[4,144,128]{2,1,0:T(8,128)} %collect.1), calls=%async_computation.1 | async-start | bytes 589824 | tf_op jit(solution)/shard_map/all_to_all | solution.py:562
  37.3 0.4 collective-permute-start.2
  37.7 0.2 collective-permute-start.3
  37.8 2.5 %collective-permute-done.2.east = f32[2,88,128]{2,1,0:T(8,128)S(1)} collective-permute-done((f32[2,88,128]{2,1,0:T(8,128)S(1)}, f32[2,88,128]{2,1,0:T(8,128)S(1)}, u32[]{:S(2)}, u32[]{:S(2)}) %collective-permute-start.2) | collective-permute-done | bytes 90144 | tf_op jit(solution)/shard_map/ppermute | solution.py:540
  40.3 2.2 %collective-permute-done.3.west = f32[2,88,128]{2,1,0:T(8,128)S(1)} collective-permute-done((f32[2,88,128]{2,1,0:T(8,128)S(1)}, f32[2,88,128]{2,1,0:T(8,128)S(1)}, u32[]{:S(2)}, u32[]{:S(2)}) %collective-permute-start.3) | collective-permute-done | bytes 90144 | tf_op jit(solution)/shard_map/ppermute | solution.py:540
  42.5 3.1 %all-to-all-done.1.recv = f32[4,144,128]{2,1,0:T(8,128)S(1)} async-done(((f32[4,144,128]{2,1,0:T(8,128)}), f32[4,144,128]{2,1,0:T(8,128)S(1)}, u32[]{:S(2)}, u32[]{:S(2)}) %all-to-all-start.1) | async-done | bytes 294944 | tf_op jit(solution)/shard_map/all_to_all | solution.py:562
  45.6 0.0 copy-done
  45.6 0.0 copy-done.1
  45.6 0.0 copy-done.2
  45.6 9.2 %finish.1 = f32[4,80,32,128]{3,2,1,0:T(8,128)} custom-call(f32[4,144,128]{2,1,0:T(8,128)S(1)} %all-to-all-done.1.recv, s32[32,128]{1,0:T(8,128)S(1)} %copy-done.2, f32[4,32,80,128]{3,2,1,0:T(8,128)} %get-tuple-element.16.mixed_h, f32[4,32,80,128]{3,2,1,0:T(8,128)} %get-tuple-element.17.first_h, f32[4,88,128]{2,1,0:T(8,128)} %copy-done, ...), custom_call_target="tpu_custom_call" | custom-call | flops 26214400 | bytes 12582912 | tf_op jit(solution)/shard_map/finish/pallas_call | solution.py:510
Async XLA Ops:
  9.1 22.0 %all-to-all-start = ((f32[32,72,128]{2,1,0:T(8,128)}), f32[32,72,128]{2,1,0:T(8,128)S(1)}, u32[]{:S(2)}, u32[]{:S(2)}) async-start(f32[32,72,128]{2,1,0:T(8,128)} %get-tuple-element.12), calls=%async_computation | async-start | bytes 2359296 | tf_op jit(solution)/shard_map/all_to_all | solution.py:554
  14.3 14.2 %collective-permute-start = (f32[4,88,128]{2,1,0:T(8,128)S(1)}, f32[4,88,128]{2,1,0:T(8,128)S(1)}, u32[]{:S(2)}, u32[]{:S(2)}) collective-permute-start(f32[4,88,128]{2,1,0:T(8,128)S(1)} %get-tuple-element.14), channel_id=1, source_target_pairs={{0,8},{8,16},{16,24},{1,9},{9,17},{17,25},{2,10},{10,18},{18,26},{... | collective-permute-start | bytes 540680 | tf_op jit(solution)/shard_map/ppermute | solution.py:540
  17.8 27.8 %copy-start.2 = (s32[32,128]{1,0:T(8,128)S(1)}, s32[32,128]{1,0:T(8,128)}, u32[]{:S(2)}) copy-start(s32[32,128]{1,0:T(8,128)} %depth_ref.1) | copy-start | bytes 49156
  17.8 10.7 %collective-permute-start.1 = (f32[4,88,128]{2,1,0:T(8,128)S(1)}, f32[4,88,128]{2,1,0:T(8,128)S(1)}, u32[]{:S(2)}, u32[]{:S(2)}) collective-permute-start(f32[4,88,128]{2,1,0:T(8,128)S(1)} %get-tuple-element.15), channel_id=1, source_target_pairs={{8,0},{16,8},{24,16},{9,1},{17,9},{25,17},{10,2},{18,10},{26,18},{... | collective-permute-start | bytes 540680 | tf_op jit(solution)/shard_map/ppermute | solution.py:540
  28.5 17.1 %copy-start = (f32[4,88,128]{2,1,0:T(8,128)}, f32[4,88,128]{2,1,0:T(8,128)S(1)}, u32[]{:S(2)}) copy-start(f32[4,88,128]{2,1,0:T(8,128)S(1)} %collective-permute-done.after_north.north_h) | copy-start | bytes 540676
  28.6 17.1 %copy-start.1 = (f32[4,88,128]{2,1,0:T(8,128)}, f32[4,88,128]{2,1,0:T(8,128)S(1)}, u32[]{:S(2)}) copy-start(f32[4,88,128]{2,1,0:T(8,128)S(1)} %collective-permute-done.1.after_south.south_h) | copy-start | bytes 540676
  32.4 13.2 %all-to-all-start.1 = ((f32[4,144,128]{2,1,0:T(8,128)}), f32[4,144,128]{2,1,0:T(8,128)S(1)}, u32[]{:S(2)}, u32[]{:S(2)}) async-start(f32[4,144,128]{2,1,0:T(8,128)} %collect.1), calls=%async_computation.1 | async-start | bytes 589824 | tf_op jit(solution)/shard_map/all_to_all | solution.py:562
  37.3 3.0 %collective-permute-start.2 = (f32[2,88,128]{2,1,0:T(8,128)S(1)}, f32[2,88,128]{2,1,0:T(8,128)S(1)}, u32[]{:S(2)}, u32[]{:S(2)}) collective-permute-start(f32[2,88,128]{2,1,0:T(8,128)S(1)} %get-tuple-element.18), channel_id=1, source_target_pairs={{0,7},{1,0},{2,1},{3,2},{4,3},{5,4},{6,5},{7,6},{8,15},{9,8},{10,9... | collective-permute-start | bytes 270344 | tf_op jit(solution)/shard_map/ppermute | solution.py:540
  37.7 4.9 %collective-permute-start.3 = (f32[2,88,128]{2,1,0:T(8,128)S(1)}, f32[2,88,128]{2,1,0:T(8,128)S(1)}, u32[]{:S(2)}, u32[]{:S(2)}) collective-permute-start(f32[2,88,128]{2,1,0:T(8,128)S(1)} %get-tuple-element.13.after_mix), channel_id=1, source_target_pairs={{0,1},{1,2},{2,3},{3,4},{4,5},{5,6},{6,7},{7,0},{8,9},{9,10},{10,1... | collective-permute-start | bytes 270344 | tf_op jit(solution)/shard_map/ppermute | solution.py:540

commit v11 on v10

--- a/solution.py
+++ b/solution.py
@@ -239,8 +239,7 @@
 
 
 def mix_kernel(
-    depth_h, state_h, inv_h, mixed_h, first_h, to_east, to_west,
-    depth_ref, state, mixed, inv, first, side, in_sems, out_sems,
+    depth_h, state_h, inv_h, mixed_h, side_h, to_east, to_west, depth_ref, state, mixed, inv, side, in_sems, out_sems
 ):
     fields, oy, levels, _ = mixed.shape
     depth_copy = pltpu.make_async_copy(depth_h, depth_ref, in_sems.at[2 * fields, 0])
@@ -279,24 +278,23 @@
                 a = inv[q, row, 0]
                 m = solve_row(a, state[q, row], level < depth_ref[row : row + 1, :])
                 mixed[q, row] = m
-                column = jnp.broadcast_to(a[:, 0:1], (levels, LANES))
-                first[q, row] = column
                 cells = jnp.where(lane // 2 == row, pltpu.roll(m, 2 * row + 1, 1), cells)
-                cells = jnp.where(lane // 2 == HALF // 2 + row, column, cells)
-            pltpu.make_async_copy(mixed.at[here], mixed_h.at[here], out_sems.at[2 * q]).start()
-            pltpu.make_async_copy(first.at[here], first_h.at[here], out_sems.at[2 * q + 1]).start()
+                cells = jnp.where(lane // 2 == HALF // 2 + row, a[:, 0:1], cells)
+            pltpu.make_async_copy(mixed.at[here], mixed_h.at[here], out_sems.at[q]).start()
         side[q, 0:levels] = cells
         side[q, levels : levels + SUB] = edge_depth
         return carry
 
     lax.fori_loop(0, fields, field, 0)
+    side_copy = pltpu.make_async_copy(side, side_h, out_sems.at[fields])
+    side_copy.start()
     even = line % 2 == 0
     for k in range(fields // 2):
         to_east[k] = jnp.where(even, side[2 * k], pltpu.roll(side[2 * k + 1], 1, 1))
         to_west[k] = jnp.where(even, pltpu.roll(side[2 * k], LANES - 1, 1), side[2 * k + 1])
     for q in range(fields):
-        pltpu.make_async_copy(mixed.at[q], mixed_h.at[q], out_sems.at[2 * q]).wait()
-        pltpu.make_async_copy(first.at[q], first_h.at[q], out_sems.at[2 * q + 1]).wait()
+        pltpu.make_async_copy(mixed.at[q], mixed_h.at[q], out_sems.at[q]).wait()
+    side_copy.wait()
 
 
 def mix(depth, state, inverses):
@@ -307,16 +305,15 @@
         mix_kernel,
         in_specs=[HBM] * 3,
         out_specs=[HBM] * 2 + [VMEM] * 2,
-        out_shape=[pltpu.HBM(full, f32), pltpu.HBM(full, f32), edge_shape, edge_shape],
+        out_shape=[pltpu.HBM(full, f32), pltpu.HBM((fields, levels + SUB, ox), f32), edge_shape, edge_shape],
         scratch_shapes=[
             pltpu.VMEM(depth.shape, jnp.int32),
             pltpu.VMEM(full, f32),
             pltpu.VMEM(full, f32),
             pltpu.VMEM(inverses.shape, f32),
-            pltpu.VMEM(full, f32),
             pltpu.VMEM((fields, levels + SUB, ox), f32),
             pltpu.SemaphoreType.DMA((2 * fields + 1, oy // SUB)),
-            pltpu.SemaphoreType.DMA((2 * fields,)),
+            pltpu.SemaphoreType.DMA((fields + 1,)),
         ],
         compiler_params=pltpu.CompilerParams(vmem_limit_bytes=32 << 20),
         cost_estimate=pl.CostEstimate(flops=2 * 4 * fields * oy * levels * levels * ox, bytes_accessed=16 << 20, transcendentals=0),
@@ -379,8 +376,8 @@
 
 
 def finish_kernel(
-    recv, depth_ref, mixed_h, first_h, north_h, south_h, east, west,
-    out_h, north, south, forcing, z, keep, halo, z_north, z_south, mixed, first, stage, edge_sems, in_sems, out_sems,
+    recv, depth_ref, mixed_h, own_h, north_h, south_h, east, west,
+    out_h, own, north, south, forcing, z, keep, halo, z_north, z_south, mixed, stage, edge_sems, in_sems, out_sems,
 ):
     fields, oy, levels, _ = mixed.shape
     level = iota((levels, LANES), 0)
@@ -391,21 +388,17 @@
     even = line % 2 == 0
     edges = [
         pltpu.make_async_copy(a, b, edge_sems.at[k])
-        for k, (a, b) in enumerate(((north_h, north), (south_h, south)))
+        for k, (a, b) in enumerate(((own_h, own), (north_h, north), (south_h, south)))
     ]
     for copy in edges:
         copy.start()
 
-    def loads(q, c):
+    def load(q, c):
         here = (q, pl.ds(c * SUB, SUB))
-        return [
-            pltpu.make_async_copy(a.at[here], b.at[here], in_sems.at[k, q, c])
-            for k, (a, b) in enumerate(((mixed_h, mixed), (first_h, first)))
-        ]
+        return pltpu.make_async_copy(mixed_h.at[here], mixed.at[here], in_sems.at[q, c])
 
     for c in range(oy // SUB):
-        for copy in loads(0, c):
-            copy.start()
+        load(0, c).start()
 
     total = recv[0]
     for a in range(1, recv.shape[0]):
@@ -457,24 +450,34 @@
 
     both = jnp.where((square_row == square_lane + 1) | (square_row == square_lane - 1), 1.0, 0.0).astype(bf16)
     both = jnp.concatenate([both, both], axis=0)
+    ones = jnp.ones((LANES, LANES), bf16)
     ends = (lanes == 0) | (lanes == LANES - 1)
 
     def field(q, carry):
         @pl.when(q + 1 < fields)
         def _():
             for c in range(oy // SUB):
-                for copy in loads(q + 1, c):
-                    copy.start()
+                load(q + 1, c).start()
 
         z[0] = z_north[q]
         z[oy + 1] = z_south[q]
         edge = halo[q]
+        names = own[q, 0:levels]
+        high = names.astype(bf16).astype(f32)
+        names = jnp.where(even, high, names - high)
 
         def solve(c):
-            for copy in loads(q, c):
-                copy.wait()
-            for r in range(c * SUB, (c + 1) * SUB):
-                forced = mixed[q, r] + first[q, r] * forcing[pl.ds(q * oy + r, 1), :]
+            load(q, c).wait()
+            rows_here = range(c * SUB, (c + 1) * SUB)
+            first = matmul(
+                jnp.concatenate(
+                    [jnp.where(lanes // 2 == HALF // 2 + r, names, 0.0).astype(bf16) for r in rows_here], axis=0
+                ),
+                ones,
+            )
+            for i, r in enumerate(rows_here):
+                first_here = first[i * levels : (i + 1) * levels]
+                forced = mixed[q, r] + first_here * forcing[pl.ds(q * oy + r, 1), :]
                 z[r + 1] = jnp.where(level < depth_ref[r : r + 1, :], forced, 0.0)
 
         def diffuse(c):
@@ -502,7 +505,7 @@
         pltpu.make_async_copy(stage.at[q], mixed_h.at[q], out_sems.at[q]).wait()
 
 
-def finish(received, depth, mixed, first, halos):
+def finish(received, depth, mixed, own, halos):
     fields, oy, levels, ox = mixed.shape
     edge = pltpu.VMEM((fields, levels, ox), f32)
     message = pltpu.VMEM((fields, levels + SUB, ox), f32)
@@ -515,6 +518,7 @@
         scratch_shapes=[
             message,
             message,
+            message,
             pltpu.VMEM((fields * oy, ox), f32),
             pltpu.VMEM((oy + 2, levels, ox), f32),
             pltpu.VMEM((oy, levels, ox), f32),
@@ -523,15 +527,14 @@
             edge,
             full,
             full,
-            full,
-            pltpu.SemaphoreType.DMA((2,)),
-            pltpu.SemaphoreType.DMA((2, fields, oy // SUB)),
+            pltpu.SemaphoreType.DMA((3,)),
+            pltpu.SemaphoreType.DMA((fields, oy // SUB)),
             pltpu.SemaphoreType.DMA((fields,)),
         ],
         compiler_params=pltpu.CompilerParams(vmem_limit_bytes=32 << 20),
         cost_estimate=pl.CostEstimate(flops=20 * fields * oy * levels * ox, bytes_accessed=12 << 20, transcendentals=0),
         name="finish",
-    )(received, depth, *in_hbm(mixed, first, *halos[0:2]), *halos[2:])
+    )(received, depth, *in_hbm(mixed, own, *halos[0:2]), *halos[2:])
 
 
 def shift(x, axis, step, wrap):
@@ -552,7 +555,7 @@
         intersection_weights, depth_levels, ocean_state, inverses,
     )
     in_plane = lax.all_to_all(slots, "lon", 0, 0, tiled=True)
-    mixed, first, to_east, to_west = mix(depth_levels, ocean_state, inverses)
+    mixed, side, to_east, to_west = mix(depth_levels, ocean_state, inverses)
     halos = (
         shift(south, "lat", 1, False),
         shift(north, "lat", -1, False),
@@ -560,7 +563,7 @@
         shift(to_east, "lon", 1, True),
     )
     received = lax.all_to_all(collect(cap, fields, oy, lat, in_plane, (to_east, *halos[0:2])), "lat", 0, 0, tiled=True)
-    return finish(received, depth_levels, mixed, first, halos)
+    return finish(received, depth_levels, mixed, side, halos)
 
 
 def solution(mesh):

time: 55.4 us -> 54.6 us (0.986)
  waiting for transfers between devices: 10.4 us -> 9.59 us
    all_to_all x1, waiting for transfers between devices: 3.1 us -> 2.32 us  [on_device(): lax.all_to_all(collect(cap, fields, oy, lat, in_plane, (to_east, *halos[0...]
where the time goes in v11:
time: 54.6 us; the launch traced here: 53.9 us
  Pallas kernels  28.9 us (53%)
  starting transfers between devices  15.3 us (28%)
  waiting for transfers between devices  9.59 us (18%)
    pallas_call x1, Pallas kernels, finish(): pl.pallas_call(finish_kernel, in_specs=[VMEM] * 2 + [HBM] * 4 + [VMEM] *...  9.44 us
    pallas_call x1, Pallas kernels, regrid(): pl.pallas_call(functools.partial(regrid_kernel, cap, lat, lon, oy, batch)...  9.13 us
    pallas_call x1, Pallas kernels, mix(): pl.pallas_call(mix_kernel, in_specs=[HBM] * 3, out_specs=[HBM] * 2 + [VME...  9.06 us
    ppermute x4, starting transfers between devices, shift(): return lax.ppermute(x, axis, pairs)  5.28 us
    all_to_all x1, starting transfers between devices, on_device(): in_plane = lax.all_to_all(slots, 'lon', 0, 0, tiled=True)  5.19 us
    all_to_all x1, starting transfers between devices, on_device(): lax.all_to_all(collect(cap, fields, oy, lat, in_plane, (to_east, *halos[0...  4.87 us
    ppermute x4, waiting for transfers between devices, shift(): return lax.ppermute(x, axis, pairs)  4.36 us
    all_to_all x1, waiting for transfers between devices, on_device(): in_plane = lax.all_to_all(slots, 'lon', 0, 0, tiled=True)  2.91 us
  transfers between devices with their start and end apart: 6, of which 4 were waited for; matrix products, arithmetic and copies ran while one was open for 0% of the time, Pallas kernels for 17%

profile of v11, /device:TPU:0, one launch (start us, length us, event | category | flops | bytes accessed | tf_op | source)
XLA Modules:
  0.0 53.9 jit_solution(8576159047582908649)
XLA Ops:
  0.0 9.1 %regrid.1 = (f32[32,72,128]{2,1,0:T(8,128)}, f32[4,88,128]{2,1,0:T(8,128)S(1)}, f32[4,88,128]{2,1,0:T(8,128)S(1)}) custom-call(s32[256]{0:T(256)} %src_h.1, s32[256]{0:T(256)} %bitcast.1, s32[256]{0:T(256)} %blk_h.1, f32[4,8]{1,0:T(4,128)} %coupling_h.1, bf16[8,64,128]{2,1,0:T(8,128)(2,1)} %atm_h.1, s32[64,128]{1,0:T(8,128)} %mask_h.1, ...), custom_call_target="tpu_custom_call" | custom-call | flops 67108864 | bytes 10485760 | tf_op jit(solution)/shard_map/regrid/pallas_call | solution.py:210
  9.1 5.2 %all-to-all-start = ((f32[32,72,128]{2,1,0:T(8,128)}), f32[32,72,128]{2,1,0:T(8,128)S(1)}, u32[]{:S(2)}, u32[]{:S(2)}) async-start(f32[32,72,128]{2,1,0:T(8,128)} %get-tuple-element.12), calls=%async_computation | async-start | bytes 2359296 | tf_op jit(solution)/shard_map/all_to_all | solution.py:557
  14.3 3.5 %collective-permute-start = (f32[4,88,128]{2,1,0:T(8,128)S(1)}, f32[4,88,128]{2,1,0:T(8,128)S(1)}, u32[]{:S(2)}, u32[]{:S(2)}) collective-permute-start(f32[4,88,128]{2,1,0:T(8,128)S(1)} %get-tuple-element.14), channel_id=1, source_target_pairs={{0,8},{8,16},{16,24},{1,9},{9,17},{17,25},{2,10},{10,18},{18,26},{... | collective-permute-start | bytes 540680 | tf_op jit(solution)/shard_map/ppermute | solution.py:543
  17.8 0.0 copy-start.2
  17.8 1.3 %collective-permute-start.1 = (f32[4,88,128]{2,1,0:T(8,128)S(1)}, f32[4,88,128]{2,1,0:T(8,128)S(1)}, u32[]{:S(2)}, u32[]{:S(2)}) collective-permute-start(f32[4,88,128]{2,1,0:T(8,128)S(1)} %get-tuple-element.15), channel_id=1, source_target_pairs={{8,0},{16,8},{24,16},{9,1},{17,9},{25,17},{10,2},{18,10},{26,18},{... | collective-permute-start | bytes 540680 | tf_op jit(solution)/shard_map/ppermute | solution.py:543
  19.1 9.1 %mix.1 = (f32[4,32,80,128]{3,2,1,0:T(8,128)}, f32[4,88,128]{2,1,0:T(8,128)}, f32[2,88,128]{2,1,0:T(8,128)S(1)}, f32[2,88,128]{2,1,0:T(8,128)S(1)}) custom-call(s32[32,128]{1,0:T(8,128)} %depth_ref.1, f32[4,80,32,128]{3,2,1,0:T(8,128)} %state_h.3, f32[4,32,1,80,80]{4,3,2,1,0:T(8,128)} %inv_h.3), custom_call_target="tpu_custom_call" | custom-call | flops 838860800 | bytes 16777216 | tf_op jit(solution)/shard_map/mix/pallas_call | solution.py:304
  28.2 0.0 collective-permute-done.after_north.north_h
  28.2 0.0 copy-start
  28.2 0.0 collective-permute-done.1.after_south.south_h
  28.2 0.0 copy-start.1
  28.2 2.9 %all-to-all-done.recv = f32[32,72,128]{2,1,0:T(8,128)S(1)} async-done(((f32[32,72,128]{2,1,0:T(8,128)}), f32[32,72,128]{2,1,0:T(8,128)S(1)}, u32[]{:S(2)}, u32[]{:S(2)}) %all-to-all-start) | async-done | bytes 1179680 | tf_op jit(solution)/shard_map/all_to_all | solution.py:557
  31.1 1.3 %collect.1 = f32[4,144,128]{2,1,0:T(8,128)} custom-call(f32[32,72,128]{2,1,0:T(8,128)S(1)} %all-to-all-done.recv, f32[2,88,128]{2,1,0:T(8,128)S(1)} %get-tuple-element.13.after_mix, f32[4,88,128]{2,1,0:T(8,128)S(1)} %collective-permute-done.after_north.north_h, f32[4,88,128]{2,1,0:T(8,128)S(1)} %collective-permute-done.1.after_south.south_h), custom_call_target="tpu_custom_call" | custom-call | tf_op jit(solution)/shard_map/collect/pallas_call | solution.py:368
  32.4 4.9 %all-to-all-start.1 = ((f32[4,144,128]{2,1,0:T(8,128)}), f32[4,144,128]{2,1,0:T(8,128)S(1)}, u32[]{:S(2)}, u32[]{:S(2)}) async-start(f32[4,144,128]{2,1,0:T(8,128)} %collect.1), calls=%async_computation.1 | async-start | bytes 589824 | tf_op jit(solution)/shard_map/all_to_all | solution.py:565
  37.3 0.0 collective-permute-start.2
  37.3 0.5 collective-permute-start.3
  37.8 2.4 %collective-permute-done.2.east = f32[2,88,128]{2,1,0:T(8,128)S(1)} collective-permute-done((f32[2,88,128]{2,1,0:T(8,128)S(1)}, f32[2,88,128]{2,1,0:T(8,128)S(1)}, u32[]{:S(2)}, u32[]{:S(2)}) %collective-permute-start.2) | collective-permute-done | bytes 90144 | tf_op jit(solution)/shard_map/ppermute | solution.py:543
  40.3 1.9 %collective-permute-done.3.west = f32[2,88,128]{2,1,0:T(8,128)S(1)} collective-permute-done((f32[2,88,128]{2,1,0:T(8,128)S(1)}, f32[2,88,128]{2,1,0:T(8,128)S(1)}, u32[]{:S(2)}, u32[]{:S(2)}) %collective-permute-start.3) | collective-permute-done | bytes 90144 | tf_op jit(solution)/shard_map/ppermute | solution.py:543
  42.2 2.3 %all-to-all-done.1.recv = f32[4,144,128]{2,1,0:T(8,128)S(1)} async-done(((f32[4,144,128]{2,1,0:T(8,128)}), f32[4,144,128]{2,1,0:T(8,128)S(1)}, u32[]{:S(2)}, u32[]{:S(2)}) %all-to-all-start.1) | async-done | bytes 294944 | tf_op jit(solution)/shard_map/all_to_all | solution.py:565
  44.5 0.0 copy-done
  44.5 0.0 copy-done.1
  44.5 0.0 copy-done.2
  44.5 9.4 %finish.1 = f32[4,80,32,128]{3,2,1,0:T(8,128)} custom-call(f32[4,144,128]{2,1,0:T(8,128)S(1)} %all-to-all-done.1.recv, s32[32,128]{1,0:T(8,128)S(1)} %copy-done.2, f32[4,32,80,128]{3,2,1,0:T(8,128)} %get-tuple-element.16.mixed_h, f32[4,88,128]{2,1,0:T(8,128)} %get-tuple-element.17.own_h, f32[4,88,128]{2,1,0:T(8,128)} %copy-done, f32[4,88,128]{2,1,0:T(8,128)} %copy-done.1, ...), custom_call_target="tpu_custom_call" | custom-call | flops 26214400 | bytes 12582912 | tf_op jit(solution)/shard_map/finish/pallas_call | solution.py:513
Async XLA Ops:
  9.1 22.0 %all-to-all-start = ((f32[32,72,128]{2,1,0:T(8,128)}), f32[32,72,128]{2,1,0:T(8,128)S(1)}, u32[]{:S(2)}, u32[]{:S(2)}) async-start(f32[32,72,128]{2,1,0:T(8,128)} %get-tuple-element.12), calls=%async_computation | async-start | bytes 2359296 | tf_op jit(solution)/shard_map/all_to_all | solution.py:557
  14.3 13.9 %collective-permute-start = (f32[4,88,128]{2,1,0:T(8,128)S(1)}, f32[4,88,128]{2,1,0:T(8,128)S(1)}, u32[]{:S(2)}, u32[]{:S(2)}) collective-permute-start(f32[4,88,128]{2,1,0:T(8,128)S(1)} %get-tuple-element.14), channel_id=1, source_target_pairs={{0,8},{8,16},{16,24},{1,9},{9,17},{17,25},{2,10},{10,18},{18,26},{... | collective-permute-start | bytes 540680 | tf_op jit(solution)/shard_map/ppermute | solution.py:543
  17.8 26.7 %copy-start.2 = (s32[32,128]{1,0:T(8,128)S(1)}, s32[32,128]{1,0:T(8,128)}, u32[]{:S(2)}) copy-start(s32[32,128]{1,0:T(8,128)} %depth_ref.1) | copy-start | bytes 49156
  17.8 10.4 %collective-permute-start.1 = (f32[4,88,128]{2,1,0:T(8,128)S(1)}, f32[4,88,128]{2,1,0:T(8,128)S(1)}, u32[]{:S(2)}, u32[]{:S(2)}) collective-permute-start(f32[4,88,128]{2,1,0:T(8,128)S(1)} %get-tuple-element.15), channel_id=1, source_target_pairs={{8,0},{16,8},{24,16},{9,1},{17,9},{25,17},{10,2},{18,10},{26,18},{... | collective-permute-start | bytes 540680 | tf_op jit(solution)/shard_map/ppermute | solution.py:543
  28.2 16.3 %copy-start = (f32[4,88,128]{2,1,0:T(8,128)}, f32[4,88,128]{2,1,0:T(8,128)S(1)}, u32[]{:S(2)}) copy-start(f32[4,88,128]{2,1,0:T(8,128)S(1)} %collective-permute-done.after_north.north_h) | copy-start | bytes 540676
  28.2 16.3 %copy-start.1 = (f32[4,88,128]{2,1,0:T(8,128)}, f32[4,88,128]{2,1,0:T(8,128)S(1)}, u32[]{:S(2)}) copy-start(f32[4,88,128]{2,1,0:T(8,128)S(1)} %collective-permute-done.1.after_south.south_h) | copy-start | bytes 540676
  32.4 12.1 %all-to-all-start.1 = ((f32[4,144,128]{2,1,0:T(8,128)}), f32[4,144,128]{2,1,0:T(8,128)S(1)}, u32[]{:S(2)}, u32[]{:S(2)}) async-start(f32[4,144,128]{2,1,0:T(8,128)} %collect.1), calls=%async_computation.1 | async-start | bytes 589824 | tf_op jit(solution)/shard_map/all_to_all | solution.py:565
  37.3 3.0 %collective-permute-start.2 = (f32[2,88,128]{2,1,0:T(8,128)S(1)}, f32[2,88,128]{2,1,0:T(8,128)S(1)}, u32[]{:S(2)}, u32[]{:S(2)}) collective-permute-start(f32[2,88,128]{2,1,0:T(8,128)S(1)} %get-tuple-element.18), channel_id=1, source_target_pairs={{0,7},{1,0},{2,1},{3,2},{4,3},{5,4},{6,5},{7,6},{8,15},{9,8},{10,9... | collective-permute-start | bytes 270344 | tf_op jit(solution)/shard_map/ppermute | solution.py:543
  37.3 4.9 %collective-permute-start.3 = (f32[2,88,128]{2,1,0:T(8,128)S(1)}, f32[2,88,128]{2,1,0:T(8,128)S(1)}, u32[]{:S(2)}, u32[]{:S(2)}) collective-permute-start(f32[2,88,128]{2,1,0:T(8,128)S(1)} %get-tuple-element.13.after_mix), channel_id=1, source_target_pairs={{0,1},{1,2},{2,3},{3,4},{4,5},{5,6},{6,7},{7,0},{8,9},{9,10},{10,1... | collective-permute-start | bytes 270344 | tf_op jit(solution)/shard_map/ppermute | solution.py:543

commit v12 on v11

--- a/solution.py
+++ b/solution.py
@@ -65,6 +65,10 @@
             )
 
 
+def extra_rows(lat):
+    return -(-3 * lat // SUB) * SUB
+
+
 def regrid_kernel(
     cap, lat, lon, oy, batch,
     src_h, dev_h, blk_h, coupling_h, atm_h, mask_h, weights_h, depth_h, state_h, inv_h,
@@ -74,10 +78,11 @@
 ):
     fluxes, atm_rows, _ = atm.shape
     fields = coupling.shape[0]
-    devices = out.shape[0]
+    devices = lat * lon
     per = fields * cap
+    slot_rows = lat * per
     parts = weights.shape[0] // batch
-    ahead = min(3, parts)
+    ahead = min(2, parts)
 
     def big(k):
         here = pl.ds(pl.multiple_of(k * batch, batch), batch)
@@ -102,12 +107,16 @@
     for k in range(ahead):
         big(k).start()
 
-    def clear(d, carry):
+    def clear_count(d, carry):
         count[d] = 0
-        out[d] = jnp.zeros(out.shape[1:], f32)
         return carry
 
-    lax.fori_loop(0, devices, clear, 0)
+    def clear(b, carry):
+        out[b] = jnp.zeros(out.shape[1:], f32)
+        return carry
+
+    lax.fori_loop(0, devices, clear_count, 0)
+    lax.fori_loop(0, lon, clear, 0)
     ids[...] = jnp.full(ids.shape, -1, jnp.int32)
     for copy in small:
         copy.wait()
@@ -135,8 +144,16 @@
 
     def place(d):
         if lon == 1 << bits:
-            return (d & (lon - 1)) * lat + lax.shift_right_logical(d, bits)
-        return lax.rem(d, lon) * lat + lax.div(d, lon)
+            return lax.shift_right_logical(d, bits), d & (lon - 1)
+        return lax.div(d, lon), lax.rem(d, lon)
+
+    def extra(d, k):
+        a, b = place(d)
+        return b, pl.ds(slot_rows + 3 * a + k, 1)
+
+    def slots(d):
+        a, b = place(d)
+        return padded_rows(out[b, pl.ds(pl.multiple_of(a * per, per), per), :], HALF)
 
     def part(k, carry):
         big(k).wait()
@@ -156,7 +173,8 @@
                 slot = jnp.minimum(count[d], cap - 1)
                 count[d] = slot + 1
                 half = both[v * SUB : v * SUB + SUB, v * LANES : (v + 1) * LANES]
-                out[place(d), pl.ds(slot * fields, fields), :] = half[0:fields] + half[fields : 2 * fields]
+                a, b = place(d)
+                out[b, pl.ds(a * per + slot * fields, fields), :] = half[0:fields] + half[fields : 2 * fields]
                 line = ids[pl.ds(d, 1), :]
                 ids[pl.ds(d, 1), :] = jnp.where(lane_slot == slot, lane_row + blk[p + v], line)
         return carry
@@ -166,28 +184,25 @@
     def send(k, start, stop):
         return pltpu.make_async_copy(out.at[:, start:stop, :], out_h.at[:, start:stop, :], out_sem.at[k])
 
-    send(0, 0, per).start()
+    send(0, 0, slot_rows).start()
 
     def halo(k):
         d = 2 * k
-        turned = jnp.concatenate(
-            [padded_rows(out[place(d + u), 0:per], HALF) for u in range(2)], axis=0
-        ).T
+        turned = jnp.concatenate([slots(d + u) for u in range(2)], axis=0).T
         first, last = turned[0:1], turned[LANES - 1 : LANES]
         first_swapped = pltpu.roll(turned[0:SUB], HALF, 1)[0:1]
         last_swapped = pltpu.roll(turned[LANES - SUB : LANES], HALF, 1)[SUB - 1 : SUB]
         for u in range(2):
-            b = lax.rem(d + u, lon)
+            _, b = place(d + u)
             east = jnp.where(b == lon - 1, d + u - (lon - 1), d + u + 1)
             west = jnp.where(b == 0, d + u + (lon - 1), d + u - 1)
-            here, to_east, to_west = place(d + u), place(east), place(west)
-            out[here, per : per + 1] = ids[pl.ds(d + u, 1), :].astype(f32)
+            out[extra(d + u, 0)] = ids[pl.ds(d + u, 1), :].astype(f32)
             sides = jnp.where(lane < HALF, ids[pl.ds(east, 1), :], ids[pl.ds(west, 1), :])
-            out[here, per + 1 : per + 2] = sides.astype(f32)
+            out[extra(d + u, 1)] = sides.astype(f32)
             column = first if u == 0 else first_swapped
-            out[to_west, per + 2 : per + 3] = jnp.where(lane < HALF, column, out[to_west, per + 2 : per + 3])
+            out[extra(west, 2)] = jnp.where(lane < HALF, column, out[extra(west, 2)])
             column = last_swapped if u == 0 else last
-            out[to_east, per + 2 : per + 3] = jnp.where(lane < HALF, out[to_east, per + 2 : per + 3], column)
+            out[extra(east, 2)] = jnp.where(lane < HALF, out[extra(east, 2)], column)
 
     def halos(k, carry):
         for u in range(4):
@@ -195,25 +210,25 @@
         return carry
 
     lax.fori_loop(0, devices // 8, halos, 0)
-    send(1, per, per + SUB).start()
-    send(0, 0, per).wait()
-    send(1, per, per + SUB).wait()
+    send(1, slot_rows, out.shape[1]).start()
+    send(0, 0, slot_rows).wait()
+    send(1, slot_rows, out.shape[1]).wait()
 
 
 def regrid(cap, lat, lon, src, dev, blk, coupling, atm, mask, weights, depth, ocean, inverses):
     pairs, cells, width = weights.shape
     fields, levels, oy, ox = ocean.shape
     message = jax.ShapeDtypeStruct((fields, levels + SUB, ox), f32)
-    batch = 32
+    batch = 64
     devices = lat * lon
-    tall = fields * cap + SUB
+    tall = lat * fields * cap + extra_rows(lat)
     return pl.pallas_call(
         functools.partial(regrid_kernel, cap, lat, lon, oy, batch),
         in_specs=[HBM] * 10,
         out_specs=[HBM, VMEM, VMEM],
-        out_shape=[pltpu.HBM((devices, tall, LANES), f32), message, message],
+        out_shape=[pltpu.HBM((lon, tall, LANES), f32), message, message],
         scratch_shapes=[
-            pltpu.VMEM((devices, tall, LANES), f32),
+            pltpu.VMEM((lon, tall, LANES), f32),
             pltpu.VMEM((atm.shape[1] * SUB, LANES), f32),
             pltpu.VMEM((devices, LANES), jnp.int32),
             pltpu.SMEM((devices,), jnp.int32),
@@ -323,8 +338,9 @@
 
 def collect_kernel(cap, fields, oy, recv, after_mix, after_north, after_south, out):
     lat = out.shape[0]
-    lon = recv.shape[0] // lat
+    lon = recv.shape[0]
     per = fields * cap
+    slot_rows = lat * per
     group = LANES // per
     forced = fields * oy
     square_row = iota((LANES, LANES), 0).astype(f32)
@@ -338,12 +354,13 @@
     for a in range(lat):
         total = jnp.zeros((LANES, 2 * LANES), f32)
         for tile in range(lon // group):
-            places = [(tile * group + s) * lat + a for s in range(group)]
-            ids = recv[places[0], per : per + 1, :]
+            places = [tile * group + s for s in range(group)]
+            named = slice(slot_rows + 3 * a, slot_rows + 3 * a + 1)
+            ids = recv[places[0], named, :]
             for s in range(1, group):
-                ids = jnp.where(line // per == s, recv[places[s], per : per + 1, :], ids)
+                ids = jnp.where(line // per == s, recv[places[s], named, :], ids)
             hot = jnp.where(square_row == ids, 1.0, 0.0).astype(bf16)
-            high, low = split(jnp.concatenate([recv[p, 0:per, :] for p in places], axis=0))
+            high, low = split(jnp.concatenate([recv[p, a * per : (a + 1) * per, :] for p in places], axis=0))
             total = total + matmul(hot, jnp.concatenate([high, low], axis=1))
         total = total[:, :LANES] + total[:, LANES:]
         out[a, 0:forced] = total
@@ -358,8 +375,9 @@
                 out[a - 1, forced + fields + q : forced + fields + q + 1] = total[q * oy : q * oy + 1]
         spread = jnp.zeros((2 * oy, LANES), f32)
         for b in range(lon):
-            place = 2.0 * (recv[b * lat + a, per + 1 : per + 2, :] - lane_base) + lane_side
-            spread = spread + jnp.where(place == row, recv[b * lat + a, per + 2 : per + 3, :], 0.0)
+            extra = recv[b, slot_rows + 3 * a + 1 : slot_rows + 3 * a + 3, :]
+            place = 2.0 * (extra[0:1] - lane_base) + lane_side
+            spread = spread + jnp.where(place == row, extra[1:2], 0.0)
         high, low = split(padded_rows(spread, LANES).T)
         out[a, forced + SUB : forced + 2 * SUB] = matmul(pick, high) + matmul(pick, low)
 
@@ -450,8 +468,11 @@
 
     both = jnp.where((square_row == square_lane + 1) | (square_row == square_lane - 1), 1.0, 0.0).astype(bf16)
     both = jnp.concatenate([both, both], axis=0)
-    ones = jnp.ones((LANES, LANES), bf16)
-    ends = (lanes == 0) | (lanes == LANES - 1)
+    nothing = jnp.zeros((LANES, LANES), f32)
+    ends = (square_lane == jnp.where(square_row % 2 == 0, LANES - 1, 0)).astype(f32)
+    spread = jnp.concatenate(
+        [jnp.concatenate([nothing + 1.0, nothing], axis=1), jnp.concatenate([nothing, ends], axis=1)], axis=0
+    ).astype(bf16)
 
     def field(q, carry):
         @pl.when(q + 1 < fields)
@@ -462,6 +483,8 @@
         z[0] = z_north[q]
         z[oy + 1] = z_south[q]
         edge = halo[q]
+        high = edge.astype(bf16).astype(f32)
+        edge = jnp.where(lanes < HALF, high, pltpu.roll(edge - high, HALF, 1))
         names = own[q, 0:levels]
         high = names.astype(bf16).astype(f32)
         names = jnp.where(even, high, names - high)
@@ -469,35 +492,46 @@
         def solve(c):
             load(q, c).wait()
             rows_here = range(c * SUB, (c + 1) * SUB)
-            first = matmul(
-                jnp.concatenate(
-                    [jnp.where(lanes // 2 == HALF // 2 + r, names, 0.0).astype(bf16) for r in rows_here], axis=0
-                ),
-                ones,
+            places = jnp.concatenate(
+                [
+                    jnp.concatenate(
+                        [
+                            jnp.where(lanes // 2 == HALF // 2 + r, names, 0.0).astype(bf16),
+                            jnp.where((lanes % HALF) // 2 == r, edge, 0.0).astype(bf16),
+                        ],
+                        axis=1,
+                    )
+                    for r in rows_here
+                ],
+                axis=0,
             )
+            placed = matmul(places, spread)
+            first = placed[:, :LANES]
             for i, r in enumerate(rows_here):
                 first_here = first[i * levels : (i + 1) * levels]
                 forced = mixed[q, r] + first_here * forcing[pl.ds(q * oy + r, 1), :]
                 z[r + 1] = jnp.where(level < depth_ref[r : r + 1, :], forced, 0.0)
-
-        def diffuse(c):
+            return placed[:, LANES:]
+
+        def diffuse(c, outside):
             start = c * SUB
             high, low = split(z[start + 1 : start + 1 + SUB].reshape(SUB * levels, LANES))
             sides = matmul(jnp.concatenate([high, low], axis=1), both)
             for i in range(SUB):
                 r = start + i
-                outside = jnp.where(ends, pltpu.roll(edge, LANES - 1 - 2 * r, 1), 0.0)
-                around = (z[r] + z[r + 2]) + (sides[i * levels : (i + 1) * levels] + outside)
+                here = slice(i * levels, (i + 1) * levels)
+                around = (z[r] + z[r + 2]) + (sides[here] + outside[here])
                 active = level < depth_ref[r : r + 1, :]
                 stage[q, r] = jnp.where(active, z[r + 1] * keep[r] + diffusion_rate * around, mixed[q, r])
             for r in range(start, start + SUB):
                 pltpu.make_async_copy(stage.at[q, r], out_h.at[q, :, r, :], out_sems.at[q]).start()
 
-        solve(0)
+        outside = solve(0)
         for c in range(1, oy // SUB):
-            solve(c)
-            diffuse(c - 1)
-        diffuse(oy // SUB - 1)
+            following = solve(c)
+            diffuse(c - 1, outside)
+            outside = following
+        diffuse(oy // SUB - 1, outside)
         return carry
 
     lax.fori_loop(0, fields, field, 0)

time: 54.6 us -> 55.1 us (level)
    all_to_all x1, waiting for transfers between devices: 2.32 us -> 3.06 us  [on_device(): lax.all_to_all(collect(cap, fields, oy, lat, in_plane, (to_east, *halos[0...]
    all_to_all x1, waiting for transfers between devices: 2.91 us -> 2.2 us  [on_device(): in_plane = lax.all_to_all(slots, 'lon', 0, 0, tiled=True)]
where the time goes in v12:
time: 55.1 us; the launch traced here: 54.8 us
  Pallas kernels  29 us (53%)
  starting transfers between devices  15.5 us (28%)
  waiting for transfers between devices  10.1 us (18%)
    pallas_call x1, Pallas kernels, finish(): pl.pallas_call(finish_kernel, in_specs=[VMEM] * 2 + [HBM] * 4 + [VMEM] *...  9.98 us
    pallas_call x1, Pallas kernels, mix(): pl.pallas_call(mix_kernel, in_specs=[HBM] * 3, out_specs=[HBM] * 2 + [VME...  9.06 us
    pallas_call x1, Pallas kernels, regrid(): pl.pallas_call(functools.partial(regrid_kernel, cap, lat, lon, oy, batch)...  8.66 us
    ppermute x4, starting transfers between devices, shift(): return lax.ppermute(x, axis, pairs)  5.48 us
    all_to_all x1, starting transfers between devices, on_device(): in_plane = lax.all_to_all(slots, 'lon', 0, 0, tiled=True)  5.19 us
    all_to_all x1, starting transfers between devices, on_device(): lax.all_to_all(collect(cap, fields, oy, lat, in_plane, (to_east, *halos[0...  4.87 us
    ppermute x4, waiting for transfers between devices, shift(): return lax.ppermute(x, axis, pairs)  4.85 us
    all_to_all x1, waiting for transfers between devices, on_device(): lax.all_to_all(collect(cap, fields, oy, lat, in_plane, (to_east, *halos[0...  3.06 us
  transfers between devices with their start and end apart: 6, of which 4 were waited for; matrix products, arithmetic and copies ran while one was open for 0% of the time, Pallas kernels for 17%

profile of v12, /device:TPU:0, one launch (start us, length us, event | category | flops | bytes accessed | tf_op | source)
XLA Modules:
  0.0 54.8 jit_solution(17378363070511709599)
XLA Ops:
  0.0 8.7 %regrid.1 = (f32[8,272,128]{2,1,0:T(8,128)}, f32[4,88,128]{2,1,0:T(8,128)S(1)}, f32[4,88,128]{2,1,0:T(8,128)S(1)}) custom-call(s32[256]{0:T(256)} %src_h.1, s32[256]{0:T(256)} %bitcast.1, s32[256]{0:T(256)} %blk_h.1, f32[4,8]{1,0:T(4,128)} %coupling_h.1, bf16[8,64,128]{2,1,0:T(8,128)(2,1)} %atm_h.1, s32[64,128]{1,0:T(8,128)} %mask_h.1, ...), custom_call_target="tpu_custom_call" | custom-call | flops 67108864 | bytes 10485760 | tf_op jit(solution)/shard_map/regrid/pallas_call | solution.py:225
  8.7 5.2 %all-to-all-start = ((f32[8,272,128]{2,1,0:T(8,128)}), f32[8,272,128]{2,1,0:T(8,128)S(1)}, u32[]{:S(2)}, u32[]{:S(2)}) async-start(f32[8,272,128]{2,1,0:T(8,128)} %get-tuple-element.12), calls=%async_computation | async-start | bytes 2228224 | tf_op jit(solution)/shard_map/all_to_all | solution.py:591
  13.9 3.5 %collective-permute-start = (f32[4,88,128]{2,1,0:T(8,128)S(1)}, f32[4,88,128]{2,1,0:T(8,128)S(1)}, u32[]{:S(2)}, u32[]{:S(2)}) collective-permute-start(f32[4,88,128]{2,1,0:T(8,128)S(1)} %get-tuple-element.14), channel_id=1, source_target_pairs={{0,8},{8,16},{16,24},{1,9},{9,17},{17,25},{2,10},{10,18},{18,26},{... | collective-permute-start | bytes 540680 | tf_op jit(solution)/shard_map/ppermute | solution.py:577
  17.3 0.0 copy-start.2
  17.4 1.3 %collective-permute-start.1 = (f32[4,88,128]{2,1,0:T(8,128)S(1)}, f32[4,88,128]{2,1,0:T(8,128)S(1)}, u32[]{:S(2)}, u32[]{:S(2)}) collective-permute-start(f32[4,88,128]{2,1,0:T(8,128)S(1)} %get-tuple-element.15), channel_id=1, source_target_pairs={{8,0},{16,8},{24,16},{9,1},{17,9},{25,17},{10,2},{18,10},{26,18},{... | collective-permute-start | bytes 540680 | tf_op jit(solution)/shard_map/ppermute | solution.py:577
  18.7 9.1 %mix.1 = (f32[4,32,80,128]{3,2,1,0:T(8,128)}, f32[4,88,128]{2,1,0:T(8,128)}, f32[2,88,128]{2,1,0:T(8,128)S(1)}, f32[2,88,128]{2,1,0:T(8,128)S(1)}) custom-call(s32[32,128]{1,0:T(8,128)} %depth_ref.1, f32[4,80,32,128]{3,2,1,0:T(8,128)} %state_h.3, f32[4,32,1,80,80]{4,3,2,1,0:T(8,128)} %inv_h.3), custom_call_target="tpu_custom_call" | custom-call | flops 838860800 | bytes 16777216 | tf_op jit(solution)/shard_map/mix/pallas_call | solution.py:319
  27.7 0.0 collective-permute-done.after_north.north_h
  27.7 0.0 copy-start
  27.7 0.0 collective-permute-done.1.after_south.south_h
  27.8 0.0 copy-start.1
  27.8 2.2 %all-to-all-done.recv = f32[8,272,128]{2,1,0:T(8,128)S(1)} async-done(((f32[8,272,128]{2,1,0:T(8,128)}), f32[8,272,128]{2,1,0:T(8,128)S(1)}, u32[]{:S(2)}, u32[]{:S(2)}) %all-to-all-start) | async-done | bytes 1114144 | tf_op jit(solution)/shard_map/all_to_all | solution.py:591
  30.0 1.3 %collect.1 = f32[4,144,128]{2,1,0:T(8,128)} custom-call(f32[8,272,128]{2,1,0:T(8,128)S(1)} %all-to-all-done.recv, f32[2,88,128]{2,1,0:T(8,128)S(1)} %get-tuple-element.13.after_mix, f32[4,88,128]{2,1,0:T(8,128)S(1)} %collective-permute-done.after_north.north_h, f32[4,88,128]{2,1,0:T(8,128)S(1)} %collective-permute-done.1.after_south.south_h), custom_call_target="tpu_custom_call" | custom-call | tf_op jit(solution)/shard_map/collect/pallas_call | solution.py:386
  31.3 4.9 %all-to-all-start.1 = ((f32[4,144,128]{2,1,0:T(8,128)}), f32[4,144,128]{2,1,0:T(8,128)S(1)}, u32[]{:S(2)}, u32[]{:S(2)}) async-start(f32[4,144,128]{2,1,0:T(8,128)} %collect.1), calls=%async_computation.1 | async-start | bytes 589824 | tf_op jit(solution)/shard_map/all_to_all | solution.py:599
  36.1 0.7 %collective-permute-start.2 = (f32[2,88,128]{2,1,0:T(8,128)S(1)}, f32[2,88,128]{2,1,0:T(8,128)S(1)}, u32[]{:S(2)}, u32[]{:S(2)}) collective-permute-start(f32[2,88,128]{2,1,0:T(8,128)S(1)} %get-tuple-element.18), channel_id=1, source_target_pairs={{0,7},{1,0},{2,1},{3,2},{4,3},{5,4},{6,5},{7,6},{8,15},{9,8},{10,9... | collective-permute-start | bytes 270344 | tf_op jit(solution)/shard_map/ppermute | solution.py:577
  36.9 0.0 collective-permute-start.3
  36.9 2.6 %collective-permute-done.2.east = f32[2,88,128]{2,1,0:T(8,128)S(1)} collective-permute-done((f32[2,88,128]{2,1,0:T(8,128)S(1)}, f32[2,88,128]{2,1,0:T(8,128)S(1)}, u32[]{:S(2)}, u32[]{:S(2)}) %collective-permute-start.2) | collective-permute-done | bytes 90144 | tf_op jit(solution)/shard_map/ppermute | solution.py:577
  39.5 2.2 %collective-permute-done.3.west = f32[2,88,128]{2,1,0:T(8,128)S(1)} collective-permute-done((f32[2,88,128]{2,1,0:T(8,128)S(1)}, f32[2,88,128]{2,1,0:T(8,128)S(1)}, u32[]{:S(2)}, u32[]{:S(2)}) %collective-permute-start.3) | collective-permute-done | bytes 90144 | tf_op jit(solution)/shard_map/ppermute | solution.py:577
  41.7 3.1 %all-to-all-done.1.recv = f32[4,144,128]{2,1,0:T(8,128)S(1)} async-done(((f32[4,144,128]{2,1,0:T(8,128)}), f32[4,144,128]{2,1,0:T(8,128)S(1)}, u32[]{:S(2)}, u32[]{:S(2)}) %all-to-all-start.1) | async-done | bytes 294944 | tf_op jit(solution)/shard_map/all_to_all | solution.py:599
  44.8 0.0 copy-done
  44.8 0.0 copy-done.1
  44.8 0.0 copy-done.2
  44.8 10.0 %finish.1 = f32[4,80,32,128]{3,2,1,0:T(8,128)} custom-call(f32[4,144,128]{2,1,0:T(8,128)S(1)} %all-to-all-done.1.recv, s32[32,128]{1,0:T(8,128)S(1)} %copy-done.2, f32[4,32,80,128]{3,2,1,0:T(8,128)} %get-tuple-element.16.mixed_h, f32[4,88,128]{2,1,0:T(8,128)} %get-tuple-element.17.own_h, f32[4,88,128]{2,1,0:T(8,128)} %copy-done, f32[4,88,128]{2,1,0:T(8,128)} %copy-done.1, ...), custom_call_target="tpu_custom_call" | custom-call | flops 26214400 | bytes 12582912 | tf_op jit(solution)/shard_map/finish/pallas_call | solution.py:547
Async XLA Ops:
  8.7 21.3 %all-to-all-start = ((f32[8,272,128]{2,1,0:T(8,128)}), f32[8,272,128]{2,1,0:T(8,128)S(1)}, u32[]{:S(2)}, u32[]{:S(2)}) async-start(f32[8,272,128]{2,1,0:T(8,128)} %get-tuple-element.12), calls=%async_computation | async-start | bytes 2228224 | tf_op jit(solution)/shard_map/all_to_all | solution.py:591
  13.9 13.9 %collective-permute-start = (f32[4,88,128]{2,1,0:T(8,128)S(1)}, f32[4,88,128]{2,1,0:T(8,128)S(1)}, u32[]{:S(2)}, u32[]{:S(2)}) collective-permute-start(f32[4,88,128]{2,1,0:T(8,128)S(1)} %get-tuple-element.14), channel_id=1, source_target_pairs={{0,8},{8,16},{16,24},{1,9},{9,17},{17,25},{2,10},{10,18},{18,26},{... | collective-permute-start | bytes 540680 | tf_op jit(solution)/shard_map/ppermute | solution.py:577
  17.3 27.4 %copy-start.2 = (s32[32,128]{1,0:T(8,128)S(1)}, s32[32,128]{1,0:T(8,128)}, u32[]{:S(2)}) copy-start(s32[32,128]{1,0:T(8,128)} %depth_ref.1) | copy-start | bytes 49156
  17.4 10.4 %collective-permute-start.1 = (f32[4,88,128]{2,1,0:T(8,128)S(1)}, f32[4,88,128]{2,1,0:T(8,128)S(1)}, u32[]{:S(2)}, u32[]{:S(2)}) collective-permute-start(f32[4,88,128]{2,1,0:T(8,128)S(1)} %get-tuple-element.15), channel_id=1, source_target_pairs={{8,0},{16,8},{24,16},{9,1},{17,9},{25,17},{10,2},{18,10},{26,18},{... | collective-permute-start | bytes 540680 | tf_op jit(solution)/shard_map/ppermute | solution.py:577
  27.7 17.0 %copy-start = (f32[4,88,128]{2,1,0:T(8,128)}, f32[4,88,128]{2,1,0:T(8,128)S(1)}, u32[]{:S(2)}) copy-start(f32[4,88,128]{2,1,0:T(8,128)S(1)} %collective-permute-done.after_north.north_h) | copy-start | bytes 540676
  27.8 17.0 %copy-start.1 = (f32[4,88,128]{2,1,0:T(8,128)}, f32[4,88,128]{2,1,0:T(8,128)S(1)}, u32[]{:S(2)}) copy-start(f32[4,88,128]{2,1,0:T(8,128)S(1)} %collective-permute-done.1.after_south.south_h) | copy-start | bytes 540676
  31.3 13.5 %all-to-all-start.1 = ((f32[4,144,128]{2,1,0:T(8,128)}), f32[4,144,128]{2,1,0:T(8,128)S(1)}, u32[]{:S(2)}, u32[]{:S(2)}) async-start(f32[4,144,128]{2,1,0:T(8,128)} %collect.1), calls=%async_computation.1 | async-start | bytes 589824 | tf_op jit(solution)/shard_map/all_to_all | solution.py:599
  36.1 3.3 %collective-permute-start.2 = (f32[2,88,128]{2,1,0:T(8,128)S(1)}, f32[2,88,128]{2,1,0:T(8,128)S(1)}, u32[]{:S(2)}, u32[]{:S(2)}) collective-permute-start(f32[2,88,128]{2,1,0:T(8,128)S(1)} %get-tuple-element.18), channel_id=1, source_target_pairs={{0,7},{1,0},{2,1},{3,2},{4,3},{5,4},{6,5},{7,6},{8,15},{9,8},{10,9... | collective-permute-start | bytes 270344 | tf_op jit(solution)/shard_map/ppermute | solution.py:577
  36.9 4.9 %collective-permute-start.3 = (f32[2,88,128]{2,1,0:T(8,128)S(1)}, f32[2,88,128]{2,1,0:T(8,128)S(1)}, u32[]{:S(2)}, u32[]{:S(2)}) collective-permute-start(f32[2,88,128]{2,1,0:T(8,128)S(1)} %get-tuple-element.13.after_mix), channel_id=1, source_target_pairs={{0,1},{1,2},{2,3},{3,4},{4,5},{5,6},{6,7},{7,0},{8,9},{9,10},{10,1... | collective-permute-start | bytes 270344 | tf_op jit(solution)/shard_map/ppermute | solution.py:577

commit v13 on v12

--- a/solution.py
+++ b/solution.py
@@ -468,11 +468,10 @@
 
     both = jnp.where((square_row == square_lane + 1) | (square_row == square_lane - 1), 1.0, 0.0).astype(bf16)
     both = jnp.concatenate([both, both], axis=0)
-    nothing = jnp.zeros((LANES, LANES), f32)
-    ends = (square_lane == jnp.where(square_row % 2 == 0, LANES - 1, 0)).astype(f32)
-    spread = jnp.concatenate(
-        [jnp.concatenate([nothing + 1.0, nothing], axis=1), jnp.concatenate([nothing, ends], axis=1)], axis=0
+    spread = jnp.where(
+        iota((2 * SUB, SUB * LANES), 0) // 2 == iota((2 * SUB, SUB * LANES), 1) // LANES, 1.0, 0.0
     ).astype(bf16)
+    ends = (lanes == 0) | (lanes == LANES - 1)
 
     def field(q, carry):
         @pl.when(q + 1 < fields)
@@ -483,8 +482,6 @@
         z[0] = z_north[q]
         z[oy + 1] = z_south[q]
         edge = halo[q]
-        high = edge.astype(bf16).astype(f32)
-        edge = jnp.where(lanes < HALF, high, pltpu.roll(edge - high, HALF, 1))
         names = own[q, 0:levels]
         high = names.astype(bf16).astype(f32)
         names = jnp.where(even, high, names - high)
@@ -492,46 +489,31 @@
         def solve(c):
             load(q, c).wait()
             rows_here = range(c * SUB, (c + 1) * SUB)
-            places = jnp.concatenate(
-                [
-                    jnp.concatenate(
-                        [
-                            jnp.where(lanes // 2 == HALF // 2 + r, names, 0.0).astype(bf16),
-                            jnp.where((lanes % HALF) // 2 == r, edge, 0.0).astype(bf16),
-                        ],
-                        axis=1,
-                    )
-                    for r in rows_here
-                ],
-                axis=0,
-            )
-            placed = matmul(places, spread)
-            first = placed[:, :LANES]
+            here = pltpu.roll(names, (HALF - 2 * SUB * c) % LANES, 1)[:, 0 : 2 * SUB].astype(bf16)
+            first = matmul(here, spread)
             for i, r in enumerate(rows_here):
-                first_here = first[i * levels : (i + 1) * levels]
+                first_here = first[:, i * LANES : (i + 1) * LANES]
                 forced = mixed[q, r] + first_here * forcing[pl.ds(q * oy + r, 1), :]
                 z[r + 1] = jnp.where(level < depth_ref[r : r + 1, :], forced, 0.0)
-            return placed[:, LANES:]
-
-        def diffuse(c, outside):
+
+        def diffuse(c):
             start = c * SUB
             high, low = split(z[start + 1 : start + 1 + SUB].reshape(SUB * levels, LANES))
             sides = matmul(jnp.concatenate([high, low], axis=1), both)
             for i in range(SUB):
                 r = start + i
-                here = slice(i * levels, (i + 1) * levels)
-                around = (z[r] + z[r + 2]) + (sides[here] + outside[here])
+                outside = jnp.where(ends, pltpu.roll(edge, LANES - 1 - 2 * r, 1), 0.0)
+                around = (z[r] + z[r + 2]) + (sides[i * levels : (i + 1) * levels] + outside)
                 active = level < depth_ref[r : r + 1, :]
                 stage[q, r] = jnp.where(active, z[r + 1] * keep[r] + diffusion_rate * around, mixed[q, r])
             for r in range(start, start + SUB):
                 pltpu.make_async_copy(stage.at[q, r], out_h.at[q, :, r, :], out_sems.at[q]).start()
 
-        outside = solve(0)
+        solve(0)
         for c in range(1, oy // SUB):
-            following = solve(c)
-            diffuse(c - 1, outside)
-            outside = following
-        diffuse(oy // SUB - 1, outside)
+            solve(c)
+            diffuse(c - 1)
+        diffuse(oy // SUB - 1)
         return carry
 
     lax.fori_loop(0, fields, field, 0)

time: 55.1 us -> 55.5 us (level)
  transfers between devices with their start and end apart: 6 -> 6, of which waited for: 4 -> 4; matrix products, arithmetic and copies ran while one was open for 0% -> 0% of each run, Pallas kernels for 17% -> 16%
where the time goes in v13:
time: 55.5 us; the launch traced here: 55.1 us
  Pallas kernels  29.3 us (53%)
  starting transfers between devices  15.5 us (28%)
  waiting for transfers between devices  10.1 us (18%)
    pallas_call x1, Pallas kernels, finish(): pl.pallas_call(finish_kernel, in_specs=[VMEM] * 2 + [HBM] * 4 + [VMEM] *...  10.3 us
    pallas_call x1, Pallas kernels, mix(): pl.pallas_call(mix_kernel, in_specs=[HBM] * 3, out_specs=[HBM] * 2 + [VME...  9.06 us
    pallas_call x1, Pallas kernels, regrid(): pl.pallas_call(functools.partial(regrid_kernel, cap, lat, lon, oy, batch)...  8.66 us
    ppermute x4, starting transfers between devices, shift(): return lax.ppermute(x, axis, pairs)  5.48 us
    all_to_all x1, starting transfers between devices, on_device(): in_plane = lax.all_to_all(slots, 'lon', 0, 0, tiled=True)  5.19 us
    all_to_all x1, starting transfers between devices, on_device(): lax.all_to_all(collect(cap, fields, oy, lat, in_plane, (to_east, *halos[0...  4.87 us
    ppermute x4, waiting for transfers between devices, shift(): return lax.ppermute(x, axis, pairs)  4.85 us
    all_to_all x1, waiting for transfers between devices, on_device(): lax.all_to_all(collect(cap, fields, oy, lat, in_plane, (to_east, *halos[0...  3.06 us
  transfers between devices with their start and end apart: 6, of which 4 were waited for; matrix products, arithmetic and copies ran while one was open for 0% of the time, Pallas kernels for 16%

profile of v13, /device:TPU:0, one launch (start us, length us, event | category | flops | bytes accessed | tf_op | source)
XLA Modules:
  0.0 55.1 jit_solution(6257964505710099653)
XLA Ops:
  0.0 8.7 %regrid.1 = (f32[8,272,128]{2,1,0:T(8,128)}, f32[4,88,128]{2,1,0:T(8,128)S(1)}, f32[4,88,128]{2,1,0:T(8,128)S(1)}) custom-call(s32[256]{0:T(256)} %src_h.1, s32[256]{0:T(256)} %bitcast.1, s32[256]{0:T(256)} %blk_h.1, f32[4,8]{1,0:T(4,128)} %coupling_h.1, bf16[8,64,128]{2,1,0:T(8,128)(2,1)} %atm_h.1, s32[64,128]{1,0:T(8,128)} %mask_h.1, ...), custom_call_target="tpu_custom_call" | custom-call | flops 67108864 | bytes 10485760 | tf_op jit(solution)/shard_map/regrid/pallas_call | solution.py:225
  8.7 5.2 %all-to-all-start = ((f32[8,272,128]{2,1,0:T(8,128)}), f32[8,272,128]{2,1,0:T(8,128)S(1)}, u32[]{:S(2)}, u32[]{:S(2)}) async-start(f32[8,272,128]{2,1,0:T(8,128)} %get-tuple-element.12), calls=%async_computation | async-start | bytes 2228224 | tf_op jit(solution)/shard_map/all_to_all | solution.py:573
  13.9 3.5 %collective-permute-start = (f32[4,88,128]{2,1,0:T(8,128)S(1)}, f32[4,88,128]{2,1,0:T(8,128)S(1)}, u32[]{:S(2)}, u32[]{:S(2)}) collective-permute-start(f32[4,88,128]{2,1,0:T(8,128)S(1)} %get-tuple-element.14), channel_id=1, source_target_pairs={{0,8},{8,16},{16,24},{1,9},{9,17},{17,25},{2,10},{10,18},{18,26},{... | collective-permute-start | bytes 540680 | tf_op jit(solution)/shard_map/ppermute | solution.py:559
  17.3 0.0 copy-start.2
  17.4 1.3 %collective-permute-start.1 = (f32[4,88,128]{2,1,0:T(8,128)S(1)}, f32[4,88,128]{2,1,0:T(8,128)S(1)}, u32[]{:S(2)}, u32[]{:S(2)}) collective-permute-start(f32[4,88,128]{2,1,0:T(8,128)S(1)} %get-tuple-element.15), channel_id=1, source_target_pairs={{8,0},{16,8},{24,16},{9,1},{17,9},{25,17},{10,2},{18,10},{26,18},{... | collective-permute-start | bytes 540680 | tf_op jit(solution)/shard_map/ppermute | solution.py:559
  18.7 9.1 %mix.1 = (f32[4,32,80,128]{3,2,1,0:T(8,128)}, f32[4,88,128]{2,1,0:T(8,128)}, f32[2,88,128]{2,1,0:T(8,128)S(1)}, f32[2,88,128]{2,1,0:T(8,128)S(1)}) custom-call(s32[32,128]{1,0:T(8,128)} %depth_ref.1, f32[4,80,32,128]{3,2,1,0:T(8,128)} %state_h.3, f32[4,32,1,80,80]{4,3,2,1,0:T(8,128)} %inv_h.3), custom_call_target="tpu_custom_call" | custom-call | flops 838860800 | bytes 16777216 | tf_op jit(solution)/shard_map/mix/pallas_call | solution.py:319
  27.7 0.0 collective-permute-done.after_north.north_h
  27.7 0.0 copy-start
  27.7 0.0 collective-permute-done.1.after_south.south_h
  27.8 0.0 copy-start.1
  27.8 2.2 %all-to-all-done.recv = f32[8,272,128]{2,1,0:T(8,128)S(1)} async-done(((f32[8,272,128]{2,1,0:T(8,128)}), f32[8,272,128]{2,1,0:T(8,128)S(1)}, u32[]{:S(2)}, u32[]{:S(2)}) %all-to-all-start) | async-done | bytes 1114144 | tf_op jit(solution)/shard_map/all_to_all | solution.py:573
  30.0 1.3 %collect.1 = f32[4,144,128]{2,1,0:T(8,128)} custom-call(f32[8,272,128]{2,1,0:T(8,128)S(1)} %all-to-all-done.recv, f32[2,88,128]{2,1,0:T(8,128)S(1)} %get-tuple-element.13.after_mix, f32[4,88,128]{2,1,0:T(8,128)S(1)} %collective-permute-done.after_north.north_h, f32[4,88,128]{2,1,0:T(8,128)S(1)} %collective-permute-done.1.after_south.south_h), custom_call_target="tpu_custom_call" | custom-call | tf_op jit(solution)/shard_map/collect/pallas_call | solution.py:386
  31.3 4.9 %all-to-all-start.1 = ((f32[4,144,128]{2,1,0:T(8,128)}), f32[4,144,128]{2,1,0:T(8,128)S(1)}, u32[]{:S(2)}, u32[]{:S(2)}) async-start(f32[4,144,128]{2,1,0:T(8,128)} %collect.1), calls=%async_computation.1 | async-start | bytes 589824 | tf_op jit(solution)/shard_map/all_to_all | solution.py:581
  36.1 0.7 %collective-permute-start.2 = (f32[2,88,128]{2,1,0:T(8,128)S(1)}, f32[2,88,128]{2,1,0:T(8,128)S(1)}, u32[]{:S(2)}, u32[]{:S(2)}) collective-permute-start(f32[2,88,128]{2,1,0:T(8,128)S(1)} %get-tuple-element.18), channel_id=1, source_target_pairs={{0,7},{1,0},{2,1},{3,2},{4,3},{5,4},{6,5},{7,6},{8,15},{9,8},{10,9... | collective-permute-start | bytes 270344 | tf_op jit(solution)/shard_map/ppermute | solution.py:559
  36.8 0.0 collective-permute-start.3
  36.9 2.6 %collective-permute-done.2.east = f32[2,88,128]{2,1,0:T(8,128)S(1)} collective-permute-done((f32[2,88,128]{2,1,0:T(8,128)S(1)}, f32[2,88,128]{2,1,0:T(8,128)S(1)}, u32[]{:S(2)}, u32[]{:S(2)}) %collective-permute-start.2) | collective-permute-done | bytes 90144 | tf_op jit(solution)/shard_map/ppermute | solution.py:559
  39.5 2.2 %collective-permute-done.3.west = f32[2,88,128]{2,1,0:T(8,128)S(1)} collective-permute-done((f32[2,88,128]{2,1,0:T(8,128)S(1)}, f32[2,88,128]{2,1,0:T(8,128)S(1)}, u32[]{:S(2)}, u32[]{:S(2)}) %collective-permute-start.3) | collective-permute-done | bytes 90144 | tf_op jit(solution)/shard_map/ppermute | solution.py:559
  41.7 3.1 %all-to-all-done.1.recv = f32[4,144,128]{2,1,0:T(8,128)S(1)} async-done(((f32[4,144,128]{2,1,0:T(8,128)}), f32[4,144,128]{2,1,0:T(8,128)S(1)}, u32[]{:S(2)}, u32[]{:S(2)}) %all-to-all-start.1) | async-done | bytes 294944 | tf_op jit(solution)/shard_map/all_to_all | solution.py:581
  44.8 0.0 copy-done
  44.8 0.0 copy-done.1
  44.8 0.0 copy-done.2
  44.8 10.3 %finish.1 = f32[4,80,32,128]{3,2,1,0:T(8,128)} custom-call(f32[4,144,128]{2,1,0:T(8,128)S(1)} %all-to-all-done.1.recv, s32[32,128]{1,0:T(8,128)S(1)} %copy-done.2, f32[4,32,80,128]{3,2,1,0:T(8,128)} %get-tuple-element.16.mixed_h, f32[4,88,128]{2,1,0:T(8,128)} %get-tuple-element.17.own_h, f32[4,88,128]{2,1,0:T(8,128)} %copy-done, f32[4,88,128]{2,1,0:T(8,128)} %copy-done.1, ...), custom_call_target="tpu_custom_call" | custom-call | flops 26214400 | bytes 12582912 | tf_op jit(solution)/shard_map/finish/pallas_call | solution.py:529
Async XLA Ops:
  8.7 21.3 %all-to-all-start = ((f32[8,272,128]{2,1,0:T(8,128)}), f32[8,272,128]{2,1,0:T(8,128)S(1)}, u32[]{:S(2)}, u32[]{:S(2)}) async-start(f32[8,272,128]{2,1,0:T(8,128)} %get-tuple-element.12), calls=%async_computation | async-start | bytes 2228224 | tf_op jit(solution)/shard_map/all_to_all | solution.py:573
  13.9 13.9 %collective-permute-start = (f32[4,88,128]{2,1,0:T(8,128)S(1)}, f32[4,88,128]{2,1,0:T(8,128)S(1)}, u32[]{:S(2)}, u32[]{:S(2)}) collective-permute-start(f32[4,88,128]{2,1,0:T(8,128)S(1)} %get-tuple-element.14), channel_id=1, source_target_pairs={{0,8},{8,16},{16,24},{1,9},{9,17},{17,25},{2,10},{10,18},{18,26},{... | collective-permute-start | bytes 540680 | tf_op jit(solution)/shard_map/ppermute | solution.py:559
  17.3 27.4 %copy-start.2 = (s32[32,128]{1,0:T(8,128)S(1)}, s32[32,128]{1,0:T(8,128)}, u32[]{:S(2)}) copy-start(s32[32,128]{1,0:T(8,128)} %depth_ref.1) | copy-start | bytes 49156
  17.4 10.4 %collective-permute-start.1 = (f32[4,88,128]{2,1,0:T(8,128)S(1)}, f32[4,88,128]{2,1,0:T(8,128)S(1)}, u32[]{:S(2)}, u32[]{:S(2)}) collective-permute-start(f32[4,88,128]{2,1,0:T(8,128)S(1)} %get-tuple-element.15), channel_id=1, source_target_pairs={{8,0},{16,8},{24,16},{9,1},{17,9},{25,17},{10,2},{18,10},{26,18},{... | collective-permute-start | bytes 540680 | tf_op jit(solution)/shard_map/ppermute | solution.py:559
  27.7 17.0 %copy-start = (f32[4,88,128]{2,1,0:T(8,128)}, f32[4,88,128]{2,1,0:T(8,128)S(1)}, u32[]{:S(2)}) copy-start(f32[4,88,128]{2,1,0:T(8,128)S(1)} %collective-permute-done.after_north.north_h) | copy-start | bytes 540676
  27.8 17.0 %copy-start.1 = (f32[4,88,128]{2,1,0:T(8,128)}, f32[4,88,128]{2,1,0:T(8,128)S(1)}, u32[]{:S(2)}) copy-start(f32[4,88,128]{2,1,0:T(8,128)S(1)} %collective-permute-done.1.after_south.south_h) | copy-start | bytes 540676
  31.3 13.5 %all-to-all-start.1 = ((f32[4,144,128]{2,1,0:T(8,128)}), f32[4,144,128]{2,1,0:T(8,128)S(1)}, u32[]{:S(2)}, u32[]{:S(2)}) async-start(f32[4,144,128]{2,1,0:T(8,128)} %collect.1), calls=%async_computation.1 | async-start | bytes 589824 | tf_op jit(solution)/shard_map/all_to_all | solution.py:581
  36.1 3.3 %collective-permute-start.2 = (f32[2,88,128]{2,1,0:T(8,128)S(1)}, f32[2,88,128]{2,1,0:T(8,128)S(1)}, u32[]{:S(2)}, u32[]{:S(2)}) collective-permute-start(f32[2,88,128]{2,1,0:T(8,128)S(1)} %get-tuple-element.18), channel_id=1, source_target_pairs={{0,7},{1,0},{2,1},{3,2},{4,3},{5,4},{6,5},{7,6},{8,15},{9,8},{10,9... | collective-permute-start | bytes 270344 | tf_op jit(solution)/shard_map/ppermute | solution.py:559
  36.8 4.9 %collective-permute-start.3 = (f32[2,88,128]{2,1,0:T(8,128)S(1)}, f32[2,88,128]{2,1,0:T(8,128)S(1)}, u32[]{:S(2)}, u32[]{:S(2)}) collective-permute-start(f32[2,88,128]{2,1,0:T(8,128)S(1)} %get-tuple-element.13.after_mix), channel_id=1, source_target_pairs={{0,1},{1,2},{2,3},{3,4},{4,5},{5,6},{6,7},{7,0},{8,9},{9,10},{10,1... | collective-permute-start | bytes 270344 | tf_op jit(solution)/shard_map/ppermute | solution.py:559

commit v14 on v13

--- a/solution.py
+++ b/solution.py
@@ -468,9 +468,8 @@
 
     both = jnp.where((square_row == square_lane + 1) | (square_row == square_lane - 1), 1.0, 0.0).astype(bf16)
     both = jnp.concatenate([both, both], axis=0)
-    spread = jnp.where(
-        iota((2 * SUB, SUB * LANES), 0) // 2 == iota((2 * SUB, SUB * LANES), 1) // LANES, 1.0, 0.0
-    ).astype(bf16)
+    ones = jnp.ones((LANES, LANES), bf16)
+    block = 2 * SUB
     ends = (lanes == 0) | (lanes == LANES - 1)
 
     def field(q, carry):
@@ -487,33 +486,38 @@
         names = jnp.where(even, high, names - high)
 
         def solve(c):
-            load(q, c).wait()
-            rows_here = range(c * SUB, (c + 1) * SUB)
-            here = pltpu.roll(names, (HALF - 2 * SUB * c) % LANES, 1)[:, 0 : 2 * SUB].astype(bf16)
-            first = matmul(here, spread)
+            rows_here = range(c * block, (c + 1) * block)
+            for part in range(rows_here.start // SUB, rows_here.stop // SUB):
+                load(q, part).wait()
+            first = matmul(
+                jnp.concatenate(
+                    [jnp.where(lanes // 2 == HALF // 2 + r, names, 0.0).astype(bf16) for r in rows_here], axis=0
+                ),
+                ones,
+            )
             for i, r in enumerate(rows_here):
-                first_here = first[:, i * LANES : (i + 1) * LANES]
+                first_here = first[i * levels : (i + 1) * levels]
                 forced = mixed[q, r] + first_here * forcing[pl.ds(q * oy + r, 1), :]
                 z[r + 1] = jnp.where(level < depth_ref[r : r + 1, :], forced, 0.0)
 
         def diffuse(c):
-            start = c * SUB
-            high, low = split(z[start + 1 : start + 1 + SUB].reshape(SUB * levels, LANES))
+            start = c * block
+            high, low = split(z[start + 1 : start + 1 + block].reshape(block * levels, LANES))
             sides = matmul(jnp.concatenate([high, low], axis=1), both)
-            for i in range(SUB):
+            for i in range(block):
                 r = start + i
                 outside = jnp.where(ends, pltpu.roll(edge, LANES - 1 - 2 * r, 1), 0.0)
                 around = (z[r] + z[r + 2]) + (sides[i * levels : (i + 1) * levels] + outside)
                 active = level < depth_ref[r : r + 1, :]
                 stage[q, r] = jnp.where(active, z[r + 1] * keep[r] + diffusion_rate * around, mixed[q, r])
-            for r in range(start, start + SUB):
+            for r in range(start, start + block):
                 pltpu.make_async_copy(stage.at[q, r], out_h.at[q, :, r, :], out_sems.at[q]).start()
 
         solve(0)
-        for c in range(1, oy // SUB):
+        for c in range(1, oy // block):
             solve(c)
             diffuse(c - 1)
-        diffuse(oy // SUB - 1)
+        diffuse(oy // block - 1)
         return carry
 
     lax.fori_loop(0, fields, field, 0)

time: 55.5 us -> 54 us (0.973)
  Pallas kernels: 29.3 us -> 27.8 us
    pallas_call x1, Pallas kernels: 10.3 us -> 8.75 us  [finish(): pl.pallas_call(finish_kernel, in_specs=[VMEM] * 2 + [HBM] * 4 + [VMEM] *...]
  transfers between devices with their start and end apart: 6 -> 6, of which waited for: 4 -> 4; matrix products, arithmetic and copies ran while one was open for 0% -> 0% of each run, Pallas kernels for 16% -> 17%
where the time goes in v14:
time: 54 us; the launch traced here: 53.5 us
  Pallas kernels  27.8 us (51%)
  starting transfers between devices  15.5 us (29%)
  waiting for transfers between devices  10.1 us (19%)
    pallas_call x1, Pallas kernels, mix(): pl.pallas_call(mix_kernel, in_specs=[HBM] * 3, out_specs=[HBM] * 2 + [VME...  9.06 us
    pallas_call x1, Pallas kernels, finish(): pl.pallas_call(finish_kernel, in_specs=[VMEM] * 2 + [HBM] * 4 + [VMEM] *...  8.75 us
    pallas_call x1, Pallas kernels, regrid(): pl.pallas_call(functools.partial(regrid_kernel, cap, lat, lon, oy, batch)...  8.66 us
    ppermute x4, starting transfers between devices, shift(): return lax.ppermute(x, axis, pairs)  5.48 us
    all_to_all x1, starting transfers between devices, on_device(): in_plane = lax.all_to_all(slots, 'lon', 0, 0, tiled=True)  5.19 us
    all_to_all x1, starting transfers between devices, on_device(): lax.all_to_all(collect(cap, fields, oy, lat, in_plane, (to_east, *halos[0...  4.87 us
    ppermute x4, waiting for transfers between devices, shift(): return lax.ppermute(x, axis, pairs)  4.85 us
    all_to_all x1, waiting for transfers between devices, on_device(): lax.all_to_all(collect(cap, fields, oy, lat, in_plane, (to_east, *halos[0...  3.06 us
  transfers between devices with their start and end apart: 6, of which 4 were waited for; matrix products, arithmetic and copies ran while one was open for 0% of the time, Pallas kernels for 17%

profile of v14, /device:TPU:0, one launch (start us, length us, event | category | flops | bytes accessed | tf_op | source)
XLA Modules:
  0.0 53.5 jit_solution(2554104616590089526)
XLA Ops:
  0.0 8.7 %regrid.1 = (f32[8,272,128]{2,1,0:T(8,128)}, f32[4,88,128]{2,1,0:T(8,128)S(1)}, f32[4,88,128]{2,1,0:T(8,128)S(1)}) custom-call(s32[256]{0:T(256)} %src_h.1, s32[256]{0:T(256)} %bitcast.1, s32[256]{0:T(256)} %blk_h.1, f32[4,8]{1,0:T(4,128)} %coupling_h.1, bf16[8,64,128]{2,1,0:T(8,128)(2,1)} %atm_h.1, s32[64,128]{1,0:T(8,128)} %mask_h.1, ...), custom_call_target="tpu_custom_call" | custom-call | flops 67108864 | bytes 10485760 | tf_op jit(solution)/shard_map/regrid/pallas_call | solution.py:225
  8.7 5.2 %all-to-all-start = ((f32[8,272,128]{2,1,0:T(8,128)}), f32[8,272,128]{2,1,0:T(8,128)S(1)}, u32[]{:S(2)}, u32[]{:S(2)}) async-start(f32[8,272,128]{2,1,0:T(8,128)} %get-tuple-element.12), calls=%async_computation | async-start | bytes 2228224 | tf_op jit(solution)/shard_map/all_to_all | solution.py:577
  13.9 3.5 %collective-permute-start = (f32[4,88,128]{2,1,0:T(8,128)S(1)}, f32[4,88,128]{2,1,0:T(8,128)S(1)}, u32[]{:S(2)}, u32[]{:S(2)}) collective-permute-start(f32[4,88,128]{2,1,0:T(8,128)S(1)} %get-tuple-element.14), channel_id=1, source_target_pairs={{0,8},{8,16},{16,24},{1,9},{9,17},{17,25},{2,10},{10,18},{18,26},{... | collective-permute-start | bytes 540680 | tf_op jit(solution)/shard_map/ppermute | solution.py:563
  17.3 0.0 copy-start.2
  17.4 1.3 %collective-permute-start.1 = (f32[4,88,128]{2,1,0:T(8,128)S(1)}, f32[4,88,128]{2,1,0:T(8,128)S(1)}, u32[]{:S(2)}, u32[]{:S(2)}) collective-permute-start(f32[4,88,128]{2,1,0:T(8,128)S(1)} %get-tuple-element.15), channel_id=1, source_target_pairs={{8,0},{16,8},{24,16},{9,1},{17,9},{25,17},{10,2},{18,10},{26,18},{... | collective-permute-start | bytes 540680 | tf_op jit(solution)/shard_map/ppermute | solution.py:563
  18.7 9.1 %mix.1 = (f32[4,32,80,128]{3,2,1,0:T(8,128)}, f32[4,88,128]{2,1,0:T(8,128)}, f32[2,88,128]{2,1,0:T(8,128)S(1)}, f32[2,88,128]{2,1,0:T(8,128)S(1)}) custom-call(s32[32,128]{1,0:T(8,128)} %depth_ref.1, f32[4,80,32,128]{3,2,1,0:T(8,128)} %state_h.3, f32[4,32,1,80,80]{4,3,2,1,0:T(8,128)} %inv_h.3), custom_call_target="tpu_custom_call" | custom-call | flops 838860800 | bytes 16777216 | tf_op jit(solution)/shard_map/mix/pallas_call | solution.py:319
  27.7 0.0 collective-permute-done.after_north.north_h
  27.7 0.0 copy-start
  27.7 0.0 collective-permute-done.1.after_south.south_h
  27.8 0.0 copy-start.1
  27.8 2.2 %all-to-all-done.recv = f32[8,272,128]{2,1,0:T(8,128)S(1)} async-done(((f32[8,272,128]{2,1,0:T(8,128)}), f32[8,272,128]{2,1,0:T(8,128)S(1)}, u32[]{:S(2)}, u32[]{:S(2)}) %all-to-all-start) | async-done | bytes 1114144 | tf_op jit(solution)/shard_map/all_to_all | solution.py:577
  30.0 1.3 %collect.1 = f32[4,144,128]{2,1,0:T(8,128)} custom-call(f32[8,272,128]{2,1,0:T(8,128)S(1)} %all-to-all-done.recv, f32[2,88,128]{2,1,0:T(8,128)S(1)} %get-tuple-element.13.after_mix, f32[4,88,128]{2,1,0:T(8,128)S(1)} %collective-permute-done.after_north.north_h, f32[4,88,128]{2,1,0:T(8,128)S(1)} %collective-permute-done.1.after_south.south_h), custom_call_target="tpu_custom_call" | custom-call | tf_op jit(solution)/shard_map/collect/pallas_call | solution.py:386
  31.3 4.9 %all-to-all-start.1 = ((f32[4,144,128]{2,1,0:T(8,128)}), f32[4,144,128]{2,1,0:T(8,128)S(1)}, u32[]{:S(2)}, u32[]{:S(2)}) async-start(f32[4,144,128]{2,1,0:T(8,128)} %collect.1), calls=%async_computation.1 | async-start | bytes 589824 | tf_op jit(solution)/shard_map/all_to_all | solution.py:585
  36.1 0.7 %collective-permute-start.2 = (f32[2,88,128]{2,1,0:T(8,128)S(1)}, f32[2,88,128]{2,1,0:T(8,128)S(1)}, u32[]{:S(2)}, u32[]{:S(2)}) collective-permute-start(f32[2,88,128]{2,1,0:T(8,128)S(1)} %get-tuple-element.18), channel_id=1, source_target_pairs={{0,7},{1,0},{2,1},{3,2},{4,3},{5,4},{6,5},{7,6},{8,15},{9,8},{10,9... | collective-permute-start | bytes 270344 | tf_op jit(solution)/shard_map/ppermute | solution.py:563
  36.9 0.0 collective-permute-start.3
  36.9 2.6 %collective-permute-done.2.east = f32[2,88,128]{2,1,0:T(8,128)S(1)} collective-permute-done((f32[2,88,128]{2,1,0:T(8,128)S(1)}, f32[2,88,128]{2,1,0:T(8,128)S(1)}, u32[]{:S(2)}, u32[]{:S(2)}) %collective-permute-start.2) | collective-permute-done | bytes 90144 | tf_op jit(solution)/shard_map/ppermute | solution.py:563
  39.5 2.2 %collective-permute-done.3.west = f32[2,88,128]{2,1,0:T(8,128)S(1)} collective-permute-done((f32[2,88,128]{2,1,0:T(8,128)S(1)}, f32[2,88,128]{2,1,0:T(8,128)S(1)}, u32[]{:S(2)}, u32[]{:S(2)}) %collective-permute-start.3) | collective-permute-done | bytes 90144 | tf_op jit(solution)/shard_map/ppermute | solution.py:563
  41.7 3.1 %all-to-all-done.1.recv = f32[4,144,128]{2,1,0:T(8,128)S(1)} async-done(((f32[4,144,128]{2,1,0:T(8,128)}), f32[4,144,128]{2,1,0:T(8,128)S(1)}, u32[]{:S(2)}, u32[]{:S(2)}) %all-to-all-start.1) | async-done | bytes 294944 | tf_op jit(solution)/shard_map/all_to_all | solution.py:585
  44.8 0.0 copy-done
  44.8 0.0 copy-done.1
  44.8 0.0 copy-done.2
  44.8 8.7 %finish.1 = f32[4,80,32,128]{3,2,1,0:T(8,128)} custom-call(f32[4,144,128]{2,1,0:T(8,128)S(1)} %all-to-all-done.1.recv, s32[32,128]{1,0:T(8,128)S(1)} %copy-done.2, f32[4,32,80,128]{3,2,1,0:T(8,128)} %get-tuple-element.16.mixed_h, f32[4,88,128]{2,1,0:T(8,128)} %get-tuple-element.17.own_h, f32[4,88,128]{2,1,0:T(8,128)} %copy-done, f32[4,88,128]{2,1,0:T(8,128)} %copy-done.1, ...), custom_call_target="tpu_custom_call" | custom-call | flops 26214400 | bytes 12582912 | tf_op jit(solution)/shard_map/finish/pallas_call | solution.py:533
Async XLA Ops:
  8.7 21.3 %all-to-all-start = ((f32[8,272,128]{2,1,0:T(8,128)}), f32[8,272,128]{2,1,0:T(8,128)S(1)}, u32[]{:S(2)}, u32[]{:S(2)}) async-start(f32[8,272,128]{2,1,0:T(8,128)} %get-tuple-element.12), calls=%async_computation | async-start | bytes 2228224 | tf_op jit(solution)/shard_map/all_to_all | solution.py:577
  13.9 13.9 %collective-permute-start = (f32[4,88,128]{2,1,0:T(8,128)S(1)}, f32[4,88,128]{2,1,0:T(8,128)S(1)}, u32[]{:S(2)}, u32[]{:S(2)}) collective-permute-start(f32[4,88,128]{2,1,0:T(8,128)S(1)} %get-tuple-element.14), channel_id=1, source_target_pairs={{0,8},{8,16},{16,24},{1,9},{9,17},{17,25},{2,10},{10,18},{18,26},{... | collective-permute-start | bytes 540680 | tf_op jit(solution)/shard_map/ppermute | solution.py:563
  17.3 27.4 %copy-start.2 = (s32[32,128]{1,0:T(8,128)S(1)}, s32[32,128]{1,0:T(8,128)}, u32[]{:S(2)}) copy-start(s32[32,128]{1,0:T(8,128)} %depth_ref.1) | copy-start | bytes 49156
  17.4 10.4 %collective-permute-start.1 = (f32[4,88,128]{2,1,0:T(8,128)S(1)}, f32[4,88,128]{2,1,0:T(8,128)S(1)}, u32[]{:S(2)}, u32[]{:S(2)}) collective-permute-start(f32[4,88,128]{2,1,0:T(8,128)S(1)} %get-tuple-element.15), channel_id=1, source_target_pairs={{8,0},{16,8},{24,16},{9,1},{17,9},{25,17},{10,2},{18,10},{26,18},{... | collective-permute-start | bytes 540680 | tf_op jit(solution)/shard_map/ppermute | solution.py:563
  27.7 17.0 %copy-start = (f32[4,88,128]{2,1,0:T(8,128)}, f32[4,88,128]{2,1,0:T(8,128)S(1)}, u32[]{:S(2)}) copy-start(f32[4,88,128]{2,1,0:T(8,128)S(1)} %collective-permute-done.after_north.north_h) | copy-start | bytes 540676
  27.8 17.0 %copy-start.1 = (f32[4,88,128]{2,1,0:T(8,128)}, f32[4,88,128]{2,1,0:T(8,128)S(1)}, u32[]{:S(2)}) copy-start(f32[4,88,128]{2,1,0:T(8,128)S(1)} %collective-permute-done.1.after_south.south_h) | copy-start | bytes 540676
  31.3 13.5 %all-to-all-start.1 = ((f32[4,144,128]{2,1,0:T(8,128)}), f32[4,144,128]{2,1,0:T(8,128)S(1)}, u32[]{:S(2)}, u32[]{:S(2)}) async-start(f32[4,144,128]{2,1,0:T(8,128)} %collect.1), calls=%async_computation.1 | async-start | bytes 589824 | tf_op jit(solution)/shard_map/all_to_all | solution.py:585
  36.1 3.3 %collective-permute-start.2 = (f32[2,88,128]{2,1,0:T(8,128)S(1)}, f32[2,88,128]{2,1,0:T(8,128)S(1)}, u32[]{:S(2)}, u32[]{:S(2)}) collective-permute-start(f32[2,88,128]{2,1,0:T(8,128)S(1)} %get-tuple-element.18), channel_id=1, source_target_pairs={{0,7},{1,0},{2,1},{3,2},{4,3},{5,4},{6,5},{7,6},{8,15},{9,8},{10,9... | collective-permute-start | bytes 270344 | tf_op jit(solution)/shard_map/ppermute | solution.py:563
  36.9 4.9 %collective-permute-start.3 = (f32[2,88,128]{2,1,0:T(8,128)S(1)}, f32[2,88,128]{2,1,0:T(8,128)S(1)}, u32[]{:S(2)}, u32[]{:S(2)}) collective-permute-start(f32[2,88,128]{2,1,0:T(8,128)S(1)} %get-tuple-element.13.after_mix), channel_id=1, source_target_pairs={{0,1},{1,2},{2,3},{3,4},{4,5},{5,6},{6,7},{7,0},{8,9},{9,10},{10,1... | collective-permute-start | bytes 270344 | tf_op jit(solution)/shard_map/ppermute | solution.py:563

commit v15 on v14

--- a/solution.py
+++ b/solution.py
@@ -143,6 +143,8 @@
     bits = lon.bit_length() - 1
 
     def place(d):
+        if isinstance(d, int):
+            return d // lon, d % lon
         if lon == 1 << bits:
             return lax.shift_right_logical(d, bits), d & (lon - 1)
         return lax.div(d, lon), lax.rem(d, lon)
@@ -153,7 +155,7 @@
 
     def slots(d):
         a, b = place(d)
-        return padded_rows(out[b, pl.ds(pl.multiple_of(a * per, per), per), :], HALF)
+        return padded_rows(out[b, a * per : (a + 1) * per, :], HALF)
 
     def part(k, carry):
         big(k).wait()
@@ -194,8 +196,8 @@
         last_swapped = pltpu.roll(turned[LANES - SUB : LANES], HALF, 1)[SUB - 1 : SUB]
         for u in range(2):
             _, b = place(d + u)
-            east = jnp.where(b == lon - 1, d + u - (lon - 1), d + u + 1)
-            west = jnp.where(b == 0, d + u + (lon - 1), d + u - 1)
+            east = d + u - b + (b + 1) % lon
+            west = d + u - b + (b - 1) % lon
             out[extra(d + u, 0)] = ids[pl.ds(d + u, 1), :].astype(f32)
             sides = jnp.where(lane < HALF, ids[pl.ds(east, 1), :], ids[pl.ds(west, 1), :])
             out[extra(d + u, 1)] = sides.astype(f32)
@@ -204,12 +206,8 @@
             column = last_swapped if u == 0 else last
             out[extra(east, 2)] = jnp.where(lane < HALF, out[extra(east, 2)], column)
 
-    def halos(k, carry):
-        for u in range(4):
-            halo(k * 4 + u)
-        return carry
-
-    lax.fori_loop(0, devices // 8, halos, 0)
+    for k in range(devices // 2):
+        halo(k)
     send(1, slot_rows, out.shape[1]).start()
     send(0, 0, slot_rows).wait()
     send(1, slot_rows, out.shape[1]).wait()
@@ -491,7 +489,7 @@
                 load(q, part).wait()
             first = matmul(
                 jnp.concatenate(
-                    [jnp.where(lanes // 2 == HALF // 2 + r, names, 0.0).astype(bf16) for r in rows_here], axis=0
+                    [(names * jnp.where(line // 2 == HALF // 2 + r, 1.0, 0.0)).astype(bf16) for r in rows_here], axis=0
                 ),
                 ones,
             )

time: 54 us -> 51.6 us (0.956)
  Pallas kernels: 27.8 us -> 25.4 us
    pallas_call x1, Pallas kernels: 8.66 us -> 6.27 us  [regrid(): pl.pallas_call(functools.partial(regrid_kernel, cap, lat, lon, oy, batch)...]
  transfers between devices with their start and end apart: 6 -> 6, of which waited for: 4 -> 4; matrix products, arithmetic and copies ran while one was open for 0% -> 0% of each run, Pallas kernels for 17% -> 18%
where the time goes in v15:
time: 51.6 us; the launch traced here: 51.2 us
  Pallas kernels  25.4 us (49%)
  starting transfers between devices  15.5 us (30%)
  waiting for transfers between devices  10.1 us (20%)
    pallas_call x1, Pallas kernels, mix(): pl.pallas_call(mix_kernel, in_specs=[HBM] * 3, out_specs=[HBM] * 2 + [VME...  9.06 us
    pallas_call x1, Pallas kernels, finish(): pl.pallas_call(finish_kernel, in_specs=[VMEM] * 2 + [HBM] * 4 + [VMEM] *...  8.77 us
    pallas_call x1, Pallas kernels, regrid(): pl.pallas_call(functools.partial(regrid_kernel, cap, lat, lon, oy, batch)...  6.27 us
    ppermute x4, starting transfers between devices, shift(): return lax.ppermute(x, axis, pairs)  5.48 us
    all_to_all x1, starting transfers between devices, on_device(): in_plane = lax.all_to_all(slots, 'lon', 0, 0, tiled=True)  5.19 us
    all_to_all x1, starting transfers between devices, on_device(): lax.all_to_all(collect(cap, fields, oy, lat, in_plane, (to_east, *halos[0...  4.87 us
    ppermute x4, waiting for transfers between devices, shift(): return lax.ppermute(x, axis, pairs)  4.85 us
    all_to_all x1, waiting for transfers between devices, on_device(): lax.all_to_all(collect(cap, fields, oy, lat, in_plane, (to_east, *halos[0...  3.06 us
  transfers between devices with their start and end apart: 6, of which 4 were waited for; matrix products, arithmetic and copies ran while one was open for 0% of the time, Pallas kernels for 18%

profile of v15, /device:TPU:0, one launch (start us, length us, event | category | flops | bytes accessed | tf_op | source)
XLA Modules:
  0.0 51.2 jit_solution(2434229472963313283)
XLA Ops:
  0.0 6.3 %regrid.1 = (f32[8,272,128]{2,1,0:T(8,128)}, f32[4,88,128]{2,1,0:T(8,128)S(1)}, f32[4,88,128]{2,1,0:T(8,128)S(1)}) custom-call(s32[256]{0:T(256)} %src_h.1, s32[256]{0:T(256)} %bitcast.1, s32[256]{0:T(256)} %blk_h.1, f32[4,8]{1,0:T(4,128)} %coupling_h.1, bf16[8,64,128]{2,1,0:T(8,128)(2,1)} %atm_h.1, s32[64,128]{1,0:T(8,128)} %mask_h.1, ...), custom_call_target="tpu_custom_call" | custom-call | flops 67108864 | bytes 10485760 | tf_op jit(solution)/shard_map/regrid/pallas_call | solution.py:223
  6.3 5.2 %all-to-all-start = ((f32[8,272,128]{2,1,0:T(8,128)}), f32[8,272,128]{2,1,0:T(8,128)S(1)}, u32[]{:S(2)}, u32[]{:S(2)}) async-start(f32[8,272,128]{2,1,0:T(8,128)} %get-tuple-element.12), calls=%async_computation | async-start | bytes 2228224 | tf_op jit(solution)/shard_map/all_to_all | solution.py:575
  11.5 3.5 %collective-permute-start = (f32[4,88,128]{2,1,0:T(8,128)S(1)}, f32[4,88,128]{2,1,0:T(8,128)S(1)}, u32[]{:S(2)}, u32[]{:S(2)}) collective-permute-start(f32[4,88,128]{2,1,0:T(8,128)S(1)} %get-tuple-element.14), channel_id=1, source_target_pairs={{0,8},{8,16},{16,24},{1,9},{9,17},{17,25},{2,10},{10,18},{18,26},{... | collective-permute-start | bytes 540680 | tf_op jit(solution)/shard_map/ppermute | solution.py:561
  15.0 0.0 copy-start.2
  15.0 1.3 %collective-permute-start.1 = (f32[4,88,128]{2,1,0:T(8,128)S(1)}, f32[4,88,128]{2,1,0:T(8,128)S(1)}, u32[]{:S(2)}, u32[]{:S(2)}) collective-permute-start(f32[4,88,128]{2,1,0:T(8,128)S(1)} %get-tuple-element.15), channel_id=1, source_target_pairs={{8,0},{16,8},{24,16},{9,1},{17,9},{25,17},{10,2},{18,10},{26,18},{... | collective-permute-start | bytes 540680 | tf_op jit(solution)/shard_map/ppermute | solution.py:561
  16.3 9.1 %mix.1 = (f32[4,32,80,128]{3,2,1,0:T(8,128)}, f32[4,88,128]{2,1,0:T(8,128)}, f32[2,88,128]{2,1,0:T(8,128)S(1)}, f32[2,88,128]{2,1,0:T(8,128)S(1)}) custom-call(s32[32,128]{1,0:T(8,128)} %depth_ref.1, f32[4,80,32,128]{3,2,1,0:T(8,128)} %state_h.3, f32[4,32,1,80,80]{4,3,2,1,0:T(8,128)} %inv_h.3), custom_call_target="tpu_custom_call" | custom-call | flops 838860800 | bytes 16777216 | tf_op jit(solution)/shard_map/mix/pallas_call | solution.py:317
  25.3 0.0 collective-permute-done.after_north.north_h
  25.3 0.0 copy-start
  25.4 0.0 collective-permute-done.1.after_south.south_h
  25.4 0.0 copy-start.1
  25.4 2.2 %all-to-all-done.recv = f32[8,272,128]{2,1,0:T(8,128)S(1)} async-done(((f32[8,272,128]{2,1,0:T(8,128)}), f32[8,272,128]{2,1,0:T(8,128)S(1)}, u32[]{:S(2)}, u32[]{:S(2)}) %all-to-all-start) | async-done | bytes 1114144 | tf_op jit(solution)/shard_map/all_to_all | solution.py:575
  27.6 1.3 %collect.1 = f32[4,144,128]{2,1,0:T(8,128)} custom-call(f32[8,272,128]{2,1,0:T(8,128)S(1)} %all-to-all-done.recv, f32[2,88,128]{2,1,0:T(8,128)S(1)} %get-tuple-element.13.after_mix, f32[4,88,128]{2,1,0:T(8,128)S(1)} %collective-permute-done.after_north.north_h, f32[4,88,128]{2,1,0:T(8,128)S(1)} %collective-permute-done.1.after_south.south_h), custom_call_target="tpu_custom_call" | custom-call | tf_op jit(solution)/shard_map/collect/pallas_call | solution.py:384
  28.9 4.9 %all-to-all-start.1 = ((f32[4,144,128]{2,1,0:T(8,128)}), f32[4,144,128]{2,1,0:T(8,128)S(1)}, u32[]{:S(2)}, u32[]{:S(2)}) async-start(f32[4,144,128]{2,1,0:T(8,128)} %collect.1), calls=%async_computation.1 | async-start | bytes 589824 | tf_op jit(solution)/shard_map/all_to_all | solution.py:583
  33.8 0.7 %collective-permute-start.2 = (f32[2,88,128]{2,1,0:T(8,128)S(1)}, f32[2,88,128]{2,1,0:T(8,128)S(1)}, u32[]{:S(2)}, u32[]{:S(2)}) collective-permute-start(f32[2,88,128]{2,1,0:T(8,128)S(1)} %get-tuple-element.18), channel_id=1, source_target_pairs={{0,7},{1,0},{2,1},{3,2},{4,3},{5,4},{6,5},{7,6},{8,15},{9,8},{10,9... | collective-permute-start | bytes 270344 | tf_op jit(solution)/shard_map/ppermute | solution.py:561
  34.5 0.0 collective-permute-start.3
  34.5 2.6 %collective-permute-done.2.east = f32[2,88,128]{2,1,0:T(8,128)S(1)} collective-permute-done((f32[2,88,128]{2,1,0:T(8,128)S(1)}, f32[2,88,128]{2,1,0:T(8,128)S(1)}, u32[]{:S(2)}, u32[]{:S(2)}) %collective-permute-start.2) | collective-permute-done | bytes 90144 | tf_op jit(solution)/shard_map/ppermute | solution.py:561
  37.1 2.2 %collective-permute-done.3.west = f32[2,88,128]{2,1,0:T(8,128)S(1)} collective-permute-done((f32[2,88,128]{2,1,0:T(8,128)S(1)}, f32[2,88,128]{2,1,0:T(8,128)S(1)}, u32[]{:S(2)}, u32[]{:S(2)}) %collective-permute-start.3) | collective-permute-done | bytes 90144 | tf_op jit(solution)/shard_map/ppermute | solution.py:561
  39.3 3.1 %all-to-all-done.1.recv = f32[4,144,128]{2,1,0:T(8,128)S(1)} async-done(((f32[4,144,128]{2,1,0:T(8,128)}), f32[4,144,128]{2,1,0:T(8,128)S(1)}, u32[]{:S(2)}, u32[]{:S(2)}) %all-to-all-start.1) | async-done | bytes 294944 | tf_op jit(solution)/shard_map/all_to_all | solution.py:583
  42.4 0.0 copy-done
  42.4 0.0 copy-done.1
  42.4 0.0 copy-done.2
  42.4 8.8 %finish.1 = f32[4,80,32,128]{3,2,1,0:T(8,128)} custom-call(f32[4,144,128]{2,1,0:T(8,128)S(1)} %all-to-all-done.1.recv, s32[32,128]{1,0:T(8,128)S(1)} %copy-done.2, f32[4,32,80,128]{3,2,1,0:T(8,128)} %get-tuple-element.16.mixed_h, f32[4,88,128]{2,1,0:T(8,128)} %get-tuple-element.17.own_h, f32[4,88,128]{2,1,0:T(8,128)} %copy-done, f32[4,88,128]{2,1,0:T(8,128)} %copy-done.1, ...), custom_call_target="tpu_custom_call" | custom-call | flops 26214400 | bytes 12582912 | tf_op jit(solution)/shard_map/finish/pallas_call | solution.py:531
Async XLA Ops:
  6.3 21.3 %all-to-all-start = ((f32[8,272,128]{2,1,0:T(8,128)}), f32[8,272,128]{2,1,0:T(8,128)S(1)}, u32[]{:S(2)}, u32[]{:S(2)}) async-start(f32[8,272,128]{2,1,0:T(8,128)} %get-tuple-element.12), calls=%async_computation | async-start | bytes 2228224 | tf_op jit(solution)/shard_map/all_to_all | solution.py:575
  11.5 13.9 %collective-permute-start = (f32[4,88,128]{2,1,0:T(8,128)S(1)}, f32[4,88,128]{2,1,0:T(8,128)S(1)}, u32[]{:S(2)}, u32[]{:S(2)}) collective-permute-start(f32[4,88,128]{2,1,0:T(8,128)S(1)} %get-tuple-element.14), channel_id=1, source_target_pairs={{0,8},{8,16},{16,24},{1,9},{9,17},{17,25},{2,10},{10,18},{18,26},{... | collective-permute-start | bytes 540680 | tf_op jit(solution)/shard_map/ppermute | solution.py:561
  15.0 27.4 %copy-start.2 = (s32[32,128]{1,0:T(8,128)S(1)}, s32[32,128]{1,0:T(8,128)}, u32[]{:S(2)}) copy-start(s32[32,128]{1,0:T(8,128)} %depth_ref.1) | copy-start | bytes 49156
  15.0 10.4 %collective-permute-start.1 = (f32[4,88,128]{2,1,0:T(8,128)S(1)}, f32[4,88,128]{2,1,0:T(8,128)S(1)}, u32[]{:S(2)}, u32[]{:S(2)}) collective-permute-start(f32[4,88,128]{2,1,0:T(8,128)S(1)} %get-tuple-element.15), channel_id=1, source_target_pairs={{8,0},{16,8},{24,16},{9,1},{17,9},{25,17},{10,2},{18,10},{26,18},{... | collective-permute-start | bytes 540680 | tf_op jit(solution)/shard_map/ppermute | solution.py:561
  25.3 17.0 %copy-start = (f32[4,88,128]{2,1,0:T(8,128)}, f32[4,88,128]{2,1,0:T(8,128)S(1)}, u32[]{:S(2)}) copy-start(f32[4,88,128]{2,1,0:T(8,128)S(1)} %collective-permute-done.after_north.north_h) | copy-start | bytes 540676
  25.4 17.0 %copy-start.1 = (f32[4,88,128]{2,1,0:T(8,128)}, f32[4,88,128]{2,1,0:T(8,128)S(1)}, u32[]{:S(2)}) copy-start(f32[4,88,128]{2,1,0:T(8,128)S(1)} %collective-permute-done.1.after_south.south_h) | copy-start | bytes 540676
  28.9 13.5 %all-to-all-start.1 = ((f32[4,144,128]{2,1,0:T(8,128)}), f32[4,144,128]{2,1,0:T(8,128)S(1)}, u32[]{:S(2)}, u32[]{:S(2)}) async-start(f32[4,144,128]{2,1,0:T(8,128)} %collect.1), calls=%async_computation.1 | async-start | bytes 589824 | tf_op jit(solution)/shard_map/all_to_all | solution.py:583
  33.8 3.3 %collective-permute-start.2 = (f32[2,88,128]{2,1,0:T(8,128)S(1)}, f32[2,88,128]{2,1,0:T(8,128)S(1)}, u32[]{:S(2)}, u32[]{:S(2)}) collective-permute-start(f32[2,88,128]{2,1,0:T(8,128)S(1)} %get-tuple-element.18), channel_id=1, source_target_pairs={{0,7},{1,0},{2,1},{3,2},{4,3},{5,4},{6,5},{7,6},{8,15},{9,8},{10,9... | collective-permute-start | bytes 270344 | tf_op jit(solution)/shard_map/ppermute | solution.py:561
  34.5 4.9 %collective-permute-start.3 = (f32[2,88,128]{2,1,0:T(8,128)S(1)}, f32[2,88,128]{2,1,0:T(8,128)S(1)}, u32[]{:S(2)}, u32[]{:S(2)}) collective-permute-start(f32[2,88,128]{2,1,0:T(8,128)S(1)} %get-tuple-element.13.after_mix), channel_id=1, source_target_pairs={{0,1},{1,2},{2,3},{3,4},{4,5},{5,6},{6,7},{7,0},{8,9},{9,10},{10,1... | collective-permute-start | bytes 270344 | tf_op jit(solution)/shard_map/ppermute | solution.py:561

commit v16 on v15

--- a/solution.py
+++ b/solution.py
@@ -470,9 +470,8 @@
     block = 2 * SUB
     ends = (lanes == 0) | (lanes == LANES - 1)
 
-    def field(q, carry):
-        @pl.when(q + 1 < fields)
-        def _():
+    def field(q):
+        if q + 1 < fields:
             for c in range(oy // SUB):
                 load(q + 1, c).start()
 
@@ -516,9 +515,9 @@
             solve(c)
             diffuse(c - 1)
         diffuse(oy // block - 1)
-        return carry
-
-    lax.fori_loop(0, fields, field, 0)
+
+    for q in range(fields):
+        field(q)
     for q in range(fields):
         pltpu.make_async_copy(stage.at[q], mixed_h.at[q], out_sems.at[q]).wait()
 

time: 51.6 us -> 51.6 us (level)
  no operation moved by 1% of the time
where the time goes in v16:
time: 51.6 us; the launch traced here: 51.2 us
  Pallas kernels  25.4 us (49%)
  starting transfers between devices  15.5 us (30%)
  waiting for transfers between devices  10.1 us (20%)
    pallas_call x1, Pallas kernels, mix(): pl.pallas_call(mix_kernel, in_specs=[HBM] * 3, out_specs=[HBM] * 2 + [VME...  9.06 us
    pallas_call x1, Pallas kernels, finish(): pl.pallas_call(finish_kernel, in_specs=[VMEM] * 2 + [HBM] * 4 + [VMEM] *...  8.8 us
    pallas_call x1, Pallas kernels, regrid(): pl.pallas_call(functools.partial(regrid_kernel, cap, lat, lon, oy, batch)...  6.28 us
    ppermute x4, starting transfers between devices, shift(): return lax.ppermute(x, axis, pairs)  5.48 us
    all_to_all x1, starting transfers between devices, on_device(): in_plane = lax.all_to_all(slots, 'lon', 0, 0, tiled=True)  5.18 us
    all_to_all x1, starting transfers between devices, on_device(): lax.all_to_all(collect(cap, fields, oy, lat, in_plane, (to_east, *halos[0...  4.87 us
    ppermute x4, waiting for transfers between devices, shift(): return lax.ppermute(x, axis, pairs)  4.85 us
    all_to_all x1, waiting for transfers between devices, on_device(): lax.all_to_all(collect(cap, fields, oy, lat, in_plane, (to_east, *halos[0...  3.06 us
  transfers between devices with their start and end apart: 6, of which 4 were waited for; matrix products, arithmetic and copies ran while one was open for 0% of the time, Pallas kernels for 18%

profile of v16, /device:TPU:0, one launch (start us, length us, event | category | flops | bytes accessed | tf_op | source)
XLA Modules:
  0.0 51.2 jit_solution(1092560553217517670)
XLA Ops:
  0.0 6.3 %regrid.1 = (f32[8,272,128]{2,1,0:T(8,128)}, f32[4,88,128]{2,1,0:T(8,128)S(1)}, f32[4,88,128]{2,1,0:T(8,128)S(1)}) custom-call(s32[256]{0:T(256)} %src_h.1, s32[256]{0:T(256)} %bitcast.1, s32[256]{0:T(256)} %blk_h.1, f32[4,8]{1,0:T(4,128)} %coupling_h.1, bf16[8,64,128]{2,1,0:T(8,128)(2,1)} %atm_h.1, s32[64,128]{1,0:T(8,128)} %mask_h.1, ...), custom_call_target="tpu_custom_call" | custom-call | flops 67108864 | bytes 10485760 | tf_op jit(solution)/shard_map/regrid/pallas_call | solution.py:223
  6.3 5.2 %all-to-all-start = ((f32[8,272,128]{2,1,0:T(8,128)}), f32[8,272,128]{2,1,0:T(8,128)S(1)}, u32[]{:S(2)}, u32[]{:S(2)}) async-start(f32[8,272,128]{2,1,0:T(8,128)} %get-tuple-element.12), calls=%async_computation | async-start | bytes 2228224 | tf_op jit(solution)/shard_map/all_to_all | solution.py:574
  11.5 3.5 %collective-permute-start = (f32[4,88,128]{2,1,0:T(8,128)S(1)}, f32[4,88,128]{2,1,0:T(8,128)S(1)}, u32[]{:S(2)}, u32[]{:S(2)}) collective-permute-start(f32[4,88,128]{2,1,0:T(8,128)S(1)} %get-tuple-element.14), channel_id=1, source_target_pairs={{0,8},{8,16},{16,24},{1,9},{9,17},{17,25},{2,10},{10,18},{18,26},{... | collective-permute-start | bytes 540680 | tf_op jit(solution)/shard_map/ppermute | solution.py:560
  15.0 0.0 copy-start.2
  15.0 1.3 %collective-permute-start.1 = (f32[4,88,128]{2,1,0:T(8,128)S(1)}, f32[4,88,128]{2,1,0:T(8,128)S(1)}, u32[]{:S(2)}, u32[]{:S(2)}) collective-permute-start(f32[4,88,128]{2,1,0:T(8,128)S(1)} %get-tuple-element.15), channel_id=1, source_target_pairs={{8,0},{16,8},{24,16},{9,1},{17,9},{25,17},{10,2},{18,10},{26,18},{... | collective-permute-start | bytes 540680 | tf_op jit(solution)/shard_map/ppermute | solution.py:560
  16.3 9.1 %mix.1 = (f32[4,32,80,128]{3,2,1,0:T(8,128)}, f32[4,88,128]{2,1,0:T(8,128)}, f32[2,88,128]{2,1,0:T(8,128)S(1)}, f32[2,88,128]{2,1,0:T(8,128)S(1)}) custom-call(s32[32,128]{1,0:T(8,128)} %depth_ref.1, f32[4,80,32,128]{3,2,1,0:T(8,128)} %state_h.3, f32[4,32,1,80,80]{4,3,2,1,0:T(8,128)} %inv_h.3), custom_call_target="tpu_custom_call" | custom-call | flops 838860800 | bytes 16777216 | tf_op jit(solution)/shard_map/mix/pallas_call | solution.py:317
  25.3 0.0 collective-permute-done.after_north.north_h
  25.3 0.0 copy-start
  25.4 0.0 collective-permute-done.1.after_south.south_h
  25.4 0.0 copy-start.1
  25.4 2.2 %all-to-all-done.recv = f32[8,272,128]{2,1,0:T(8,128)S(1)} async-done(((f32[8,272,128]{2,1,0:T(8,128)}), f32[8,272,128]{2,1,0:T(8,128)S(1)}, u32[]{:S(2)}, u32[]{:S(2)}) %all-to-all-start) | async-done | bytes 1114144 | tf_op jit(solution)/shard_map/all_to_all | solution.py:574
  27.6 1.3 %collect.1 = f32[4,144,128]{2,1,0:T(8,128)} custom-call(f32[8,272,128]{2,1,0:T(8,128)S(1)} %all-to-all-done.recv, f32[2,88,128]{2,1,0:T(8,128)S(1)} %get-tuple-element.13.after_mix, f32[4,88,128]{2,1,0:T(8,128)S(1)} %collective-permute-done.after_north.north_h, f32[4,88,128]{2,1,0:T(8,128)S(1)} %collective-permute-done.1.after_south.south_h), custom_call_target="tpu_custom_call" | custom-call | tf_op jit(solution)/shard_map/collect/pallas_call | solution.py:384
  28.9 4.9 %all-to-all-start.1 = ((f32[4,144,128]{2,1,0:T(8,128)}), f32[4,144,128]{2,1,0:T(8,128)S(1)}, u32[]{:S(2)}, u32[]{:S(2)}) async-start(f32[4,144,128]{2,1,0:T(8,128)} %collect.1), calls=%async_computation.1 | async-start | bytes 589824 | tf_op jit(solution)/shard_map/all_to_all | solution.py:582
  33.8 0.7 %collective-permute-start.2 = (f32[2,88,128]{2,1,0:T(8,128)S(1)}, f32[2,88,128]{2,1,0:T(8,128)S(1)}, u32[]{:S(2)}, u32[]{:S(2)}) collective-permute-start(f32[2,88,128]{2,1,0:T(8,128)S(1)} %get-tuple-element.18), channel_id=1, source_target_pairs={{0,7},{1,0},{2,1},{3,2},{4,3},{5,4},{6,5},{7,6},{8,15},{9,8},{10,9... | collective-permute-start | bytes 270344 | tf_op jit(solution)/shard_map/ppermute | solution.py:560
  34.5 0.0 collective-permute-start.3
  34.5 2.6 %collective-permute-done.2.east = f32[2,88,128]{2,1,0:T(8,128)S(1)} collective-permute-done((f32[2,88,128]{2,1,0:T(8,128)S(1)}, f32[2,88,128]{2,1,0:T(8,128)S(1)}, u32[]{:S(2)}, u32[]{:S(2)}) %collective-permute-start.2) | collective-permute-done | bytes 90144 | tf_op jit(solution)/shard_map/ppermute | solution.py:560
  37.1 2.2 %collective-permute-done.3.west = f32[2,88,128]{2,1,0:T(8,128)S(1)} collective-permute-done((f32[2,88,128]{2,1,0:T(8,128)S(1)}, f32[2,88,128]{2,1,0:T(8,128)S(1)}, u32[]{:S(2)}, u32[]{:S(2)}) %collective-permute-start.3) | collective-permute-done | bytes 90144 | tf_op jit(solution)/shard_map/ppermute | solution.py:560
  39.3 3.1 %all-to-all-done.1.recv = f32[4,144,128]{2,1,0:T(8,128)S(1)} async-done(((f32[4,144,128]{2,1,0:T(8,128)}), f32[4,144,128]{2,1,0:T(8,128)S(1)}, u32[]{:S(2)}, u32[]{:S(2)}) %all-to-all-start.1) | async-done | bytes 294944 | tf_op jit(solution)/shard_map/all_to_all | solution.py:582
  42.4 0.0 copy-done
  42.4 0.0 copy-done.1
  42.4 0.0 copy-done.2
  42.4 8.8 %finish.1 = f32[4,80,32,128]{3,2,1,0:T(8,128)} custom-call(f32[4,144,128]{2,1,0:T(8,128)S(1)} %all-to-all-done.1.recv, s32[32,128]{1,0:T(8,128)S(1)} %copy-done.2, f32[4,32,80,128]{3,2,1,0:T(8,128)} %get-tuple-element.16.mixed_h, f32[4,88,128]{2,1,0:T(8,128)} %get-tuple-element.17.own_h, f32[4,88,128]{2,1,0:T(8,128)} %copy-done, f32[4,88,128]{2,1,0:T(8,128)} %copy-done.1, ...), custom_call_target="tpu_custom_call" | custom-call | flops 26214400 | bytes 12582912 | tf_op jit(solution)/shard_map/finish/pallas_call | solution.py:530
Async XLA Ops:
  6.3 21.3 %all-to-all-start = ((f32[8,272,128]{2,1,0:T(8,128)}), f32[8,272,128]{2,1,0:T(8,128)S(1)}, u32[]{:S(2)}, u32[]{:S(2)}) async-start(f32[8,272,128]{2,1,0:T(8,128)} %get-tuple-element.12), calls=%async_computation | async-start | bytes 2228224 | tf_op jit(solution)/shard_map/all_to_all | solution.py:574
  11.5 13.9 %collective-permute-start = (f32[4,88,128]{2,1,0:T(8,128)S(1)}, f32[4,88,128]{2,1,0:T(8,128)S(1)}, u32[]{:S(2)}, u32[]{:S(2)}) collective-permute-start(f32[4,88,128]{2,1,0:T(8,128)S(1)} %get-tuple-element.14), channel_id=1, source_target_pairs={{0,8},{8,16},{16,24},{1,9},{9,17},{17,25},{2,10},{10,18},{18,26},{... | collective-permute-start | bytes 540680 | tf_op jit(solution)/shard_map/ppermute | solution.py:560
  15.0 27.4 %copy-start.2 = (s32[32,128]{1,0:T(8,128)S(1)}, s32[32,128]{1,0:T(8,128)}, u32[]{:S(2)}) copy-start(s32[32,128]{1,0:T(8,128)} %depth_ref.1) | copy-start | bytes 49156
  15.0 10.4 %collective-permute-start.1 = (f32[4,88,128]{2,1,0:T(8,128)S(1)}, f32[4,88,128]{2,1,0:T(8,128)S(1)}, u32[]{:S(2)}, u32[]{:S(2)}) collective-permute-start(f32[4,88,128]{2,1,0:T(8,128)S(1)} %get-tuple-element.15), channel_id=1, source_target_pairs={{8,0},{16,8},{24,16},{9,1},{17,9},{25,17},{10,2},{18,10},{26,18},{... | collective-permute-start | bytes 540680 | tf_op jit(solution)/shard_map/ppermute | solution.py:560
  25.3 17.0 %copy-start = (f32[4,88,128]{2,1,0:T(8,128)}, f32[4,88,128]{2,1,0:T(8,128)S(1)}, u32[]{:S(2)}) copy-start(f32[4,88,128]{2,1,0:T(8,128)S(1)} %collective-permute-done.after_north.north_h) | copy-start | bytes 540676
  25.4 17.0 %copy-start.1 = (f32[4,88,128]{2,1,0:T(8,128)}, f32[4,88,128]{2,1,0:T(8,128)S(1)}, u32[]{:S(2)}) copy-start(f32[4,88,128]{2,1,0:T(8,128)S(1)} %collective-permute-done.1.after_south.south_h) | copy-start | bytes 540676
  28.9 13.5 %all-to-all-start.1 = ((f32[4,144,128]{2,1,0:T(8,128)}), f32[4,144,128]{2,1,0:T(8,128)S(1)}, u32[]{:S(2)}, u32[]{:S(2)}) async-start(f32[4,144,128]{2,1,0:T(8,128)} %collect.1), calls=%async_computation.1 | async-start | bytes 589824 | tf_op jit(solution)/shard_map/all_to_all | solution.py:582
  33.8 3.3 %collective-permute-start.2 = (f32[2,88,128]{2,1,0:T(8,128)S(1)}, f32[2,88,128]{2,1,0:T(8,128)S(1)}, u32[]{:S(2)}, u32[]{:S(2)}) collective-permute-start(f32[2,88,128]{2,1,0:T(8,128)S(1)} %get-tuple-element.18), channel_id=1, source_target_pairs={{0,7},{1,0},{2,1},{3,2},{4,3},{5,4},{6,5},{7,6},{8,15},{9,8},{10,9... | collective-permute-start | bytes 270344 | tf_op jit(solution)/shard_map/ppermute | solution.py:560
  34.5 4.9 %collective-permute-start.3 = (f32[2,88,128]{2,1,0:T(8,128)S(1)}, f32[2,88,128]{2,1,0:T(8,128)S(1)}, u32[]{:S(2)}, u32[]{:S(2)}) collective-permute-start(f32[2,88,128]{2,1,0:T(8,128)S(1)} %get-tuple-element.13.after_mix), channel_id=1, source_target_pairs={{0,1},{1,2},{2,3},{3,4},{4,5},{5,6},{6,7},{7,0},{8,9},{9,10},{10,1... | collective-permute-start | bytes 270344 | tf_op jit(solution)/shard_map/ppermute | solution.py:560

commit v17 on v16

--- a/solution.py
+++ b/solution.py
@@ -82,10 +82,10 @@
     per = fields * cap
     slot_rows = lat * per
     parts = weights.shape[0] // batch
-    ahead = min(2, parts)
+    ahead = min(3, parts)
 
     def big(k):
-        here = pl.ds(pl.multiple_of(k * batch, batch), batch)
+        here = pl.ds(k * batch, batch)
         return pltpu.make_async_copy(weights_h.at[here], weights.at[here], big_sem.at[k])
 
     small = [
@@ -157,11 +157,9 @@
         a, b = place(d)
         return padded_rows(out[b, a * per : (a + 1) * per, :], HALF)
 
-    def part(k, carry):
+    def part(k):
         big(k).wait()
-
-        @pl.when(k + ahead < parts)
-        def _():
+        if k + ahead < parts:
             big(k + ahead).start()
 
         for u in range(0, batch, 2):
@@ -179,9 +177,9 @@
                 out[b, pl.ds(a * per + slot * fields, fields), :] = half[0:fields] + half[fields : 2 * fields]
                 line = ids[pl.ds(d, 1), :]
                 ids[pl.ds(d, 1), :] = jnp.where(lane_slot == slot, lane_row + blk[p + v], line)
-        return carry
-
-    lax.fori_loop(0, parts, part, 0)
+
+    for k in range(parts):
+        part(k)
 
     def send(k, start, stop):
         return pltpu.make_async_copy(out.at[:, start:stop, :], out_h.at[:, start:stop, :], out_sem.at[k])
@@ -217,7 +215,7 @@
     pairs, cells, width = weights.shape
     fields, levels, oy, ox = ocean.shape
     message = jax.ShapeDtypeStruct((fields, levels + SUB, ox), f32)
-    batch = 64
+    batch = 32
     devices = lat * lon
     tall = lat * fields * cap + extra_rows(lat)
     return pl.pallas_call(

time: 51.6 us -> 52.3 us (1.014)
  transfers between devices with their start and end apart: 6 -> 6, of which waited for: 4 -> 4; matrix products, arithmetic and copies ran while one was open for 0% -> 0% of each run, Pallas kernels for 18% -> 17%
where the time goes in v17:
time: 52.3 us; the launch traced here: 51.9 us
  Pallas kernels  25.9 us (50%)
  starting transfers between devices  15.5 us (30%)
  waiting for transfers between devices  10.1 us (19%)
    pallas_call x1, Pallas kernels, mix(): pl.pallas_call(mix_kernel, in_specs=[HBM] * 3, out_specs=[HBM] * 2 + [VME...  9.06 us
    pallas_call x1, Pallas kernels, finish(): pl.pallas_call(finish_kernel, in_specs=[VMEM] * 2 + [HBM] * 4 + [VMEM] *...  8.8 us
    pallas_call x1, Pallas kernels, regrid(): pl.pallas_call(functools.partial(regrid_kernel, cap, lat, lon, oy, batch)...  6.78 us
    ppermute x4, starting transfers between devices, shift(): return lax.ppermute(x, axis, pairs)  5.48 us
    all_to_all x1, starting transfers between devices, on_device(): in_plane = lax.all_to_all(slots, 'lon', 0, 0, tiled=True)  5.18 us
    all_to_all x1, starting transfers between devices, on_device(): lax.all_to_all(collect(cap, fields, oy, lat, in_plane, (to_east, *halos[0...  4.87 us
    ppermute x4, waiting for transfers between devices, shift(): return lax.ppermute(x, axis, pairs)  4.85 us
    all_to_all x1, waiting for transfers between devices, on_device(): lax.all_to_all(collect(cap, fields, oy, lat, in_plane, (to_east, *halos[0...  3.06 us
  transfers between devices with their start and end apart: 6, of which 4 were waited for; matrix products, arithmetic and copies ran while one was open for 0% of the time, Pallas kernels for 17%

profile of v17, /device:TPU:0, one launch (start us, length us, event | category | flops | bytes accessed | tf_op | source)
XLA Modules:
  0.0 51.9 jit_solution(12529104063208360390)
XLA Ops:
  0.0 6.8 %regrid.1 = (f32[8,272,128]{2,1,0:T(8,128)}, f32[4,88,128]{2,1,0:T(8,128)S(1)}, f32[4,88,128]{2,1,0:T(8,128)S(1)}) custom-call(s32[256]{0:T(256)} %src_h.1, s32[256]{0:T(256)} %bitcast.1, s32[256]{0:T(256)} %blk_h.1, f32[4,8]{1,0:T(4,128)} %coupling_h.1, bf16[8,64,128]{2,1,0:T(8,128)(2,1)} %atm_h.1, s32[64,128]{1,0:T(8,128)} %mask_h.1, ...), custom_call_target="tpu_custom_call" | custom-call | flops 67108864 | bytes 10485760 | tf_op jit(solution)/shard_map/regrid/pallas_call | solution.py:221
  6.8 5.2 %all-to-all-start = ((f32[8,272,128]{2,1,0:T(8,128)}), f32[8,272,128]{2,1,0:T(8,128)S(1)}, u32[]{:S(2)}, u32[]{:S(2)}) async-start(f32[8,272,128]{2,1,0:T(8,128)} %get-tuple-element.12), calls=%async_computation | async-start | bytes 2228224 | tf_op jit(solution)/shard_map/all_to_all | solution.py:572
  12.0 3.5 %collective-permute-start = (f32[4,88,128]{2,1,0:T(8,128)S(1)}, f32[4,88,128]{2,1,0:T(8,128)S(1)}, u32[]{:S(2)}, u32[]{:S(2)}) collective-permute-start(f32[4,88,128]{2,1,0:T(8,128)S(1)} %get-tuple-element.14), channel_id=1, source_target_pairs={{0,8},{8,16},{16,24},{1,9},{9,17},{17,25},{2,10},{10,18},{18,26},{... | collective-permute-start | bytes 540680 | tf_op jit(solution)/shard_map/ppermute | solution.py:558
  15.5 0.0 copy-start.2
  15.5 1.3 %collective-permute-start.1 = (f32[4,88,128]{2,1,0:T(8,128)S(1)}, f32[4,88,128]{2,1,0:T(8,128)S(1)}, u32[]{:S(2)}, u32[]{:S(2)}) collective-permute-start(f32[4,88,128]{2,1,0:T(8,128)S(1)} %get-tuple-element.15), channel_id=1, source_target_pairs={{8,0},{16,8},{24,16},{9,1},{17,9},{25,17},{10,2},{18,10},{26,18},{... | collective-permute-start | bytes 540680 | tf_op jit(solution)/shard_map/ppermute | solution.py:558
  16.8 9.1 %mix.1 = (f32[4,32,80,128]{3,2,1,0:T(8,128)}, f32[4,88,128]{2,1,0:T(8,128)}, f32[2,88,128]{2,1,0:T(8,128)S(1)}, f32[2,88,128]{2,1,0:T(8,128)S(1)}) custom-call(s32[32,128]{1,0:T(8,128)} %depth_ref.1, f32[4,80,32,128]{3,2,1,0:T(8,128)} %state_h.3, f32[4,32,1,80,80]{4,3,2,1,0:T(8,128)} %inv_h.3), custom_call_target="tpu_custom_call" | custom-call | flops 838860800 | bytes 16777216 | tf_op jit(solution)/shard_map/mix/pallas_call | solution.py:315
  25.8 0.0 collective-permute-done.after_north.north_h
  25.8 0.0 copy-start
  25.9 0.0 collective-permute-done.1.after_south.south_h
  25.9 0.0 copy-start.1
  25.9 2.2 %all-to-all-done.recv = f32[8,272,128]{2,1,0:T(8,128)S(1)} async-done(((f32[8,272,128]{2,1,0:T(8,128)}), f32[8,272,128]{2,1,0:T(8,128)S(1)}, u32[]{:S(2)}, u32[]{:S(2)}) %all-to-all-start) | async-done | bytes 1114144 | tf_op jit(solution)/shard_map/all_to_all | solution.py:572
  28.1 1.3 %collect.1 = f32[4,144,128]{2,1,0:T(8,128)} custom-call(f32[8,272,128]{2,1,0:T(8,128)S(1)} %all-to-all-done.recv, f32[2,88,128]{2,1,0:T(8,128)S(1)} %get-tuple-element.13.after_mix, f32[4,88,128]{2,1,0:T(8,128)S(1)} %collective-permute-done.after_north.north_h, f32[4,88,128]{2,1,0:T(8,128)S(1)} %collective-permute-done.1.after_south.south_h), custom_call_target="tpu_custom_call" | custom-call | tf_op jit(solution)/shard_map/collect/pallas_call | solution.py:382
  29.4 4.9 %all-to-all-start.1 = ((f32[4,144,128]{2,1,0:T(8,128)}), f32[4,144,128]{2,1,0:T(8,128)S(1)}, u32[]{:S(2)}, u32[]{:S(2)}) async-start(f32[4,144,128]{2,1,0:T(8,128)} %collect.1), calls=%async_computation.1 | async-start | bytes 589824 | tf_op jit(solution)/shard_map/all_to_all | solution.py:580
  34.3 0.7 %collective-permute-start.2 = (f32[2,88,128]{2,1,0:T(8,128)S(1)}, f32[2,88,128]{2,1,0:T(8,128)S(1)}, u32[]{:S(2)}, u32[]{:S(2)}) collective-permute-start(f32[2,88,128]{2,1,0:T(8,128)S(1)} %get-tuple-element.18), channel_id=1, source_target_pairs={{0,7},{1,0},{2,1},{3,2},{4,3},{5,4},{6,5},{7,6},{8,15},{9,8},{10,9... | collective-permute-start | bytes 270344 | tf_op jit(solution)/shard_map/ppermute | solution.py:558
  35.0 0.0 collective-permute-start.3
  35.0 2.6 %collective-permute-done.2.east = f32[2,88,128]{2,1,0:T(8,128)S(1)} collective-permute-done((f32[2,88,128]{2,1,0:T(8,128)S(1)}, f32[2,88,128]{2,1,0:T(8,128)S(1)}, u32[]{:S(2)}, u32[]{:S(2)}) %collective-permute-start.2) | collective-permute-done | bytes 90144 | tf_op jit(solution)/shard_map/ppermute | solution.py:558
  37.6 2.2 %collective-permute-done.3.west = f32[2,88,128]{2,1,0:T(8,128)S(1)} collective-permute-done((f32[2,88,128]{2,1,0:T(8,128)S(1)}, f32[2,88,128]{2,1,0:T(8,128)S(1)}, u32[]{:S(2)}, u32[]{:S(2)}) %collective-permute-start.3) | collective-permute-done | bytes 90144 | tf_op jit(solution)/shard_map/ppermute | solution.py:558
  39.8 3.1 %all-to-all-done.1.recv = f32[4,144,128]{2,1,0:T(8,128)S(1)} async-done(((f32[4,144,128]{2,1,0:T(8,128)}), f32[4,144,128]{2,1,0:T(8,128)S(1)}, u32[]{:S(2)}, u32[]{:S(2)}) %all-to-all-start.1) | async-done | bytes 294944 | tf_op jit(solution)/shard_map/all_to_all | solution.py:580
  42.9 0.0 copy-done
  42.9 0.0 copy-done.1
  42.9 0.0 copy-done.2
  42.9 8.8 %finish.1 = f32[4,80,32,128]{3,2,1,0:T(8,128)} custom-call(f32[4,144,128]{2,1,0:T(8,128)S(1)} %all-to-all-done.1.recv, s32[32,128]{1,0:T(8,128)S(1)} %copy-done.2, f32[4,32,80,128]{3,2,1,0:T(8,128)} %get-tuple-element.16.mixed_h, f32[4,88,128]{2,1,0:T(8,128)} %get-tuple-element.17.own_h, f32[4,88,128]{2,1,0:T(8,128)} %copy-done, f32[4,88,128]{2,1,0:T(8,128)} %copy-done.1, ...), custom_call_target="tpu_custom_call" | custom-call | flops 26214400 | bytes 12582912 | tf_op jit(solution)/shard_map/finish/pallas_call | solution.py:528
Async XLA Ops:
  6.8 21.3 %all-to-all-start = ((f32[8,272,128]{2,1,0:T(8,128)}), f32[8,272,128]{2,1,0:T(8,128)S(1)}, u32[]{:S(2)}, u32[]{:S(2)}) async-start(f32[8,272,128]{2,1,0:T(8,128)} %get-tuple-element.12), calls=%async_computation | async-start | bytes 2228224 | tf_op jit(solution)/shard_map/all_to_all | solution.py:572
  12.0 13.9 %collective-permute-start = (f32[4,88,128]{2,1,0:T(8,128)S(1)}, f32[4,88,128]{2,1,0:T(8,128)S(1)}, u32[]{:S(2)}, u32[]{:S(2)}) collective-permute-start(f32[4,88,128]{2,1,0:T(8,128)S(1)} %get-tuple-element.14), channel_id=1, source_target_pairs={{0,8},{8,16},{16,24},{1,9},{9,17},{17,25},{2,10},{10,18},{18,26},{... | collective-permute-start | bytes 540680 | tf_op jit(solution)/shard_map/ppermute | solution.py:558
  15.5 27.4 %copy-start.2 = (s32[32,128]{1,0:T(8,128)S(1)}, s32[32,128]{1,0:T(8,128)}, u32[]{:S(2)}) copy-start(s32[32,128]{1,0:T(8,128)} %depth_ref.1) | copy-start | bytes 49156
  15.5 10.4 %collective-permute-start.1 = (f32[4,88,128]{2,1,0:T(8,128)S(1)}, f32[4,88,128]{2,1,0:T(8,128)S(1)}, u32[]{:S(2)}, u32[]{:S(2)}) collective-permute-start(f32[4,88,128]{2,1,0:T(8,128)S(1)} %get-tuple-element.15), channel_id=1, source_target_pairs={{8,0},{16,8},{24,16},{9,1},{17,9},{25,17},{10,2},{18,10},{26,18},{... | collective-permute-start | bytes 540680 | tf_op jit(solution)/shard_map/ppermute | solution.py:558
  25.8 17.0 %copy-start = (f32[4,88,128]{2,1,0:T(8,128)}, f32[4,88,128]{2,1,0:T(8,128)S(1)}, u32[]{:S(2)}) copy-start(f32[4,88,128]{2,1,0:T(8,128)S(1)} %collective-permute-done.after_north.north_h) | copy-start | bytes 540676
  25.9 17.0 %copy-start.1 = (f32[4,88,128]{2,1,0:T(8,128)}, f32[4,88,128]{2,1,0:T(8,128)S(1)}, u32[]{:S(2)}) copy-start(f32[4,88,128]{2,1,0:T(8,128)S(1)} %collective-permute-done.1.after_south.south_h) | copy-start | bytes 540676
  29.4 13.5 %all-to-all-start.1 = ((f32[4,144,128]{2,1,0:T(8,128)}), f32[4,144,128]{2,1,0:T(8,128)S(1)}, u32[]{:S(2)}, u32[]{:S(2)}) async-start(f32[4,144,128]{2,1,0:T(8,128)} %collect.1), calls=%async_computation.1 | async-start | bytes 589824 | tf_op jit(solution)/shard_map/all_to_all | solution.py:580
  34.3 3.3 %collective-permute-start.2 = (f32[2,88,128]{2,1,0:T(8,128)S(1)}, f32[2,88,128]{2,1,0:T(8,128)S(1)}, u32[]{:S(2)}, u32[]{:S(2)}) collective-permute-start(f32[2,88,128]{2,1,0:T(8,128)S(1)} %get-tuple-element.18), channel_id=1, source_target_pairs={{0,7},{1,0},{2,1},{3,2},{4,3},{5,4},{6,5},{7,6},{8,15},{9,8},{10,9... | collective-permute-start | bytes 270344 | tf_op jit(solution)/shard_map/ppermute | solution.py:558
  35.0 4.9 %collective-permute-start.3 = (f32[2,88,128]{2,1,0:T(8,128)S(1)}, f32[2,88,128]{2,1,0:T(8,128)S(1)}, u32[]{:S(2)}, u32[]{:S(2)}) collective-permute-start(f32[2,88,128]{2,1,0:T(8,128)S(1)} %get-tuple-element.13.after_mix), channel_id=1, source_target_pairs={{0,1},{1,2},{2,3},{3,4},{4,5},{5,6},{6,7},{7,0},{8,9},{9,10},{10,1... | collective-permute-start | bytes 270344 | tf_op jit(solution)/shard_map/ppermute | solution.py:558
